TPU v7x, 512 devices: a whole 4x8x8 slice. The times are simulated.
512 devices in a mesh: mic: 16 (over y, core), tm: 32 (over x, z).
Axes of the slice: x: 4, y: 8, z: 8, core: 2. Of those that a mesh axis runs over, the one named last changes fastest.
Arguments:
- frames_in: bfloat16 [16, 4096, 768], P('mic', 'tm'), may hold values from -6 to 6
- cotangent: bfloat16 [16, 4096, 768], P('mic', 'tm'), may hold values from -6 to 6
- norm_gain: float32 [768], replicated, may hold values from 0.25 to 1.75
- w_qkv: bfloat16 [768, 2304], P('tm'), may hold values from -0.21875 to 0.21875
- w_out: bfloat16 [768, 768], P('tm'), may hold values from -0.21875 to 0.21875
- lengths: int32 [2], replicated, may hold values from 512 to 2048, as said below
Outputs:
- output: bfloat16 [16, 4096, 768], P('mic', 'tm')
- grad_input: bfloat16 [16, 4096, 768], P('mic', 'tm')
- grad_wout: float32 [768, 768], P('tm')
Inputs may be any that keep to these rules, and one draw needn't show every extreme that they name: Session lengths are between a quarter of a session's 4096 / 2 slots and all of them; at least one session fills all its slots.
All inputs are finite; a program needn't handle non-finite values.
Results may differ from a plain program's by a relative error of at most 0.025.
Values may be sent and summed in bfloat16 or wider, within the bound.
No kernel may reach another device: no remote copies, remote signals or barrier semaphores. Data moves between devices by JAX's collectives and lax.ppermute only.
A program may use at most 64 MiB of HBM per device.

v0:
```python
import jax
import jax.numpy as jnp
from jax import lax
from jax.sharding import PartitionSpec as P

HD = 64
FRM_DEV = 128
SESS = 2


def contract(form, left, right):
    return jnp.einsum(form, left, right, preferred_element_type=jnp.float32)


def frame_valid(frame_ids, lengths, slot_len):
    session = frame_ids // slot_len
    offset = frame_ids - session * slot_len
    session_hit = (
        session[:, None] == jnp.arange(lengths.shape[0], dtype=jnp.int32)[None, :]
    ).astype(jnp.int32)
    valid_len = jnp.sum(session_hit * lengths[None, :], axis=1)
    return (offset < valid_len).astype(jnp.float32)


def block_math(x_block, g_block, valid_rows, norm_gain, w_qkv, w_out):
    mic_count, frame_count, model_width = x_block.shape
    head_count = model_width // HD
    row_total = mic_count * frame_count
    x_float = x_block.astype(jnp.float32)
    inv_rms = lax.rsqrt(jnp.mean(x_float * x_float, axis=-1, keepdims=True) + 1e-05)
    normed = (x_float * inv_rms * norm_gain).astype(jnp.bfloat16)
    rows_qkv = jnp.dot(
        normed.reshape(row_total, model_width), w_qkv, preferred_element_type=jnp.float32
    ).astype(jnp.bfloat16)
    split_rows = rows_qkv.reshape(mic_count, frame_count, 3, head_count, HD)
    queries = split_rows[:, :, 0]
    key_part = split_rows[:, :, 1]
    values_part = split_rows[:, :, 2]
    scores = contract("mfhd,nfhd->fhmn", queries, key_part) * HD ** (-0.5)
    softmax_probs = jax.nn.softmax(scores, axis=-1)
    probs_low = softmax_probs.astype(jnp.bfloat16)
    attended = (
        contract("fhmn,nfhd->mfhd", probs_low, values_part)
        .astype(jnp.bfloat16)
        .reshape(row_total, model_width)
    )
    mixed_out = jnp.dot(attended, w_out, preferred_element_type=jnp.float32).reshape(
        mic_count, frame_count, model_width
    )
    valid_wide = valid_rows[None, :, None]
    output = (valid_wide * (x_float + mixed_out)).astype(jnp.bfloat16)
    grad_y = g_block.astype(jnp.float32) * valid_wide
    grad_z = grad_y.astype(jnp.bfloat16).reshape(row_total, model_width)
    grad_att = jnp.dot(grad_z, w_out.T, preferred_element_type=jnp.float32).astype(jnp.bfloat16)
    grad_att = grad_att.reshape(mic_count, frame_count, head_count, HD)
    grad_probs = contract("mfhd,nfhd->fhmn", grad_att, values_part)
    grad_scores = (
        softmax_probs
        * (grad_probs - jnp.sum(softmax_probs * grad_probs, axis=-1, keepdims=True))
        * HD ** (-0.5)
    )
    grad_low = grad_scores.astype(jnp.bfloat16)
    grad_query = contract("fhmn,nfhd->mfhd", grad_low, key_part)
    grad_key = contract("fhmn,mfhd->nfhd", grad_low, queries)
    grad_value = contract("fhmn,mfhd->nfhd", probs_low, grad_att)
    grad_qkv = (
        jnp.stack([grad_query, grad_key, grad_value], axis=2)
        .astype(jnp.bfloat16)
        .reshape(row_total, 3 * model_width)
    )
    grad_normed = jnp.dot(grad_qkv, w_qkv.T, preferred_element_type=jnp.float32).reshape(
        mic_count, frame_count, model_width
    )
    grad_hat = grad_normed * norm_gain
    inner = jnp.mean(grad_hat * x_float, axis=-1, keepdims=True)
    grad_x = grad_y + inv_rms * (grad_hat - x_float * inv_rms * inv_rms * inner)
    return (output, grad_x.astype(jnp.bfloat16), attended, grad_z)


def per_device(frames_in, cotangent, norm_gain, w_qkv, w_out, lengths):
    full_qkv, full_out = (
        lax.all_gather(w_qkv, "tm", axis=0, tiled=True),
        lax.all_gather(w_out, "tm", axis=0, tiled=True),
    )
    local_x, local_g = (
        lax.all_to_all(frames_in, "mic", split_axis=1, concat_axis=0, tiled=True),
        lax.all_to_all(cotangent, "mic", split_axis=1, concat_axis=0, tiled=True),
    )
    frame_count = local_x.shape[1]
    time_count = lax.axis_size("tm")
    first_frame = lax.axis_index("tm") * FRM_DEV + lax.axis_index("mic") * frame_count
    frame_ids = first_frame + jnp.arange(frame_count, dtype=jnp.int32)
    valid_rows = frame_valid(frame_ids, lengths, FRM_DEV * time_count // SESS)
    output, grad_x, attended, grad_z = block_math(
        local_x, local_g, valid_rows, norm_gain, full_qkv, full_out
    )
    out_y, out_dx = (
        lax.all_to_all(output, "mic", split_axis=0, concat_axis=1, tiled=True),
        lax.all_to_all(grad_x, "mic", split_axis=0, concat_axis=1, tiled=True),
    )
    local_term = jnp.dot(attended.T, grad_z, preferred_element_type=jnp.float32)
    mic_sum = lax.psum(local_term.astype(jnp.bfloat16), "mic")
    grad_wout = lax.psum_scatter(mic_sum, "tm", scatter_dimension=0, tiled=True).astype(jnp.float32)
    return (out_y, out_dx, grad_wout)


def solution(mesh):
    return jax.shard_map(
        per_device,
        mesh=mesh,
        in_specs=(
            P("mic", "tm", None),
            P("mic", "tm", None),
            P(),
            P("tm", None),
            P("tm", None),
            P(),
        ),
        out_specs=(P("mic", "tm", None), P("mic", "tm", None), P("tm", None)),
        check_vma=False,
    )
```

profile of v0, /device:TPU:1, one launch (start us, length us, event | category | flops | bytes accessed | tf_op | source)
XLA Modules:
  0.0 456.8 jit_solution(17353197115874694086)
XLA Ops:
  8.7 1.2 copy.109
  10.4 1.8 reduce.1
  12.2 0.8 reshape.152
  13.0 10.2 %all-to-all-start = ((bf16[16,2,3072]{2,1,0:T(2,128)(2,1)}), bf16[16,2,3072]{2,1,0:T(2,128)(2,1)S(1)}, u32[]{:S(2)}, u32[]{:S(2)}) async-start(bf16[16,2,3072]{2,1,0:T(2,128)(2,1)} %reshape.152), calls=%async_computation | async-start | bytes 393216 | tf_op jit(solution)/shard_map/all_to_all | solution.py:86
  23.7 1.8 reduce.2
  25.5 0.7 reshape.154
  26.3 7.3 %all-to-all-done = bf16[16,2,3072]{2,1,0:T(2,128)(2,1)S(1)} async-done(((bf16[16,2,3072]{2,1,0:T(2,128)(2,1)}), bf16[16,2,3072]{2,1,0:T(2,128)(2,1)S(1)}, u32[]{:S(2)}, u32[]{:S(2)}) %all-to-all-start) | async-done | bytes 196640 | tf_op jit(solution)/shard_map/all_to_all | solution.py:86
  33.5 3.4 all-to-all-start.2
  37.4 9.4 %all-to-all-done.2 = bf16[16,2,3072]{2,1,0:T(2,128)(2,1)S(1)} async-done(((bf16[16,2,3072]{2,1,0:T(2,128)(2,1)}), bf16[16,2,3072]{2,1,0:T(2,128)(2,1)S(1)}, u32[]{:S(2)}, u32[]{:S(2)}) %all-to-all-start.2) | async-done | bytes 196640 | tf_op jit(solution)/shard_map/all_to_all | solution.py:87
  47.0 47.9 %all-gather.5.cloned.1.call-done = bf16[768,768]{1,0:T(8,128)(2,1)} async-done(((bf16[24,768]{1,0:T(8,128)(2,1)}), bf16[768,768]{1,0:T(8,128)(2,1)}) %all-gather.5.cloned.1.call-update) | async-done | bytes 1179664 | tf_op jit(solution)/shard_map/all_gather | solution.py:83
  94.8 1.8 convolution_convert_fusion.6
  97.0 86.1 %all-gather.3.cloned.1.call-done = bf16[768,2304]{1,0:T(8,128)(2,1)} async-done(((bf16[24,2304]{1,0:T(8,128)(2,1)}), bf16[768,2304]{1,0:T(8,128)(2,1)}) %all-gather.3.cloned.1.call-update) | async-done | bytes 3538960 | tf_op jit(solution)/shard_map/all_gather | solution.py:82
  183.1 2.7 convolution_convert_fusion
  185.8 1.0 reshape.143
  186.8 1.5 fusion.68
  188.3 2.8 fusion.69
  191.1 1.5 fusion.10
  193.4 1.6 convolution_convert_fusion.1
  195.0 1.0 fusion.19
  196.0 11.1 %all-to-all-start.1 = ((bf16[16,8,768]{2,1,0:T(8,128)(2,1)}), bf16[16,8,768]{2,1,0:T(8,128)(2,1)}, u32[]{:S(2)}, u32[]{:S(2)}) async-start(bf16[16,8,768]{2,1,0:T(8,128)(2,1)} %fusion.19), calls=%async_computation.1 | async-start | bytes 393216 | tf_op jit(solution)/shard_map/all_to_all | solution.py:98
  207.6 2.0 fusion.11
  209.7 2.0 fusion.12
  211.7 1.5 fusion.13
  213.5 1.6 copy.64
  215.1 2.9 convert_element_type.114
  218.0 2.5 fusion.35
  220.6 1.1 fusion.34
  221.6 7.2 %all-to-all-start.3 = ((bf16[16,8,768]{2,1,0:T(8,128)(2,1)}), bf16[16,8,768]{2,1,0:T(8,128)(2,1)S(1)}, u32[]{:S(2)}, u32[]{:S(2)}) async-start(bf16[16,8,768]{2,1,0:T(8,128)(2,1)} %fusion.34), calls=%async_computation.3 | async-start | bytes 393216 | tf_op jit(solution)/shard_map/all_to_all | solution.py:99
  228.9 10.3 %all-to-all-done.3 = bf16[16,8,768]{2,1,0:T(8,128)(2,1)S(1)} async-done(((bf16[16,8,768]{2,1,0:T(8,128)(2,1)}), bf16[16,8,768]{2,1,0:T(8,128)(2,1)S(1)}, u32[]{:S(2)}, u32[]{:S(2)}) %all-to-all-start.3) | async-done | bytes 196640 | tf_op jit(solution)/shard_map/all_to_all | solution.py:99
  239.2 159.4 %reduce-scatter.2.cloned.1.call-done = bf16[24,768]{1,0:T(8,128)(2,1)} async-done(((bf16[768,768]{1,0:T(8,128)(2,1)}), bf16[24,768]{1,0:T(8,128)(2,1)}) %reduce-scatter.2.cloned.1.call-update) | async-done | bytes 36880 | tf_op jit(solution)/shard_map/reduce_scatter | solution.py:103
  398.5 48.8 %psum.8 = bf16[24,768]{1,0:T(8,128)(2,1)S(1)} all-reduce(bf16[24,768]{1,0:T(8,128)(2,1)} %reduce-scatter.2.cloned.1.call-done), channel_id=1, replica_groups=mesh['mic'=16,'tm'=32] {'mic'}, use_global_device_ids=true, to_apply=%region_6.7 | all-reduce | flops 18432 | bytes 73728 | tf_op jit(solution)/shard_map/psum | solution.py:102
  448.0 1.6 copy.112
  (50 shorter events, 6.3 us)
Async XLA Ops:
  7.2 16.0 %copy-start.10 = (s32[2]{0:T(128)S(1)}, s32[2]{0:T(128)}, u32[]{:S(2)}) copy-start(s32[2]{0:T(128)} %param.11) | copy-start | bytes 28
  7.2 16.2 %copy-start.8 = (bf16[1,128,768]{2,1,0:T(8,128)(2,1)S(1)}, bf16[1,128,768]{2,1,0:T(8,128)(2,1)}, u32[]{:S(2)}) copy-start(bf16[1,128,768]{2,1,0:T(8,128)(2,1)} %param.7) | copy-start | bytes 589828
  7.2 87.6 %all-gather.5.cloned.1.call-start = ((), (), s32[]{:S(2)}) async-start(), calls=%async_computation.6 | async-start | bytes 1216512 | tf_op jit(solution)/shard_map/all_gather | solution.py:83
  7.9 175.2 %all-gather.3.cloned.1.call-start = ((), (), s32[]{:S(2)}) async-start(), calls=%async_computation.5 | async-start | bytes 3649536 | tf_op jit(solution)/shard_map/all_gather | solution.py:82
  13.0 20.6 %all-to-all-start = ((bf16[16,2,3072]{2,1,0:T(2,128)(2,1)}), bf16[16,2,3072]{2,1,0:T(2,128)(2,1)S(1)}, u32[]{:S(2)}, u32[]{:S(2)}) async-start(bf16[16,2,3072]{2,1,0:T(2,128)(2,1)} %reshape.152), calls=%async_computation | async-start | bytes 393216 | tf_op jit(solution)/shard_map/all_to_all | solution.py:86
  33.5 13.2 %all-to-all-start.2 = ((bf16[16,2,3072]{2,1,0:T(2,128)(2,1)}), bf16[16,2,3072]{2,1,0:T(2,128)(2,1)S(1)}, u32[]{:S(2)}, u32[]{:S(2)}) async-start(bf16[16,2,3072]{2,1,0:T(2,128)(2,1)} %reshape.154), calls=%async_computation.2 | async-start | bytes 393216 | tf_op jit(solution)/shard_map/all_to_all | solution.py:87
  37.0 361.6 %reduce-scatter.2.cloned.1.call-start = ((), (), s32[]{:S(2)}) async-start(), calls=%async_computation.7 | async-start | bytes 1216512 | tf_op jit(solution)/shard_map/reduce_scatter | solution.py:103
  37.3 157.7 %copy-start.1 = (bf16[1,128,768]{2,1,0:T(8,128)(2,1)}, bf16[1,128,768]{2,1,0:T(8,128)(2,1)S(1)}, u32[]{:S(2)}) copy-start(bf16[1,128,768]{2,1,0:T(8,128)(2,1)S(1)} %get-tuple-element.4) | copy-start | bytes 589828
  46.9 146.4 %copy-start.4 = (bf16[128,1,768]{2,1,0:T(2,128)(2,1)}, bf16[128,1,768]{2,1,0:T(2,128)(2,1)S(1)}, u32[]{:S(2)}) copy-start(bf16[128,1,768]{2,1,0:T(2,128)(2,1)S(1)} %reshape.155) | copy-start | bytes 589828
  46.9 136.2 %copy-start.9 = (f32[768]{0:T(1024)S(1)}, f32[768]{0:T(1024)}, u32[]{:S(2)}) copy-start(f32[768]{0:T(1024)} %param.8) | copy-start | bytes 9220
  193.4 1.6 copy-start.3
  196.0 11.6 %copy-start.7 = (bf16[16,8,1,12,64]{4,3,2,1,0:T(8,128)(2,1)S(1)}, bf16[16,8,1,12,64]{4,3,2,1,0:T(8,128)(2,1)}, u32[]{:S(2)}) copy-start(bf16[16,8,1,12,64]{4,3,2,1,0:T(8,128)(2,1)} %get-tuple-element.5) | copy-start | bytes 589828
  196.0 25.6 %all-to-all-start.1 = ((bf16[16,8,768]{2,1,0:T(8,128)(2,1)}), bf16[16,8,768]{2,1,0:T(8,128)(2,1)}, u32[]{:S(2)}, u32[]{:S(2)}) async-start(bf16[16,8,768]{2,1,0:T(8,128)(2,1)} %fusion.19), calls=%async_computation.1 | async-start | bytes 393216 | tf_op jit(solution)/shard_map/all_to_all | solution.py:98
  207.6 2.1 copy-start.6
  213.5 4.5 copy-start
  218.0 2.6 copy-start.2
  218.0 2.6 copy-start.5
  221.6 17.5 %all-to-all-start.3 = ((bf16[16,8,768]{2,1,0:T(8,128)(2,1)}), bf16[16,8,768]{2,1,0:T(8,128)(2,1)S(1)}, u32[]{:S(2)}, u32[]{:S(2)}) async-start(bf16[16,8,768]{2,1,0:T(8,128)(2,1)} %fusion.34), calls=%async_computation.3 | async-start | bytes 393216 | tf_op jit(solution)/shard_map/all_to_all | solution.py:99
Sparse Core Ops, SparseCore 0:
  11.2 83.5 all-gather.4
  98.0 85.0 all-gather.2
  195.1 203.3 reduce-scatter.1
where the time goes:
time: 459 us; the launch traced here: 457 us
  waiting for transfers between devices  322 us (70%)
  blocking collectives  48.8 us (11%)
  starting transfers between devices  32 us (7%)
  matrix products  20 us (4%)
  local copies, waits for them, and re-layouts  14.4 us (3%)
  between operations  14 us (3%)
  other arithmetic  5.82 us (1%)
    reduce_scatter x1, waiting for transfers between devices, per_device(): lax.psum_scatter(mic_sum, 'tm', scatter_dimension=0, tiled=True)  159 us
    all_gather x1, waiting for transfers between devices, per_device(): lax.all_gather(w_qkv, 'tm', axis=0, tiled=True)  86.1 us
    psum x1, blocking collectives, per_device(): mic_sum = lax.psum(local_term.astype(jnp.bfloat16), 'mic')  48.8 us
    all_gather x1, waiting for transfers between devices, per_device(): lax.all_gather(w_out, 'tm', axis=0, tiled=True)  47.9 us
    all_to_all x1, starting transfers between devices, per_device(): lax.all_to_all(output, 'mic', split_axis=0, concat_axis=1, tiled=True)  11.1 us
    all_to_all x1, waiting for transfers between devices, per_device(): lax.all_to_all(grad_x, 'mic', split_axis=0, concat_axis=1, tiled=True)  10.3 us
    all_to_all x1, starting transfers between devices, per_device(): lax.all_to_all(frames_in, 'mic', split_axis=1, concat_axis=0, tiled=True)  10.2 us
    all_to_all x1, waiting for transfers between devices, per_device(): lax.all_to_all(cotangent, 'mic', split_axis=1, concat_axis=0, tiled=True)  9.38 us
  transfers between devices with their start and end apart: 7, of which 6 were waited for; matrix products, arithmetic and copies ran while one was open for 6% of the time, Pallas kernels for 0%

commit v1 on v0

v1 whole, which is shorter than its diff:
```python
import jax
import jax.numpy as jnp
from jax import lax
from jax.experimental import pallas as pl
from jax.experimental.pallas import tpu as pltpu
from jax.sharding import Mesh, PartitionSpec as P

HD = 64
SESS = 2
MIC = ("y", "core")
TM = ("x", "z")
NEG = -1e30
VMEM_LIMIT = 56 * 1024 * 1024


def dot_nn(a, b):
    return lax.dot_general(a, b, (((1,), (0,)), ((), ())), preferred_element_type=jnp.float32)


def dot_nt(a, b):
    return lax.dot_general(a, b, (((1,), (1,)), ((), ())), preferred_element_type=jnp.float32)


def dot_tn(a, b):
    return lax.dot_general(a, b, (((0,), (0,)), ((), ())), preferred_element_type=jnp.float32)


def low_half(rows):
    return lax.broadcasted_iota(jnp.int32, (rows, 2 * HD), 1) < HD


def fwd_kernel(frames, xp_ref, gain_ref, w_ref, g_ref, valid_ref, qkv_ref, p_ref, att_ref, gw_ref):
    rows, width = xp_ref.shape
    cores, half = w_ref.shape[1], w_ref.shape[3]
    xf = xp_ref[...].astype(jnp.float32)
    inv = lax.rsqrt(jnp.mean(xf * xf, axis=-1, keepdims=True) + 1e-05)
    normed = (xf * inv * gain_ref[...]).astype(jnp.bfloat16)
    for c in range(cores):
        part = dot_nn(normed, w_ref[:, c].reshape(width, half))
        qkv_ref[:, c * half : (c + 1) * half] = part.astype(jnp.bfloat16)
    row_at = lax.broadcasted_iota(jnp.int32, (rows, rows), 0)
    col_at = lax.broadcasted_iota(jnp.int32, (rows, rows), 1)
    same = lax.rem(row_at, frames) == lax.rem(col_at, frames)
    low = low_half(rows)
    for pair in range(width // (2 * HD)):
        at = pair * 2 * HD
        q = qkv_ref[:, at : at + 2 * HD]
        k = qkv_ref[:, width + at : width + at + 2 * HD]
        v = qkv_ref[:, 2 * width + at : 2 * width + at + 2 * HD]
        mixed = []
        for i in range(2):
            qi = jnp.where(low == (i == 0), q, jnp.zeros_like(q))
            s = jnp.where(same, dot_nt(qi, k) * HD ** (-0.5), NEG)
            e = jnp.exp(s - jnp.max(s, axis=-1, keepdims=True))
            p = e / jnp.sum(e, axis=-1, keepdims=True)
            p_ref[2 * pair + i] = p
            mixed.append(dot_nn(p.astype(jnp.bfloat16), v))
        att_ref[:, at : at + 2 * HD] = jnp.where(low, mixed[0], mixed[1]).astype(jnp.bfloat16)
    gz = (g_ref[...].astype(jnp.float32) * valid_ref[...]).astype(jnp.bfloat16)
    cut = width // cores
    for c in range(cores):
        gw_ref[c] = dot_tn(att_ref[...], gz[:, c * cut : (c + 1) * cut])


def out_kernel(x_ref, att_ref, wo_ref, valid_ref, out_ref):
    cores, _, cut = wo_ref.shape
    for c in range(cores):
        mixed = dot_nn(att_ref[...], wo_ref[c])
        x = x_ref[:, c * cut : (c + 1) * cut].astype(jnp.float32)
        out_ref[:, c * cut : (c + 1) * cut] = (valid_ref[...] * (x + mixed)).astype(jnp.bfloat16)


def bwd_kernel(
    g_ref, valid_ref, wo_ref, qkv_ref, p_ref, xp_ref, gp_ref, gain_ref, w_ref, perm_ref, dx_ref, gqkv_ref
):
    rows, width = xp_ref.shape
    cores, _, cut = wo_ref.shape
    half = w_ref.shape[3]
    valid = valid_ref[...]
    gz = (g_ref[...].astype(jnp.float32) * valid).astype(jnp.bfloat16)
    ga_all = sum(dot_nt(gz[:, c * cut : (c + 1) * cut], wo_ref[c]) for c in range(cores))
    ga_all = ga_all.astype(jnp.bfloat16)
    low = low_half(rows)
    for pair in range(width // (2 * HD)):
        at = pair * 2 * HD
        q = qkv_ref[:, at : at + 2 * HD]
        k = qkv_ref[:, width + at : width + at + 2 * HD]
        v = qkv_ref[:, 2 * width + at : 2 * width + at + 2 * HD]
        ga = ga_all[:, at : at + 2 * HD]
        dq, dk, dv = [], [], []
        for i in range(2):
            gi = jnp.where(low == (i == 0), ga, jnp.zeros_like(ga))
            p = p_ref[2 * pair + i]
            gp = dot_nt(gi, v)
            ds = p * (gp - jnp.sum(p * gp, axis=-1, keepdims=True)) * HD ** (-0.5)
            ds = ds.astype(jnp.bfloat16)
            dq.append(dot_nn(ds, k))
            dk.append(dot_tn(ds, q))
            dv.append(dot_tn(p.astype(jnp.bfloat16), ga))
        for j, grad in enumerate((dq, dk, dv)):
            gqkv_ref[:, j * width + at : j * width + at + 2 * HD] = jnp.where(
                low, grad[0], grad[1]
            ).astype(jnp.bfloat16)
    gh = sum(
        dot_nt(gqkv_ref[:, c * half : (c + 1) * half], w_ref[:, c].reshape(width, half))
        for c in range(cores)
    )
    gh = gh * gain_ref[...]
    xf = xp_ref[...].astype(jnp.float32)
    inv = lax.rsqrt(jnp.mean(xf * xf, axis=-1, keepdims=True) + 1e-05)
    inner = jnp.mean(gh * xf, axis=-1, keepdims=True)
    gy = gp_ref[...].astype(jnp.float32) * valid
    dx = (gy + inv * (gh - xf * inv * inv * inner)).astype(jnp.bfloat16)
    dx_ref[...] = dot_nt(dx, perm_ref[...]).astype(jnp.bfloat16)


def call(kernel, outs, scratch, flops, *operands):
    size = sum(o.size * o.dtype.itemsize for o in outs + operands)
    return pl.pallas_call(
        kernel,
        out_shape=outs,
        scratch_shapes=scratch,
        compiler_params=pltpu.CompilerParams(vmem_limit_bytes=VMEM_LIMIT),
        cost_estimate=pl.CostEstimate(flops=flops, bytes_accessed=size, transcendentals=0),
    )(*operands)


def swap(v, axis):
    return lax.ppermute(v, axis, [(0, 1), (1, 0)])


def exchange(v, axes):
    return lax.all_to_all(v, axes, split_axis=0, concat_axis=0, tiled=True)


def after(v, first):
    return lax.optimization_barrier((v, first))[0]


def per_device(frames_in, cotangent, norm_gain, w_qkv, w_out, lengths):
    bf, f32 = jnp.bfloat16, jnp.float32
    y_at, core_at = lax.axis_index("y"), lax.axis_index("core")
    ys, cores, tms = lax.axis_size("y"), lax.axis_size("core"), lax.axis_size("x") * lax.axis_size("z")
    mics = ys * cores
    frame_dev, width = frames_in.shape[1:]
    frames = frame_dev // mics
    rows = mics * frames
    piece, wide = w_qkv.shape
    rows_y, half, cut = piece // ys, wide // cores, width // cores

    mine = lax.dynamic_slice(w_qkv, (y_at * rows_y, core_at * half), (rows_y, half))
    mine = exchange(jnp.broadcast_to(mine[None], (tms, rows_y, half)), TM).reshape(tms * rows_y, half)
    w_full = lax.all_gather(mine, MIC, axis=0, tiled=False).reshape(ys, cores, tms * rows_y, half)

    both = jnp.concatenate(
        [frames_in.reshape(mics, frames, width), cotangent.reshape(mics, frames, width)], axis=1
    )
    both = exchange(after(both, mine), MIC)

    wo_mine = lax.dynamic_slice(w_out, (0, core_at * cut), (piece, cut))
    wo_mine = after(jnp.broadcast_to(wo_mine[None], (tms, piece, cut)), both)
    wo_mine = exchange(wo_mine, TM).reshape(width, cut)
    wo_other = swap(wo_mine, "core")
    first = core_at == 0
    wo = jnp.stack([jnp.where(first, wo_mine, wo_other), jnp.where(first, wo_other, wo_mine)])

    spot = jnp.arange(width, dtype=jnp.int32)
    block = tms * rows_y
    feature = (spot % block) // rows_y * piece + spot // block * rows_y + spot % rows_y
    perm = (spot[:, None] == feature[None, :]).astype(bf)
    both_p = jnp.dot(both.reshape(2 * rows, width), perm, preferred_element_type=f32).astype(bf)
    both_p = both_p.reshape(mics, 2, frames, width)
    both = both.reshape(mics, 2, frames, width)
    x, g = both[:, 0].reshape(rows, width), both[:, 1].reshape(rows, width)
    xp, gp = both_p[:, 0].reshape(rows, width), both_p[:, 1].reshape(rows, width)
    gain = norm_gain[feature].reshape(1, width)

    first_frame = (lax.axis_index(TM) * mics + lax.axis_index(MIC)) * frames
    frame_ids = first_frame + jnp.arange(frames, dtype=jnp.int32)
    slot_len = frame_dev * tms // SESS
    session = frame_ids // slot_len
    hit = session[:, None] == jnp.arange(lengths.shape[0], dtype=jnp.int32)[None, :]
    valid_len = jnp.sum(jnp.where(hit, lengths[None, :], 0), axis=1)
    valid = (frame_ids - session * slot_len < valid_len).astype(f32)
    valid = jnp.tile(valid, mics).reshape(rows, 1)

    def shape(dims, dtype):
        return jax.ShapeDtypeStruct(dims, dtype)

    heads = width // HD
    big = 2 * rows * width * wide
    qkv, probs, att, gw = call(
        lambda *refs: fwd_kernel(frames, *refs),
        (
            shape((rows, wide), bf),
            shape((heads, rows, rows), f32),
            shape((rows, width), bf),
            shape((cores, width, cut), f32),
        ),
        (),
        2 * big,
        xp, gain, w_full, g, valid,
    )

    keep = lax.dynamic_index_in_dim(gw, core_at, 0, keepdims=False)
    give = lax.dynamic_index_in_dim(gw, 1 - core_at, 0, keepdims=False).astype(bf)
    term = (keep + swap(give, "core").astype(f32)).astype(bf)
    term = exchange(term.reshape(tms, piece, cut), TM)
    term = jnp.sum(term.astype(f32), axis=0).astype(bf)
    term = exchange(jnp.broadcast_to(term[None], (mics, piece, cut)), MIC)
    term = jnp.sum(term.astype(f32).reshape(ys, cores, piece, cut), axis=0)
    grad_wout = term.transpose(1, 0, 2).reshape(piece, width)

    (out,) = call(out_kernel, (shape((rows, width), bf),), (), big // 3, x, att, wo, valid)
    out = exchange(out.reshape(mics, frames, width), MIC).reshape(1, frame_dev, width)
    (dx,) = call(
        bwd_kernel,
        (shape((rows, width), bf),),
        (pltpu.VMEM((rows, wide), bf),),
        3 * big,
        g, valid, wo, qkv, probs, xp, gp, gain, w_full, perm,
    )
    dx = exchange(dx.reshape(mics, frames, width), MIC).reshape(1, frame_dev, width)
    return (out, dx, grad_wout)


def solution(mesh):
    grid = Mesh(mesh.devices.reshape(-1, 2, 4, mesh.devices.shape[1] // 4), ("y", "core", "x", "z"))
    return jax.shard_map(
        per_device,
        mesh=grid,
        in_specs=(P(MIC, TM, None), P(MIC, TM, None), P(), P(TM, None), P(TM, None), P()),
        out_specs=(P(MIC, TM, None), P(MIC, TM, None), P(TM, None)),
        check_vma=False,
    )
```

time: 459 us -> 192 us (0.42)
  waiting for transfers between devices: 322 us -> 76.1 us
  blocking collectives: 48.8 us -> 23.5 us
  Pallas kernels: 0 us -> 21.2 us
  matrix products: 20 us -> 0.7 us
  starting transfers between devices: 32 us -> 37.5 us
    reduce_scatter x1 -> x0, waiting for transfers between devices: 159 us -> none  [per_device(): lax.psum_scatter(mic_sum, 'tm', scatter_dimension=0, tiled=True)]
    all_gather x2 -> x1, waiting for transfers between devices: 134 us -> 0.01 us  [per_device(): lax.all_gather(mine, MIC, axis=0, tiled=False)]
    all_to_all x4 -> x6, waiting for transfers between devices: 27 us -> 76 us  [exchange(): return lax.all_to_all(v, axes, split_axis=0, concat_axis=0, tiled=True)]
    psum x1 -> x0, blocking collectives: 48.8 us -> none  [per_device(): mic_sum = lax.psum(local_term.astype(jnp.bfloat16), 'mic')]
    all_to_all x0 -> x1, blocking collectives: none -> 23.5 us  [exchange(): return lax.all_to_all(v, axes, split_axis=0, concat_axis=0, tiled=True)]
    pallas_call x0 -> x3, Pallas kernels: none -> 21.2 us  [call(): pl.pallas_call(kernel, out_shape=outs, scratch_shapes=scratch, compiler_p...]
    dot_general x10 -> x1, matrix products: 17.2 us -> 0.7 us  [per_device(): jnp.dot(both.reshape(2 * rows, width), perm, preferred_element_type=f32)]
    unnamed x31 -> x14, local copies, waits for them, and re-layouts: 6.17 us -> 1.38 us
  transfers between devices with their start and end apart: 7 -> 9, of which waited for: 6 -> 6; matrix products, arithmetic and copies ran while one was open for 6% -> 7% of each run, Pallas kernels for 0% -> 11%
where the time goes in v1:
time: 192 us; the launch traced here: 191 us
  waiting for transfers between devices  76.1 us (40%)
  starting transfers between devices  37.5 us (20%)
  blocking collectives  23.5 us (12%)
  Pallas kernels  21.2 us (11%)
  between operations  14.2 us (7%)
  local copies, waits for them, and re-layouts  13.1 us (7%)
  other arithmetic  4.98 us (3%)
    all_to_all x6, waiting for transfers between devices, exchange(): return lax.all_to_all(v, axes, split_axis=0, concat_axis=0, tiled=True)  76 us
    all_to_all x6, starting transfers between devices, exchange(): return lax.all_to_all(v, axes, split_axis=0, concat_axis=0, tiled=True)  33.1 us
    all_to_all x1, blocking collectives, exchange(): return lax.all_to_all(v, axes, split_axis=0, concat_axis=0, tiled=True)  23.5 us
    pallas_call x3, Pallas kernels, call(): pl.pallas_call(kernel, out_shape=outs, scratch_shapes=scratch, compiler_p...  21.2 us
    ppermute x2, starting transfers between devices, swap(): return lax.ppermute(v, axis, [(0, 1), (1, 0)])  4.3 us
  transfers between devices with their start and end apart: 9, of which 6 were waited for; matrix products, arithmetic and copies ran while one was open for 7% of the time, Pallas kernels for 11%

profile of v1, /device:TPU:1, one launch (start us, length us, event | category | flops | bytes accessed | tf_op | source)
XLA Modules:
  0.0 191.2 jit_solution(461703442508304228)
XLA Ops:
  7.3 1.0 dynamic_slice.13
  8.3 23.5 %all_to_all.35 = bf16[32,3,1152]{2,1,0:T(4,128)(2,1)S(1)} all-to-all(bf16[32,3,1152]{2,1,0:T(4,128)(2,1)S(1)} %broadcast_in_dim.14), channel_id=1, replica_groups=mesh['y'=8,'core'=2,'x'=4,'z'=8] {'x','z'}, dimensions={0} | all-to-all | bytes 442368 | tf_op jit(solution)/shard_map/all_to_all | solution.py:133
  31.8 0.9 all_gather_reshape.3
  32.7 0.8 pad_maximum_fusion.1
  33.5 11.2 %all-to-all-start = ((bf16[16,16,768]{2,1,0:T(8,128)(2,1)}), bf16[16,16,768]{2,1,0:T(8,128)(2,1)S(1)}, u32[]{:S(2)}, u32[]{:S(2)}) async-start(bf16[16,16,768]{2,1,0:T(8,128)(2,1)} %pad_maximum_fusion.1), calls=%async_computation | async-start | bytes 786432 | tf_op jit(solution)/shard_map/all_to_all | solution.py:133
  44.7 18.1 %all-to-all-done = bf16[16,16,768]{2,1,0:T(8,128)(2,1)S(1)} async-done(((bf16[16,16,768]{2,1,0:T(8,128)(2,1)}), bf16[16,16,768]{2,1,0:T(8,128)(2,1)S(1)}, u32[]{:S(2)}, u32[]{:S(2)}) %all-to-all-start) | async-done | bytes 393248 | tf_op jit(solution)/shard_map/all_to_all | solution.py:133
  62.8 0.9 broadcast_in_dim.17
  63.7 3.9 %all-to-all-start.2 = ((bf16[32,24,384]{2,1,0:T(8,128)(2,1)}), bf16[32,24,384]{2,1,0:T(8,128)(2,1)S(1)}, u32[]{:S(2)}, u32[]{:S(2)}) async-start(bf16[32,24,384]{2,1,0:T(8,128)(2,1)} %broadcast_in_dim.17), calls=%async_computation.2 | async-start | bytes 1179648 | tf_op jit(solution)/shard_map/all_to_all | solution.py:133
  67.7 0.7 reshape_tile.4.refs_4_.valid_ref
  68.5 3.2 %gather_fusion = f32[768]{0:T(1024)S(1)} fusion(f32[768]{0:T(1024)S(1)} %copy-done.1, s32[1024]{0:T(1024)S(1)} %pad_clamp_fusion), kind=kCustom, calls=%fused_computation | custom fusion | bytes 9216 | tf_op jit(solution)/shard_map/gather | solution.py:176
  72.3 1.5 fusion.perm_ref
  73.8 11.6 %all-to-all-done.2 = bf16[32,24,384]{2,1,0:T(8,128)(2,1)S(1)} async-done(((bf16[32,24,384]{2,1,0:T(8,128)(2,1)}), bf16[32,24,384]{2,1,0:T(8,128)(2,1)S(1)}, u32[]{:S(2)}, u32[]{:S(2)}) %all-to-all-start.2) | async-done | bytes 589856 | tf_op jit(solution)/shard_map/all_to_all | solution.py:133
  85.4 1.9 collective-permute-start
  87.3 0.7 fusion.2
  88.0 0.9 slice_bitcast_fusion
  88.9 8.4 %shard_map.85 = (bf16[128,2304]{1,0:T(8,128)(2,1)}, f32[12,128,128]{2,1,0:T(8,128)}, bf16[128,768]{1,0:T(8,128)(2,1)}, f32[2,768,384]{2,1,0:T(8,128)}) custom-call(bf16[128,768]{1,0:T(8,128)(2,1)} %get-tuple-element.16.refs_0_.xp_ref, f32[1,768]{1,0:T(1,128)} %reshape.257.refs_1_.gain_ref, bf16[8,2,96,1152]{3,2,1,0:T(8,128)(2,1)} %bitcast.42, ...), custom_call_target="tpu_custom_call" | custom-call | flops 905969664 | bytes 7867904 | tf_op jit(solution)/shard_map/pallas_call | solution.py:119
  97.3 2.2 %fusion.5 = bf16[768,384]{1,0:T(8,128)(2,1)} fusion(f32[2,768,384]{2,1,0:T(8,128)} %get-tuple-element.12, s32[]{:T(128)S(6)} %select_n.152), kind=kLoop, calls=%fused_computation.10 | loop fusion | bytes 1179652 | tf_op jit(solution)/shard_map/convert_element_type | solution.py:206
  99.5 2.4 %collective-permute-start.1 = (bf16[768,384]{1,0:T(8,128)(2,1)}, bf16[768,384]{1,0:T(8,128)(2,1)S(1)}, u32[]{:S(2)}, u32[]{:S(2)}) collective-permute-start(bf16[768,384]{1,0:T(8,128)(2,1)} %fusion.5), channel_id=1, source_target_pairs={{0,32},{32,0},{1,33},{33,1},{2,34},{34,2},{3,35},{35,3},{4,36},{36... | collective-permute-start | bytes 1769480 | tf_op jit(solution)/shard_map/ppermute | solution.py:129
  102.1 1.2 pad_maximum_fusion.wo_ref
  103.3 10.3 %shard_map.87 = bf16[128,768]{1,0:T(8,128)(2,1)} custom-call(bf16[128,768]{1,0:T(8,128)(2,1)} %get-tuple-element.20.refs_3_.g_ref, f32[128,1]{1,0:T(8,128)} %reshape_tile.4.refs_4_.valid_ref, bf16[2,768,384]{2,1,0:T(8,128)(2,1)} %pad_maximum_fusion.wo_ref, bf16[128,2304]{1,0:T(8,128)(2,1)} %get-tuple-element.10.qkv_ref, ...), custom_call_target="tpu_custom_call" | custom-call | flops 1358954496 | bytes 8064512 | tf_op jit(solution)/shard_map/pallas_call | solution.py:119
  113.6 4.1 %all-to-all-start.4 = ((bf16[16,8,768]{2,1,0:T(8,128)(2,1)}), bf16[16,8,768]{2,1,0:T(8,128)(2,1)S(1)}, u32[]{:S(2)}, u32[]{:S(2)}) async-start(bf16[16,8,768]{2,1,0:T(8,128)(2,1)} %bitcast.51), calls=%async_computation.4 | async-start | bytes 393216 | tf_op jit(solution)/shard_map/all_to_all | solution.py:133
  117.7 1.0 fusion.3
  118.6 9.4 %all-to-all-done.4 = bf16[16,8,768]{2,1,0:T(8,128)(2,1)S(1)} async-done(((bf16[16,8,768]{2,1,0:T(8,128)(2,1)}), bf16[16,8,768]{2,1,0:T(8,128)(2,1)S(1)}, u32[]{:S(2)}, u32[]{:S(2)}) %all-to-all-start.4) | async-done | bytes 196640 | tf_op jit(solution)/shard_map/all_to_all | solution.py:133
  128.0 5.6 %all-to-all-start.5 = ((bf16[32,24,384]{2,1,0:T(8,128)(2,1)}), bf16[32,24,384]{2,1,0:T(8,128)(2,1)S(1)}, u32[]{:S(2)}, u32[]{:S(2)}) async-start(bf16[32,24,384]{2,1,0:T(8,128)(2,1)} %bitcast.19), calls=%async_computation.5 | async-start | bytes 1179648 | tf_op jit(solution)/shard_map/all_to_all | solution.py:133
  133.6 2.5 %shard_map.86 = bf16[128,768]{1,0:T(8,128)(2,1)} custom-call(bf16[128,768]{1,0:T(8,128)(2,1)} %get-tuple-element.19.x_ref, bf16[128,768]{1,0:T(8,128)(2,1)} %get-tuple-element.8.att_ref, bf16[2,768,384]{2,1,0:T(8,128)(2,1)} %pad_maximum_fusion.wo_ref, f32[128,1]{1,0:T(8,128)} %reshape_tile.4.refs_4_.valid_ref), custom_call_target="tpu_custom_call" | custom-call | flops 150994944 | bytes 1769984 | tf_op jit(solution)/shard_map/pallas_call | solution.py:119
  136.1 14.8 %all-to-all-done.5 = bf16[32,24,384]{2,1,0:T(8,128)(2,1)S(1)} async-done(((bf16[32,24,384]{2,1,0:T(8,128)(2,1)}), bf16[32,24,384]{2,1,0:T(8,128)(2,1)S(1)}, u32[]{:S(2)}, u32[]{:S(2)}) %all-to-all-start.5) | async-done | bytes 589856 | tf_op jit(solution)/shard_map/all_to_all | solution.py:133
  150.8 5.0 %all-to-all-start.3 = ((bf16[16,8,768]{2,1,0:T(8,128)(2,1)}), bf16[16,8,768]{2,1,0:T(8,128)(2,1)S(1)}, u32[]{:S(2)}, u32[]{:S(2)}) async-start(bf16[16,8,768]{2,1,0:T(8,128)(2,1)} %bitcast.48), calls=%async_computation.3 | async-start | bytes 393216 | tf_op jit(solution)/shard_map/all_to_all | solution.py:133
  155.9 10.3 %all-to-all-done.3 = bf16[16,8,768]{2,1,0:T(8,128)(2,1)S(1)} async-done(((bf16[16,8,768]{2,1,0:T(8,128)(2,1)}), bf16[16,8,768]{2,1,0:T(8,128)(2,1)S(1)}, u32[]{:S(2)}, u32[]{:S(2)}) %all-to-all-start.3) | async-done | bytes 196640 | tf_op jit(solution)/shard_map/all_to_all | solution.py:133
  166.2 0.7 broadcast_in_dim.22
  166.9 3.4 %all-to-all-start.6 = ((bf16[16,24,384]{2,1,0:T(8,128)(2,1)}), bf16[16,24,384]{2,1,0:T(8,128)(2,1)S(1)}, u32[]{:S(2)}, u32[]{:S(2)}) async-start(bf16[16,24,384]{2,1,0:T(8,128)(2,1)} %broadcast_in_dim.22), calls=%async_computation.6 | async-start | bytes 589824 | tf_op jit(solution)/shard_map/all_to_all | solution.py:133
  170.4 11.9 %all-to-all-done.6 = bf16[16,24,384]{2,1,0:T(8,128)(2,1)S(1)} async-done(((bf16[16,24,384]{2,1,0:T(8,128)(2,1)}), bf16[16,24,384]{2,1,0:T(8,128)(2,1)S(1)}, u32[]{:S(2)}, u32[]{:S(2)}) %all-to-all-start.6) | async-done | bytes 294944 | tf_op jit(solution)/shard_map/all_to_all | solution.py:133
  183.0 0.7 copy.40
  (32 shorter events, 2.7 us)
Async XLA Ops:
  7.2 37.5 %copy-start = (bf16[24,768]{1,0:T(8,128)(2,1)S(1)}, bf16[24,768]{1,0:T(8,128)(2,1)}, u32[]{:S(2)}) copy-start(bf16[24,768]{1,0:T(8,128)(2,1)} %param.10) | copy-start | bytes 110596
  7.2 25.5 %copy-start.4 = (bf16[1,128,768]{2,1,0:T(8,128)(2,1)S(1)}, bf16[1,128,768]{2,1,0:T(8,128)(2,1)}, u32[]{:S(2)}) copy-start(bf16[1,128,768]{2,1,0:T(8,128)(2,1)} %param.6) | copy-start | bytes 589828
  7.2 25.5 %copy-start.3 = (bf16[1,128,768]{2,1,0:T(8,128)(2,1)S(1)}, bf16[1,128,768]{2,1,0:T(8,128)(2,1)}, u32[]{:S(2)}) copy-start(bf16[1,128,768]{2,1,0:T(8,128)(2,1)} %param.7) | copy-start | bytes 589828
  7.2 81.7 %all-gather.2.cloned.1.call-start = ((), (), s32[]{:S(2)}) async-start(), calls=%async_computation.7 | async-start | bytes 3760128 | tf_op jit(solution)/shard_map/all_gather | solution.py:153
  33.5 34.1 %copy-start.5 = (s32[2]{0:T(128)S(1)}, s32[2]{0:T(128)}, u32[]{:S(2)}) copy-start(s32[2]{0:T(128)} %param.11) | copy-start | bytes 28
  33.5 35.0 %copy-start.1 = (f32[768]{0:T(1024)S(1)}, f32[768]{0:T(1024)}, u32[]{:S(2)}) copy-start(f32[768]{0:T(1024)} %param.8) | copy-start | bytes 9220
  33.5 29.3 %all-to-all-start = ((bf16[16,16,768]{2,1,0:T(8,128)(2,1)}), bf16[16,16,768]{2,1,0:T(8,128)(2,1)S(1)}, u32[]{:S(2)}, u32[]{:S(2)}) async-start(bf16[16,16,768]{2,1,0:T(8,128)(2,1)} %pad_maximum_fusion.1), calls=%async_computation | async-start | bytes 786432 | tf_op jit(solution)/shard_map/all_to_all | solution.py:133
  63.7 21.7 %all-to-all-start.2 = ((bf16[32,24,384]{2,1,0:T(8,128)(2,1)}), bf16[32,24,384]{2,1,0:T(8,128)(2,1)S(1)}, u32[]{:S(2)}, u32[]{:S(2)}) async-start(bf16[32,24,384]{2,1,0:T(8,128)(2,1)} %broadcast_in_dim.17), calls=%async_computation.2 | async-start | bytes 1179648 | tf_op jit(solution)/shard_map/all_to_all | solution.py:133
  85.4 16.5 %collective-permute-start = (bf16[768,384]{1,0:T(8,128)(2,1)S(1)}, bf16[768,384]{1,0:T(8,128)(2,1)S(1)}, u32[]{:S(2)}, u32[]{:S(2)}) collective-permute-start(bf16[768,384]{1,0:T(8,128)(2,1)S(1)} %bitcast.44), channel_id=1, source_target_pairs={{0,32},{32,0},{1,33},{33,1},{2,34},{34,2},{3,35},{35,3},{4,36},{36... | collective-permute-start | bytes 1769480 | tf_op jit(solution)/shard_map/ppermute | solution.py:129
  99.5 18.2 %collective-permute-start.1 = (bf16[768,384]{1,0:T(8,128)(2,1)}, bf16[768,384]{1,0:T(8,128)(2,1)S(1)}, u32[]{:S(2)}, u32[]{:S(2)}) collective-permute-start(bf16[768,384]{1,0:T(8,128)(2,1)} %fusion.5), channel_id=1, source_target_pairs={{0,32},{32,0},{1,33},{33,1},{2,34},{34,2},{3,35},{35,3},{4,36},{36... | collective-permute-start | bytes 1769480 | tf_op jit(solution)/shard_map/ppermute | solution.py:129
  103.3 14.3 %copy-start.2 = (f32[2,768,384]{2,1,0:T(8,128)S(1)}, f32[2,768,384]{2,1,0:T(8,128)}, u32[]{:S(2)}) copy-start(f32[2,768,384]{2,1,0:T(8,128)} %get-tuple-element.12) | copy-start | bytes 7077892
  113.6 14.4 %all-to-all-start.4 = ((bf16[16,8,768]{2,1,0:T(8,128)(2,1)}), bf16[16,8,768]{2,1,0:T(8,128)(2,1)S(1)}, u32[]{:S(2)}, u32[]{:S(2)}) async-start(bf16[16,8,768]{2,1,0:T(8,128)(2,1)} %bitcast.51), calls=%async_computation.4 | async-start | bytes 393216 | tf_op jit(solution)/shard_map/all_to_all | solution.py:133
  128.0 22.9 %all-to-all-start.5 = ((bf16[32,24,384]{2,1,0:T(8,128)(2,1)}), bf16[32,24,384]{2,1,0:T(8,128)(2,1)S(1)}, u32[]{:S(2)}, u32[]{:S(2)}) async-start(bf16[32,24,384]{2,1,0:T(8,128)(2,1)} %bitcast.19), calls=%async_computation.5 | async-start | bytes 1179648 | tf_op jit(solution)/shard_map/all_to_all | solution.py:133
  150.8 15.4 %all-to-all-start.3 = ((bf16[16,8,768]{2,1,0:T(8,128)(2,1)}), bf16[16,8,768]{2,1,0:T(8,128)(2,1)S(1)}, u32[]{:S(2)}, u32[]{:S(2)}) async-start(bf16[16,8,768]{2,1,0:T(8,128)(2,1)} %bitcast.48), calls=%async_computation.3 | async-start | bytes 393216 | tf_op jit(solution)/shard_map/all_to_all | solution.py:133
  166.9 15.4 %all-to-all-start.6 = ((bf16[16,24,384]{2,1,0:T(8,128)(2,1)}), bf16[16,24,384]{2,1,0:T(8,128)(2,1)S(1)}, u32[]{:S(2)}, u32[]{:S(2)}) async-start(bf16[16,24,384]{2,1,0:T(8,128)(2,1)} %broadcast_in_dim.22), calls=%async_computation.6 | async-start | bytes 589824 | tf_op jit(solution)/shard_map/all_to_all | solution.py:133
Sparse Core Ops, SparseCore 0:
  32.8 49.9 all-gather.1

commit v2 on v1

v2 whole, which is shorter than its diff:
```python
import jax
import jax.numpy as jnp
from jax import lax
from jax.experimental import pallas as pl
from jax.experimental.pallas import tpu as pltpu
from jax.sharding import Mesh, PartitionSpec as P

HD = 64
SESS = 2
MIC = ("y", "core")
TM = ("x", "z")
NEG = -1e30
VMEM_LIMIT = 56 * 1024 * 1024
FWD_COST, BWD_COST, END_COST = 8_000_000_000, 10_000_000_000, 2_000_000_000


def dot_nn(a, b):
    return lax.dot_general(a, b, (((1,), (0,)), ((), ())), preferred_element_type=jnp.float32)


def dot_nt(a, b):
    return lax.dot_general(a, b, (((1,), (1,)), ((), ())), preferred_element_type=jnp.float32)


def dot_tn(a, b):
    return lax.dot_general(a, b, (((0,), (0,)), ((), ())), preferred_element_type=jnp.float32)


def low_half(rows):
    return lax.broadcasted_iota(jnp.int32, (rows, 2 * HD), 1) < HD


def same_frame(rows, frames):
    row_at = lax.broadcasted_iota(jnp.int32, (rows, rows), 0)
    col_at = lax.broadcasted_iota(jnp.int32, (rows, rows), 1)
    return lax.rem(row_at, frames) == lax.rem(col_at, frames)


def pairs_of(rows, width):
    at = 0
    for start in (0, rows):
        for col in range(0, width, 2 * HD):
            yield start, col, at
            at += 2


def fwd_kernel(
    frames, core_ref, xp_ref, gain_ref, w_ref, g_ref, valid_ref, qkv_ref, p_ref, att_ref, keep_ref, give_ref
):
    width = xp_ref.shape[1]
    rows, mine = xp_ref.shape[0] // 2, att_ref.shape[1]
    xf = xp_ref[...].astype(jnp.float32)
    inv = lax.rsqrt(jnp.mean(xf * xf, axis=-1, keepdims=True) + 1e-05)
    normed = (xf * inv * gain_ref[...]).astype(jnp.bfloat16)
    qkv_ref[...] = dot_nn(normed, w_ref[...].reshape(width, 3 * mine)).astype(jnp.bfloat16)
    same = same_frame(rows, frames)
    low = low_half(rows)
    for start, at, index in pairs_of(rows, mine):
        here = pl.ds(start, rows)
        q = qkv_ref[here, at : at + 2 * HD]
        k = qkv_ref[here, mine + at : mine + at + 2 * HD]
        v = qkv_ref[here, 2 * mine + at : 2 * mine + at + 2 * HD]
        mixed = []
        for i in range(2):
            qi = jnp.where(low == (i == 0), q, jnp.zeros_like(q))
            s = jnp.where(same, dot_nt(qi, k) * HD ** (-0.5), NEG)
            e = jnp.exp(s - jnp.max(s, axis=-1, keepdims=True))
            p = e / jnp.sum(e, axis=-1, keepdims=True)
            p_ref[index + i] = p
            mixed.append(dot_nn(p.astype(jnp.bfloat16), v))
        att_ref[here, at : at + 2 * HD] = jnp.where(low, mixed[0], mixed[1]).astype(jnp.bfloat16)
    gz = (g_ref[...].astype(jnp.float32) * valid_ref[...]).astype(jnp.bfloat16)
    cut = width // 2
    low_cut, high_cut = gz[:, :cut], gz[:, cut:]
    first = core_ref[0] == 0
    att = att_ref[...]
    keep_ref[...] = dot_tn(att, jnp.where(first, low_cut, high_cut)).astype(jnp.bfloat16)
    give_ref[...] = dot_tn(att, jnp.where(first, high_cut, low_cut)).astype(jnp.bfloat16)


def bwd_kernel(
    g_ref, valid_ref, wo_ref, att_ref, qkv_ref, p_ref, w_ref, _, own_ref, other_ref, gqkv_ref
):
    width = g_ref.shape[1]
    rows, mine = g_ref.shape[0] // 2, att_ref.shape[1]
    cut = wo_ref.shape[2]
    att = att_ref[...]
    for c in range(2):
        part = dot_nn(att, wo_ref[c])
        own_ref[:, c * cut : (c + 1) * cut] = part[:rows]
        other_ref[:, c * cut : (c + 1) * cut] = part[rows:].astype(jnp.bfloat16)
    gz = (g_ref[...].astype(jnp.float32) * valid_ref[...]).astype(jnp.bfloat16)
    ga_all = dot_nt(gz[:, :cut], wo_ref[0]) + dot_nt(gz[:, cut:], wo_ref[1])
    ga_all = ga_all.astype(jnp.bfloat16)
    low = low_half(rows)
    for start, at, index in pairs_of(rows, mine):
        here = pl.ds(start, rows)
        q = qkv_ref[here, at : at + 2 * HD]
        k = qkv_ref[here, mine + at : mine + at + 2 * HD]
        v = qkv_ref[here, 2 * mine + at : 2 * mine + at + 2 * HD]
        ga = ga_all[start : start + rows, at : at + 2 * HD]
        dq, dk, dv = [], [], []
        for i in range(2):
            gi = jnp.where(low == (i == 0), ga, jnp.zeros_like(ga))
            p = p_ref[index + i]
            gp = dot_nt(gi, v)
            ds = p * (gp - jnp.sum(p * gp, axis=-1, keepdims=True)) * HD ** (-0.5)
            ds = ds.astype(jnp.bfloat16)
            dq.append(dot_nn(ds, k))
            dk.append(dot_tn(ds, q))
            dv.append(dot_tn(p.astype(jnp.bfloat16), ga))
        for j, grad in enumerate((dq, dk, dv)):
            gqkv_ref[here, j * mine + at : j * mine + at + 2 * HD] = jnp.where(
                low, grad[0], grad[1]
            ).astype(jnp.bfloat16)
    gh = dot_nt(gqkv_ref[...], w_ref[...].reshape(width, 3 * mine))
    own_ref[:, width:] = gh[:rows]
    other_ref[:, width:] = gh[rows:].astype(jnp.bfloat16)


def end_kernel(x_ref, valid_ref, xp_ref, gp_ref, gain_ref, own_ref, got_ref, perm_ref, both_ref):
    width = x_ref.shape[1]
    valid = valid_ref[...]
    mixed = own_ref[:, :width] + got_ref[:, :width].astype(jnp.float32)
    out = valid * (x_ref[...].astype(jnp.float32) + mixed)
    both_ref[:, :width] = out.astype(jnp.bfloat16)
    gh = (own_ref[:, width:] + got_ref[:, width:].astype(jnp.float32)) * gain_ref[...]
    xf = xp_ref[...].astype(jnp.float32)
    inv = lax.rsqrt(jnp.mean(xf * xf, axis=-1, keepdims=True) + 1e-05)
    inner = jnp.mean(gh * xf, axis=-1, keepdims=True)
    gy = gp_ref[...].astype(jnp.float32) * valid
    dx = (gy + inv * (gh - xf * inv * inv * inner)).astype(jnp.bfloat16)
    both_ref[:, width:] = dot_nt(dx, perm_ref[...]).astype(jnp.bfloat16)


def call(kernel, outs, scratch, flops, *operands, behind=()):
    size = sum(o.size * o.dtype.itemsize for o in outs + operands)
    return pl.pallas_call(
        kernel,
        out_shape=outs,
        in_specs=[
            pl.BlockSpec(memory_space=pltpu.SMEM if o.dtype == jnp.int32 else pltpu.VMEM)
            for o in operands
        ]
        + [pl.BlockSpec(memory_space=pl.ANY)] * len(behind),
        scratch_shapes=scratch,
        compiler_params=pltpu.CompilerParams(vmem_limit_bytes=VMEM_LIMIT),
        cost_estimate=pl.CostEstimate(flops=flops, bytes_accessed=size, transcendentals=0),
    )(*operands, *behind)


def swap(v, axis):
    return lax.ppermute(v, axis, [(0, 1), (1, 0)])


def exchange(v, axes):
    return lax.all_to_all(v, axes, split_axis=0, concat_axis=0, tiled=True)


def after(v, first):
    t = first[(0,) * first.ndim]
    return jnp.where(t == t, v, jnp.zeros_like(v))


def valid_of(first_frame, frames, slot_len, lengths):
    frame_ids = first_frame + jnp.arange(frames, dtype=jnp.int32)
    session = frame_ids // slot_len
    hit = session[:, None] == jnp.arange(lengths.shape[0], dtype=jnp.int32)[None, :]
    valid_len = jnp.sum(jnp.where(hit, lengths[None, :], 0), axis=1)
    return (frame_ids - session * slot_len < valid_len).astype(jnp.float32)


def per_device(frames_in, cotangent, norm_gain, w_qkv, w_out, lengths):
    bf, f32 = jnp.bfloat16, jnp.float32
    y_at, core_at = lax.axis_index("y"), lax.axis_index("core")
    ys, cores, tms = lax.axis_size("y"), lax.axis_size("core"), lax.axis_size("x") * lax.axis_size("z")
    mics = ys * cores
    frame_dev, width = frames_in.shape[1:]
    frames = frame_dev // mics
    rows = mics * frames
    piece, wide = w_qkv.shape
    rows_y, half, cut = piece // ys, wide // cores, width // cores
    first = core_at == 0

    mine = jnp.concatenate(
        [
            lax.dynamic_slice(w_qkv, (y_at * rows_y, j * width + core_at * cut), (rows_y, cut))
            for j in range(3)
        ],
        axis=1,
    )
    mine = exchange(jnp.broadcast_to(mine[None], (tms, rows_y, half)), TM)
    w_mine = lax.all_gather(mine.reshape(tms * rows_y, half), "y", axis=0, tiled=False)

    both = jnp.concatenate(
        [frames_in.reshape(mics, frames, width), cotangent.reshape(mics, frames, width)], axis=1
    )
    both = exchange(after(both, mine), MIC)
    next_both = swap(both, "core")

    wo_part = lax.dynamic_slice(w_out, (0, core_at * cut), (piece, cut))
    wo_part = after(jnp.broadcast_to(wo_part[None], (tms, piece, cut)), both)
    wo_part = exchange(wo_part, TM).reshape(cores, cut, cut)
    wo_keep = lax.dynamic_index_in_dim(wo_part, core_at, 0, keepdims=False)
    wo_got = swap(lax.dynamic_index_in_dim(wo_part, 1 - core_at, 0, keepdims=False), "core")
    wo = jnp.stack([jnp.where(first, wo_keep, wo_got), jnp.where(first, wo_got, wo_keep)])

    spot = jnp.arange(width, dtype=jnp.int32)
    block = tms * rows_y
    feature = (spot % block) // rows_y * piece + spot // block * rows_y + spot % rows_y
    perm = (spot[:, None] == feature[None, :]).astype(bf)
    gain = norm_gain[feature].reshape(1, width)
    own, near = both.reshape(mics, 2, frames, width), next_both.reshape(mics, 2, frames, width)
    x, g = own[:, 0].reshape(rows, width), own[:, 1].reshape(rows, width)
    near_x, near_g = near[:, 0].reshape(rows, width), near[:, 1].reshape(rows, width)
    placed = jnp.dot(
        jnp.concatenate([x, near_x, g]), perm, preferred_element_type=f32
    ).astype(bf)
    xp, gp = placed[: 2 * rows], placed[2 * rows :]
    g_all = jnp.concatenate([g, near_g])

    slot_len = frame_dev * tms // SESS
    start = (lax.axis_index(TM) * mics + y_at * cores) * frames
    valid = [
        jnp.tile(valid_of(start + c * frames, frames, slot_len, lengths), mics)
        for c in (core_at, 1 - core_at)
    ]
    valid_own = valid[0].reshape(rows, 1)
    valid_all = jnp.concatenate(valid).reshape(2 * rows, 1)

    def shape(dims, dtype):
        return jax.ShapeDtypeStruct(dims, dtype)

    heads = width // HD
    qkv, probs, att, keep, give = call(
        lambda *refs: fwd_kernel(frames, *refs),
        (
            shape((2 * rows, half), bf),
            shape((heads, rows, rows), f32),
            shape((2 * rows, cut), bf),
            shape((cut, cut), bf),
            shape((cut, cut), bf),
        ),
        (),
        FWD_COST,
        core_at.reshape(1).astype(jnp.int32), xp, gain, w_mine, g_all, valid_all,
    )

    got = swap(give, "core")
    term = jnp.where(first, jnp.concatenate([keep, got]), jnp.concatenate([got, keep]))
    own_part, other_part = call(
        bwd_kernel,
        (shape((rows, 2 * width), f32), shape((rows, 2 * width), bf)),
        (pltpu.VMEM((2 * rows, half), bf),),
        BWD_COST,
        g_all, valid_all, wo, att, qkv, probs, w_mine, behind=(term,),
    )
    term = exchange(term.reshape(tms, piece, cut), TM)
    term = jnp.sum(term.astype(f32), axis=0).astype(bf)
    got_part = swap(other_part, "core")
    (done,) = call(
        end_kernel,
        (shape((rows, 2 * width), bf),),
        (),
        END_COST,
        x, valid_own, xp[:rows], gp, gain, own_part, got_part, perm,
    )

    low = piece // frames
    term = term.reshape(low, frames, cut).transpose(1, 0, 2).reshape(frames, low * cut)
    term = jnp.broadcast_to(term[None], (mics, frames, low * cut))
    sent = jnp.concatenate([done.reshape(mics, frames, 2 * width), term], axis=2)
    sent = exchange(sent, MIC)
    out = sent[:, :, :width].reshape(1, frame_dev, width)
    dx = sent[:, :, width : 2 * width].reshape(1, frame_dev, width)
    term = jnp.sum(sent[:, :, 2 * width :].astype(f32).reshape(ys, cores, frames, low, cut), axis=0)
    grad_wout = term.transpose(2, 1, 0, 3).reshape(piece, width)
    return (out, dx, grad_wout)


def solution(mesh):
    grid = Mesh(mesh.devices.reshape(-1, 2, 4, mesh.devices.shape[1] // 4), ("y", "core", "x", "z"))
    return jax.shard_map(
        per_device,
        mesh=grid,
        in_specs=(P(MIC, TM, None), P(MIC, TM, None), P(), P(TM, None), P(TM, None), P()),
        out_specs=(P(MIC, TM, None), P(MIC, TM, None), P(TM, None)),
        check_vma=False,
    )
```

time: 192 us -> 162 us (0.84)
  waiting for transfers between devices: 76.1 us -> 26.1 us
  blocking collectives: 23.5 us -> 49.1 us
  starting transfers between devices: 37.5 us -> 30.6 us
  Pallas kernels: 21.2 us -> 18.3 us
  between operations: 14.2 us -> 16.9 us
    all_to_all x6 -> x3, waiting for transfers between devices: 76 us -> 25.3 us  [exchange(): return lax.all_to_all(v, axes, split_axis=0, concat_axis=0, tiled=True)]
    all_to_all x1 -> x2, blocking collectives: 23.5 us -> 49.1 us  [exchange(): return lax.all_to_all(v, axes, split_axis=0, concat_axis=0, tiled=True)]
    all_to_all x6 -> x3, starting transfers between devices: 33.1 us -> 20.9 us  [exchange(): return lax.all_to_all(v, axes, split_axis=0, concat_axis=0, tiled=True)]
    ppermute x2 -> x4, starting transfers between devices: 4.3 us -> 9.71 us  [swap(): return lax.ppermute(v, axis, [(0, 1), (1, 0)])]
    pallas_call x3, Pallas kernels: 21.2 us -> 18.3 us  [call(): pl.pallas_call(kernel, out_shape=outs, in_specs=[pl.BlockSpec(memory_spac...]
    slice x0 -> x5, local copies, waits for them, and re-layouts: none -> 2.6 us  [the longest x2 1.55 us: per_device(): xp, gp = (placed[:2 * rows], placed[2 * rows:])]
    convert_element_type x1 -> x0, local copies, waits for them, and re-layouts: 2.15 us -> none  [per_device(): lax.dynamic_index_in_dim(gw, 1 - core_at, 0, keepdims=False).astype(bf)]
  transfers between devices with their start and end apart: 9 -> 8, of which waited for: 6 -> 3; matrix products, arithmetic and copies ran while one was open for 7% -> 9% of each run, Pallas kernels for 11% -> 11%
where the time goes in v2:
time: 162 us; the launch traced here: 161 us
  blocking collectives  49.1 us (30%)
  starting transfers between devices  30.6 us (19%)
  waiting for transfers between devices  26.1 us (16%)
  Pallas kernels  18.3 us (11%)
  between operations  16.9 us (10%)
  local copies, waits for them, and re-layouts  14 us (9%)
  other arithmetic  5.51 us (3%)
    all_to_all x2, blocking collectives, exchange(): return lax.all_to_all(v, axes, split_axis=0, concat_axis=0, tiled=True)  49.1 us
    all_to_all x3, waiting for transfers between devices, exchange(): return lax.all_to_all(v, axes, split_axis=0, concat_axis=0, tiled=True)  25.3 us
    all_to_all x3, starting transfers between devices, exchange(): return lax.all_to_all(v, axes, split_axis=0, concat_axis=0, tiled=True)  20.9 us
    pallas_call x3, Pallas kernels, call(): pl.pallas_call(kernel, out_shape=outs, in_specs=[pl.BlockSpec(memory_spac...  18.3 us
    ppermute x4, starting transfers between devices, swap(): return lax.ppermute(v, axis, [(0, 1), (1, 0)])  9.71 us
  transfers between devices with their start and end apart: 8, of which 3 were waited for; matrix products, arithmetic and copies ran while one was open for 9% of the time, Pallas kernels for 11%

profile of v2, /device:TPU:1, one launch (start us, length us, event | category | flops | bytes accessed | tf_op | source)
XLA Modules:
  0.0 161.3 jit_solution(4251284029883801187)
XLA Ops:
  7.3 0.9 fusion.41
  8.3 23.5 %all_to_all.25 = bf16[32,3,1152]{2,1,0:T(4,128)(2,1)S(1)} all-to-all(bf16[32,3,1152]{2,1,0:T(4,128)(2,1)S(1)} %broadcast_in_dim.28), channel_id=1, replica_groups=mesh['y'=8,'core'=2,'x'=4,'z'=8] {'x','z'}, dimensions={0} | all-to-all | bytes 442368 | tf_op jit(solution)/shard_map/all_to_all | solution.py:157
  31.8 0.9 all_gather_reshape.3
  34.5 0.8 maximum_select_fusion.1
  35.3 11.0 %all-to-all-start.1 = ((bf16[16,16,768]{2,1,0:T(8,128)(2,1)}), bf16[16,16,768]{2,1,0:T(8,128)(2,1)S(1)}, u32[]{:S(2)}, u32[]{:S(2)}) async-start(bf16[16,16,768]{2,1,0:T(8,128)(2,1)} %maximum_select_fusion.1), calls=%async_computation.1 | async-start | bytes 786432 | tf_op jit(solution)/shard_map/all_to_all | solution.py:157
  46.8 17.6 %all-to-all-done.1 = bf16[16,16,768]{2,1,0:T(8,128)(2,1)S(1)} async-done(((bf16[16,16,768]{2,1,0:T(8,128)(2,1)}), bf16[16,16,768]{2,1,0:T(8,128)(2,1)S(1)}, u32[]{:S(2)}, u32[]{:S(2)}) %all-to-all-start.1) | async-done | bytes 393248 | tf_op jit(solution)/shard_map/all_to_all | solution.py:157
  66.2 0.9 broadcast_in_dim.55
  67.1 4.3 %all-to-all-start.2 = ((bf16[32,24,384]{2,1,0:T(8,128)(2,1)}), bf16[32,24,384]{2,1,0:T(8,128)(2,1)S(1)}, u32[]{:S(2)}, u32[]{:S(2)}) async-start(bf16[32,24,384]{2,1,0:T(8,128)(2,1)} %broadcast_in_dim.55), calls=%async_computation.2 | async-start | bytes 1179648 | tf_op jit(solution)/shard_map/all_to_all | solution.py:157
  71.3 1.9 %collective-permute-start = (bf16[16,16,768]{2,1,0:T(8,128)(2,1)S(1)}, bf16[16,16,768]{2,1,0:T(8,128)(2,1)S(1)}, u32[]{:S(2)}, u32[]{:S(2)}) collective-permute-start(bf16[16,16,768]{2,1,0:T(8,128)(2,1)S(1)} %all-to-all-done.1), channel_id=1, source_target_pairs={{0,32},{32,0},{1,33},{33,1},{2,34},{34,2},{3,35},{35,3},{4,36},{36... | collective-permute-start | bytes 1179656 | tf_op jit(solution)/shard_map/ppermute | solution.py:153
  73.3 0.7 reshape_tile.4.valid_ref
  74.0 0.8 copy.21.refs_5_.valid_ref
  74.8 3.2 %gather_fusion = f32[768]{0:T(1024)S(1)} fusion(f32[768]{0:T(1024)S(1)} %copy-done, s32[1024]{0:T(1024)S(1)} %pad_clamp_fusion), kind=kCustom, calls=%fused_computation | custom fusion | bytes 9216 | tf_op jit(solution)/shard_map/gather | solution.py:212
  78.7 0.7 fusion.2
  79.4 0.8 slice.59.refs_1_
  80.2 0.8 pad_maximum_fusion.2.refs_4_.g_ref
  81.0 7.7 %all-to-all-done.2 = bf16[32,24,384]{2,1,0:T(8,128)(2,1)S(1)} async-done(((bf16[32,24,384]{2,1,0:T(8,128)(2,1)}), bf16[32,24,384]{2,1,0:T(8,128)(2,1)S(1)}, u32[]{:S(2)}, u32[]{:S(2)}) %all-to-all-start.2) | async-done | bytes 589856 | tf_op jit(solution)/shard_map/all_to_all | solution.py:157
  88.8 3.4 %collective-permute-start.1 = (bf16[384,384]{1,0:T(8,128)(2,1)S(1)}, bf16[384,384]{1,0:T(8,128)(2,1)S(1)}, u32[]{:S(2)}, u32[]{:S(2)}) collective-permute-start(bf16[384,384]{1,0:T(8,128)(2,1)S(1)} %dynamic-slice_bitcast_fusion), channel_id=1, source_target_pairs={{0,32},{32,0},{1,33},{33,1},{2,34},{34,2},{3,35},{35,3},{4,36},{36... | collective-permute-start | bytes 884744 | tf_op jit(solution)/shard_map/ppermute | solution.py:153
  92.2 7.1 %shard_map.85 = (bf16[256,1152]{1,0:T(8,128)(2,1)}, f32[12,128,128]{2,1,0:T(8,128)}, bf16[256,384]{1,0:T(8,128)(2,1)}, bf16[384,384]{1,0:T(8,128)(2,1)}, bf16[384,384]{1,0:T(8,128)(2,1)}) custom-call(s32[1]{0:T(128)} %bitcast.16.refs_0_, bf16[256,768]{1,0:T(8,128)(2,1)} %slice.59.refs_1_, f32[1,768]{1,0:T(1,128)} %reshape.302.refs_2_.gain_ref, ...), custom_call_target="tpu_custom_call" | custom-call | flops 8000000000 | bytes 4722692 | tf_op jit(solution)/shard_map/pallas_call | solution.py:138
  99.4 2.0 %collective-permute-start.2 = (bf16[384,384]{1,0:T(8,128)(2,1)}, bf16[384,384]{1,0:T(8,128)(2,1)S(1)}, u32[]{:S(2)}, u32[]{:S(2)}) collective-permute-start(bf16[384,384]{1,0:T(8,128)(2,1)} %get-tuple-element.14), channel_id=1, source_target_pairs={{0,32},{32,0},{1,33},{33,1},{2,34},{34,2},{3,35},{35,3},{4,36},{36... | collective-permute-start | bytes 884744 | tf_op jit(solution)/shard_map/ppermute | solution.py:153
  101.5 0.9 pad_maximum_fusion.1.wo_ref
  102.4 0.8 collective-permute-done.2
  103.2 1.0 maximum_select_fusion._
  104.2 5.6 %all-to-all-start.3 = ((bf16[32,24,384]{2,1,0:T(8,128)(2,1)}), bf16[32,24,384]{2,1,0:T(8,128)(2,1)S(1)}, u32[]{:S(2)}, u32[]{:S(2)}) async-start(bf16[32,24,384]{2,1,0:T(8,128)(2,1)} %bitcast.18), calls=%async_computation.3 | async-start | bytes 1179648 | tf_op jit(solution)/shard_map/all_to_all | solution.py:157
  109.8 7.8 %shard_map.86 = (f32[128,1536]{1,0:T(8,128)}, bf16[128,1536]{1,0:T(8,128)(2,1)}) custom-call(bf16[256,768]{1,0:T(8,128)(2,1)} %pad_maximum_fusion.2.refs_4_.g_ref, f32[256,1]{1,0:T(8,128)} %copy.21.refs_5_.valid_ref, bf16[2,384,384]{2,1,0:T(8,128)(2,1)} %pad_maximum_fusion.1.wo_ref, bf16[256,384]{1,0:T(8,128)(2,1)} %get-tuple-element.10.att_ref, ...), custom_call_target="tpu_custom_call" | custom-call | flops 10000000000 | bytes 5506048 | tf_op jit(solution)/shard_map/pallas_call | solution.py:138
  117.7 2.3 %collective-permute-start.3 = (bf16[128,1536]{1,0:T(8,128)(2,1)}, bf16[128,1536]{1,0:T(8,128)(2,1)S(1)}, u32[]{:S(2)}, u32[]{:S(2)}) collective-permute-start(bf16[128,1536]{1,0:T(8,128)(2,1)} %get-tuple-element.16), channel_id=1, source_target_pairs={{0,32},{32,0},{1,33},{33,1},{2,34},{34,2},{3,35},{35,3},{4,36},{36... | collective-permute-start | bytes 1179656 | tf_op jit(solution)/shard_map/ppermute | solution.py:153
  120.0 1.5 fusion.perm_ref
  121.5 0.8 fusion.40
  122.2 0.7 copy-done.8
  123.0 3.3 %shard_map.87 = bf16[128,1536]{1,0:T(8,128)(2,1)} custom-call(bf16[128,768]{1,0:T(8,128)(2,1)} %copy-done.5, f32[128,1]{1,0:T(8,128)} %reshape_tile.4.valid_ref, bf16[128,768]{1,0:T(8,128)(2,1)} %get-tuple-element.24.xp_ref, bf16[128,768]{1,0:T(8,128)(2,1)} %get-tuple-element.23.gp_ref, f32[1,768]{1,0:T(1,128)} %reshape.302.refs_2_.gain_ref, ...), custom_call_target="tpu_custom_call" | custom-call | flops 2000000000 | bytes 3345920 | tf_op jit(solution)/shard_map/pallas_call | solution.py:138
  126.4 0.9 copy-done.1
  127.3 25.6 %all_to_all.26 = bf16[16,8,2688]{2,1,0:T(8,128)(2,1)S(1)} all-to-all(bf16[16,8,2688]{2,1,0:T(8,128)(2,1)S(1)} %pad_maximum_fusion), channel_id=1, replica_groups=mesh['y'=8,'core'=2,'x'=4,'z'=8] {'y','core'}, dimensions={0} | all-to-all | bytes 1376256 | tf_op jit(solution)/shard_map/all_to_all | solution.py:157
  153.7 0.8 slice_bitcast_fusion
  (52 shorter events, 3.3 us)
Async XLA Ops:
  7.2 67.6 %copy-start = (f32[768]{0:T(1024)S(1)}, f32[768]{0:T(1024)}, u32[]{:S(2)}) copy-start(f32[768]{0:T(1024)} %param.8) | copy-start | bytes 9220
  7.2 27.3 %copy-start.4 = (bf16[1,128,768]{2,1,0:T(8,128)(2,1)S(1)}, bf16[1,128,768]{2,1,0:T(8,128)(2,1)}, u32[]{:S(2)}) copy-start(bf16[1,128,768]{2,1,0:T(8,128)(2,1)} %param.6) | copy-start | bytes 589828
  7.2 27.3 %copy-start.3 = (bf16[1,128,768]{2,1,0:T(8,128)(2,1)S(1)}, bf16[1,128,768]{2,1,0:T(8,128)(2,1)}, u32[]{:S(2)}) copy-start(bf16[1,128,768]{2,1,0:T(8,128)(2,1)} %param.7) | copy-start | bytes 589828
  7.2 85.0 %all-gather.2.cloned.1.call-start = ((), (), s32[]{:S(2)}) async-start(), calls=%async_computation.5 | async-start | bytes 1990656 | tf_op jit(solution)/shard_map/all_gather | solution.py:193
  31.8 14.7 %copy-start.7 = (s32[2]{0:T(128)S(1)}, s32[2]{0:T(128)}, u32[]{:S(2)}) copy-start(s32[2]{0:T(128)} %param.11) | copy-start | bytes 28
  31.8 34.4 %copy-start.6 = (bf16[24,768]{1,0:T(8,128)(2,1)S(1)}, bf16[24,768]{1,0:T(8,128)(2,1)}, u32[]{:S(2)}) copy-start(bf16[24,768]{1,0:T(8,128)(2,1)} %param.10) | copy-start | bytes 110596
  35.3 29.0 %all-to-all-start.1 = ((bf16[16,16,768]{2,1,0:T(8,128)(2,1)}), bf16[16,16,768]{2,1,0:T(8,128)(2,1)S(1)}, u32[]{:S(2)}, u32[]{:S(2)}) async-start(bf16[16,16,768]{2,1,0:T(8,128)(2,1)} %maximum_select_fusion.1), calls=%async_computation.1 | async-start | bytes 786432 | tf_op jit(solution)/shard_map/all_to_all | solution.py:157
  67.1 21.7 %all-to-all-start.2 = ((bf16[32,24,384]{2,1,0:T(8,128)(2,1)}), bf16[32,24,384]{2,1,0:T(8,128)(2,1)S(1)}, u32[]{:S(2)}, u32[]{:S(2)}) async-start(bf16[32,24,384]{2,1,0:T(8,128)(2,1)} %broadcast_in_dim.55), calls=%async_computation.2 | async-start | bytes 1179648 | tf_op jit(solution)/shard_map/all_to_all | solution.py:157
  71.3 7.3 %collective-permute-start = (bf16[16,16,768]{2,1,0:T(8,128)(2,1)S(1)}, bf16[16,16,768]{2,1,0:T(8,128)(2,1)S(1)}, u32[]{:S(2)}, u32[]{:S(2)}) collective-permute-start(bf16[16,16,768]{2,1,0:T(8,128)(2,1)S(1)} %all-to-all-done.1), channel_id=1, source_target_pairs={{0,32},{32,0},{1,33},{33,1},{2,34},{34,2},{3,35},{35,3},{4,36},{36... | collective-permute-start | bytes 1179656 | tf_op jit(solution)/shard_map/ppermute | solution.py:153
  78.6 0.8 copy-start.5
  88.8 12.7 %collective-permute-start.1 = (bf16[384,384]{1,0:T(8,128)(2,1)S(1)}, bf16[384,384]{1,0:T(8,128)(2,1)S(1)}, u32[]{:S(2)}, u32[]{:S(2)}) collective-permute-start(bf16[384,384]{1,0:T(8,128)(2,1)S(1)} %dynamic-slice_bitcast_fusion), channel_id=1, source_target_pairs={{0,32},{32,0},{1,33},{33,1},{2,34},{34,2},{3,35},{35,3},{4,36},{36... | collective-permute-start | bytes 884744 | tf_op jit(solution)/shard_map/ppermute | solution.py:153
  99.4 3.8 %copy-start.2 = (bf16[384,384]{1,0:T(8,128)(2,1)S(1)}, bf16[384,384]{1,0:T(8,128)(2,1)}, u32[]{:S(2)}) copy-start(bf16[384,384]{1,0:T(8,128)(2,1)} %get-tuple-element.13) | copy-start | bytes 884740
  99.4 3.8 %collective-permute-start.2 = (bf16[384,384]{1,0:T(8,128)(2,1)}, bf16[384,384]{1,0:T(8,128)(2,1)S(1)}, u32[]{:S(2)}, u32[]{:S(2)}) collective-permute-start(bf16[384,384]{1,0:T(8,128)(2,1)} %get-tuple-element.14), channel_id=1, source_target_pairs={{0,32},{32,0},{1,33},{33,1},{2,34},{34,2},{3,35},{35,3},{4,36},{36... | collective-permute-start | bytes 884744 | tf_op jit(solution)/shard_map/ppermute | solution.py:153
  104.2 22.1 %all-to-all-start.3 = ((bf16[32,24,384]{2,1,0:T(8,128)(2,1)}), bf16[32,24,384]{2,1,0:T(8,128)(2,1)S(1)}, u32[]{:S(2)}, u32[]{:S(2)}) async-start(bf16[32,24,384]{2,1,0:T(8,128)(2,1)} %bitcast.18), calls=%async_computation.3 | async-start | bytes 1179648 | tf_op jit(solution)/shard_map/all_to_all | solution.py:157
  117.7 4.6 %collective-permute-start.3 = (bf16[128,1536]{1,0:T(8,128)(2,1)}, bf16[128,1536]{1,0:T(8,128)(2,1)S(1)}, u32[]{:S(2)}, u32[]{:S(2)}) collective-permute-start(bf16[128,1536]{1,0:T(8,128)(2,1)} %get-tuple-element.16), channel_id=1, source_target_pairs={{0,32},{32,0},{1,33},{33,1},{2,34},{34,2},{3,35},{35,3},{4,36},{36... | collective-permute-start | bytes 1179656 | tf_op jit(solution)/shard_map/ppermute | solution.py:153
  122.2 0.7 copy-start.8
  126.3 1.0 copy-start.1
Sparse Core Ops, SparseCore 0:
  32.8 45.6 all-gather.1

commit v3 on v2

--- a/solution.py
+++ b/solution.py
@@ -158,8 +158,7 @@
 
 
 def after(v, first):
-    t = first[(0,) * first.ndim]
-    return jnp.where(t == t, v, jnp.zeros_like(v))
+    return lax.optimization_barrier((v, first))[0]
 
 
 def valid_of(first_frame, frames, slot_len, lengths):
@@ -173,24 +172,22 @@
 def per_device(frames_in, cotangent, norm_gain, w_qkv, w_out, lengths):
     bf, f32 = jnp.bfloat16, jnp.float32
     y_at, core_at = lax.axis_index("y"), lax.axis_index("core")
-    ys, cores, tms = lax.axis_size("y"), lax.axis_size("core"), lax.axis_size("x") * lax.axis_size("z")
+    ys, cores = lax.axis_size("y"), lax.axis_size("core")
+    xs, zs = lax.axis_size("x"), lax.axis_size("z")
+    tms = xs * zs
     mics = ys * cores
     frame_dev, width = frames_in.shape[1:]
     frames = frame_dev // mics
     rows = mics * frames
     piece, wide = w_qkv.shape
-    rows_y, half, cut = piece // ys, wide // cores, width // cores
+    half, cut = wide // cores, width // cores
     first = core_at == 0
 
     mine = jnp.concatenate(
-        [
-            lax.dynamic_slice(w_qkv, (y_at * rows_y, j * width + core_at * cut), (rows_y, cut))
-            for j in range(3)
-        ],
-        axis=1,
-    )
-    mine = exchange(jnp.broadcast_to(mine[None], (tms, rows_y, half)), TM)
-    w_mine = lax.all_gather(mine.reshape(tms * rows_y, half), "y", axis=0, tiled=False)
+        [lax.dynamic_slice(w_qkv, (0, j * width + core_at * cut), (piece, cut)) for j in range(3)], axis=1
+    )
+    mine = exchange(jnp.broadcast_to(mine[None], (xs, piece, half)), "x")
+    w_mine = lax.all_gather(mine.reshape(xs * piece, half), "z", axis=0, tiled=False)
 
     both = jnp.concatenate(
         [frames_in.reshape(mics, frames, width), cotangent.reshape(mics, frames, width)], axis=1
@@ -201,13 +198,9 @@
     wo_part = lax.dynamic_slice(w_out, (0, core_at * cut), (piece, cut))
     wo_part = after(jnp.broadcast_to(wo_part[None], (tms, piece, cut)), both)
     wo_part = exchange(wo_part, TM).reshape(cores, cut, cut)
-    wo_keep = lax.dynamic_index_in_dim(wo_part, core_at, 0, keepdims=False)
-    wo_got = swap(lax.dynamic_index_in_dim(wo_part, 1 - core_at, 0, keepdims=False), "core")
-    wo = jnp.stack([jnp.where(first, wo_keep, wo_got), jnp.where(first, wo_got, wo_keep)])
 
     spot = jnp.arange(width, dtype=jnp.int32)
-    block = tms * rows_y
-    feature = (spot % block) // rows_y * piece + spot // block * rows_y + spot % rows_y
+    feature = (spot // piece % xs * zs + spot // (piece * xs)) * piece + spot % piece
     perm = (spot[:, None] == feature[None, :]).astype(bf)
     gain = norm_gain[feature].reshape(1, width)
     own, near = both.reshape(mics, 2, frames, width), next_both.reshape(mics, 2, frames, width)
@@ -246,6 +239,11 @@
         core_at.reshape(1).astype(jnp.int32), xp, gain, w_mine, g_all, valid_all,
     )
 
+    wo_part = after(wo_part, keep)
+    wo_keep = lax.dynamic_index_in_dim(wo_part, core_at, 0, keepdims=False)
+    wo_got = swap(lax.dynamic_index_in_dim(wo_part, 1 - core_at, 0, keepdims=False), "core")
+    wo = jnp.stack([jnp.where(first, wo_keep, wo_got), jnp.where(first, wo_got, wo_keep)])
+
     got = swap(give, "core")
     term = jnp.where(first, jnp.concatenate([keep, got]), jnp.concatenate([got, keep]))
     own_part, other_part = call(

time: 162 us -> 151 us (0.932)
  starting transfers between devices: 30.6 us -> 43.2 us
  waiting for transfers between devices: 26.1 us -> 14.2 us
  blocking collectives: 49.1 us -> 40.6 us
  between operations: 16.9 us -> 14.3 us
  local copies, waits for them, and re-layouts: 14 us -> 12 us
    all_to_all x3, waiting for transfers between devices: 25.3 us -> 14.1 us  [exchange(): return lax.all_to_all(v, axes, split_axis=0, concat_axis=0, tiled=True)]
    all_to_all x2, blocking collectives: 49.1 us -> 40.6 us  [exchange(): return lax.all_to_all(v, axes, split_axis=0, concat_axis=0, tiled=True)]
    ppermute x4, starting transfers between devices: 9.71 us -> 16 us  [swap(): return lax.ppermute(v, axis, [(0, 1), (1, 0)])]
    all_to_all x3, starting transfers between devices: 20.9 us -> 27.1 us  [exchange(): return lax.all_to_all(v, axes, split_axis=0, concat_axis=0, tiled=True)]
  transfers between devices with their start and end apart: 8 -> 8, of which waited for: 3 -> 1; matrix products, arithmetic and copies ran while one was open for 9% -> 10% of each run, Pallas kernels for 11% -> 12%
where the time goes in v3:
time: 151 us; the launch traced here: 150 us
  starting transfers between devices  43.2 us (29%)
  blocking collectives  40.6 us (27%)
  Pallas kernels  18.3 us (12%)
  between operations  14.3 us (9%)
  waiting for transfers between devices  14.2 us (9%)
  local copies, waits for them, and re-layouts  12 us (8%)
  other arithmetic  6.44 us (4%)
    all_to_all x2, blocking collectives, exchange(): return lax.all_to_all(v, axes, split_axis=0, concat_axis=0, tiled=True)  40.6 us
    all_to_all x3, starting transfers between devices, exchange(): return lax.all_to_all(v, axes, split_axis=0, concat_axis=0, tiled=True)  27.1 us
    pallas_call x3, Pallas kernels, call(): pl.pallas_call(kernel, out_shape=outs, in_specs=[pl.BlockSpec(memory_spac...  18.3 us
    ppermute x4, starting transfers between devices, swap(): return lax.ppermute(v, axis, [(0, 1), (1, 0)])  16 us
    all_to_all x3, waiting for transfers between devices, exchange(): return lax.all_to_all(v, axes, split_axis=0, concat_axis=0, tiled=True)  14.1 us
    gather x1, local copies, waits for them, and re-layouts, per_device(): gain = norm_gain[feature].reshape(1, width)  3.18 us
  transfers between devices with their start and end apart: 8, of which 1 were waited for; matrix products, arithmetic and copies ran while one was open for 10% of the time, Pallas kernels for 12%

profile of v3, /device:TPU:1, one launch (start us, length us, event | category | flops | bytes accessed | tf_op | source)
XLA Modules:
  0.0 149.8 jit_solution(16269171013457434891)
XLA Ops:
  7.3 0.9 constant_dynamic-slice_fusion.3
  8.2 10.1 %all_to_all.25 = bf16[4,24,1152]{2,1,0:T(8,128)(2,1)} all-to-all(bf16[4,24,1152]{2,1,0:T(8,128)(2,1)S(1)} %broadcast_in_dim.24), channel_id=1, replica_groups=mesh['y'=8,'core'=2,'x'=4,'z'=8] {'x'}, dimensions={0} | all-to-all | bytes 442368 | tf_op jit(solution)/shard_map/all_to_all | solution.py:157
  18.3 0.8 pad_maximum_fusion.2
  19.1 9.7 %all-to-all-start.1 = ((bf16[16,16,768]{2,1,0:T(8,128)(2,1)}), bf16[16,16,768]{2,1,0:T(8,128)(2,1)S(1)}, u32[]{:S(2)}, u32[]{:S(2)}) async-start(bf16[16,16,768]{2,1,0:T(8,128)(2,1)} %pad_maximum_fusion.2), calls=%async_computation.1 | async-start | bytes 786432 | tf_op jit(solution)/shard_map/all_to_all | solution.py:157
  29.2 14.1 %all-to-all-done.1 = bf16[16,16,768]{2,1,0:T(8,128)(2,1)S(1)} async-done(((bf16[16,16,768]{2,1,0:T(8,128)(2,1)}), bf16[16,16,768]{2,1,0:T(8,128)(2,1)S(1)}, u32[]{:S(2)}, u32[]{:S(2)}) %all-to-all-start.1) | async-done | bytes 393248 | tf_op jit(solution)/shard_map/all_to_all | solution.py:157
  43.4 1.9 %collective-permute-start = (bf16[16,16,768]{2,1,0:T(8,128)(2,1)S(1)}, bf16[16,16,768]{2,1,0:T(8,128)(2,1)S(1)}, u32[]{:S(2)}, u32[]{:S(2)}) collective-permute-start(bf16[16,16,768]{2,1,0:T(8,128)(2,1)S(1)} %all-to-all-done.1), channel_id=1, source_target_pairs={{0,32},{32,0},{1,33},{33,1},{2,34},{34,2},{3,35},{35,3},{4,36},{36... | collective-permute-start | bytes 1179656 | tf_op jit(solution)/shard_map/ppermute | solution.py:153
  45.3 0.8 copy.21.refs_5_.valid_ref
  46.1 3.2 %gather_fusion = f32[768]{0:T(1024)S(1)} fusion(f32[768]{0:T(1024)S(1)} %copy-done.1, s32[1024]{0:T(1024)S(1)} %pad_clamp_fusion), kind=kCustom, calls=%fused_computation | custom fusion | bytes 9216 | tf_op jit(solution)/shard_map/gather | solution.py:205
  49.3 0.6 reshape.316.refs_2_.gain_ref
  49.9 0.9 broadcast_in_dim.27
  50.8 10.6 %all-to-all-start.2 = ((bf16[32,24,384]{2,1,0:T(8,128)(2,1)}), bf16[32,24,384]{2,1,0:T(8,128)(2,1)S(1)}, u32[]{:S(2)}, u32[]{:S(2)}) async-start(bf16[32,24,384]{2,1,0:T(8,128)(2,1)} %broadcast_in_dim.27), calls=%async_computation.2 | async-start | bytes 1179648 | tf_op jit(solution)/shard_map/all_to_all | solution.py:157
  61.4 0.7 fusion.2
  62.2 0.8 slice.49.refs_1_
  63.0 0.8 pad_maximum_fusion.3.refs_4_.g_ref
  63.8 7.2 %shard_map.85 = (bf16[256,1152]{1,0:T(8,128)(2,1)}, f32[12,128,128]{2,1,0:T(8,128)}, bf16[256,384]{1,0:T(8,128)(2,1)}, bf16[384,384]{1,0:T(8,128)(2,1)}, bf16[384,384]{1,0:T(8,128)(2,1)}) custom-call(s32[1]{0:T(128)} %bitcast.10.refs_0_, bf16[256,768]{1,0:T(8,128)(2,1)} %slice.49.refs_1_, f32[1,768]{1,0:T(1,128)} %reshape.316.refs_2_.gain_ref, ...), custom_call_target="tpu_custom_call" | custom-call | flops 8000000000 | bytes 4722692 | tf_op jit(solution)/shard_map/pallas_call | solution.py:138
  70.9 8.5 %collective-permute-start.2 = (bf16[384,384]{1,0:T(8,128)(2,1)}, bf16[384,384]{1,0:T(8,128)(2,1)S(1)}, u32[]{:S(2)}, u32[]{:S(2)}) collective-permute-start(bf16[384,384]{1,0:T(8,128)(2,1)} %get-tuple-element.20), channel_id=1, source_target_pairs={{0,32},{32,0},{1,33},{33,1},{2,34},{34,2},{3,35},{35,3},{4,36},{36... | collective-permute-start | bytes 884744 | tf_op jit(solution)/shard_map/ppermute | solution.py:153
  79.5 2.9 %collective-permute-start.1 = (bf16[384,384]{1,0:T(8,128)(2,1)S(1)}, bf16[384,384]{1,0:T(8,128)(2,1)S(1)}, u32[]{:S(2)}, u32[]{:S(2)}) collective-permute-start(bf16[384,384]{1,0:T(8,128)(2,1)S(1)} %dynamic-slice_bitcast_fusion), channel_id=1, source_target_pairs={{0,32},{32,0},{1,33},{33,1},{2,34},{34,2},{3,35},{35,3},{4,36},{36... | collective-permute-start | bytes 884744 | tf_op jit(solution)/shard_map/ppermute | solution.py:153
  82.4 0.7 reshape_tile.4.valid_ref
  83.1 2.0 %maximum_select_fusion._ = bf16[768,384]{1,0:T(8,128)(2,1)} fusion(bf16[384,384]{1,0:T(8,128)(2,1)S(1)} %collective-permute-done.2, bf16[384,384]{1,0:T(8,128)(2,1)} %get-tuple-element.15, pred[]{:T(512)S(6)} %eq.60), kind=kLoop, calls=%fused_computation.13 | loop fusion | flops 2654208 | bytes 1179649 | tf_op jit(solution)/shard_map/jit(_where)/select_n | solution.py:248
  85.2 6.9 %all-to-all-start.3 = ((bf16[32,24,384]{2,1,0:T(8,128)(2,1)}), bf16[32,24,384]{2,1,0:T(8,128)(2,1)S(1)}, u32[]{:S(2)}, u32[]{:S(2)}) async-start(bf16[32,24,384]{2,1,0:T(8,128)(2,1)} %bitcast.17), calls=%async_computation.3 | async-start | bytes 1179648 | tf_op jit(solution)/shard_map/all_to_all | solution.py:157
  92.1 0.9 pad_maximum_fusion.1.wo_ref
  93.0 7.8 %shard_map.86 = (f32[128,1536]{1,0:T(8,128)}, bf16[128,1536]{1,0:T(8,128)(2,1)}) custom-call(bf16[256,768]{1,0:T(8,128)(2,1)} %pad_maximum_fusion.3.refs_4_.g_ref, f32[256,1]{1,0:T(8,128)} %copy.21.refs_5_.valid_ref, bf16[2,384,384]{2,1,0:T(8,128)(2,1)} %pad_maximum_fusion.1.wo_ref, bf16[256,384]{1,0:T(8,128)(2,1)} %get-tuple-element.17.att_ref, ...), custom_call_target="tpu_custom_call" | custom-call | flops 10000000000 | bytes 5506048 | tf_op jit(solution)/shard_map/pallas_call | solution.py:138
  100.9 2.7 %collective-permute-start.3 = (bf16[128,1536]{1,0:T(8,128)(2,1)}, bf16[128,1536]{1,0:T(8,128)(2,1)S(1)}, u32[]{:S(2)}, u32[]{:S(2)}) collective-permute-start(bf16[128,1536]{1,0:T(8,128)(2,1)} %get-tuple-element.22), channel_id=1, source_target_pairs={{0,32},{32,0},{1,33},{33,1},{2,34},{34,2},{3,35},{35,3},{4,36},{36... | collective-permute-start | bytes 1179656 | tf_op jit(solution)/shard_map/ppermute | solution.py:153
  103.5 1.4 fusion.perm_ref
  105.0 0.8 fusion.34
  105.8 0.8 copy-done.7
  106.5 3.3 %shard_map.87 = bf16[128,1536]{1,0:T(8,128)(2,1)} custom-call(bf16[128,768]{1,0:T(8,128)(2,1)} %copy-done.5, f32[128,1]{1,0:T(8,128)} %reshape_tile.4.valid_ref, bf16[128,768]{1,0:T(8,128)(2,1)} %get-tuple-element.30.xp_ref, bf16[128,768]{1,0:T(8,128)(2,1)} %get-tuple-element.29.gp_ref, f32[1,768]{1,0:T(1,128)} %reshape.316.refs_2_.gain_ref, ...), custom_call_target="tpu_custom_call" | custom-call | flops 2000000000 | bytes 3345920 | tf_op jit(solution)/shard_map/pallas_call | solution.py:138
  109.8 0.1 reduce_sum.41
  110.0 0.9 copy-done.2
  110.9 30.5 %all_to_all.26 = bf16[16,8,2688]{2,1,0:T(8,128)(2,1)S(1)} all-to-all(bf16[16,8,2688]{2,1,0:T(8,128)(2,1)S(1)} %pad_maximum_fusion), channel_id=1, replica_groups=mesh['y'=8,'core'=2,'x'=4,'z'=8] {'y','core'}, dimensions={0} | all-to-all | bytes 1376256 | tf_op jit(solution)/shard_map/all_to_all | solution.py:157
  141.5 0.6 copy.24
  142.2 0.8 slice_bitcast_fusion
  (47 shorter events, 0.9 us)
Async XLA Ops:
  7.2 42.7 %copy-start = (bf16[24,768]{1,0:T(8,128)(2,1)S(1)}, bf16[24,768]{1,0:T(8,128)(2,1)}, u32[]{:S(2)}) copy-start(bf16[24,768]{1,0:T(8,128)(2,1)} %param.10) | copy-start | bytes 110596
  7.2 11.1 %copy-start.4 = (bf16[1,128,768]{2,1,0:T(8,128)(2,1)S(1)}, bf16[1,128,768]{2,1,0:T(8,128)(2,1)}, u32[]{:S(2)}) copy-start(bf16[1,128,768]{2,1,0:T(8,128)(2,1)} %param.6) | copy-start | bytes 589828
  7.2 11.1 %copy-start.3 = (bf16[1,128,768]{2,1,0:T(8,128)(2,1)S(1)}, bf16[1,128,768]{2,1,0:T(8,128)(2,1)}, u32[]{:S(2)}) copy-start(bf16[1,128,768]{2,1,0:T(8,128)(2,1)} %param.7) | copy-start | bytes 589828
  7.2 56.6 %all-gather.2.cloned.1.call-start = ((), (), s32[]{:S(2)}) async-start(), calls=%async_computation.5 | async-start | bytes 1990656 | tf_op jit(solution)/shard_map/all_gather | solution.py:190
  8.2 20.7 %copy-start.6 = (s32[2]{0:T(128)S(1)}, s32[2]{0:T(128)}, u32[]{:S(2)}) copy-start(s32[2]{0:T(128)} %param.11) | copy-start | bytes 28
  8.2 37.9 %copy-start.1 = (f32[768]{0:T(1024)S(1)}, f32[768]{0:T(1024)}, u32[]{:S(2)}) copy-start(f32[768]{0:T(1024)} %param.8) | copy-start | bytes 9220
  19.1 24.2 %all-to-all-start.1 = ((bf16[16,16,768]{2,1,0:T(8,128)(2,1)}), bf16[16,16,768]{2,1,0:T(8,128)(2,1)S(1)}, u32[]{:S(2)}, u32[]{:S(2)}) async-start(bf16[16,16,768]{2,1,0:T(8,128)(2,1)} %pad_maximum_fusion.2), calls=%async_computation.1 | async-start | bytes 786432 | tf_op jit(solution)/shard_map/all_to_all | solution.py:157
  43.4 18.0 %collective-permute-start = (bf16[16,16,768]{2,1,0:T(8,128)(2,1)S(1)}, bf16[16,16,768]{2,1,0:T(8,128)(2,1)S(1)}, u32[]{:S(2)}, u32[]{:S(2)}) collective-permute-start(bf16[16,16,768]{2,1,0:T(8,128)(2,1)S(1)} %all-to-all-done.1), channel_id=1, source_target_pairs={{0,32},{32,0},{1,33},{33,1},{2,34},{34,2},{3,35},{35,3},{4,36},{36... | collective-permute-start | bytes 1179656 | tf_op jit(solution)/shard_map/ppermute | solution.py:153
  50.8 28.7 %all-to-all-start.2 = ((bf16[32,24,384]{2,1,0:T(8,128)(2,1)}), bf16[32,24,384]{2,1,0:T(8,128)(2,1)S(1)}, u32[]{:S(2)}, u32[]{:S(2)}) async-start(bf16[32,24,384]{2,1,0:T(8,128)(2,1)} %broadcast_in_dim.27), calls=%async_computation.2 | async-start | bytes 1179648 | tf_op jit(solution)/shard_map/all_to_all | solution.py:157
  61.4 0.8 copy-start.5
  70.9 12.2 %collective-permute-start.2 = (bf16[384,384]{1,0:T(8,128)(2,1)}, bf16[384,384]{1,0:T(8,128)(2,1)S(1)}, u32[]{:S(2)}, u32[]{:S(2)}) collective-permute-start(bf16[384,384]{1,0:T(8,128)(2,1)} %get-tuple-element.20), channel_id=1, source_target_pairs={{0,32},{32,0},{1,33},{33,1},{2,34},{34,2},{3,35},{35,3},{4,36},{36... | collective-permute-start | bytes 884744 | tf_op jit(solution)/shard_map/ppermute | solution.py:153
  79.5 12.6 %collective-permute-start.1 = (bf16[384,384]{1,0:T(8,128)(2,1)S(1)}, bf16[384,384]{1,0:T(8,128)(2,1)S(1)}, u32[]{:S(2)}, u32[]{:S(2)}) collective-permute-start(bf16[384,384]{1,0:T(8,128)(2,1)S(1)} %dynamic-slice_bitcast_fusion), channel_id=1, source_target_pairs={{0,32},{32,0},{1,33},{33,1},{2,34},{34,2},{3,35},{35,3},{4,36},{36... | collective-permute-start | bytes 884744 | tf_op jit(solution)/shard_map/ppermute | solution.py:153
  85.2 24.6 %all-to-all-start.3 = ((bf16[32,24,384]{2,1,0:T(8,128)(2,1)}), bf16[32,24,384]{2,1,0:T(8,128)(2,1)S(1)}, u32[]{:S(2)}, u32[]{:S(2)}) async-start(bf16[32,24,384]{2,1,0:T(8,128)(2,1)} %bitcast.17), calls=%async_computation.3 | async-start | bytes 1179648 | tf_op jit(solution)/shard_map/all_to_all | solution.py:157
  100.9 4.9 %collective-permute-start.3 = (bf16[128,1536]{1,0:T(8,128)(2,1)}, bf16[128,1536]{1,0:T(8,128)(2,1)S(1)}, u32[]{:S(2)}, u32[]{:S(2)}) collective-permute-start(bf16[128,1536]{1,0:T(8,128)(2,1)} %get-tuple-element.22), channel_id=1, source_target_pairs={{0,32},{32,0},{1,33},{33,1},{2,34},{34,2},{3,35},{35,3},{4,36},{36... | collective-permute-start | bytes 1179656 | tf_op jit(solution)/shard_map/ppermute | solution.py:153
  105.8 0.8 copy-start.7
  109.8 1.0 copy-start.2
Sparse Core Ops, SparseCore 0:
  18.4 44.1 all-gather.1

commit v4 on v3

--- a/solution.py
+++ b/solution.py
@@ -11,7 +11,7 @@
 TM = ("x", "z")
 NEG = -1e30
 VMEM_LIMIT = 56 * 1024 * 1024
-FWD_COST, BWD_COST, END_COST = 8_000_000_000, 10_000_000_000, 2_000_000_000
+FWD_COST, BWD_COST, END_COST = 8_000_000_000, 1000, 1000
 
 
 def dot_nn(a, b):
@@ -79,19 +79,17 @@
 
 
 def bwd_kernel(
-    g_ref, valid_ref, wo_ref, att_ref, qkv_ref, p_ref, w_ref, _, own_ref, other_ref, gqkv_ref
+    core_ref, g_ref, valid_ref, wo_ref, att_ref, order_ref, qkv_ref, p_ref, w_ref, _, own_ref, other_ref, gqkv_ref
 ):
     width = g_ref.shape[1]
     rows, mine = g_ref.shape[0] // 2, att_ref.shape[1]
-    cut = wo_ref.shape[2]
-    att = att_ref[...]
-    for c in range(2):
-        part = dot_nn(att, wo_ref[c])
-        own_ref[:, c * cut : (c + 1) * cut] = part[:rows]
-        other_ref[:, c * cut : (c + 1) * cut] = part[rows:].astype(jnp.bfloat16)
+    wo = wo_ref[:, core_ref[0]].reshape(mine, width)
+    part = dot_nn(att_ref[...], wo)
+    own_ref[:, :width] = part[:rows]
+    other_ref[:, :width] = part[rows:].astype(jnp.bfloat16)
     gz = (g_ref[...].astype(jnp.float32) * valid_ref[...]).astype(jnp.bfloat16)
-    ga_all = dot_nt(gz[:, :cut], wo_ref[0]) + dot_nt(gz[:, cut:], wo_ref[1])
-    ga_all = ga_all.astype(jnp.bfloat16)
+    ga_all = dot_nt(gz, wo).astype(jnp.bfloat16)
+    ga_all = dot_nt(ga_all, order_ref[...]).astype(jnp.bfloat16)
     low = low_half(rows)
     for start, at, index in pairs_of(rows, mine):
         here = pl.ds(start, rows)
@@ -182,6 +180,7 @@
     piece, wide = w_qkv.shape
     half, cut = wide // cores, width // cores
     first = core_at == 0
+    core = core_at.reshape(1).astype(jnp.int32)
 
     mine = jnp.concatenate(
         [lax.dynamic_slice(w_qkv, (0, j * width + core_at * cut), (piece, cut)) for j in range(3)], axis=1
@@ -195,9 +194,9 @@
     both = exchange(after(both, mine), MIC)
     next_both = swap(both, "core")
 
-    wo_part = lax.dynamic_slice(w_out, (0, core_at * cut), (piece, cut))
-    wo_part = after(jnp.broadcast_to(wo_part[None], (tms, piece, cut)), both)
-    wo_part = exchange(wo_part, TM).reshape(cores, cut, cut)
+    wo_part = exchange(after(jnp.broadcast_to(w_out[None], (xs, piece, width)), both), "x")
+    wo = lax.all_gather(wo_part.reshape(xs * piece, width), "z", axis=0, tiled=False)
+    wo = wo.reshape(zs, cores, xs // cores * piece, width)
 
     spot = jnp.arange(width, dtype=jnp.int32)
     feature = (spot // piece % xs * zs + spot // (piece * xs)) * piece + spot % piece
@@ -236,22 +235,23 @@
         ),
         (),
         FWD_COST,
-        core_at.reshape(1).astype(jnp.int32), xp, gain, w_mine, g_all, valid_all,
-    )
-
-    wo_part = after(wo_part, keep)
-    wo_keep = lax.dynamic_index_in_dim(wo_part, core_at, 0, keepdims=False)
-    wo_got = swap(lax.dynamic_index_in_dim(wo_part, 1 - core_at, 0, keepdims=False), "core")
-    wo = jnp.stack([jnp.where(first, wo_keep, wo_got), jnp.where(first, wo_got, wo_keep)])
+        core, xp, gain, w_mine, g_all, valid_all,
+    )
 
     got = swap(give, "core")
     term = jnp.where(first, jnp.concatenate([keep, got]), jnp.concatenate([got, keep]))
+    spot = jnp.arange(cut, dtype=jnp.int32)
+    near_xs = xs // cores
+    row = (spot // piece % near_xs * zs + spot // (piece * near_xs)) * piece + spot % piece
+    order = (spot[:, None] == row[None, :]).astype(bf)
+    att = jnp.dot(att, order, preferred_element_type=f32).astype(bf)
+
     own_part, other_part = call(
         bwd_kernel,
         (shape((rows, 2 * width), f32), shape((rows, 2 * width), bf)),
         (pltpu.VMEM((2 * rows, half), bf),),
         BWD_COST,
-        g_all, valid_all, wo, att, qkv, probs, w_mine, behind=(term,),
+        core, g_all, valid_all, after(wo, term), att, order, qkv, probs, w_mine, behind=(term,),
     )
     term = exchange(term.reshape(tms, piece, cut), TM)
     term = jnp.sum(term.astype(f32), axis=0).astype(bf)

time: 151 us -> 171 us (1.13)
  waiting for transfers between devices: 14.2 us -> 44.6 us
  starting transfers between devices: 43.2 us -> 34 us
  blocking collectives: 40.6 us -> 38 us
    all_gather x0 -> x1, waiting for transfers between devices: none -> 23.3 us  [per_device(): lax.all_gather(wo_part.reshape(xs * piece, width), 'z', axis=0, tiled=False)]
    all_to_all x3, starting transfers between devices: 27.1 us -> 20.7 us  [exchange(): return lax.all_to_all(v, axes, split_axis=0, concat_axis=0, tiled=True)]
    all_to_all x3, waiting for transfers between devices: 14.1 us -> 19 us  [exchange(): return lax.all_to_all(v, axes, split_axis=0, concat_axis=0, tiled=True)]
    ppermute x4 -> x3, starting transfers between devices: 16 us -> 13.2 us  [swap(): return lax.ppermute(v, axis, [(0, 1), (1, 0)])]
    all_to_all x2, blocking collectives: 40.6 us -> 38 us  [exchange(): return lax.all_to_all(v, axes, split_axis=0, concat_axis=0, tiled=True)]
  transfers between devices with their start and end apart: 8 -> 8, of which waited for: 1 -> 5; matrix products, arithmetic and copies ran while one was open for 10% -> 9% of each run, Pallas kernels for 12% -> 11%
where the time goes in v4:
time: 171 us
  waiting for transfers between devices  44.6 us (26%)
  blocking collectives  38 us (22%)
  starting transfers between devices  34 us (20%)
  Pallas kernels  19.3 us (11%)
  between operations  14.3 us (8%)
  local copies, waits for them, and re-layouts  12.4 us (7%)
  other arithmetic  6.35 us (4%)
  matrix products  1.72 us (1%)
    all_to_all x2, blocking collectives, exchange(): return lax.all_to_all(v, axes, split_axis=0, concat_axis=0, tiled=True)  38 us
    all_gather x1, waiting for transfers between devices, per_device(): lax.all_gather(wo_part.reshape(xs * piece, width), 'z', axis=0, tiled=False)  23.3 us
    all_to_all x3, starting transfers between devices, exchange(): return lax.all_to_all(v, axes, split_axis=0, concat_axis=0, tiled=True)  20.7 us
    pallas_call x3, Pallas kernels, call(): pl.pallas_call(kernel, out_shape=outs, in_specs=[pl.BlockSpec(memory_spac...  19.3 us
    all_to_all x3, waiting for transfers between devices, exchange(): return lax.all_to_all(v, axes, split_axis=0, concat_axis=0, tiled=True)  19 us
    ppermute x3, starting transfers between devices, swap(): return lax.ppermute(v, axis, [(0, 1), (1, 0)])  13.2 us
  transfers between devices with their start and end apart: 8, of which 5 were waited for; matrix products, arithmetic and copies ran while one was open for 9% of the time, Pallas kernels for 11%

profile of v4, /device:TPU:1, one launch (start us, length us, event | category | flops | bytes accessed | tf_op | source)
XLA Modules:
  0.0 170.6 jit_solution(8725209382769891178)
XLA Ops:
  7.3 0.9 constant_dynamic-slice_fusion.2
  8.2 10.1 %all_to_all.25 = bf16[4,24,1152]{2,1,0:T(8,128)(2,1)} all-to-all(bf16[4,24,1152]{2,1,0:T(8,128)(2,1)S(1)} %broadcast_in_dim.24), channel_id=1, replica_groups=mesh['y'=8,'core'=2,'x'=4,'z'=8] {'x'}, dimensions={0} | all-to-all | bytes 442368 | tf_op jit(solution)/shard_map/all_to_all | solution.py:155
  18.3 0.8 pad_maximum_fusion.1
  19.1 9.7 %all-to-all-start.1 = ((bf16[16,16,768]{2,1,0:T(8,128)(2,1)}), bf16[16,16,768]{2,1,0:T(8,128)(2,1)S(1)}, u32[]{:S(2)}, u32[]{:S(2)}) async-start(bf16[16,16,768]{2,1,0:T(8,128)(2,1)} %pad_maximum_fusion.1), calls=%async_computation.1 | async-start | bytes 786432 | tf_op jit(solution)/shard_map/all_to_all | solution.py:155
  29.2 14.2 %all-to-all-done.1 = bf16[16,16,768]{2,1,0:T(8,128)(2,1)S(1)} async-done(((bf16[16,16,768]{2,1,0:T(8,128)(2,1)}), bf16[16,16,768]{2,1,0:T(8,128)(2,1)S(1)}, u32[]{:S(2)}, u32[]{:S(2)}) %all-to-all-start.1) | async-done | bytes 393248 | tf_op jit(solution)/shard_map/all_to_all | solution.py:155
  43.3 1.9 %collective-permute-start = (bf16[16,16,768]{2,1,0:T(8,128)(2,1)S(1)}, bf16[16,16,768]{2,1,0:T(8,128)(2,1)S(1)}, u32[]{:S(2)}, u32[]{:S(2)}) collective-permute-start(bf16[16,16,768]{2,1,0:T(8,128)(2,1)S(1)} %all-to-all-done.1), channel_id=1, source_target_pairs={{0,32},{32,0},{1,33},{33,1},{2,34},{34,2},{3,35},{35,3},{4,36},{36... | collective-permute-start | bytes 1179656 | tf_op jit(solution)/shard_map/ppermute | solution.py:151
  45.2 0.8 copy.21.refs_5_.valid_ref
  46.0 3.2 %gather_fusion = f32[768]{0:T(1024)S(1)} fusion(f32[768]{0:T(1024)S(1)} %copy-done, s32[1024]{0:T(1024)S(1)} %pad_clamp_fusion), kind=kCustom, calls=%fused_computation | custom fusion | bytes 9216 | tf_op jit(solution)/shard_map/gather | solution.py:204
  50.5 3.3 %all-to-all-start.2 = ((bf16[4,24,768]{2,1,0:T(8,128)(2,1)}), bf16[4,24,768]{2,1,0:T(8,128)(2,1)S(1)}, u32[]{:S(2)}, u32[]{:S(2)}) async-start(bf16[4,24,768]{2,1,0:T(8,128)(2,1)} %broadcast_in_dim.27), calls=%async_computation.2 | async-start | bytes 294912 | tf_op jit(solution)/shard_map/all_to_all | solution.py:155
  54.0 4.8 %all-to-all-done.2 = bf16[4,24,768]{2,1,0:T(8,128)(2,1)S(1)} async-done(((bf16[4,24,768]{2,1,0:T(8,128)(2,1)}), bf16[4,24,768]{2,1,0:T(8,128)(2,1)S(1)}, u32[]{:S(2)}, u32[]{:S(2)}) %all-to-all-start.2) | async-done | bytes 147488 | tf_op jit(solution)/shard_map/all_to_all | solution.py:155
  59.5 0.7 fusion.2
  60.3 0.8 slice.49.refs_1_
  61.0 0.8 pad_maximum_fusion.2.refs_4_.g_ref
  61.8 0.9 all-gather.5.cloned.1.call-done.refs_3_.w_ref
  62.7 7.1 %shard_map.85 = (bf16[256,1152]{1,0:T(8,128)(2,1)}, f32[12,128,128]{2,1,0:T(8,128)}, bf16[256,384]{1,0:T(8,128)(2,1)}, bf16[384,384]{1,0:T(8,128)(2,1)}, bf16[384,384]{1,0:T(8,128)(2,1)}) custom-call(s32[1]{0:T(128)} %bitcast.7.refs_0_.core_ref, bf16[256,768]{1,0:T(8,128)(2,1)} %slice.49.refs_1_, f32[1,768]{1,0:T(1,128)} %reshape.356.refs_2_.gain_ref, ...), custom_call_target="tpu_custom_call" | custom-call | flops 8000000000 | bytes 4722692 | tf_op jit(solution)/shard_map/pallas_call | solution.py:136
  69.8 5.5 %collective-permute-start.1 = (bf16[384,384]{1,0:T(8,128)(2,1)}, bf16[384,384]{1,0:T(8,128)(2,1)S(1)}, u32[]{:S(2)}, u32[]{:S(2)}) collective-permute-start(bf16[384,384]{1,0:T(8,128)(2,1)} %get-tuple-element.16), channel_id=1, source_target_pairs={{0,32},{32,0},{1,33},{33,1},{2,34},{34,2},{3,35},{35,3},{4,36},{36... | collective-permute-start | bytes 884744 | tf_op jit(solution)/shard_map/ppermute | solution.py:151
  75.4 1.4 collective-permute-done.1
  76.8 2.1 %maximum_select_fusion._ = bf16[768,384]{1,0:T(8,128)(2,1)} fusion(bf16[384,384]{1,0:T(8,128)(2,1)S(1)} %collective-permute-done.1, bf16[384,384]{1,0:T(8,128)(2,1)} %get-tuple-element.15, pred[]{:T(512)S(6)} %eq.82), kind=kLoop, calls=%fused_computation.13 | loop fusion | flops 2654208 | bytes 1179649 | tf_op jit(solution)/shard_map/jit(_where)/select_n | solution.py:242
  78.9 7.6 %all-to-all-start.3 = ((bf16[32,24,384]{2,1,0:T(8,128)(2,1)}), bf16[32,24,384]{2,1,0:T(8,128)(2,1)S(1)}, u32[]{:S(2)}, u32[]{:S(2)}) async-start(bf16[32,24,384]{2,1,0:T(8,128)(2,1)} %bitcast.14), calls=%async_computation.3 | async-start | bytes 1179648 | tf_op jit(solution)/shard_map/all_to_all | solution.py:155
  86.5 0.7 reshape_tile.4.valid_ref
  87.3 0.8 fusion.9.order_ref
  88.1 1.0 convolution_convert_fusion.att_ref
  89.1 23.3 %all-gather.3.cloned.1.call-done = bf16[8,96,768]{2,1,0:T(8,128)(2,1)} async-done(((bf16[1,96,768]{2,1,0:T(8,128)(2,1)}), bf16[8,96,768]{2,1,0:T(8,128)(2,1)}) %all-gather.3.cloned.1.call-update) | async-done | bytes 1179664 | tf_op jit(solution)/shard_map/all_gather | solution.py:198
  112.4 8.8 %shard_map.86 = (f32[128,1536]{1,0:T(8,128)}, bf16[128,1536]{1,0:T(8,128)(2,1)}) custom-call(s32[1]{0:T(128)} %bitcast.7.refs_0_.core_ref, bf16[256,768]{1,0:T(8,128)(2,1)} %pad_maximum_fusion.2.refs_4_.g_ref, f32[256,1]{1,0:T(8,128)} %copy.21.refs_5_.valid_ref, bf16[8,2,48,768]{3,2,1,0:T(8,128)(2,1)} %bitcast.40, ...), custom_call_target="tpu_custom_call" | custom-call | flops 1000 | bytes 6390788 | tf_op jit(solution)/shard_map/pallas_call | solution.py:136
  121.2 5.8 %collective-permute-start.2 = (bf16[128,1536]{1,0:T(8,128)(2,1)}, bf16[128,1536]{1,0:T(8,128)(2,1)S(1)}, u32[]{:S(2)}, u32[]{:S(2)}) collective-permute-start(bf16[128,1536]{1,0:T(8,128)(2,1)} %get-tuple-element.22), channel_id=1, source_target_pairs={{0,32},{32,0},{1,33},{33,1},{2,34},{34,2},{3,35},{35,3},{4,36},{36... | collective-permute-start | bytes 1179656 | tf_op jit(solution)/shard_map/ppermute | solution.py:151
  127.0 1.5 fusion.perm_ref
  128.4 0.8 fusion.46
  129.2 0.8 copy-done.4
  130.0 3.3 %shard_map.87 = bf16[128,1536]{1,0:T(8,128)(2,1)} custom-call(bf16[128,768]{1,0:T(8,128)(2,1)} %copy-done.2, f32[128,1]{1,0:T(8,128)} %reshape_tile.4.valid_ref, bf16[128,768]{1,0:T(8,128)(2,1)} %get-tuple-element.28.xp_ref, bf16[128,768]{1,0:T(8,128)(2,1)} %get-tuple-element.27.gp_ref, f32[1,768]{1,0:T(1,128)} %reshape.356.refs_2_.gain_ref, ...), custom_call_target="tpu_custom_call" | custom-call | flops 1000 | bytes 3345920 | tf_op jit(solution)/shard_map/pallas_call | solution.py:136
  133.4 0.9 copy-done.1
  134.3 27.9 %all_to_all.26 = bf16[16,8,2688]{2,1,0:T(8,128)(2,1)S(1)} all-to-all(bf16[16,8,2688]{2,1,0:T(8,128)(2,1)S(1)} %pad_maximum_fusion), channel_id=1, replica_groups=mesh['y'=8,'core'=2,'x'=4,'z'=8] {'y','core'}, dimensions={0} | all-to-all | bytes 1376256 | tf_op jit(solution)/shard_map/all_to_all | solution.py:155
  163.0 0.8 slice_bitcast_fusion
  (51 shorter events, 3.5 us)
Async XLA Ops:
  7.2 38.9 %copy-start = (f32[768]{0:T(1024)S(1)}, f32[768]{0:T(1024)}, u32[]{:S(2)}) copy-start(f32[768]{0:T(1024)} %param.8) | copy-start | bytes 9220
  7.2 11.1 %copy-start.6 = (bf16[1,128,768]{2,1,0:T(8,128)(2,1)S(1)}, bf16[1,128,768]{2,1,0:T(8,128)(2,1)}, u32[]{:S(2)}) copy-start(bf16[1,128,768]{2,1,0:T(8,128)(2,1)} %param.6) | copy-start | bytes 589828
  7.2 11.1 %copy-start.5 = (bf16[1,128,768]{2,1,0:T(8,128)(2,1)S(1)}, bf16[1,128,768]{2,1,0:T(8,128)(2,1)}, u32[]{:S(2)}) copy-start(bf16[1,128,768]{2,1,0:T(8,128)(2,1)} %param.7) | copy-start | bytes 589828
  7.2 55.5 %all-gather.5.cloned.1.call-start = ((), (), s32[]{:S(2)}) async-start(), calls=%async_computation.6 | async-start | bytes 1990656 | tf_op jit(solution)/shard_map/all_gather | solution.py:189
  8.2 20.6 %copy-start.8 = (s32[2]{0:T(128)S(1)}, s32[2]{0:T(128)}, u32[]{:S(2)}) copy-start(s32[2]{0:T(128)} %param.11) | copy-start | bytes 28
  19.1 24.2 %all-to-all-start.1 = ((bf16[16,16,768]{2,1,0:T(8,128)(2,1)}), bf16[16,16,768]{2,1,0:T(8,128)(2,1)S(1)}, u32[]{:S(2)}, u32[]{:S(2)}) async-start(bf16[16,16,768]{2,1,0:T(8,128)(2,1)} %pad_maximum_fusion.1), calls=%async_computation.1 | async-start | bytes 786432 | tf_op jit(solution)/shard_map/all_to_all | solution.py:155
  43.3 16.2 %collective-permute-start = (bf16[16,16,768]{2,1,0:T(8,128)(2,1)S(1)}, bf16[16,16,768]{2,1,0:T(8,128)(2,1)S(1)}, u32[]{:S(2)}, u32[]{:S(2)}) collective-permute-start(bf16[16,16,768]{2,1,0:T(8,128)(2,1)S(1)} %all-to-all-done.1), channel_id=1, source_target_pairs={{0,32},{32,0},{1,33},{33,1},{2,34},{34,2},{3,35},{35,3},{4,36},{36... | collective-permute-start | bytes 1179656 | tf_op jit(solution)/shard_map/ppermute | solution.py:151
  46.0 3.8 %copy-start.7 = (bf16[24,768]{1,0:T(8,128)(2,1)S(1)}, bf16[24,768]{1,0:T(8,128)(2,1)}, u32[]{:S(2)}) copy-start(bf16[24,768]{1,0:T(8,128)(2,1)} %param.10) | copy-start | bytes 110596
  50.5 8.3 %all-to-all-start.2 = ((bf16[4,24,768]{2,1,0:T(8,128)(2,1)}), bf16[4,24,768]{2,1,0:T(8,128)(2,1)S(1)}, u32[]{:S(2)}, u32[]{:S(2)}) async-start(bf16[4,24,768]{2,1,0:T(8,128)(2,1)} %broadcast_in_dim.27), calls=%async_computation.2 | async-start | bytes 294912 | tf_op jit(solution)/shard_map/all_to_all | solution.py:155
  53.9 58.5 %all-gather.3.cloned.1.call-start = ((), (), s32[]{:S(2)}) async-start(), calls=%async_computation.5 | async-start | bytes 1327104 | tf_op jit(solution)/shard_map/all_gather | solution.py:198
  53.9 6.3 %copy-start.2 = (bf16[128,768]{1,0:T(8,128)(2,1)}, bf16[128,768]{1,0:T(8,128)(2,1)S(1)}, u32[]{:S(2)}) copy-start(bf16[128,768]{1,0:T(8,128)(2,1)S(1)} %get-tuple-element.31.x_ref) | copy-start | bytes 589828
  58.8 0.7 copy-start.3
  69.8 6.9 %collective-permute-start.1 = (bf16[384,384]{1,0:T(8,128)(2,1)}, bf16[384,384]{1,0:T(8,128)(2,1)S(1)}, u32[]{:S(2)}, u32[]{:S(2)}) collective-permute-start(bf16[384,384]{1,0:T(8,128)(2,1)} %get-tuple-element.16), channel_id=1, source_target_pairs={{0,32},{32,0},{1,33},{33,1},{2,34},{34,2},{3,35},{35,3},{4,36},{36... | collective-permute-start | bytes 884744 | tf_op jit(solution)/shard_map/ppermute | solution.py:151
  76.8 11.3 %copy-start.9 = (bf16[256,384]{1,0:T(8,128)(2,1)S(1)}, bf16[256,384]{1,0:T(8,128)(2,1)}, u32[]{:S(2)}) copy-start(bf16[256,384]{1,0:T(8,128)(2,1)} %get-tuple-element.18) | copy-start | bytes 589828
  78.9 54.4 %all-to-all-start.3 = ((bf16[32,24,384]{2,1,0:T(8,128)(2,1)}), bf16[32,24,384]{2,1,0:T(8,128)(2,1)S(1)}, u32[]{:S(2)}, u32[]{:S(2)}) async-start(bf16[32,24,384]{2,1,0:T(8,128)(2,1)} %bitcast.14), calls=%async_computation.3 | async-start | bytes 1179648 | tf_op jit(solution)/shard_map/all_to_all | solution.py:155
  121.2 8.0 %collective-permute-start.2 = (bf16[128,1536]{1,0:T(8,128)(2,1)}, bf16[128,1536]{1,0:T(8,128)(2,1)S(1)}, u32[]{:S(2)}, u32[]{:S(2)}) collective-permute-start(bf16[128,1536]{1,0:T(8,128)(2,1)} %get-tuple-element.22), channel_id=1, source_target_pairs={{0,32},{32,0},{1,33},{33,1},{2,34},{34,2},{3,35},{35,3},{4,36},{36... | collective-permute-start | bytes 1179656 | tf_op jit(solution)/shard_map/ppermute | solution.py:151
  129.2 0.8 copy-start.4
  133.3 1.0 copy-start.1
Sparse Core Ops, SparseCore 0:
  18.4 44.2 all-gather.4
  64.8 47.5 all-gather.2

commit v5 on v4

--- a/solution.py
+++ b/solution.py
@@ -44,15 +44,16 @@
             at += 2
 
 
-def fwd_kernel(
-    frames, core_ref, xp_ref, gain_ref, w_ref, g_ref, valid_ref, qkv_ref, p_ref, att_ref, keep_ref, give_ref
-):
-    width = xp_ref.shape[1]
+def fwd_kernel(frames, zs, core_ref, xp_ref, gain_ref, g_ref, valid_ref, *refs):
+    blocks, (qkv_ref, p_ref, att_ref, keep_ref, give_ref, w_ref) = refs[:zs], refs[zs:]
     rows, mine = xp_ref.shape[0] // 2, att_ref.shape[1]
+    width, deep = xp_ref.shape[1], blocks[0].shape[0]
+    for i, block in enumerate(blocks):
+        w_ref[i * deep : (i + 1) * deep, :] = block[:, : 3 * mine]
     xf = xp_ref[...].astype(jnp.float32)
     inv = lax.rsqrt(jnp.mean(xf * xf, axis=-1, keepdims=True) + 1e-05)
     normed = (xf * inv * gain_ref[...]).astype(jnp.bfloat16)
-    qkv_ref[...] = dot_nn(normed, w_ref[...].reshape(width, 3 * mine)).astype(jnp.bfloat16)
+    qkv_ref[...] = dot_nn(normed, w_ref[...]).astype(jnp.bfloat16)
     same = same_frame(rows, frames)
     low = low_half(rows)
     for start, at, index in pairs_of(rows, mine):
@@ -78,12 +79,16 @@
     give_ref[...] = dot_tn(att, jnp.where(first, high_cut, low_cut)).astype(jnp.bfloat16)
 
 
-def bwd_kernel(
-    core_ref, g_ref, valid_ref, wo_ref, att_ref, order_ref, qkv_ref, p_ref, w_ref, _, own_ref, other_ref, gqkv_ref
-):
-    width = g_ref.shape[1]
+def bwd_kernel(zs, g_ref, valid_ref, att_ref, order_ref, qkv_ref, p_ref, *refs):
+    blocks, (_, own_ref, other_ref, gqkv_ref, w_ref, wo_ref) = refs[:zs], refs[zs:]
     rows, mine = g_ref.shape[0] // 2, att_ref.shape[1]
-    wo = wo_ref[:, core_ref[0]].reshape(mine, width)
+    width, deep = g_ref.shape[1], blocks[0].shape[0]
+    for i, block in enumerate(blocks):
+        w_ref[i * deep : (i + 1) * deep, :] = block[:, : 3 * mine]
+        here = pl.ds(i * deep // 2, deep // 2)
+        wo_ref[here, :mine] = block[: deep // 2, 3 * mine :]
+        wo_ref[here, mine:] = block[deep // 2 :, 3 * mine :]
+    wo = wo_ref[...]
     part = dot_nn(att_ref[...], wo)
     own_ref[:, :width] = part[:rows]
     other_ref[:, :width] = part[rows:].astype(jnp.bfloat16)
@@ -111,7 +116,7 @@
             gqkv_ref[here, j * mine + at : j * mine + at + 2 * HD] = jnp.where(
                 low, grad[0], grad[1]
             ).astype(jnp.bfloat16)
-    gh = dot_nt(gqkv_ref[...], w_ref[...].reshape(width, 3 * mine))
+    gh = dot_nt(gqkv_ref[...], w_ref[...])
     own_ref[:, width:] = gh[:rows]
     other_ref[:, width:] = gh[rows:].astype(jnp.bfloat16)
 
@@ -151,6 +156,15 @@
     return lax.ppermute(v, axis, [(0, 1), (1, 0)])
 
 
+def ring(v, axis, shift, steps):
+    size = lax.axis_size(axis)
+    got = []
+    for _ in range(steps):
+        v = lax.ppermute(v, axis, [(i, (i + shift) % size) for i in range(size)])
+        got.append(v)
+    return got
+
+
 def exchange(v, axes):
     return lax.all_to_all(v, axes, split_axis=0, concat_axis=0, tiled=True)
 
@@ -183,10 +197,18 @@
     core = core_at.reshape(1).astype(jnp.int32)
 
     mine = jnp.concatenate(
-        [lax.dynamic_slice(w_qkv, (0, j * width + core_at * cut), (piece, cut)) for j in range(3)], axis=1
-    )
-    mine = exchange(jnp.broadcast_to(mine[None], (xs, piece, half)), "x")
-    w_mine = lax.all_gather(mine.reshape(xs * piece, half), "z", axis=0, tiled=False)
+        [lax.dynamic_slice(w_qkv, (0, j * width + core_at * cut), (piece, cut)) for j in range(3)]
+        + [w_out],
+        axis=1,
+    )
+    mine = exchange(jnp.broadcast_to(mine[None], (xs, piece, half + width)), "x")
+    near_xs = xs // cores
+    wo_mine = lax.dynamic_slice_in_dim(mine[:, :, half:], core_at * near_xs, near_xs)
+    wo_mine = wo_mine.reshape(near_xs * piece, width)
+    wo_mine = jnp.concatenate([wo_mine[:, :cut], wo_mine[:, cut:]])
+    block = jnp.concatenate([mine[:, :, :half].reshape(xs * piece, half), wo_mine], axis=1)
+    ups, downs = zs // 2, zs - 1 - zs // 2
+    blocks = [block] + ring(block, "z", 1, ups) + ring(block, "z", -1, downs)
 
     both = jnp.concatenate(
         [frames_in.reshape(mics, frames, width), cotangent.reshape(mics, frames, width)], axis=1
@@ -194,14 +216,18 @@
     both = exchange(after(both, mine), MIC)
     next_both = swap(both, "core")
 
-    wo_part = exchange(after(jnp.broadcast_to(w_out[None], (xs, piece, width)), both), "x")
-    wo = lax.all_gather(wo_part.reshape(xs * piece, width), "z", axis=0, tiled=False)
-    wo = wo.reshape(zs, cores, xs // cores * piece, width)
-
-    spot = jnp.arange(width, dtype=jnp.int32)
-    feature = (spot // piece % xs * zs + spot // (piece * xs)) * piece + spot % piece
-    perm = (spot[:, None] == feature[None, :]).astype(bf)
-    gain = norm_gain[feature].reshape(1, width)
+    z_at = lax.axis_index("z")
+
+    def order_of(size, block_rows):
+        spot = jnp.arange(size, dtype=jnp.int32)
+        step, x_of = spot // block_rows, spot % block_rows // piece
+        z_of = (z_at + jnp.where(step <= ups, -step, step - ups) + zs) % zs
+        return (x_of * zs + z_of) * piece + spot % piece
+
+    feature = order_of(width, xs * piece)
+    hit = jnp.arange(width, dtype=jnp.int32)[:, None] == feature[None, :]
+    perm = hit.astype(bf)
+    gain = jnp.sum(jnp.where(hit, norm_gain[:, None], 0.0), axis=0, keepdims=True)
     own, near = both.reshape(mics, 2, frames, width), next_both.reshape(mics, 2, frames, width)
     x, g = own[:, 0].reshape(rows, width), own[:, 1].reshape(rows, width)
     near_x, near_g = near[:, 0].reshape(rows, width), near[:, 1].reshape(rows, width)
@@ -225,7 +251,7 @@
 
     heads = width // HD
     qkv, probs, att, keep, give = call(
-        lambda *refs: fwd_kernel(frames, *refs),
+        lambda *refs: fwd_kernel(frames, zs, *refs),
         (
             shape((2 * rows, half), bf),
             shape((heads, rows, rows), f32),
@@ -233,25 +259,27 @@
             shape((cut, cut), bf),
             shape((cut, cut), bf),
         ),
-        (),
+        (pltpu.VMEM((width, half), bf),),
         FWD_COST,
-        core, xp, gain, w_mine, g_all, valid_all,
+        core, xp, gain, g_all, valid_all, *blocks,
     )
 
     got = swap(give, "core")
     term = jnp.where(first, jnp.concatenate([keep, got]), jnp.concatenate([got, keep]))
-    spot = jnp.arange(cut, dtype=jnp.int32)
-    near_xs = xs // cores
-    row = (spot // piece % near_xs * zs + spot // (piece * near_xs)) * piece + spot % piece
-    order = (spot[:, None] == row[None, :]).astype(bf)
+    row = order_of(cut, near_xs * piece)
+    order = (jnp.arange(cut, dtype=jnp.int32)[:, None] == row[None, :]).astype(bf)
     att = jnp.dot(att, order, preferred_element_type=f32).astype(bf)
 
     own_part, other_part = call(
-        bwd_kernel,
+        lambda *refs: bwd_kernel(zs, *refs),
         (shape((rows, 2 * width), f32), shape((rows, 2 * width), bf)),
-        (pltpu.VMEM((2 * rows, half), bf),),
+        (
+            pltpu.VMEM((2 * rows, half), bf),
+            pltpu.VMEM((width, half), bf),
+            pltpu.VMEM((cut, width), bf),
+        ),
         BWD_COST,
-        core, g_all, valid_all, after(wo, term), att, order, qkv, probs, w_mine, behind=(term,),
+        g_all, valid_all, att, order, qkv, probs, *blocks, behind=(term,),
     )
     term = exchange(term.reshape(tms, piece, cut), TM)
     term = jnp.sum(term.astype(f32), axis=0).astype(bf)

time: 171 us -> 144 us (0.84)
  waiting for transfers between devices: 44.6 us -> 19.4 us
  starting transfers between devices: 34 us -> 57.4 us
  between operations: 14.3 us -> 1.03 us
  blocking collectives: 38 us -> 27.5 us
  local copies, waits for them, and re-layouts: 12.4 us -> 9.4 us
    ppermute x0 -> x7, starting transfers between devices: none -> 27.3 us  [ring(): v = lax.ppermute(v, axis, [(i, (i + shift) % size) for i in range(size)])]
    all_gather x2 -> x0, waiting for transfers between devices: 24.2 us -> none  [the longest x1 23.3 us: per_device(): lax.all_gather(wo_part.reshape(xs * piece, width), 'z', axis=0, tiled=False)]
    all_to_all x3, waiting for transfers between devices: 19 us -> 5.32 us  [exchange(): return lax.all_to_all(v, axes, split_axis=0, concat_axis=0, tiled=True)]
    ppermute x0 -> x7, waiting for transfers between devices: none -> 12.7 us  [ring(): v = lax.ppermute(v, axis, [(i, (i + shift) % size) for i in range(size)])]
    all_to_all x2 -> x1, blocking collectives: 38 us -> 27.5 us  [exchange(): return lax.all_to_all(v, axes, split_axis=0, concat_axis=0, tiled=True)]
    gather x1 -> x0, local copies, waits for them, and re-layouts: 3.18 us -> none  [per_device(): gain = norm_gain[feature].reshape(1, width)]
    ppermute x3, starting transfers between devices: 13.2 us -> 11 us  [swap(): return lax.ppermute(v, axis, [(0, 1), (1, 0)])]
  transfers between devices with their start and end apart: 8 -> 13, of which waited for: 5 -> 6; matrix products, arithmetic and copies ran while one was open for 9% -> 7% of each run, Pallas kernels for 11% -> 8%
where the time goes in v5:
time: 144 us; the launch traced here: 143 us
  starting transfers between devices  57.4 us (40%)
  blocking collectives  27.5 us (19%)
  waiting for transfers between devices  19.4 us (13%)
  Pallas kernels  19.3 us (13%)
  local copies, waits for them, and re-layouts  9.4 us (7%)
  other arithmetic  7.4 us (5%)
  matrix products  1.72 us (1%)
    all_to_all x1, blocking collectives, exchange(): return lax.all_to_all(v, axes, split_axis=0, concat_axis=0, tiled=True)  27.5 us
    ppermute x7, starting transfers between devices, ring(): v = lax.ppermute(v, axis, [(i, (i + shift) % size) for i in range(size)])  27.3 us
    pallas_call x3, Pallas kernels, call(): pl.pallas_call(kernel, out_shape=outs, in_specs=[pl.BlockSpec(memory_spac...  19.3 us
    all_to_all x3, starting transfers between devices, exchange(): return lax.all_to_all(v, axes, split_axis=0, concat_axis=0, tiled=True)  19.1 us
    ppermute x7, waiting for transfers between devices, ring(): v = lax.ppermute(v, axis, [(i, (i + shift) % size) for i in range(size)])  12.7 us
    ppermute x3, starting transfers between devices, swap(): return lax.ppermute(v, axis, [(0, 1), (1, 0)])  11 us
    all_to_all x3, waiting for transfers between devices, exchange(): return lax.all_to_all(v, axes, split_axis=0, concat_axis=0, tiled=True)  5.32 us
    unnamed x33, local copies, waits for them, and re-layouts  3.03 us
  transfers between devices with their start and end apart: 13, of which 6 were waited for; matrix products, arithmetic and copies ran while one was open for 7% of the time, Pallas kernels for 8%

profile of v5, /device:TPU:1, one launch (start us, length us, event | category | flops | bytes accessed | tf_op | source)
XLA Modules:
  0.0 143.2 jit_solution(6337072133127811956)
XLA Ops:
  0.7 0.8 constant_dynamic-slice_fusion.3
  1.5 0.8 pad_maximum_fusion.3
  3.0 4.8 %all-to-all-start = ((bf16[4,24,1920]{2,1,0:T(8,128)(2,1)}), bf16[4,24,1920]{2,1,0:T(8,128)(2,1)S(1)}, u32[]{:S(2)}, u32[]{:S(2)}) async-start(bf16[4,24,1920]{2,1,0:T(8,128)(2,1)} %broadcast_in_dim.55), calls=%async_computation | async-start | bytes 737280 | tf_op jit(solution)/shard_map/all_to_all | solution.py:169
  8.6 5.3 %all-to-all-done = bf16[4,24,1920]{2,1,0:T(8,128)(2,1)S(1)} async-done(((bf16[4,24,1920]{2,1,0:T(8,128)(2,1)}), bf16[4,24,1920]{2,1,0:T(8,128)(2,1)S(1)}, u32[]{:S(2)}, u32[]{:S(2)}) %all-to-all-start) | async-done | bytes 368672 | tf_op jit(solution)/shard_map/all_to_all | solution.py:169
  14.0 10.0 %all-to-all-start.1 = ((bf16[16,16,768]{2,1,0:T(8,128)(2,1)}), bf16[16,16,768]{2,1,0:T(8,128)(2,1)S(1)}, u32[]{:S(2)}, u32[]{:S(2)}) async-start(bf16[16,16,768]{2,1,0:T(8,128)(2,1)} %pad_maximum_fusion.1), calls=%async_computation.1 | async-start | bytes 786432 | tf_op jit(solution)/shard_map/all_to_all | solution.py:169
  24.0 3.8 %collective-permute-start.1 = (bf16[96,1536]{1,0:T(8,128)(2,1)S(1)}, bf16[96,1536]{1,0:T(8,128)(2,1)S(1)}, u32[]{:S(2)}, u32[]{:S(2)}) collective-permute-start(bf16[96,1536]{1,0:T(8,128)(2,1)S(1)} %maximum_maximum_fusion.refs_5_.refs_6_), channel_id=1, source_target_pairs={{0,1},{1,2},{2,3},{3,4},{4,5},{5,6},{6,7},{7,0},{8,9},{9,10},{10,1... | collective-permute-start | bytes 884744 | tf_op jit(solution)/shard_map/ppermute | solution.py:163
  27.9 8.6 %collective-permute-start.5 = (bf16[96,1536]{1,0:T(8,128)(2,1)S(1)}, bf16[96,1536]{1,0:T(8,128)(2,1)S(1)}, u32[]{:S(2)}, u32[]{:S(2)}) collective-permute-start(bf16[96,1536]{1,0:T(8,128)(2,1)S(1)} %maximum_maximum_fusion.refs_5_.refs_6_), channel_id=1, source_target_pairs={{0,7},{1,0},{2,1},{3,2},{4,3},{5,4},{6,5},{7,6},{8,15},{9,8},{10,9... | collective-permute-start | bytes 884744 | tf_op jit(solution)/shard_map/ppermute | solution.py:163
  36.6 5.2 %collective-permute-done.1.refs_6_.refs_7_ = bf16[96,1536]{1,0:T(8,128)(2,1)S(1)} collective-permute-done((bf16[96,1536]{1,0:T(8,128)(2,1)S(1)}, bf16[96,1536]{1,0:T(8,128)(2,1)S(1)}, u32[]{:S(2)}, u32[]{:S(2)}) %collective-permute-start.1) | collective-permute-done | bytes 294944 | tf_op jit(solution)/shard_map/ppermute | solution.py:163
  41.8 1.9 %collective-permute-start.2 = (bf16[96,1536]{1,0:T(8,128)(2,1)S(1)}, bf16[96,1536]{1,0:T(8,128)(2,1)S(1)}, u32[]{:S(2)}, u32[]{:S(2)}) collective-permute-start(bf16[96,1536]{1,0:T(8,128)(2,1)S(1)} %collective-permute-done.1.refs_6_.refs_7_), channel_id=1, source_target_pairs={{0,1},{1,2},{2,3},{3,4},{4,5},{5,6},{6,7},{7,0},{8,9},{9,10},{10,1... | collective-permute-start | bytes 884744 | tf_op jit(solution)/shard_map/ppermute | solution.py:163
  43.8 4.6 %collective-permute-start.6 = (bf16[96,1536]{1,0:T(8,128)(2,1)S(1)}, bf16[96,1536]{1,0:T(8,128)(2,1)S(1)}, u32[]{:S(2)}, u32[]{:S(2)}) collective-permute-start(bf16[96,1536]{1,0:T(8,128)(2,1)S(1)} %collective-permute-done.5.refs_10_.refs_11_), channel_id=1, source_target_pairs={{0,7},{1,0},{2,1},{3,2},{4,3},{5,4},{6,5},{7,6},{8,15},{9,8},{10,9... | collective-permute-start | bytes 884744 | tf_op jit(solution)/shard_map/ppermute | solution.py:163
  48.4 3.2 %collective-permute-start = (bf16[16,16,768]{2,1,0:T(8,128)(2,1)S(1)}, bf16[16,16,768]{2,1,0:T(8,128)(2,1)S(1)}, u32[]{:S(2)}, u32[]{:S(2)}) collective-permute-start(bf16[16,16,768]{2,1,0:T(8,128)(2,1)S(1)} %all-to-all-done.1), channel_id=1, source_target_pairs={{0,32},{32,0},{1,33},{33,1},{2,34},{34,2},{3,35},{35,3},{4,36},{36... | collective-permute-start | bytes 1179656 | tf_op jit(solution)/shard_map/ppermute | solution.py:156
  52.8 1.9 %collective-permute-start.3 = (bf16[96,1536]{1,0:T(8,128)(2,1)S(1)}, bf16[96,1536]{1,0:T(8,128)(2,1)S(1)}, u32[]{:S(2)}, u32[]{:S(2)}) collective-permute-start(bf16[96,1536]{1,0:T(8,128)(2,1)S(1)} %collective-permute-done.2.refs_7_.refs_8_), channel_id=1, source_target_pairs={{0,1},{1,2},{2,3},{3,4},{4,5},{5,6},{6,7},{7,0},{8,9},{9,10},{10,1... | collective-permute-start | bytes 884744 | tf_op jit(solution)/shard_map/ppermute | solution.py:163
  54.7 0.8 copy.21.refs_4_.refs_1_
  56.1 4.6 %collective-permute-start.7 = (bf16[96,1536]{1,0:T(8,128)(2,1)S(1)}, bf16[96,1536]{1,0:T(8,128)(2,1)S(1)}, u32[]{:S(2)}, u32[]{:S(2)}) collective-permute-start(bf16[96,1536]{1,0:T(8,128)(2,1)S(1)} %collective-permute-done.6.refs_11_.refs_12_), channel_id=1, source_target_pairs={{0,7},{1,0},{2,1},{3,2},{4,3},{5,4},{6,5},{7,6},{8,15},{9,8},{10,9... | collective-permute-start | bytes 884744 | tf_op jit(solution)/shard_map/ppermute | solution.py:163
  60.7 2.1 %collective-permute-done.3.refs_8_.refs_9_ = bf16[96,1536]{1,0:T(8,128)(2,1)S(1)} collective-permute-done((bf16[96,1536]{1,0:T(8,128)(2,1)S(1)}, bf16[96,1536]{1,0:T(8,128)(2,1)S(1)}, u32[]{:S(2)}, u32[]{:S(2)}) %collective-permute-start.3) | collective-permute-done | bytes 294944 | tf_op jit(solution)/shard_map/ppermute | solution.py:163
  62.8 1.9 %collective-permute-start.4 = (bf16[96,1536]{1,0:T(8,128)(2,1)S(1)}, bf16[96,1536]{1,0:T(8,128)(2,1)S(1)}, u32[]{:S(2)}, u32[]{:S(2)}) collective-permute-start(bf16[96,1536]{1,0:T(8,128)(2,1)S(1)} %collective-permute-done.3.refs_8_.refs_9_), channel_id=1, source_target_pairs={{0,1},{1,2},{2,3},{3,4},{4,5},{5,6},{6,7},{7,0},{8,9},{9,10},{10,1... | collective-permute-start | bytes 884744 | tf_op jit(solution)/shard_map/ppermute | solution.py:163
  66.3 0.8 pad_maximum_fusion.2.refs_3_.refs_0_
  67.1 4.8 %collective-permute-done.4.refs_9_.refs_10_ = bf16[96,1536]{1,0:T(8,128)(2,1)S(1)} collective-permute-done((bf16[96,1536]{1,0:T(8,128)(2,1)S(1)}, bf16[96,1536]{1,0:T(8,128)(2,1)S(1)}, u32[]{:S(2)}, u32[]{:S(2)}) %collective-permute-start.4) | collective-permute-done | bytes 294944 | tf_op jit(solution)/shard_map/ppermute | solution.py:163
  72.6 7.5 %shard_map.85 = (bf16[256,1152]{1,0:T(8,128)(2,1)}, f32[12,128,128]{2,1,0:T(8,128)}, bf16[256,384]{1,0:T(8,128)(2,1)}, bf16[384,384]{1,0:T(8,128)(2,1)}, bf16[384,384]{1,0:T(8,128)(2,1)}) custom-call(s32[1]{0:T(128)} %bitcast.9.refs_0_, bf16[256,768]{1,0:T(8,128)(2,1)} %slice.63.refs_1_, f32[1,768]{1,0:T(1,128)} %broadcast_in_dim.60.refs_2_.gain_ref, ...), custom_call_target="tpu_custom_call" | custom-call | flops 8000000000 | bytes 5312516 | tf_op jit(solution)/shard_map/pallas_call | solution.py:141
  80.1 5.3 %collective-permute-start.8 = (bf16[384,384]{1,0:T(8,128)(2,1)}, bf16[384,384]{1,0:T(8,128)(2,1)S(1)}, u32[]{:S(2)}, u32[]{:S(2)}) collective-permute-start(bf16[384,384]{1,0:T(8,128)(2,1)} %get-tuple-element.16), channel_id=1, source_target_pairs={{0,32},{32,0},{1,33},{33,1},{2,34},{34,2},{3,35},{35,3},{4,36},{36... | collective-permute-start | bytes 884744 | tf_op jit(solution)/shard_map/ppermute | solution.py:156
  85.4 1.4 collective-permute-done.8
  86.8 2.1 %maximum_select_fusion.refs_14_ = bf16[768,384]{1,0:T(8,128)(2,1)} fusion(bf16[384,384]{1,0:T(8,128)(2,1)S(1)} %collective-permute-done.8, bf16[384,384]{1,0:T(8,128)(2,1)} %get-tuple-element.15, pred[]{:T(512)S(6)} %eq.75), kind=kLoop, calls=%fused_computation.13 | loop fusion | flops 2654208 | bytes 1179649 | tf_op jit(solution)/shard_map/jit(_where)/select_n | solution.py:268
  88.9 4.3 %all-to-all-start.2 = ((bf16[32,24,384]{2,1,0:T(8,128)(2,1)}), bf16[32,24,384]{2,1,0:T(8,128)(2,1)S(1)}, u32[]{:S(2)}, u32[]{:S(2)}) async-start(bf16[32,24,384]{2,1,0:T(8,128)(2,1)} %bitcast.13), calls=%async_computation.2 | async-start | bytes 1179648 | tf_op jit(solution)/shard_map/all_to_all | solution.py:169
  93.9 0.8 fusion.9.refs_3_
  94.7 1.0 convolution_convert_fusion.refs_2_
  95.7 8.5 %shard_map.86 = (f32[128,1536]{1,0:T(8,128)}, bf16[128,1536]{1,0:T(8,128)(2,1)}) custom-call(bf16[256,768]{1,0:T(8,128)(2,1)} %pad_maximum_fusion.2.refs_3_.refs_0_, f32[256,1]{1,0:T(8,128)} %copy.21.refs_4_.refs_1_, bf16[256,384]{1,0:T(8,128)(2,1)} %convolution_convert_fusion.refs_2_, bf16[384,384]{1,0:T(8,128)(2,1)} %fusion.9.refs_3_, ...), custom_call_target="tpu_custom_call" | custom-call | flops 1000 | bytes 5800960 | tf_op jit(solution)/shard_map/pallas_call | solution.py:141
  104.2 2.6 %collective-permute-start.9 = (bf16[128,1536]{1,0:T(8,128)(2,1)}, bf16[128,1536]{1,0:T(8,128)(2,1)S(1)}, u32[]{:S(2)}, u32[]{:S(2)}) collective-permute-start(bf16[128,1536]{1,0:T(8,128)(2,1)} %get-tuple-element.18), channel_id=1, source_target_pairs={{0,32},{32,0},{1,33},{33,1},{2,34},{34,2},{3,35},{35,3},{4,36},{36... | collective-permute-start | bytes 1179656 | tf_op jit(solution)/shard_map/ppermute | solution.py:156
  106.8 1.5 %fusion.perm_ref = bf16[768,768]{1,0:T(8,128)(2,1)} fusion(s32[768]{0:T(1024)S(1)} %fusion.14), kind=kLoop, calls=%fused_computation.2 | loop fusion | flops 1179648 | bytes 1182720 | tf_op jit(solution)/shard_map/convert_element_type | solution.py:229
  108.3 0.8 fusion.41
  109.8 3.3 %shard_map.87 = bf16[128,1536]{1,0:T(8,128)(2,1)} custom-call(bf16[128,768]{1,0:T(8,128)(2,1)} %copy-done.2, f32[128,1]{1,0:T(8,128)} %reshape_tile.4.valid_ref, bf16[128,768]{1,0:T(8,128)(2,1)} %get-tuple-element.24.xp_ref, bf16[128,768]{1,0:T(8,128)(2,1)} %get-tuple-element.23.gp_ref, f32[1,768]{1,0:T(1,128)} %broadcast_in_dim.60.refs_2_.gain_ref, ...), custom_call_target="tpu_custom_call" | custom-call | flops 1000 | bytes 3345920 | tf_op jit(solution)/shard_map/pallas_call | solution.py:141
  113.2 0.9 copy-done
  114.2 27.5 %all_to_all.20 = bf16[16,8,2688]{2,1,0:T(8,128)(2,1)S(1)} all-to-all(bf16[16,8,2688]{2,1,0:T(8,128)(2,1)S(1)} %pad_maximum_fusion), channel_id=1, replica_groups=mesh['y'=8,'core'=2,'x'=4,'z'=8] {'y','core'}, dimensions={0} | all-to-all | bytes 1376256 | tf_op jit(solution)/shard_map/all_to_all | solution.py:169
  (72 shorter events, 9.1 us)
Async XLA Ops:
  0.6 7.2 %copy-start.12 = (bf16[1,128,768]{2,1,0:T(8,128)(2,1)S(1)}, bf16[1,128,768]{2,1,0:T(8,128)(2,1)}, u32[]{:S(2)}) copy-start(bf16[1,128,768]{2,1,0:T(8,128)(2,1)} %param.6) | copy-start | bytes 589828
  0.6 7.2 %copy-start.11 = (bf16[1,128,768]{2,1,0:T(8,128)(2,1)S(1)}, bf16[1,128,768]{2,1,0:T(8,128)(2,1)}, u32[]{:S(2)}) copy-start(bf16[1,128,768]{2,1,0:T(8,128)(2,1)} %param.7) | copy-start | bytes 589828
  3.0 10.9 %all-to-all-start = ((bf16[4,24,1920]{2,1,0:T(8,128)(2,1)}), bf16[4,24,1920]{2,1,0:T(8,128)(2,1)S(1)}, u32[]{:S(2)}, u32[]{:S(2)}) async-start(bf16[4,24,1920]{2,1,0:T(8,128)(2,1)} %broadcast_in_dim.55), calls=%async_computation | async-start | bytes 737280 | tf_op jit(solution)/shard_map/all_to_all | solution.py:169
  8.6 27.9 %copy-start.14 = (s32[2]{0:T(128)S(1)}, s32[2]{0:T(128)}, u32[]{:S(2)}) copy-start(s32[2]{0:T(128)} %param.11) | copy-start | bytes 28
  8.6 42.9 %copy-start.13 = (f32[768]{0:T(1024)S(1)}, f32[768]{0:T(1024)}, u32[]{:S(2)}) copy-start(f32[768]{0:T(1024)} %param.8) | copy-start | bytes 9220
  14.0 34.4 %all-to-all-start.1 = ((bf16[16,16,768]{2,1,0:T(8,128)(2,1)}), bf16[16,16,768]{2,1,0:T(8,128)(2,1)S(1)}, u32[]{:S(2)}, u32[]{:S(2)}) async-start(bf16[16,16,768]{2,1,0:T(8,128)(2,1)} %pad_maximum_fusion.1), calls=%async_computation.1 | async-start | bytes 786432 | tf_op jit(solution)/shard_map/all_to_all | solution.py:169
  24.0 41.5 %copy-start.1 = (bf16[96,1536]{1,0:T(8,128)(2,1)}, bf16[96,1536]{1,0:T(8,128)(2,1)S(1)}, u32[]{:S(2)}) copy-start(bf16[96,1536]{1,0:T(8,128)(2,1)S(1)} %maximum_maximum_fusion.refs_5_.refs_6_) | copy-start | bytes 884740
  24.0 17.8 %collective-permute-start.1 = (bf16[96,1536]{1,0:T(8,128)(2,1)S(1)}, bf16[96,1536]{1,0:T(8,128)(2,1)S(1)}, u32[]{:S(2)}, u32[]{:S(2)}) collective-permute-start(bf16[96,1536]{1,0:T(8,128)(2,1)S(1)} %maximum_maximum_fusion.refs_5_.refs_6_), channel_id=1, source_target_pairs={{0,1},{1,2},{2,3},{3,4},{4,5},{5,6},{6,7},{7,0},{8,9},{9,10},{10,1... | collective-permute-start | bytes 884744 | tf_op jit(solution)/shard_map/ppermute | solution.py:163
  27.9 15.8 %collective-permute-start.5 = (bf16[96,1536]{1,0:T(8,128)(2,1)S(1)}, bf16[96,1536]{1,0:T(8,128)(2,1)S(1)}, u32[]{:S(2)}, u32[]{:S(2)}) collective-permute-start(bf16[96,1536]{1,0:T(8,128)(2,1)S(1)} %maximum_maximum_fusion.refs_5_.refs_6_), channel_id=1, source_target_pairs={{0,7},{1,0},{2,1},{3,2},{4,3},{5,4},{6,5},{7,6},{8,15},{9,8},{10,9... | collective-permute-start | bytes 884744 | tf_op jit(solution)/shard_map/ppermute | solution.py:163
  41.8 23.7 %copy-start.4 = (bf16[96,1536]{1,0:T(8,128)(2,1)}, bf16[96,1536]{1,0:T(8,128)(2,1)S(1)}, u32[]{:S(2)}) copy-start(bf16[96,1536]{1,0:T(8,128)(2,1)S(1)} %collective-permute-done.1.refs_6_.refs_7_) | copy-start | bytes 884740
  41.8 11.0 %collective-permute-start.2 = (bf16[96,1536]{1,0:T(8,128)(2,1)S(1)}, bf16[96,1536]{1,0:T(8,128)(2,1)S(1)}, u32[]{:S(2)}, u32[]{:S(2)}) collective-permute-start(bf16[96,1536]{1,0:T(8,128)(2,1)S(1)} %collective-permute-done.1.refs_6_.refs_7_), channel_id=1, source_target_pairs={{0,1},{1,2},{2,3},{3,4},{4,5},{5,6},{6,7},{7,0},{8,9},{9,10},{10,1... | collective-permute-start | bytes 884744 | tf_op jit(solution)/shard_map/ppermute | solution.py:163
  43.8 21.8 %copy-start.5 = (bf16[96,1536]{1,0:T(8,128)(2,1)}, bf16[96,1536]{1,0:T(8,128)(2,1)S(1)}, u32[]{:S(2)}) copy-start(bf16[96,1536]{1,0:T(8,128)(2,1)S(1)} %collective-permute-done.5.refs_10_.refs_11_) | copy-start | bytes 884740
  43.8 12.3 %collective-permute-start.6 = (bf16[96,1536]{1,0:T(8,128)(2,1)S(1)}, bf16[96,1536]{1,0:T(8,128)(2,1)S(1)}, u32[]{:S(2)}, u32[]{:S(2)}) collective-permute-start(bf16[96,1536]{1,0:T(8,128)(2,1)S(1)} %collective-permute-done.5.refs_10_.refs_11_), channel_id=1, source_target_pairs={{0,7},{1,0},{2,1},{3,2},{4,3},{5,4},{6,5},{7,6},{8,15},{9,8},{10,9... | collective-permute-start | bytes 884744 | tf_op jit(solution)/shard_map/ppermute | solution.py:163
  48.4 16.3 %collective-permute-start = (bf16[16,16,768]{2,1,0:T(8,128)(2,1)S(1)}, bf16[16,16,768]{2,1,0:T(8,128)(2,1)S(1)}, u32[]{:S(2)}, u32[]{:S(2)}) collective-permute-start(bf16[16,16,768]{2,1,0:T(8,128)(2,1)S(1)} %all-to-all-done.1), channel_id=1, source_target_pairs={{0,32},{32,0},{1,33},{33,1},{2,34},{34,2},{3,35},{35,3},{4,36},{36... | collective-permute-start | bytes 1179656 | tf_op jit(solution)/shard_map/ppermute | solution.py:156
  52.8 12.8 %copy-start.6 = (bf16[96,1536]{1,0:T(8,128)(2,1)}, bf16[96,1536]{1,0:T(8,128)(2,1)S(1)}, u32[]{:S(2)}) copy-start(bf16[96,1536]{1,0:T(8,128)(2,1)S(1)} %collective-permute-done.2.refs_7_.refs_8_) | copy-start | bytes 884740
  52.8 10.0 %collective-permute-start.3 = (bf16[96,1536]{1,0:T(8,128)(2,1)S(1)}, bf16[96,1536]{1,0:T(8,128)(2,1)S(1)}, u32[]{:S(2)}, u32[]{:S(2)}) collective-permute-start(bf16[96,1536]{1,0:T(8,128)(2,1)S(1)} %collective-permute-done.2.refs_7_.refs_8_), channel_id=1, source_target_pairs={{0,1},{1,2},{2,3},{3,4},{4,5},{5,6},{6,7},{7,0},{8,9},{9,10},{10,1... | collective-permute-start | bytes 884744 | tf_op jit(solution)/shard_map/ppermute | solution.py:163
  56.1 9.5 %copy-start.7 = (bf16[96,1536]{1,0:T(8,128)(2,1)}, bf16[96,1536]{1,0:T(8,128)(2,1)S(1)}, u32[]{:S(2)}) copy-start(bf16[96,1536]{1,0:T(8,128)(2,1)S(1)} %collective-permute-done.6.refs_11_.refs_12_) | copy-start | bytes 884740
  56.1 11.1 %collective-permute-start.7 = (bf16[96,1536]{1,0:T(8,128)(2,1)S(1)}, bf16[96,1536]{1,0:T(8,128)(2,1)S(1)}, u32[]{:S(2)}, u32[]{:S(2)}) collective-permute-start(bf16[96,1536]{1,0:T(8,128)(2,1)S(1)} %collective-permute-done.6.refs_11_.refs_12_), channel_id=1, source_target_pairs={{0,7},{1,0},{2,1},{3,2},{4,3},{5,4},{6,5},{7,6},{8,15},{9,8},{10,9... | collective-permute-start | bytes 884744 | tf_op jit(solution)/shard_map/ppermute | solution.py:163
  60.7 4.9 %copy-start.2 = (bf16[128,768]{1,0:T(8,128)(2,1)}, bf16[128,768]{1,0:T(8,128)(2,1)S(1)}, u32[]{:S(2)}) copy-start(bf16[128,768]{1,0:T(8,128)(2,1)S(1)} %get-tuple-element.27.x_ref) | copy-start | bytes 589828
  62.8 2.8 %copy-start.8 = (bf16[96,1536]{1,0:T(8,128)(2,1)}, bf16[96,1536]{1,0:T(8,128)(2,1)S(1)}, u32[]{:S(2)}) copy-start(bf16[96,1536]{1,0:T(8,128)(2,1)S(1)} %collective-permute-done.3.refs_8_.refs_9_) | copy-start | bytes 884740
  62.8 9.1 %collective-permute-start.4 = (bf16[96,1536]{1,0:T(8,128)(2,1)S(1)}, bf16[96,1536]{1,0:T(8,128)(2,1)S(1)}, u32[]{:S(2)}, u32[]{:S(2)}) collective-permute-start(bf16[96,1536]{1,0:T(8,128)(2,1)S(1)} %collective-permute-done.3.refs_8_.refs_9_), channel_id=1, source_target_pairs={{0,1},{1,2},{2,3},{3,4},{4,5},{5,6},{6,7},{7,0},{8,9},{9,10},{10,1... | collective-permute-start | bytes 884744 | tf_op jit(solution)/shard_map/ppermute | solution.py:163
  67.1 4.8 %copy-start.9 = (bf16[96,1536]{1,0:T(8,128)(2,1)}, bf16[96,1536]{1,0:T(8,128)(2,1)S(1)}, u32[]{:S(2)}) copy-start(bf16[96,1536]{1,0:T(8,128)(2,1)S(1)} %collective-permute-done.7.refs_12_.refs_13_) | copy-start | bytes 884740
  71.9 0.7 copy-start.10
  80.1 6.7 %collective-permute-start.8 = (bf16[384,384]{1,0:T(8,128)(2,1)}, bf16[384,384]{1,0:T(8,128)(2,1)S(1)}, u32[]{:S(2)}, u32[]{:S(2)}) collective-permute-start(bf16[384,384]{1,0:T(8,128)(2,1)} %get-tuple-element.16), channel_id=1, source_target_pairs={{0,32},{32,0},{1,33},{33,1},{2,34},{34,2},{3,35},{35,3},{4,36},{36... | collective-permute-start | bytes 884744 | tf_op jit(solution)/shard_map/ppermute | solution.py:156
  86.8 7.9 %copy-start.15 = (bf16[256,384]{1,0:T(8,128)(2,1)S(1)}, bf16[256,384]{1,0:T(8,128)(2,1)}, u32[]{:S(2)}) copy-start(bf16[256,384]{1,0:T(8,128)(2,1)} %get-tuple-element.12) | copy-start | bytes 589828
  88.9 24.3 %all-to-all-start.2 = ((bf16[32,24,384]{2,1,0:T(8,128)(2,1)}), bf16[32,24,384]{2,1,0:T(8,128)(2,1)S(1)}, u32[]{:S(2)}, u32[]{:S(2)}) async-start(bf16[32,24,384]{2,1,0:T(8,128)(2,1)} %bitcast.13), calls=%async_computation.2 | async-start | bytes 1179648 | tf_op jit(solution)/shard_map/all_to_all | solution.py:169
  104.2 4.8 %collective-permute-start.9 = (bf16[128,1536]{1,0:T(8,128)(2,1)}, bf16[128,1536]{1,0:T(8,128)(2,1)S(1)}, u32[]{:S(2)}, u32[]{:S(2)}) collective-permute-start(bf16[128,1536]{1,0:T(8,128)(2,1)} %get-tuple-element.18), channel_id=1, source_target_pairs={{0,32},{32,0},{1,33},{33,1},{2,34},{34,2},{3,35},{35,3},{4,36},{36... | collective-permute-start | bytes 1179656 | tf_op jit(solution)/shard_map/ppermute | solution.py:156
  109.0 0.7 copy-start.3
  113.1 1.0 copy-start

commit v6 on v3

v6 whole, which is shorter than its diff:
```python
import jax
import jax.numpy as jnp
from jax import lax
from jax.experimental import pallas as pl
from jax.experimental.pallas import tpu as pltpu
from jax.sharding import Mesh, PartitionSpec as P

HD = 64
SESS = 2
XS = 4
MIC = ("y", "core")
TM = ("x", "z")
NEG = -1e30
VMEM_LIMIT = 56 * 1024 * 1024
FWD_COST, BWD_COST, END_COST = 8_000_000_000, 1000, 1000


def dot_nn(a, b):
    return lax.dot_general(a, b, (((1,), (0,)), ((), ())), preferred_element_type=jnp.float32)


def dot_nt(a, b):
    return lax.dot_general(a, b, (((1,), (1,)), ((), ())), preferred_element_type=jnp.float32)


def dot_tn(a, b):
    return lax.dot_general(a, b, (((0,), (0,)), ((), ())), preferred_element_type=jnp.float32)


def low_half(rows):
    return lax.broadcasted_iota(jnp.int32, (rows, 2 * HD), 1) < HD


def same_frame(rows, frames):
    row_at = lax.broadcasted_iota(jnp.int32, (rows, rows), 0)
    col_at = lax.broadcasted_iota(jnp.int32, (rows, rows), 1)
    return lax.rem(row_at, frames) == lax.rem(col_at, frames)


def valid_rows(rows, frames, left):
    frame = lax.rem(lax.broadcasted_iota(jnp.int32, (rows, 1), 0), frames)
    return (frame < left).astype(jnp.float32)


def masked_grad(frames, scalars, own_ref, near_ref):
    rows, width = own_ref.shape[0], own_ref.shape[1] // 2
    parts = [
        (ref[:, width:].astype(jnp.float32) * valid_rows(rows, frames, scalars[1 + i])).astype(
            jnp.bfloat16
        )
        for i, ref in enumerate((own_ref, near_ref))
    ]
    return jnp.concatenate(parts)


def pairs_of(rows, width):
    at = 0
    for start in (0, rows):
        for col in range(0, width, 2 * HD):
            yield start, col, at
            at += 2


def inv_rms_of(x):
    return lax.rsqrt(jnp.mean(x * x, axis=-1, keepdims=True) + 1e-05)


def fwd_kernel(
    frames,
    scalars,
    own_ref,
    near_ref,
    gain_ref,
    block_ref,
    up_ref,
    down_ref,
    far_low_ref,
    far_high_ref,
    qkv_ref,
    p_ref,
    att_ref,
    w_ref,
    wo_ref,
    give_ref,
    gw_ref,
    all_ref,
):
    rows, width = own_ref.shape[0], own_ref.shape[1] // 2
    mine, deep = att_ref.shape[1], block_ref.shape[0]
    core, x_at = scalars[0], scalars[3]
    first = core == 0
    far = lax.rem(x_at + 2, XS) * deep
    places = (
        (block_ref, x_at * deep),
        (up_ref, lax.rem(x_at + XS - 1, XS) * deep),
        (down_ref, lax.rem(x_at + 1, XS) * deep),
        (far_low_ref, far),
        (far_high_ref, far + deep // 2),
    )
    for ref, at in places:
        here = pl.ds(pl.multiple_of(at, deep // 2), ref.shape[0])
        w_ref[here, :] = ref[:, : 3 * mine]
        all_ref[here, :] = ref[:, 3 * mine :]
    mid = width // 2
    wo_ref[...] = all_ref[pl.ds(pl.multiple_of(core * mid, mid), mid), :]
    give_ref[mid:, :] = all_ref[pl.ds(pl.multiple_of((1 - core) * mid, mid), mid), :]

    for i, ref in enumerate((own_ref, near_ref)):
        x = ref[:, :width].astype(jnp.float32)
        normed = (x * inv_rms_of(x) * gain_ref[...]).astype(jnp.bfloat16)
        qkv_ref[i * rows : (i + 1) * rows, :] = normed_dot(normed, w_ref)
    same = same_frame(rows, frames)
    low = low_half(rows)
    for start, at, index in pairs_of(rows, mine):
        here = pl.ds(start, rows)
        q = qkv_ref[here, at : at + 2 * HD]
        k = qkv_ref[here, mine + at : mine + at + 2 * HD]
        v = qkv_ref[here, 2 * mine + at : 2 * mine + at + 2 * HD]
        mixed = []
        for i in range(2):
            qi = jnp.where(low == (i == 0), q, jnp.zeros_like(q))
            s = jnp.where(same, dot_nt(qi, k) * HD ** (-0.5), NEG)
            e = jnp.exp(s - jnp.max(s, axis=-1, keepdims=True))
            p = e / jnp.sum(e, axis=-1, keepdims=True)
            p_ref[index + i] = p
            mixed.append(dot_nn(p.astype(jnp.bfloat16), v))
        att_ref[here, at : at + 2 * HD] = jnp.where(low, mixed[0], mixed[1]).astype(jnp.bfloat16)
    gz = masked_grad(frames, scalars, own_ref, near_ref)
    low_cols, high_cols = gz[:, :mid], gz[:, mid:]
    att = att_ref[...]
    keep = dot_tn(att, jnp.where(first, low_cols, high_cols))
    gw_ref[pl.ds(pl.multiple_of(core * mid, mid), mid), :] = keep.astype(jnp.bfloat16)
    give_ref[:mid, :] = dot_tn(att, jnp.where(first, high_cols, low_cols)).astype(jnp.bfloat16)


def normed_dot(normed, w_ref):
    return dot_nn(normed, w_ref[...]).astype(jnp.bfloat16)


def bwd_kernel(
    frames,
    scalars,
    own_ref,
    near_ref,
    wo_ref,
    got_ref,
    att_ref,
    qkv_ref,
    p_ref,
    w_ref,
    _,
    sum_ref,
    other_ref,
    gqkv_ref,
):
    rows, width = own_ref.shape[0], own_ref.shape[1] // 2
    mine, mid = att_ref.shape[1], width // 2
    first = scalars[0] == 0
    att = att_ref[...]
    kept, got = dot_nn(att, wo_ref[...]), dot_nn(att, got_ref[mid:, :])
    for at, part in ((0, jnp.where(first, kept, got)), (mid, jnp.where(first, got, kept))):
        sum_ref[:, at : at + mid] = part[:rows]
        other_ref[:, at : at + mid] = part[rows:].astype(jnp.bfloat16)
    gz = masked_grad(frames, scalars, own_ref, near_ref)
    low_cols, high_cols = gz[:, :mid], gz[:, mid:]
    ga_all = dot_nt(jnp.where(first, low_cols, high_cols), wo_ref[...])
    ga_all += dot_nt(jnp.where(first, high_cols, low_cols), got_ref[mid:, :])
    ga_all = ga_all.astype(jnp.bfloat16)
    low = low_half(rows)
    for start, at, index in pairs_of(rows, mine):
        here = pl.ds(start, rows)
        q = qkv_ref[here, at : at + 2 * HD]
        k = qkv_ref[here, mine + at : mine + at + 2 * HD]
        v = qkv_ref[here, 2 * mine + at : 2 * mine + at + 2 * HD]
        ga = ga_all[start : start + rows, at : at + 2 * HD]
        dq, dk, dv = [], [], []
        for i in range(2):
            gi = jnp.where(low == (i == 0), ga, jnp.zeros_like(ga))
            p = p_ref[index + i]
            gp = dot_nt(gi, v)
            ds = p * (gp - jnp.sum(p * gp, axis=-1, keepdims=True)) * HD ** (-0.5)
            ds = ds.astype(jnp.bfloat16)
            dq.append(dot_nn(ds, k))
            dk.append(dot_tn(ds, q))
            dv.append(dot_tn(p.astype(jnp.bfloat16), ga))
        for j, grad in enumerate((dq, dk, dv)):
            gqkv_ref[here, j * mine + at : j * mine + at + 2 * HD] = jnp.where(
                low, grad[0], grad[1]
            ).astype(jnp.bfloat16)
    gh = dot_nt(gqkv_ref[...], w_ref[...])
    sum_ref[:, width:] = gh[:rows]
    other_ref[:, width:] = gh[rows:].astype(jnp.bfloat16)


def end_kernel(frames, scalars, own_ref, gain_ref, sum_ref, got_ref, both_ref):
    rows, width = own_ref.shape[0], own_ref.shape[1] // 2
    valid = valid_rows(rows, frames, scalars[1])
    x = own_ref[:, :width].astype(jnp.float32)
    mixed = sum_ref[:, :width] + got_ref[:, :width].astype(jnp.float32)
    both_ref[:, :width] = (valid * (x + mixed)).astype(jnp.bfloat16)
    gh = (sum_ref[:, width:] + got_ref[:, width:].astype(jnp.float32)) * gain_ref[...]
    inv = inv_rms_of(x)
    inner = jnp.mean(gh * x, axis=-1, keepdims=True)
    gy = own_ref[:, width:].astype(jnp.float32) * valid
    both_ref[:, width:] = (gy + inv * (gh - x * inv * inv * inner)).astype(jnp.bfloat16)


def call(kernel, outs, scratch, flops, *operands, behind=()):
    size = sum(o.size * o.dtype.itemsize for o in outs + operands)
    return pl.pallas_call(
        kernel,
        out_shape=outs,
        in_specs=[
            pl.BlockSpec(memory_space=pltpu.SMEM if o.dtype == jnp.int32 else pltpu.VMEM)
            for o in operands
        ]
        + [pl.BlockSpec(memory_space=pl.ANY)] * len(behind),
        scratch_shapes=scratch,
        compiler_params=pltpu.CompilerParams(vmem_limit_bytes=VMEM_LIMIT),
        cost_estimate=pl.CostEstimate(flops=flops, bytes_accessed=size, transcendentals=0),
    )(*operands, *behind)


def shift(v, axis, by):
    size = lax.axis_size(axis)
    return lax.ppermute(v, axis, [(i, (i + by) % size) for i in range(size)])


def exchange(v, axes):
    return lax.all_to_all(v, axes, split_axis=0, concat_axis=0, tiled=True)


def after(v, first):
    return lax.optimization_barrier((v, first))[0]


def per_device(frames_in, cotangent, norm_gain, w_qkv, w_out, lengths):
    bf, f32 = jnp.bfloat16, jnp.float32
    y_at, core_at, x_at = (lax.axis_index(axis) for axis in ("y", "core", "x"))
    ys, cores, zs = (lax.axis_size(axis) for axis in ("y", "core", "z"))
    tms, mics = XS * zs, ys * cores
    frame_dev, width = frames_in.shape[1:]
    frames = frame_dev // mics
    rows = mics * frames
    piece, wide = w_qkv.shape
    half, cut = wide // cores, width // cores

    mine = [lax.dynamic_slice(w_qkv, (0, j * width + core_at * cut), (piece, cut)) for j in range(3)]
    mine.append(lax.dynamic_slice(w_out, (0, core_at * cut), (piece, cut)))
    mine = jnp.concatenate(mine, axis=1)
    block = exchange(jnp.broadcast_to(mine[None], (zs, piece, half + cut)), "z")
    block = block.reshape(zs * piece, half + cut)
    up, down = shift(block, "x", 1), shift(block, "x", -1)
    mid = zs * piece // 2
    far_low, far_high = shift(up[:mid], "x", 1), shift(down[mid:], "x", -1)

    both = jnp.concatenate(
        [frames_in.reshape(mics, frames, width), cotangent.reshape(mics, frames, width)], axis=2
    )
    own = exchange(after(both, block), MIC).reshape(rows, 2 * width)
    near = shift(own, "core", 1)

    slot_len = frame_dev * tms // SESS
    start = lax.axis_index(TM) * frame_dev
    session = start // slot_len
    left = lengths[session] + session * slot_len - start - y_at * cores * frames
    scalars = [core_at, left - core_at * frames, left - (1 - core_at) * frames, x_at]
    scalars = jnp.stack(scalars).astype(jnp.int32)
    gain = norm_gain.reshape(1, width)

    def shape(dims, dtype):
        return jax.ShapeDtypeStruct(dims, dtype)

    heads = width // HD
    qkv, probs, att, w, wo, give, gw = call(
        lambda *refs: fwd_kernel(frames, *refs),
        (
            shape((2 * rows, half), bf),
            shape((heads, rows, rows), f32),
            shape((2 * rows, cut), bf),
            shape((width, half), bf),
            shape((cut, cut), bf),
            shape((width, cut), bf),
            shape((width, cut), bf),
        ),
        (pltpu.VMEM((width, cut), bf),),
        FWD_COST,
        scalars, own, near, gain, block, up, down, far_low, far_high,
    )

    got = shift(give, "core", 1)
    term = lax.dynamic_update_slice(gw, got[:cut], ((1 - core_at) * cut, 0))

    sum_part, other_part = call(
        lambda *refs: bwd_kernel(frames, *refs),
        (shape((rows, 2 * width), f32), shape((rows, 2 * width), bf)),
        (pltpu.VMEM((2 * rows, half), bf),),
        BWD_COST,
        scalars, own, near, wo, got, att, qkv, probs, w, behind=(term,),
    )
    term = exchange(term.reshape(tms, piece, cut), TM)
    term = jnp.sum(term.astype(f32), axis=0).astype(bf)
    got_part = shift(other_part, "core", 1)
    (done,) = call(
        lambda *refs: end_kernel(frames, *refs),
        (shape((rows, 2 * width), bf),),
        (),
        END_COST,
        scalars, own, gain, sum_part, got_part,
    )

    low = piece // frames
    term = term.reshape(low, frames, cut).transpose(1, 0, 2).reshape(frames, low * cut)
    term = jnp.broadcast_to(term[None], (mics, frames, low * cut))
    sent = jnp.concatenate([done.reshape(mics, frames, 2 * width), term], axis=2)
    sent = exchange(sent, MIC)
    out = sent[:, :, :width].reshape(1, frame_dev, width)
    dx = sent[:, :, width : 2 * width].reshape(1, frame_dev, width)
    term = jnp.sum(sent[:, :, 2 * width :].astype(f32).reshape(ys, cores, frames, low, cut), axis=0)
    grad_wout = term.transpose(2, 1, 0, 3).reshape(piece, width)
    return (out, dx, grad_wout)


def solution(mesh):
    grid = Mesh(mesh.devices.reshape(-1, 2, XS, mesh.devices.shape[1] // XS), ("y", "core", "x", "z"))
    return jax.shard_map(
        per_device,
        mesh=grid,
        in_specs=(P(MIC, TM, None), P(MIC, TM, None), P(), P(TM, None), P(TM, None), P()),
        out_specs=(P(MIC, TM, None), P(MIC, TM, None), P(TM, None)),
        check_vma=False,
    )
```

time: 151 us -> 143 us (0.947)
  waiting for transfers between devices: 14.2 us -> 37.7 us
  between operations: 14.3 us -> 1.58 us
  blocking collectives: 40.6 us -> 30.5 us
  local copies, waits for them, and re-layouts: 12 us -> 6.75 us
  other arithmetic: 6.44 us -> 2.56 us
    all_to_all x3, waiting for transfers between devices: 14.1 us -> 27.6 us  [exchange(): return lax.all_to_all(v, axes, split_axis=0, concat_axis=0, tiled=True)]
    all_to_all x2 -> x1, blocking collectives: 40.6 us -> 30.5 us  [exchange(): return lax.all_to_all(v, axes, split_axis=0, concat_axis=0, tiled=True)]
    ppermute x4 -> x7, waiting for transfers between devices: 0.01 us -> 10.1 us  [shift(): return lax.ppermute(v, axis, [(i, (i + by) % size) for i in range(size)])]
    ppermute x4 -> x7, starting transfers between devices: 16 us -> 21.7 us  [shift(): return lax.ppermute(v, axis, [(i, (i + by) % size) for i in range(size)])]
    all_to_all x3, starting transfers between devices: 27.1 us -> 22.4 us  [exchange(): return lax.all_to_all(v, axes, split_axis=0, concat_axis=0, tiled=True)]
    gather x1 -> x0, local copies, waits for them, and re-layouts: 3.18 us -> none  [per_device(): gain = norm_gain[feature].reshape(1, width)]
    select_n x4 -> x0, other arithmetic: 2.12 us -> none  [the longest x1 2.05 us: per_device(): jnp.where(first, jnp.concatenate([keep, got]), jnp.concatenate([got, keep]))]
    slice x2, local copies, waits for them, and re-layouts: 1.56 us -> 0.04 us  [per_device(): far_low, far_high = (shift(up[:mid], 'x', 1), shift(down[mid:], 'x', -1))]
  transfers between devices with their start and end apart: 8 -> 10, of which waited for: 1 -> 8; matrix products, arithmetic and copies ran while one was open for 10% -> 2% of each run, Pallas kernels for 12% -> 7%
where the time goes in v6:
time: 143 us; the launch traced here: 142 us
  starting transfers between devices  44.1 us (31%)
  waiting for transfers between devices  37.7 us (26%)
  blocking collectives  30.5 us (21%)
  Pallas kernels  18.9 us (13%)
  local copies, waits for them, and re-layouts  6.75 us (5%)
  other arithmetic  2.56 us (2%)
  between operations  1.58 us (1%)
    all_to_all x1, blocking collectives, exchange(): return lax.all_to_all(v, axes, split_axis=0, concat_axis=0, tiled=True)  30.5 us
    all_to_all x3, waiting for transfers between devices, exchange(): return lax.all_to_all(v, axes, split_axis=0, concat_axis=0, tiled=True)  27.6 us
    all_to_all x3, starting transfers between devices, exchange(): return lax.all_to_all(v, axes, split_axis=0, concat_axis=0, tiled=True)  22.4 us
    ppermute x7, starting transfers between devices, shift(): return lax.ppermute(v, axis, [(i, (i + by) % size) for i in range(size)])  21.7 us
    pallas_call x3, Pallas kernels, call(): pl.pallas_call(kernel, out_shape=outs, in_specs=[pl.BlockSpec(memory_spac...  18.9 us
    ppermute x7, waiting for transfers between devices, shift(): return lax.ppermute(v, axis, [(i, (i + by) % size) for i in range(size)])  10.1 us
  transfers between devices with their start and end apart: 10, of which 8 were waited for; matrix products, arithmetic and copies ran while one was open for 2% of the time, Pallas kernels for 7%

profile of v6, /device:TPU:1, one launch (start us, length us, event | category | flops | bytes accessed | tf_op | source)
XLA Modules:
  0.0 142.0 jit_solution(10740806446691995160)
XLA Ops:
  0.7 0.8 constant_dynamic-slice_fusion.3
  1.5 0.9 broadcast_in_dim.6
  2.4 10.9 %all-to-all-start = ((bf16[8,24,1536]{2,1,0:T(8,128)(2,1)}), bf16[8,24,1536]{2,1,0:T(8,128)(2,1)S(1)}, u32[]{:S(2)}, u32[]{:S(2)}) async-start(bf16[8,24,1536]{2,1,0:T(8,128)(2,1)} %broadcast_in_dim.6), calls=%async_computation | async-start | bytes 1179648 | tf_op jit(solution)/shard_map/all_to_all | solution.py:230
  13.3 0.8 pad_maximum_fusion.1
  14.1 18.5 %all-to-all-done = bf16[8,24,1536]{2,1,0:T(8,128)(2,1)S(1)} async-done(((bf16[8,24,1536]{2,1,0:T(8,128)(2,1)}), bf16[8,24,1536]{2,1,0:T(8,128)(2,1)S(1)}, u32[]{:S(2)}, u32[]{:S(2)}) %all-to-all-start) | async-done | bytes 589856 | tf_op jit(solution)/shard_map/all_to_all | solution.py:230
  32.6 7.6 %all-to-all-start.1 = ((bf16[16,8,1536]{2,1,0:T(8,128)(2,1)}), bf16[16,8,1536]{2,1,0:T(8,128)(2,1)S(1)}, u32[]{:S(2)}, u32[]{:S(2)}) async-start(bf16[16,8,1536]{2,1,0:T(8,128)(2,1)} %pad_maximum_fusion.1), calls=%async_computation.1 | async-start | bytes 786432 | tf_op jit(solution)/shard_map/all_to_all | solution.py:230
  40.2 4.4 %collective-permute-start.2 = (bf16[192,1536]{1,0:T(8,128)(2,1)S(1)}, bf16[192,1536]{1,0:T(8,128)(2,1)S(1)}, u32[]{:S(2)}, u32[]{:S(2)}) collective-permute-start(bf16[192,1536]{1,0:T(8,128)(2,1)S(1)} %bitcast.35), channel_id=1, source_target_pairs={{0,24},{8,0},{16,8},{24,16},{1,25},{9,1},{17,9},{25,17},{2,26},{10... | collective-permute-start | bytes 1769480 | tf_op jit(solution)/shard_map/ppermute | solution.py:226
  44.6 1.9 %collective-permute-start.1 = (bf16[192,1536]{1,0:T(8,128)(2,1)S(1)}, bf16[192,1536]{1,0:T(8,128)(2,1)S(1)}, u32[]{:S(2)}, u32[]{:S(2)}) collective-permute-start(bf16[192,1536]{1,0:T(8,128)(2,1)S(1)} %bitcast.36), channel_id=1, source_target_pairs={{0,8},{8,16},{16,24},{24,0},{1,9},{9,17},{17,25},{25,1},{2,10},{10... | collective-permute-start | bytes 1769480 | tf_op jit(solution)/shard_map/ppermute | solution.py:226
  46.6 8.2 %all-to-all-done.1 = bf16[16,8,1536]{2,1,0:T(8,128)(2,1)S(1)} async-done(((bf16[16,8,1536]{2,1,0:T(8,128)(2,1)}), bf16[16,8,1536]{2,1,0:T(8,128)(2,1)S(1)}, u32[]{:S(2)}, u32[]{:S(2)}) %all-to-all-start.1) | async-done | bytes 393248 | tf_op jit(solution)/shard_map/all_to_all | solution.py:230
  54.8 1.9 %collective-permute-start = (bf16[128,1536]{1,0:T(8,128)(2,1)S(1)}, bf16[128,1536]{1,0:T(8,128)(2,1)S(1)}, u32[]{:S(2)}, u32[]{:S(2)}) collective-permute-start(bf16[128,1536]{1,0:T(8,128)(2,1)S(1)} %bitcast.28), channel_id=1, source_target_pairs={{0,32},{32,0},{1,33},{33,1},{2,34},{34,2},{3,35},{35,3},{4,36},{36... | collective-permute-start | bytes 1179656 | tf_op jit(solution)/shard_map/ppermute | solution.py:226
  56.7 0.6 collective-permute-done.2.refs_6_
  57.3 5.3 %collective-permute-start.4 = (bf16[96,1536]{1,0:T(8,128)(2,1)S(1)}, bf16[96,1536]{1,0:T(8,128)(2,1)}, u32[]{:S(2)}, u32[]{:S(2)}) collective-permute-start(bf16[96,1536]{1,0:T(8,128)(2,1)S(1)} %slice.25), channel_id=1, source_target_pairs={{0,24},{8,0},{16,8},{24,16},{1,25},{9,1},{17,9},{25,17},{2,26},{10... | collective-permute-start | bytes 884744 | tf_op jit(solution)/shard_map/ppermute | solution.py:226
  62.7 1.9 %collective-permute-start.3 = (bf16[96,1536]{1,0:T(8,128)(2,1)S(1)}, bf16[96,1536]{1,0:T(8,128)(2,1)}, u32[]{:S(2)}, u32[]{:S(2)}) collective-permute-start(bf16[96,1536]{1,0:T(8,128)(2,1)S(1)} %slice.24), channel_id=1, source_target_pairs={{0,8},{8,16},{16,24},{24,0},{1,9},{9,17},{17,25},{25,1},{2,10},{10... | collective-permute-start | bytes 884744 | tf_op jit(solution)/shard_map/ppermute | solution.py:226
  64.7 0.6 dynamic_slice.15
  67.1 1.0 collective-permute-done.4.refs_8_
  68.1 5.2 %collective-permute-done.3.refs_7_ = bf16[96,1536]{1,0:T(8,128)(2,1)} collective-permute-done((bf16[96,1536]{1,0:T(8,128)(2,1)S(1)}, bf16[96,1536]{1,0:T(8,128)(2,1)}, u32[]{:S(2)}, u32[]{:S(2)}) %collective-permute-start.3) | collective-permute-done | bytes 294944 | tf_op jit(solution)/shard_map/ppermute | solution.py:226
  73.3 0.7 copy-done.3
  74.0 8.6 %shard_map.85 = (bf16[256,1152]{1,0:T(8,128)(2,1)}, f32[12,128,128]{2,1,0:T(8,128)}, bf16[256,384]{1,0:T(8,128)(2,1)}, bf16[768,1152]{1,0:T(8,128)(2,1)}, bf16[3...) custom-call(s32[4]{0:T(128)} %pad_add_fusion.refs_0_, bf16[128,1536]{1,0:T(8,128)(2,1)} %bitcast.29, ...), custom_call_target="tpu_custom_call" | custom-call | flops 8000000000 | bytes 7965712 | tf_op jit(solution)/shard_map/pallas_call | solution.py:210
  82.6 4.0 %collective-permute-start.5 = (bf16[768,384]{1,0:T(8,128)(2,1)}, bf16[768,384]{1,0:T(8,128)(2,1)S(1)}, u32[]{:S(2)}, u32[]{:S(2)}) collective-permute-start(bf16[768,384]{1,0:T(8,128)(2,1)} %get-tuple-element.15), channel_id=1, source_target_pairs={{0,32},{32,0},{1,33},{33,1},{2,34},{34,2},{3,35},{35,3},{4,36},{36... | collective-permute-start | bytes 1769480 | tf_op jit(solution)/shard_map/ppermute | solution.py:226
  86.6 1.8 %collective-permute-done.5.refs_4_ = bf16[768,384]{1,0:T(8,128)(2,1)S(1)} collective-permute-done((bf16[768,384]{1,0:T(8,128)(2,1)}, bf16[768,384]{1,0:T(8,128)(2,1)S(1)}, u32[]{:S(2)}, u32[]{:S(2)}) %collective-permute-start.5) | collective-permute-done | bytes 589856 | tf_op jit(solution)/shard_map/ppermute | solution.py:226
  88.4 0.8 slice_dynamic-update-slice_fusion.refs_9_
  89.2 3.9 %all-to-all-start.2 = ((bf16[32,24,384]{2,1,0:T(8,128)(2,1)}), bf16[32,24,384]{2,1,0:T(8,128)(2,1)S(1)}, u32[]{:S(2)}, u32[]{:S(2)}) async-start(bf16[32,24,384]{2,1,0:T(8,128)(2,1)} %bitcast.32), calls=%async_computation.2 | async-start | bytes 1179648 | tf_op jit(solution)/shard_map/all_to_all | solution.py:230
  93.1 7.9 %shard_map.86 = (f32[128,1536]{1,0:T(8,128)}, bf16[128,1536]{1,0:T(8,128)(2,1)}) custom-call(s32[4]{0:T(128)} %pad_add_fusion.refs_0_, bf16[128,1536]{1,0:T(8,128)(2,1)} %bitcast.30, bf16[128,1536]{1,0:T(8,128)(2,1)} %copy-done.3, bf16[384,384]{1,0:T(8,128)(2,1)} %get-tuple-element.14.refs_3_, bf16[768,384]{1,0:T(8,128)(2,1)} %copy-done.1, ...), custom_call_target="tpu_custom_call" | custom-call | flops 1000 | bytes 6193168 | tf_op jit(solution)/shard_map/pallas_call | solution.py:210
  101.0 2.3 %collective-permute-start.6 = (bf16[128,1536]{1,0:T(8,128)(2,1)}, bf16[128,1536]{1,0:T(8,128)(2,1)S(1)}, u32[]{:S(2)}, u32[]{:S(2)}) collective-permute-start(bf16[128,1536]{1,0:T(8,128)(2,1)} %get-tuple-element.22), channel_id=1, source_target_pairs={{0,32},{32,0},{1,33},{33,1},{2,34},{34,2},{3,35},{35,3},{4,36},{36... | collective-permute-start | bytes 1179656 | tf_op jit(solution)/shard_map/ppermute | solution.py:226
  103.3 1.5 %collective-permute-done.6.refs_4_ = bf16[128,1536]{1,0:T(8,128)(2,1)S(1)} collective-permute-done((bf16[128,1536]{1,0:T(8,128)(2,1)}, bf16[128,1536]{1,0:T(8,128)(2,1)S(1)}, u32[]{:S(2)}, u32[]{:S(2)}) %collective-permute-start.6) | collective-permute-done | bytes 393248 | tf_op jit(solution)/shard_map/ppermute | solution.py:226
  104.8 0.8 copy-done.4
  105.6 2.4 %shard_map.87 = bf16[128,1536]{1,0:T(8,128)(2,1)} custom-call(s32[4]{0:T(128)} %pad_add_fusion.refs_0_, bf16[128,1536]{1,0:T(8,128)(2,1)} %bitcast.31, f32[1,768]{1,0:T(1,128)} %reshape.51.refs_3_.refs_2_, f32[128,1536]{1,0:T(8,128)} %get-tuple-element.21.refs_3_, bf16[128,1536]{1,0:T(8,128)(2,1)} %copy-done.4), custom_call_target="tpu_custom_call" | custom-call | flops 1000 | bytes 1969168 | tf_op jit(solution)/shard_map/pallas_call | solution.py:210
  108.0 0.8 all-to-all-done.2
  109.0 1.0 pad_maximum_fusion
  110.0 30.5 %all_to_all.20 = bf16[16,8,2688]{2,1,0:T(8,128)(2,1)S(1)} all-to-all(bf16[16,8,2688]{2,1,0:T(8,128)(2,1)S(1)} %pad_maximum_fusion), channel_id=1, replica_groups=mesh['y'=8,'core'=2,'x'=4,'z'=8] {'y','core'}, dimensions={0} | all-to-all | bytes 1376256 | tf_op jit(solution)/shard_map/all_to_all | solution.py:230
  140.6 0.6 copy.10
  141.2 0.8 slice_bitcast_fusion
  (32 shorter events, 1.5 us)
Async XLA Ops:
  0.6 12.6 %copy-start.5 = (bf16[1,128,768]{2,1,0:T(8,128)(2,1)S(1)}, bf16[1,128,768]{2,1,0:T(8,128)(2,1)}, u32[]{:S(2)}) copy-start(bf16[1,128,768]{2,1,0:T(8,128)(2,1)} %param.7) | copy-start | bytes 589828
  0.6 12.6 %copy-start.6 = (bf16[1,128,768]{2,1,0:T(8,128)(2,1)S(1)}, bf16[1,128,768]{2,1,0:T(8,128)(2,1)}, u32[]{:S(2)}) copy-start(bf16[1,128,768]{2,1,0:T(8,128)(2,1)} %param.6) | copy-start | bytes 589828
  2.4 30.2 %all-to-all-start = ((bf16[8,24,1536]{2,1,0:T(8,128)(2,1)}), bf16[8,24,1536]{2,1,0:T(8,128)(2,1)S(1)}, u32[]{:S(2)}, u32[]{:S(2)}) async-start(bf16[8,24,1536]{2,1,0:T(8,128)(2,1)} %broadcast_in_dim.6), calls=%async_computation | async-start | bytes 1179648 | tf_op jit(solution)/shard_map/all_to_all | solution.py:230
  13.3 51.4 %copy-start.10 = (s32[2]{0:T(128)S(1)}, s32[2]{0:T(128)}, u32[]{:S(2)}) copy-start(s32[2]{0:T(128)} %param.11) | copy-start | bytes 28
  13.3 52.6 %copy-start.9 = (f32[768]{0:T(1024)S(1)}, f32[768]{0:T(1024)}, u32[]{:S(2)}) copy-start(f32[768]{0:T(1024)} %param.8) | copy-start | bytes 9220
  32.6 40.6 %copy-start.2 = (bf16[8,24,1536]{2,1,0:T(8,128)(2,1)}, bf16[8,24,1536]{2,1,0:T(8,128)(2,1)S(1)}, u32[]{:S(2)}) copy-start(bf16[8,24,1536]{2,1,0:T(8,128)(2,1)S(1)} %all-to-all-done) | copy-start | bytes 1769476
  32.6 22.2 %all-to-all-start.1 = ((bf16[16,8,1536]{2,1,0:T(8,128)(2,1)}), bf16[16,8,1536]{2,1,0:T(8,128)(2,1)S(1)}, u32[]{:S(2)}, u32[]{:S(2)}) async-start(bf16[16,8,1536]{2,1,0:T(8,128)(2,1)} %pad_maximum_fusion.1), calls=%async_computation.1 | async-start | bytes 786432 | tf_op jit(solution)/shard_map/all_to_all | solution.py:230
  40.2 17.1 %collective-permute-start.2 = (bf16[192,1536]{1,0:T(8,128)(2,1)S(1)}, bf16[192,1536]{1,0:T(8,128)(2,1)S(1)}, u32[]{:S(2)}, u32[]{:S(2)}) collective-permute-start(bf16[192,1536]{1,0:T(8,128)(2,1)S(1)} %bitcast.35), channel_id=1, source_target_pairs={{0,24},{8,0},{16,8},{24,16},{1,25},{9,1},{17,9},{25,17},{2,26},{10... | collective-permute-start | bytes 1769480 | tf_op jit(solution)/shard_map/ppermute | solution.py:226
  44.6 18.0 %collective-permute-start.1 = (bf16[192,1536]{1,0:T(8,128)(2,1)S(1)}, bf16[192,1536]{1,0:T(8,128)(2,1)S(1)}, u32[]{:S(2)}, u32[]{:S(2)}) collective-permute-start(bf16[192,1536]{1,0:T(8,128)(2,1)S(1)} %bitcast.36), channel_id=1, source_target_pairs={{0,8},{8,16},{16,24},{24,0},{1,9},{9,17},{17,25},{25,1},{2,10},{10... | collective-permute-start | bytes 1769480 | tf_op jit(solution)/shard_map/ppermute | solution.py:226
  54.8 18.5 %copy-start = (bf16[16,8,1536]{2,1,0:T(8,128)(2,1)}, bf16[16,8,1536]{2,1,0:T(8,128)(2,1)S(1)}, u32[]{:S(2)}) copy-start(bf16[16,8,1536]{2,1,0:T(8,128)(2,1)S(1)} %all-to-all-done.1) | copy-start | bytes 1179652
  54.8 18.5 %collective-permute-start = (bf16[128,1536]{1,0:T(8,128)(2,1)S(1)}, bf16[128,1536]{1,0:T(8,128)(2,1)S(1)}, u32[]{:S(2)}, u32[]{:S(2)}) collective-permute-start(bf16[128,1536]{1,0:T(8,128)(2,1)S(1)} %bitcast.28), channel_id=1, source_target_pairs={{0,32},{32,0},{1,33},{33,1},{2,34},{34,2},{3,35},{35,3},{4,36},{36... | collective-permute-start | bytes 1179656 | tf_op jit(solution)/shard_map/ppermute | solution.py:226
  57.3 16.0 %copy-start.7 = (bf16[192,1536]{1,0:T(8,128)(2,1)}, bf16[192,1536]{1,0:T(8,128)(2,1)S(1)}, u32[]{:S(2)}) copy-start(bf16[192,1536]{1,0:T(8,128)(2,1)S(1)} %collective-permute-done.2.refs_6_) | copy-start | bytes 1769476
  57.3 10.8 %collective-permute-start.4 = (bf16[96,1536]{1,0:T(8,128)(2,1)S(1)}, bf16[96,1536]{1,0:T(8,128)(2,1)}, u32[]{:S(2)}, u32[]{:S(2)}) collective-permute-start(bf16[96,1536]{1,0:T(8,128)(2,1)S(1)} %slice.25), channel_id=1, source_target_pairs={{0,24},{8,0},{16,8},{24,16},{1,25},{9,1},{17,9},{25,17},{2,26},{10... | collective-permute-start | bytes 884744 | tf_op jit(solution)/shard_map/ppermute | solution.py:226
  62.6 10.6 %copy-start.8 = (bf16[192,1536]{1,0:T(8,128)(2,1)}, bf16[192,1536]{1,0:T(8,128)(2,1)S(1)}, u32[]{:S(2)}) copy-start(bf16[192,1536]{1,0:T(8,128)(2,1)S(1)} %collective-permute-done.1.refs_5_) | copy-start | bytes 1769476
  62.7 10.6 %collective-permute-start.3 = (bf16[96,1536]{1,0:T(8,128)(2,1)S(1)}, bf16[96,1536]{1,0:T(8,128)(2,1)}, u32[]{:S(2)}, u32[]{:S(2)}) collective-permute-start(bf16[96,1536]{1,0:T(8,128)(2,1)S(1)} %slice.24), channel_id=1, source_target_pairs={{0,8},{8,16},{16,24},{24,0},{1,9},{9,17},{17,25},{25,1},{2,10},{10... | collective-permute-start | bytes 884744 | tf_op jit(solution)/shard_map/ppermute | solution.py:226
  73.3 0.8 copy-start.3
  82.6 5.8 %collective-permute-start.5 = (bf16[768,384]{1,0:T(8,128)(2,1)}, bf16[768,384]{1,0:T(8,128)(2,1)S(1)}, u32[]{:S(2)}, u32[]{:S(2)}) collective-permute-start(bf16[768,384]{1,0:T(8,128)(2,1)} %get-tuple-element.15), channel_id=1, source_target_pairs={{0,32},{32,0},{1,33},{33,1},{2,34},{34,2},{3,35},{35,3},{4,36},{36... | collective-permute-start | bytes 1769480 | tf_op jit(solution)/shard_map/ppermute | solution.py:226
  88.4 4.7 %copy-start.1 = (bf16[768,384]{1,0:T(8,128)(2,1)}, bf16[768,384]{1,0:T(8,128)(2,1)S(1)}, u32[]{:S(2)}) copy-start(bf16[768,384]{1,0:T(8,128)(2,1)S(1)} %collective-permute-done.5.refs_4_) | copy-start | bytes 1769476
  89.2 19.6 %all-to-all-start.2 = ((bf16[32,24,384]{2,1,0:T(8,128)(2,1)}), bf16[32,24,384]{2,1,0:T(8,128)(2,1)S(1)}, u32[]{:S(2)}, u32[]{:S(2)}) async-start(bf16[32,24,384]{2,1,0:T(8,128)(2,1)} %bitcast.32), calls=%async_computation.2 | async-start | bytes 1179648 | tf_op jit(solution)/shard_map/all_to_all | solution.py:230
  101.0 3.8 %collective-permute-start.6 = (bf16[128,1536]{1,0:T(8,128)(2,1)}, bf16[128,1536]{1,0:T(8,128)(2,1)S(1)}, u32[]{:S(2)}, u32[]{:S(2)}) collective-permute-start(bf16[128,1536]{1,0:T(8,128)(2,1)} %get-tuple-element.22), channel_id=1, source_target_pairs={{0,32},{32,0},{1,33},{33,1},{2,34},{34,2},{3,35},{35,3},{4,36},{36... | collective-permute-start | bytes 1179656 | tf_op jit(solution)/shard_map/ppermute | solution.py:226
  104.8 0.8 copy-start.4

commit v7 on v6

--- a/solution.py
+++ b/solution.py
@@ -12,7 +12,7 @@
 TM = ("x", "z")
 NEG = -1e30
 VMEM_LIMIT = 56 * 1024 * 1024
-FWD_COST, BWD_COST, END_COST = 8_000_000_000, 1000, 1000
+FWD_COST, BWD_COST, END_COST, HALVES_COST = 8_000_000_000, 1000, 1000, 20_000_000_000
 
 
 def dot_nn(a, b):
@@ -53,23 +53,38 @@
     return jnp.concatenate(parts)
 
 
-def pairs_of(rows, width):
-    at = 0
-    for start in (0, rows):
-        for col in range(0, width, 2 * HD):
-            yield start, col, at
-            at += 2
-
-
 def inv_rms_of(x):
     return lax.rsqrt(jnp.mean(x * x, axis=-1, keepdims=True) + 1e-05)
 
 
-def fwd_kernel(
+def attend(same, qkv_ref, p_ref, att_ref):
+    rows, mine = att_ref.shape
+    low = low_half(rows)
+    for index, at in enumerate(range(0, mine, 2 * HD)):
+        q = qkv_ref[:, at : at + 2 * HD]
+        k = qkv_ref[:, mine + at : mine + at + 2 * HD]
+        v = qkv_ref[:, 2 * mine + at : 2 * mine + at + 2 * HD]
+        mixed = []
+        for i in range(2):
+            qi = jnp.where(low == (i == 0), q, jnp.zeros_like(q))
+            s = jnp.where(same, dot_nt(qi, k) * HD ** (-0.5), NEG)
+            e = jnp.exp(s - jnp.max(s, axis=-1, keepdims=True))
+            p = e / jnp.sum(e, axis=-1, keepdims=True)
+            p_ref[2 * index + i] = p
+            mixed.append(dot_nn(p.astype(jnp.bfloat16), v))
+        att_ref[:, at : at + 2 * HD] = jnp.where(low, mixed[0], mixed[1]).astype(jnp.bfloat16)
+
+
+def project(rows_ref, gain_ref, w_ref, qkv_ref):
+    x = rows_ref[:, : w_ref.shape[0]].astype(jnp.float32)
+    normed = (x * inv_rms_of(x) * gain_ref[...]).astype(jnp.bfloat16)
+    qkv_ref[...] = dot_nn(normed, w_ref[...]).astype(jnp.bfloat16)
+
+
+def own_kernel(
     frames,
     scalars,
     own_ref,
-    near_ref,
     gain_ref,
     block_ref,
     up_ref,
@@ -82,13 +97,11 @@
     w_ref,
     wo_ref,
     give_ref,
-    gw_ref,
     all_ref,
 ):
-    rows, width = own_ref.shape[0], own_ref.shape[1] // 2
-    mine, deep = att_ref.shape[1], block_ref.shape[0]
+    rows, mine = att_ref.shape
+    width, deep = w_ref.shape[0], block_ref.shape[0]
     core, x_at = scalars[0], scalars[3]
-    first = core == 0
     far = lax.rem(x_at + 2, XS) * deep
     places = (
         (block_ref, x_at * deep),
@@ -103,38 +116,35 @@
         all_ref[here, :] = ref[:, 3 * mine :]
     mid = width // 2
     wo_ref[...] = all_ref[pl.ds(pl.multiple_of(core * mid, mid), mid), :]
-    give_ref[mid:, :] = all_ref[pl.ds(pl.multiple_of((1 - core) * mid, mid), mid), :]
-
-    for i, ref in enumerate((own_ref, near_ref)):
-        x = ref[:, :width].astype(jnp.float32)
-        normed = (x * inv_rms_of(x) * gain_ref[...]).astype(jnp.bfloat16)
-        qkv_ref[i * rows : (i + 1) * rows, :] = normed_dot(normed, w_ref)
-    same = same_frame(rows, frames)
-    low = low_half(rows)
-    for start, at, index in pairs_of(rows, mine):
-        here = pl.ds(start, rows)
-        q = qkv_ref[here, at : at + 2 * HD]
-        k = qkv_ref[here, mine + at : mine + at + 2 * HD]
-        v = qkv_ref[here, 2 * mine + at : 2 * mine + at + 2 * HD]
-        mixed = []
-        for i in range(2):
-            qi = jnp.where(low == (i == 0), q, jnp.zeros_like(q))
-            s = jnp.where(same, dot_nt(qi, k) * HD ** (-0.5), NEG)
-            e = jnp.exp(s - jnp.max(s, axis=-1, keepdims=True))
-            p = e / jnp.sum(e, axis=-1, keepdims=True)
-            p_ref[index + i] = p
-            mixed.append(dot_nn(p.astype(jnp.bfloat16), v))
-        att_ref[here, at : at + 2 * HD] = jnp.where(low, mixed[0], mixed[1]).astype(jnp.bfloat16)
+    give_ref[...] = all_ref[pl.ds(pl.multiple_of((1 - core) * mid, mid), mid), :]
+    project(own_ref, gain_ref, w_ref, qkv_ref)
+    attend(same_frame(rows, frames), qkv_ref, p_ref, att_ref)
+
+
+def near_kernel(
+    frames,
+    scalars,
+    own_ref,
+    near_ref,
+    gain_ref,
+    w_ref,
+    own_att_ref,
+    qkv_ref,
+    p_ref,
+    att_ref,
+    give_ref,
+    gw_ref,
+):
+    project(near_ref, gain_ref, w_ref, qkv_ref)
+    attend(same_frame(att_ref.shape[0], frames), qkv_ref, p_ref, att_ref)
+    core, mid = scalars[0], w_ref.shape[0] // 2
+    first = core == 0
     gz = masked_grad(frames, scalars, own_ref, near_ref)
     low_cols, high_cols = gz[:, :mid], gz[:, mid:]
-    att = att_ref[...]
+    att = jnp.concatenate([own_att_ref[...], att_ref[...]])
     keep = dot_tn(att, jnp.where(first, low_cols, high_cols))
     gw_ref[pl.ds(pl.multiple_of(core * mid, mid), mid), :] = keep.astype(jnp.bfloat16)
-    give_ref[:mid, :] = dot_tn(att, jnp.where(first, high_cols, low_cols)).astype(jnp.bfloat16)
-
-
-def normed_dot(normed, w_ref):
-    return dot_nn(normed, w_ref[...]).astype(jnp.bfloat16)
+    give_ref[...] = dot_tn(att, jnp.where(first, high_cols, low_cols)).astype(jnp.bfloat16)
 
 
 def bwd_kernel(
@@ -144,9 +154,12 @@
     near_ref,
     wo_ref,
     got_ref,
-    att_ref,
-    qkv_ref,
-    p_ref,
+    own_att_ref,
+    near_att_ref,
+    own_qkv_ref,
+    near_qkv_ref,
+    own_p_ref,
+    near_p_ref,
     w_ref,
     _,
     sum_ref,
@@ -154,39 +167,40 @@
     gqkv_ref,
 ):
     rows, width = own_ref.shape[0], own_ref.shape[1] // 2
-    mine, mid = att_ref.shape[1], width // 2
+    mine, mid = own_att_ref.shape[1], width // 2
     first = scalars[0] == 0
-    att = att_ref[...]
-    kept, got = dot_nn(att, wo_ref[...]), dot_nn(att, got_ref[mid:, :])
+    att = jnp.concatenate([own_att_ref[...], near_att_ref[...]])
+    kept, got = dot_nn(att, wo_ref[...]), dot_nn(att, got_ref[...])
     for at, part in ((0, jnp.where(first, kept, got)), (mid, jnp.where(first, got, kept))):
         sum_ref[:, at : at + mid] = part[:rows]
         other_ref[:, at : at + mid] = part[rows:].astype(jnp.bfloat16)
     gz = masked_grad(frames, scalars, own_ref, near_ref)
     low_cols, high_cols = gz[:, :mid], gz[:, mid:]
     ga_all = dot_nt(jnp.where(first, low_cols, high_cols), wo_ref[...])
-    ga_all += dot_nt(jnp.where(first, high_cols, low_cols), got_ref[mid:, :])
+    ga_all += dot_nt(jnp.where(first, high_cols, low_cols), got_ref[...])
     ga_all = ga_all.astype(jnp.bfloat16)
     low = low_half(rows)
-    for start, at, index in pairs_of(rows, mine):
-        here = pl.ds(start, rows)
-        q = qkv_ref[here, at : at + 2 * HD]
-        k = qkv_ref[here, mine + at : mine + at + 2 * HD]
-        v = qkv_ref[here, 2 * mine + at : 2 * mine + at + 2 * HD]
-        ga = ga_all[start : start + rows, at : at + 2 * HD]
-        dq, dk, dv = [], [], []
-        for i in range(2):
-            gi = jnp.where(low == (i == 0), ga, jnp.zeros_like(ga))
-            p = p_ref[index + i]
-            gp = dot_nt(gi, v)
-            ds = p * (gp - jnp.sum(p * gp, axis=-1, keepdims=True)) * HD ** (-0.5)
-            ds = ds.astype(jnp.bfloat16)
-            dq.append(dot_nn(ds, k))
-            dk.append(dot_tn(ds, q))
-            dv.append(dot_tn(p.astype(jnp.bfloat16), ga))
-        for j, grad in enumerate((dq, dk, dv)):
-            gqkv_ref[here, j * mine + at : j * mine + at + 2 * HD] = jnp.where(
-                low, grad[0], grad[1]
-            ).astype(jnp.bfloat16)
+    sets = ((0, own_qkv_ref, own_p_ref), (rows, near_qkv_ref, near_p_ref))
+    for start, qkv_ref, p_ref in sets:
+        for index, at in enumerate(range(0, mine, 2 * HD)):
+            q = qkv_ref[:, at : at + 2 * HD]
+            k = qkv_ref[:, mine + at : mine + at + 2 * HD]
+            v = qkv_ref[:, 2 * mine + at : 2 * mine + at + 2 * HD]
+            ga = ga_all[start : start + rows, at : at + 2 * HD]
+            dq, dk, dv = [], [], []
+            for i in range(2):
+                gi = jnp.where(low == (i == 0), ga, jnp.zeros_like(ga))
+                p = p_ref[2 * index + i]
+                gp = dot_nt(gi, v)
+                ds = p * (gp - jnp.sum(p * gp, axis=-1, keepdims=True)) * HD ** (-0.5)
+                ds = ds.astype(jnp.bfloat16)
+                dq.append(dot_nn(ds, k))
+                dk.append(dot_tn(ds, q))
+                dv.append(dot_tn(p.astype(jnp.bfloat16), ga))
+            for j, grad in enumerate((dq, dk, dv)):
+                gqkv_ref[start : start + rows, j * mine + at : j * mine + at + 2 * HD] = jnp.where(
+                    low, grad[0], grad[1]
+                ).astype(jnp.bfloat16)
     gh = dot_nt(gqkv_ref[...], w_ref[...])
     sum_ref[:, width:] = gh[:rows]
     other_ref[:, width:] = gh[rows:].astype(jnp.bfloat16)
@@ -221,6 +235,27 @@
     )(*operands, *behind)
 
 
+def halves(up, down, mid):
+    def kernel(up_ref, down_ref, low_ref, high_ref):
+        low_ref[...] = up_ref[...]
+        high_ref[...] = down_ref[...]
+
+    cols = up.shape[1]
+    return pl.pallas_call(
+        kernel,
+        grid=(1,),
+        out_shape=[jax.ShapeDtypeStruct((mid, cols), up.dtype)] * 2,
+        in_specs=[
+            pl.BlockSpec((mid, cols), lambda i: (0, 0)),
+            pl.BlockSpec((mid, cols), lambda i: (1, 0)),
+        ],
+        out_specs=[pl.BlockSpec((mid, cols), lambda i: (0, 0))] * 2,
+        cost_estimate=pl.CostEstimate(
+            flops=HALVES_COST, bytes_accessed=4 * mid * cols * 2, transcendentals=0
+        ),
+    )(up, down)
+
+
 def shift(v, axis, by):
     size = lax.axis_size(axis)
     return lax.ppermute(v, axis, [(i, (i + by) % size) for i in range(size)])
@@ -252,7 +287,8 @@
     block = block.reshape(zs * piece, half + cut)
     up, down = shift(block, "x", 1), shift(block, "x", -1)
     mid = zs * piece // 2
-    far_low, far_high = shift(up[:mid], "x", 1), shift(down[mid:], "x", -1)
+    far_low, far_high = halves(up, down, mid)
+    far_low, far_high = shift(far_low, "x", 1), shift(far_high, "x", -1)
 
     both = jnp.concatenate(
         [frames_in.reshape(mics, frames, width), cotangent.reshape(mics, frames, width)], axis=2
@@ -271,32 +307,38 @@
     def shape(dims, dtype):
         return jax.ShapeDtypeStruct(dims, dtype)
 
-    heads = width // HD
-    qkv, probs, att, w, wo, give, gw = call(
-        lambda *refs: fwd_kernel(frames, *refs),
-        (
-            shape((2 * rows, half), bf),
-            shape((heads, rows, rows), f32),
-            shape((2 * rows, cut), bf),
-            shape((width, half), bf),
-            shape((cut, cut), bf),
-            shape((width, cut), bf),
-            shape((width, cut), bf),
-        ),
+    heads = width // HD // cores
+    results = (
+        shape((rows, half), bf),
+        shape((heads, rows, rows), f32),
+        shape((rows, cut), bf),
+    )
+    own_qkv, own_p, own_att, w, wo, wo_give = call(
+        lambda *refs: own_kernel(frames, *refs),
+        results + (shape((width, half), bf), shape((cut, cut), bf), shape((cut, cut), bf)),
         (pltpu.VMEM((width, cut), bf),),
         FWD_COST,
-        scalars, own, near, gain, block, up, down, far_low, far_high,
+        scalars, own, gain, block, up, down, far_low, far_high,
+    )
+    wo_got = shift(wo_give, "core", 1)
+    near_qkv, near_p, near_att, give, gw = call(
+        lambda *refs: near_kernel(frames, *refs),
+        results + (shape((cut, cut), bf), shape((width, cut), bf)),
+        (),
+        FWD_COST,
+        scalars, own, near, gain, w, own_att,
     )
 
     got = shift(give, "core", 1)
-    term = lax.dynamic_update_slice(gw, got[:cut], ((1 - core_at) * cut, 0))
+    term = lax.dynamic_update_slice(gw, got, ((1 - core_at) * cut, 0))
 
     sum_part, other_part = call(
         lambda *refs: bwd_kernel(frames, *refs),
         (shape((rows, 2 * width), f32), shape((rows, 2 * width), bf)),
         (pltpu.VMEM((2 * rows, half), bf),),
         BWD_COST,
-        scalars, own, near, wo, got, att, qkv, probs, w, behind=(term,),
+        scalars, own, near, wo, wo_got, own_att, near_att, own_qkv, near_qkv, own_p, near_p, w,
+        behind=(term,),
     )
     term = exchange(term.reshape(tms, piece, cut), TM)
     term = jnp.sum(term.astype(f32), axis=0).astype(bf)

time: 143 us -> 140 us (0.979)
  waiting for transfers between devices: 37.7 us -> 7.24 us
  blocking collectives: 30.5 us -> 56.2 us
  starting transfers between devices: 44.1 us -> 41 us
  Pallas kernels: 18.9 us -> 21.6 us
  local copies, waits for them, and re-layouts: 6.75 us -> 8.77 us
    all_to_all x3 -> x2, waiting for transfers between devices: 27.6 us -> 0.1 us  [exchange(): return lax.all_to_all(v, axes, split_axis=0, concat_axis=0, tiled=True)]
    all_to_all x1 -> x2, blocking collectives: 30.5 us -> 56.2 us  [exchange(): return lax.all_to_all(v, axes, split_axis=0, concat_axis=0, tiled=True)]
    all_to_all x3 -> x2, starting transfers between devices: 22.4 us -> 15.4 us  [exchange(): return lax.all_to_all(v, axes, split_axis=0, concat_axis=0, tiled=True)]
    ppermute x7 -> x8, starting transfers between devices: 21.7 us -> 25.6 us  [shift(): return lax.ppermute(v, axis, [(i, (i + by) % size) for i in range(size)])]
    ppermute x7 -> x8, waiting for transfers between devices: 10.1 us -> 7.14 us  [shift(): return lax.ppermute(v, axis, [(i, (i + by) % size) for i in range(size)])]
    unnamed x23 -> x29, local copies, waits for them, and re-layouts: 2.19 us -> 5.11 us
    pallas_call x0 -> x1, Pallas kernels: none -> 1.89 us  [halves(): pl.pallas_call(kernel, grid=(1,), out_shape=[jax.ShapeDtypeStruct((mid, c...]
    pallas_call x3 -> x4, Pallas kernels: 18.9 us -> 19.7 us  [call(): pl.pallas_call(kernel, out_shape=outs, in_specs=[pl.BlockSpec(memory_spac...]
  transfers between devices with their start and end apart: 10 -> 10, of which waited for: 8 -> 5; matrix products, arithmetic and copies ran while one was open for 2% -> 2% of each run, Pallas kernels for 7% -> 12%
where the time goes in v7:
time: 140 us; the launch traced here: 139 us
  blocking collectives  56.2 us (40%)
  starting transfers between devices  41 us (29%)
  Pallas kernels  21.6 us (15%)
  local copies, waits for them, and re-layouts  8.77 us (6%)
  waiting for transfers between devices  7.24 us (5%)
  other arithmetic  2.63 us (2%)
  between operations  1.6 us (1%)
    all_to_all x2, blocking collectives, exchange(): return lax.all_to_all(v, axes, split_axis=0, concat_axis=0, tiled=True)  56.2 us
    ppermute x8, starting transfers between devices, shift(): return lax.ppermute(v, axis, [(i, (i + by) % size) for i in range(size)])  25.6 us
    pallas_call x4, Pallas kernels, call(): pl.pallas_call(kernel, out_shape=outs, in_specs=[pl.BlockSpec(memory_spac...  19.7 us
    all_to_all x2, starting transfers between devices, exchange(): return lax.all_to_all(v, axes, split_axis=0, concat_axis=0, tiled=True)  15.4 us
    ppermute x8, waiting for transfers between devices, shift(): return lax.ppermute(v, axis, [(i, (i + by) % size) for i in range(size)])  7.14 us
    unnamed x29, local copies, waits for them, and re-layouts  5.11 us
  transfers between devices with their start and end apart: 10, of which 5 were waited for; matrix products, arithmetic and copies ran while one was open for 2% of the time, Pallas kernels for 12%

profile of v7, /device:TPU:1, one launch (start us, length us, event | category | flops | bytes accessed | tf_op | source)
XLA Modules:
  0.0 139.1 jit_solution(8709819151872114381)
XLA Ops:
  0.7 0.8 constant_dynamic-slice_fusion.3
  1.6 28.1 %all_to_all.20 = bf16[8,24,1536]{2,1,0:T(8,128)(2,1)S(1)} all-to-all(bf16[8,24,1536]{2,1,0:T(8,128)(2,1)S(1)} %broadcast_in_dim.6), channel_id=1, replica_groups=mesh['y'=8,'core'=2,'x'=4,'z'=8] {'z'}, dimensions={0} | all-to-all | bytes 1179648 | tf_op jit(solution)/shard_map/all_to_all | solution.py:265
  29.7 4.4 %collective-permute-start.2 = (bf16[192,1536]{1,0:T(8,128)(2,1)S(1)}, bf16[192,1536]{1,0:T(8,128)(2,1)S(1)}, u32[]{:S(2)}, u32[]{:S(2)}) collective-permute-start(bf16[192,1536]{1,0:T(8,128)(2,1)S(1)} %bitcast.36), channel_id=1, source_target_pairs={{0,24},{8,0},{16,8},{24,16},{1,25},{9,1},{17,9},{25,17},{2,26},{10... | collective-permute-start | bytes 1769480 | tf_op jit(solution)/shard_map/ppermute | solution.py:261
  34.1 1.9 %collective-permute-start.1 = (bf16[192,1536]{1,0:T(8,128)(2,1)S(1)}, bf16[192,1536]{1,0:T(8,128)(2,1)S(1)}, u32[]{:S(2)}, u32[]{:S(2)}) collective-permute-start(bf16[192,1536]{1,0:T(8,128)(2,1)S(1)} %bitcast.37), channel_id=1, source_target_pairs={{0,8},{8,16},{16,24},{24,0},{1,9},{9,17},{17,25},{25,1},{2,10},{10... | collective-permute-start | bytes 1769480 | tf_op jit(solution)/shard_map/ppermute | solution.py:261
  36.0 0.8 pad_maximum_fusion.1
  36.8 9.8 %all-to-all-start.1 = ((bf16[16,8,1536]{2,1,0:T(8,128)(2,1)}), bf16[16,8,1536]{2,1,0:T(8,128)(2,1)S(1)}, u32[]{:S(2)}, u32[]{:S(2)}) async-start(bf16[16,8,1536]{2,1,0:T(8,128)(2,1)} %pad_maximum_fusion.1), calls=%async_computation.1 | async-start | bytes 786432 | tf_op jit(solution)/shard_map/all_to_all | solution.py:265
  46.6 2.7 %collective-permute-done.1.up_ref.refs_4_ = bf16[192,1536]{1,0:T(8,128)(2,1)S(1)} collective-permute-done((bf16[192,1536]{1,0:T(8,128)(2,1)S(1)}, bf16[192,1536]{1,0:T(8,128)(2,1)S(1)}, u32[]{:S(2)}, u32[]{:S(2)}) %collective-permute-start.1) | collective-permute-done | bytes 589856 | tf_op jit(solution)/shard_map/ppermute | solution.py:261
  49.3 0.8 copy-done.9
  50.1 1.9 %shard_map.85 = (bf16[96,1536]{1,0:T(8,128)(2,1)}, bf16[96,1536]{1,0:T(8,128)(2,1)}) custom-call(bf16[192,1536]{1,0:T(8,128)(2,1)} %copy-done.9, bf16[192,1536]{1,0:T(8,128)(2,1)} %copy-done.8), custom_call_target="tpu_custom_call" | custom-call | flops 20000000000 | bytes 1179648 | tf_op jit(solution)/shard_map/pallas_call | solution.py:244
  52.0 1.9 %collective-permute-start.3 = (bf16[96,1536]{1,0:T(8,128)(2,1)}, bf16[96,1536]{1,0:T(8,128)(2,1)S(1)}, u32[]{:S(2)}, u32[]{:S(2)}) collective-permute-start(bf16[96,1536]{1,0:T(8,128)(2,1)} %get-tuple-element.20), channel_id=1, source_target_pairs={{0,8},{8,16},{16,24},{24,0},{1,9},{9,17},{17,25},{25,1},{2,10},{10... | collective-permute-start | bytes 884744 | tf_op jit(solution)/shard_map/ppermute | solution.py:261
  53.9 4.6 %collective-permute-start.4 = (bf16[96,1536]{1,0:T(8,128)(2,1)}, bf16[96,1536]{1,0:T(8,128)(2,1)S(1)}, u32[]{:S(2)}, u32[]{:S(2)}) collective-permute-start(bf16[96,1536]{1,0:T(8,128)(2,1)} %get-tuple-element.21), channel_id=1, source_target_pairs={{0,24},{8,0},{16,8},{24,16},{1,25},{9,1},{17,9},{25,17},{2,26},{10... | collective-permute-start | bytes 884744 | tf_op jit(solution)/shard_map/ppermute | solution.py:261
  61.1 6.0 %collective-permute-start = (bf16[128,1536]{1,0:T(8,128)(2,1)S(1)}, bf16[128,1536]{1,0:T(8,128)(2,1)S(1)}, u32[]{:S(2)}, u32[]{:S(2)}) collective-permute-start(bf16[128,1536]{1,0:T(8,128)(2,1)S(1)} %bitcast.28), channel_id=1, source_target_pairs={{0,32},{32,0},{1,33},{33,1},{2,34},{34,2},{3,35},{35,3},{4,36},{36... | collective-permute-start | bytes 1179656 | tf_op jit(solution)/shard_map/ppermute | solution.py:261
  67.2 0.7 copy-done.10
  67.9 0.7 copy-done.11
  68.6 4.7 %shard_map.86 = (bf16[128,1152]{1,0:T(8,128)(2,1)}, f32[6,128,128]{2,1,0:T(8,128)}, bf16[128,384]{1,0:T(8,128)(2,1)}, bf16[768,1152]{1,0:T(8,128)(2,1)}, bf16[38...) custom-call(s32[4]{0:T(128)} %pad_add_fusion.refs_0_, bf16[128,1536]{1,0:T(8,128)(2,1)} %bitcast.29, ...), custom_call_target="tpu_custom_call" | custom-call | flops 8000000000 | bytes 5901328 | tf_op jit(solution)/shard_map/pallas_call | solution.py:224
  73.3 0.7 copy-done.3
  74.0 4.8 %shard_map.87 = (bf16[128,1152]{1,0:T(8,128)(2,1)}, f32[6,128,128]{2,1,0:T(8,128)}, bf16[128,384]{1,0:T(8,128)(2,1)}, bf16[384,384]{1,0:T(8,128)(2,1)}, bf16[768,384]{1,0:T(8,128)(2,1)}) custom-call(s32[4]{0:T(128)} %pad_add_fusion.refs_0_, bf16[128,1536]{1,0:T(8,128)(2,1)} %bitcast.30, bf16[128,1536]{1,0:T(8,128)(2,1)} %copy-done.3, ...), custom_call_target="tpu_custom_call" | custom-call | flops 8000000000 | bytes 4328464 | tf_op jit(solution)/shard_map/pallas_call | solution.py:224
  78.8 2.0 %collective-permute-start.6 = (bf16[384,384]{1,0:T(8,128)(2,1)}, bf16[384,384]{1,0:T(8,128)(2,1)S(1)}, u32[]{:S(2)}, u32[]{:S(2)}) collective-permute-start(bf16[384,384]{1,0:T(8,128)(2,1)} %get-tuple-element.32), channel_id=1, source_target_pairs={{0,32},{32,0},{1,33},{33,1},{2,34},{34,2},{3,35},{35,3},{4,36},{36... | collective-permute-start | bytes 884744 | tf_op jit(solution)/shard_map/ppermute | solution.py:261
  80.9 1.8 %collective-permute-done.6 = bf16[384,384]{1,0:T(8,128)(2,1)S(1)} collective-permute-done((bf16[384,384]{1,0:T(8,128)(2,1)}, bf16[384,384]{1,0:T(8,128)(2,1)S(1)}, u32[]{:S(2)}, u32[]{:S(2)}) %collective-permute-start.6) | collective-permute-done | bytes 294944 | tf_op jit(solution)/shard_map/ppermute | solution.py:261
  82.6 0.8 constant_dynamic-update-slice_fusion.refs_12_
  83.4 5.6 %all-to-all-start.2 = ((bf16[32,24,384]{2,1,0:T(8,128)(2,1)}), bf16[32,24,384]{2,1,0:T(8,128)(2,1)S(1)}, u32[]{:S(2)}, u32[]{:S(2)}) async-start(bf16[32,24,384]{2,1,0:T(8,128)(2,1)} %bitcast.33), calls=%async_computation.2 | async-start | bytes 1179648 | tf_op jit(solution)/shard_map/all_to_all | solution.py:265
  89.0 2.5 %collective-permute-start.5 = (bf16[384,384]{1,0:T(8,128)(2,1)S(1)}, bf16[384,384]{1,0:T(8,128)(2,1)S(1)}, u32[]{:S(2)}, u32[]{:S(2)}) collective-permute-start(bf16[384,384]{1,0:T(8,128)(2,1)S(1)} %copy-done.12), channel_id=1, source_target_pairs={{0,32},{32,0},{1,33},{33,1},{2,34},{34,2},{3,35},{35,3},{4,36},{36... | collective-permute-start | bytes 884744 | tf_op jit(solution)/shard_map/ppermute | solution.py:261
  91.6 1.2 collective-permute-done.5.refs_4_
  92.7 0.7 copy-done.4
  93.5 7.8 %shard_map.88 = (f32[128,1536]{1,0:T(8,128)}, bf16[128,1536]{1,0:T(8,128)(2,1)}) custom-call(s32[4]{0:T(128)} %pad_add_fusion.refs_0_, bf16[128,1536]{1,0:T(8,128)(2,1)} %bitcast.31, bf16[128,1536]{1,0:T(8,128)(2,1)} %copy-done.3, bf16[384,384]{1,0:T(8,128)(2,1)} %get-tuple-element.22.refs_3_, bf16[384,384]{1,0:T(8,128)(2,1)} %copy-done.4, ...), custom_call_target="tpu_custom_call" | custom-call | flops 1000 | bytes 5898256 | tf_op jit(solution)/shard_map/pallas_call | solution.py:224
  101.3 2.3 %collective-permute-start.7 = (bf16[128,1536]{1,0:T(8,128)(2,1)}, bf16[128,1536]{1,0:T(8,128)(2,1)S(1)}, u32[]{:S(2)}, u32[]{:S(2)}) collective-permute-start(bf16[128,1536]{1,0:T(8,128)(2,1)} %get-tuple-element.34), channel_id=1, source_target_pairs={{0,32},{32,0},{1,33},{33,1},{2,34},{34,2},{3,35},{35,3},{4,36},{36... | collective-permute-start | bytes 1179656 | tf_op jit(solution)/shard_map/ppermute | solution.py:261
  103.6 1.5 %collective-permute-done.7.refs_4_ = bf16[128,1536]{1,0:T(8,128)(2,1)S(1)} collective-permute-done((bf16[128,1536]{1,0:T(8,128)(2,1)}, bf16[128,1536]{1,0:T(8,128)(2,1)S(1)}, u32[]{:S(2)}, u32[]{:S(2)}) %collective-permute-start.7) | collective-permute-done | bytes 393248 | tf_op jit(solution)/shard_map/ppermute | solution.py:261
  105.1 0.7 copy-done.2
  105.8 2.4 %shard_map.89 = bf16[128,1536]{1,0:T(8,128)(2,1)} custom-call(s32[4]{0:T(128)} %pad_add_fusion.refs_0_, bf16[128,1536]{1,0:T(8,128)(2,1)} %bitcast.32, f32[1,768]{1,0:T(1,128)} %reshape.51.refs_2_.refs_3_, f32[128,1536]{1,0:T(8,128)} %get-tuple-element.33.refs_3_, bf16[128,1536]{1,0:T(8,128)(2,1)} %copy-done.2), custom_call_target="tpu_custom_call" | custom-call | flops 1000 | bytes 1969168 | tf_op jit(solution)/shard_map/pallas_call | solution.py:224
  108.4 1.0 pad_maximum_fusion
  109.4 28.1 %all_to_all.21 = bf16[16,8,2688]{2,1,0:T(8,128)(2,1)S(1)} all-to-all(bf16[16,8,2688]{2,1,0:T(8,128)(2,1)S(1)} %pad_maximum_fusion), channel_id=1, replica_groups=mesh['y'=8,'core'=2,'x'=4,'z'=8] {'y','core'}, dimensions={0} | all-to-all | bytes 1376256 | tf_op jit(solution)/shard_map/all_to_all | solution.py:265
  138.3 0.8 slice_bitcast_fusion
  (39 shorter events, 2.9 us)
Async XLA Ops:
  0.6 35.4 %copy-start.5 = (bf16[1,128,768]{2,1,0:T(8,128)(2,1)S(1)}, bf16[1,128,768]{2,1,0:T(8,128)(2,1)}, u32[]{:S(2)}) copy-start(bf16[1,128,768]{2,1,0:T(8,128)(2,1)} %param.7) | copy-start | bytes 589828
  0.6 35.4 %copy-start.6 = (bf16[1,128,768]{2,1,0:T(8,128)(2,1)S(1)}, bf16[1,128,768]{2,1,0:T(8,128)(2,1)}, u32[]{:S(2)}) copy-start(bf16[1,128,768]{2,1,0:T(8,128)(2,1)} %param.6) | copy-start | bytes 589828
  29.7 22.3 %copy-start.1 = (bf16[8,24,1536]{2,1,0:T(8,128)(2,1)}, bf16[8,24,1536]{2,1,0:T(8,128)(2,1)S(1)}, u32[]{:S(2)}) copy-start(bf16[8,24,1536]{2,1,0:T(8,128)(2,1)S(1)} %all_to_all.20) | copy-start | bytes 1769476
  29.7 16.9 %collective-permute-start.2 = (bf16[192,1536]{1,0:T(8,128)(2,1)S(1)}, bf16[192,1536]{1,0:T(8,128)(2,1)S(1)}, u32[]{:S(2)}, u32[]{:S(2)}) collective-permute-start(bf16[192,1536]{1,0:T(8,128)(2,1)S(1)} %bitcast.36), channel_id=1, source_target_pairs={{0,24},{8,0},{16,8},{24,16},{1,25},{9,1},{17,9},{25,17},{2,26},{10... | collective-permute-start | bytes 1769480 | tf_op jit(solution)/shard_map/ppermute | solution.py:261
  34.1 15.2 %collective-permute-start.1 = (bf16[192,1536]{1,0:T(8,128)(2,1)S(1)}, bf16[192,1536]{1,0:T(8,128)(2,1)S(1)}, u32[]{:S(2)}, u32[]{:S(2)}) collective-permute-start(bf16[192,1536]{1,0:T(8,128)(2,1)S(1)} %bitcast.37), channel_id=1, source_target_pairs={{0,8},{8,16},{16,24},{24,0},{1,9},{9,17},{17,25},{25,1},{2,10},{10... | collective-permute-start | bytes 1769480 | tf_op jit(solution)/shard_map/ppermute | solution.py:261
  36.8 24.4 %all-to-all-start.1 = ((bf16[16,8,1536]{2,1,0:T(8,128)(2,1)}), bf16[16,8,1536]{2,1,0:T(8,128)(2,1)S(1)}, u32[]{:S(2)}, u32[]{:S(2)}) async-start(bf16[16,8,1536]{2,1,0:T(8,128)(2,1)} %pad_maximum_fusion.1), calls=%async_computation.1 | async-start | bytes 786432 | tf_op jit(solution)/shard_map/all_to_all | solution.py:265
  46.6 11.9 %copy-start.13 = (s32[2]{0:T(128)S(1)}, s32[2]{0:T(128)}, u32[]{:S(2)}) copy-start(s32[2]{0:T(128)} %param.11) | copy-start | bytes 28
  46.6 13.2 %copy-start.7 = (f32[768]{0:T(1024)S(1)}, f32[768]{0:T(1024)}, u32[]{:S(2)}) copy-start(f32[768]{0:T(1024)} %param.8) | copy-start | bytes 9220
  46.6 2.7 %copy-start.8 = (bf16[192,1536]{1,0:T(8,128)(2,1)}, bf16[192,1536]{1,0:T(8,128)(2,1)S(1)}, u32[]{:S(2)}) copy-start(bf16[192,1536]{1,0:T(8,128)(2,1)S(1)} %collective-permute-done.2.down_ref.refs_5_) | copy-start | bytes 1769476
  49.3 0.8 copy-start.9
  52.0 15.1 %collective-permute-start.3 = (bf16[96,1536]{1,0:T(8,128)(2,1)}, bf16[96,1536]{1,0:T(8,128)(2,1)S(1)}, u32[]{:S(2)}, u32[]{:S(2)}) collective-permute-start(bf16[96,1536]{1,0:T(8,128)(2,1)} %get-tuple-element.20), channel_id=1, source_target_pairs={{0,8},{8,16},{16,24},{24,0},{1,9},{9,17},{17,25},{25,1},{2,10},{10... | collective-permute-start | bytes 884744 | tf_op jit(solution)/shard_map/ppermute | solution.py:261
  53.9 13.2 %collective-permute-start.4 = (bf16[96,1536]{1,0:T(8,128)(2,1)}, bf16[96,1536]{1,0:T(8,128)(2,1)S(1)}, u32[]{:S(2)}, u32[]{:S(2)}) collective-permute-start(bf16[96,1536]{1,0:T(8,128)(2,1)} %get-tuple-element.21), channel_id=1, source_target_pairs={{0,24},{8,0},{16,8},{24,16},{1,25},{9,1},{17,9},{25,17},{2,26},{10... | collective-permute-start | bytes 884744 | tf_op jit(solution)/shard_map/ppermute | solution.py:261
  61.1 6.0 %copy-start = (bf16[16,8,1536]{2,1,0:T(8,128)(2,1)}, bf16[16,8,1536]{2,1,0:T(8,128)(2,1)S(1)}, u32[]{:S(2)}) copy-start(bf16[16,8,1536]{2,1,0:T(8,128)(2,1)S(1)} %all-to-all-done.1) | copy-start | bytes 1179652
  61.1 12.1 %collective-permute-start = (bf16[128,1536]{1,0:T(8,128)(2,1)S(1)}, bf16[128,1536]{1,0:T(8,128)(2,1)S(1)}, u32[]{:S(2)}, u32[]{:S(2)}) collective-permute-start(bf16[128,1536]{1,0:T(8,128)(2,1)S(1)} %bitcast.28), channel_id=1, source_target_pairs={{0,32},{32,0},{1,33},{33,1},{2,34},{34,2},{3,35},{35,3},{4,36},{36... | collective-permute-start | bytes 1179656 | tf_op jit(solution)/shard_map/ppermute | solution.py:261
  67.1 0.7 copy-start.10
  67.9 0.7 copy-start.11
  73.3 0.7 copy-start.3
  78.8 10.2 %copy-start.12 = (bf16[384,384]{1,0:T(8,128)(2,1)S(1)}, bf16[384,384]{1,0:T(8,128)(2,1)}, u32[]{:S(2)}) copy-start(bf16[384,384]{1,0:T(8,128)(2,1)} %get-tuple-element.23) | copy-start | bytes 884740
  78.8 3.8 %collective-permute-start.6 = (bf16[384,384]{1,0:T(8,128)(2,1)}, bf16[384,384]{1,0:T(8,128)(2,1)S(1)}, u32[]{:S(2)}, u32[]{:S(2)}) collective-permute-start(bf16[384,384]{1,0:T(8,128)(2,1)} %get-tuple-element.32), channel_id=1, source_target_pairs={{0,32},{32,0},{1,33},{33,1},{2,34},{34,2},{3,35},{35,3},{4,36},{36... | collective-permute-start | bytes 884744 | tf_op jit(solution)/shard_map/ppermute | solution.py:261
  83.4 24.9 %all-to-all-start.2 = ((bf16[32,24,384]{2,1,0:T(8,128)(2,1)}), bf16[32,24,384]{2,1,0:T(8,128)(2,1)S(1)}, u32[]{:S(2)}, u32[]{:S(2)}) async-start(bf16[32,24,384]{2,1,0:T(8,128)(2,1)} %bitcast.33), calls=%async_computation.2 | async-start | bytes 1179648 | tf_op jit(solution)/shard_map/all_to_all | solution.py:265
  89.0 3.7 %collective-permute-start.5 = (bf16[384,384]{1,0:T(8,128)(2,1)S(1)}, bf16[384,384]{1,0:T(8,128)(2,1)S(1)}, u32[]{:S(2)}, u32[]{:S(2)}) collective-permute-start(bf16[384,384]{1,0:T(8,128)(2,1)S(1)} %copy-done.12), channel_id=1, source_target_pairs={{0,32},{32,0},{1,33},{33,1},{2,34},{34,2},{3,35},{35,3},{4,36},{36... | collective-permute-start | bytes 884744 | tf_op jit(solution)/shard_map/ppermute | solution.py:261
  92.7 0.7 copy-start.4
  101.3 3.8 %collective-permute-start.7 = (bf16[128,1536]{1,0:T(8,128)(2,1)}, bf16[128,1536]{1,0:T(8,128)(2,1)S(1)}, u32[]{:S(2)}, u32[]{:S(2)}) collective-permute-start(bf16[128,1536]{1,0:T(8,128)(2,1)} %get-tuple-element.34), channel_id=1, source_target_pairs={{0,32},{32,0},{1,33},{33,1},{2,34},{34,2},{3,35},{35,3},{4,36},{36... | collective-permute-start | bytes 1179656 | tf_op jit(solution)/shard_map/ppermute | solution.py:261
  105.1 0.7 copy-start.2

commit v8 on v7

--- a/solution.py
+++ b/solution.py
@@ -12,7 +12,12 @@
 TM = ("x", "z")
 NEG = -1e30
 VMEM_LIMIT = 56 * 1024 * 1024
-FWD_COST, BWD_COST, END_COST, HALVES_COST = 8_000_000_000, 1000, 1000, 20_000_000_000
+OWN_COST = 8_000_000_000
+NEAR_COST = 8_000_000_000
+PLACE_COST = 1000
+STEP_COST = 20_000_000_000
+BWD_COST = 1000
+END_COST = 1000
 
 
 def dot_nn(a, b):
@@ -81,16 +86,32 @@
     qkv_ref[...] = dot_nn(normed, w_ref[...]).astype(jnp.bfloat16)
 
 
+def place(ref, at, w_ref, wo_ref):
+    here = pl.ds(pl.multiple_of(at, ref.shape[0]), ref.shape[0])
+    w_ref[here, :] = ref[:, : w_ref.shape[1]]
+    wo_ref[here, :] = ref[:, w_ref.shape[1] :]
+
+
+def near_blocks_kernel(
+    scalars, low_ref, high_ref, up_low, up_high, down_low, down_high, w_ref, wo_ref
+):
+    x_at, deep = scalars[3], 2 * low_ref.shape[0]
+    pairs = ((low_ref, high_ref, 0), (up_low, up_high, XS - 1), (down_low, down_high, 1))
+    for low, high, step in pairs:
+        at = lax.rem(x_at + step, XS) * deep
+        place(low, at, w_ref, wo_ref)
+        place(high, at + deep // 2, w_ref, wo_ref)
+
+
 def own_kernel(
     frames,
     scalars,
     own_ref,
     gain_ref,
-    block_ref,
-    up_ref,
-    down_ref,
     far_low_ref,
     far_high_ref,
+    some_w_ref,
+    some_wo_ref,
     qkv_ref,
     p_ref,
     att_ref,
@@ -99,22 +120,14 @@
     give_ref,
     all_ref,
 ):
-    rows, mine = att_ref.shape
-    width, deep = w_ref.shape[0], block_ref.shape[0]
+    rows, mid = att_ref.shape
     core, x_at = scalars[0], scalars[3]
-    far = lax.rem(x_at + 2, XS) * deep
-    places = (
-        (block_ref, x_at * deep),
-        (up_ref, lax.rem(x_at + XS - 1, XS) * deep),
-        (down_ref, lax.rem(x_at + 1, XS) * deep),
-        (far_low_ref, far),
-        (far_high_ref, far + deep // 2),
-    )
-    for ref, at in places:
-        here = pl.ds(pl.multiple_of(at, deep // 2), ref.shape[0])
-        w_ref[here, :] = ref[:, : 3 * mine]
-        all_ref[here, :] = ref[:, 3 * mine :]
-    mid = width // 2
+    deep = far_low_ref.shape[0]
+    far = lax.rem(x_at + 2, XS) * (2 * deep)
+    w_ref[...] = some_w_ref[...]
+    all_ref[...] = some_wo_ref[...]
+    place(far_low_ref, far, w_ref, all_ref)
+    place(far_high_ref, far + deep, w_ref, all_ref)
     wo_ref[...] = all_ref[pl.ds(pl.multiple_of(core * mid, mid), mid), :]
     give_ref[...] = all_ref[pl.ds(pl.multiple_of((1 - core) * mid, mid), mid), :]
     project(own_ref, gain_ref, w_ref, qkv_ref)
@@ -235,25 +248,15 @@
     )(*operands, *behind)
 
 
-def halves(up, down, mid):
-    def kernel(up_ref, down_ref, low_ref, high_ref):
-        low_ref[...] = up_ref[...]
-        high_ref[...] = down_ref[...]
-
-    cols = up.shape[1]
+def as_they_are(*arrays):
     return pl.pallas_call(
-        kernel,
-        grid=(1,),
-        out_shape=[jax.ShapeDtypeStruct((mid, cols), up.dtype)] * 2,
-        in_specs=[
-            pl.BlockSpec((mid, cols), lambda i: (0, 0)),
-            pl.BlockSpec((mid, cols), lambda i: (1, 0)),
-        ],
-        out_specs=[pl.BlockSpec((mid, cols), lambda i: (0, 0))] * 2,
-        cost_estimate=pl.CostEstimate(
-            flops=HALVES_COST, bytes_accessed=4 * mid * cols * 2, transcendentals=0
-        ),
-    )(up, down)
+        lambda *refs: None,
+        out_shape=[jax.ShapeDtypeStruct(v.shape, v.dtype) for v in arrays],
+        in_specs=[pl.BlockSpec(memory_space=pl.ANY)] * len(arrays),
+        out_specs=[pl.BlockSpec(memory_space=pl.ANY)] * len(arrays),
+        input_output_aliases={i: i for i in range(len(arrays))},
+        cost_estimate=pl.CostEstimate(flops=STEP_COST, bytes_accessed=0, transcendentals=0),
+    )(*arrays)
 
 
 def shift(v, axis, by):
@@ -285,10 +288,12 @@
     mine = jnp.concatenate(mine, axis=1)
     block = exchange(jnp.broadcast_to(mine[None], (zs, piece, half + cut)), "z")
     block = block.reshape(zs * piece, half + cut)
-    up, down = shift(block, "x", 1), shift(block, "x", -1)
     mid = zs * piece // 2
-    far_low, far_high = halves(up, down, mid)
-    far_low, far_high = shift(far_low, "x", 1), shift(far_high, "x", -1)
+    low, high = block[:mid], block[mid:]
+    up_low, down_high = shift(low, "x", 1), shift(high, "x", -1)
+    up_high, down_low = shift(high, "x", 1), shift(low, "x", -1)
+    up_low, down_high = as_they_are(up_low, down_high)
+    far_low, far_high = shift(up_low, "x", 1), shift(down_high, "x", -1)
 
     both = jnp.concatenate(
         [frames_in.reshape(mics, frames, width), cotangent.reshape(mics, frames, width)], axis=2
@@ -307,6 +312,13 @@
     def shape(dims, dtype):
         return jax.ShapeDtypeStruct(dims, dtype)
 
+    some_w, some_wo = call(
+        near_blocks_kernel,
+        (shape((width, half), bf), shape((width, cut), bf)),
+        (),
+        PLACE_COST,
+        scalars, low, high, up_low, up_high, down_low, down_high,
+    )
     heads = width // HD // cores
     results = (
         shape((rows, half), bf),
@@ -317,15 +329,15 @@
         lambda *refs: own_kernel(frames, *refs),
         results + (shape((width, half), bf), shape((cut, cut), bf), shape((cut, cut), bf)),
         (pltpu.VMEM((width, cut), bf),),
-        FWD_COST,
-        scalars, own, gain, block, up, down, far_low, far_high,
+        OWN_COST,
+        scalars, own, gain, far_low, far_high, some_w, some_wo,
     )
     wo_got = shift(wo_give, "core", 1)
     near_qkv, near_p, near_att, give, gw = call(
         lambda *refs: near_kernel(frames, *refs),
         results + (shape((cut, cut), bf), shape((width, cut), bf)),
         (),
-        FWD_COST,
+        NEAR_COST,
         scalars, own, near, gain, w, own_att,
     )
 

time: 140 us -> 142 us (1.014)
  waiting for transfers between devices: 7.24 us -> 4.96 us
  starting transfers between devices: 41 us -> 42.7 us
  local copies, waits for them, and re-layouts: 8.77 us -> 10.2 us
    pallas_call x4 -> x5, Pallas kernels: 19.7 us -> 23 us  [call(): pl.pallas_call(kernel, out_shape=outs, in_specs=[pl.BlockSpec(memory_spac...]
    ppermute x8 -> x10, starting transfers between devices: 25.6 us -> 28.7 us  [shift(): return lax.ppermute(v, axis, [(i, (i + by) % size) for i in range(size)])]
    ppermute x8 -> x10, waiting for transfers between devices: 7.14 us -> 4.95 us  [shift(): return lax.ppermute(v, axis, [(i, (i + by) % size) for i in range(size)])]
    pallas_call x1, Pallas kernels: 1.89 us -> 0.01 us  [as_they_are(): pl.pallas_call(lambda *refs: None, out_shape=[jax.ShapeDtypeStruct(v.shap...]
    unnamed x29 -> x35, local copies, waits for them, and re-layouts: 5.11 us -> 6.56 us
  transfers between devices with their start and end apart: 10 -> 12, of which waited for: 5 -> 3; matrix products, arithmetic and copies ran while one was open for 2% -> 2% of each run, Pallas kernels for 12% -> 13%
where the time goes in v8:
time: 142 us; the launch traced here: 141 us
  blocking collectives  56.2 us (40%)
  starting transfers between devices  42.7 us (30%)
  Pallas kernels  23 us (16%)
  local copies, waits for them, and re-layouts  10.2 us (7%)
  waiting for transfers between devices  4.96 us (3%)
  other arithmetic  2.61 us (2%)
  between operations  1.66 us (1%)
    all_to_all x2, blocking collectives, exchange(): return lax.all_to_all(v, axes, split_axis=0, concat_axis=0, tiled=True)  56.2 us
    ppermute x10, starting transfers between devices, shift(): return lax.ppermute(v, axis, [(i, (i + by) % size) for i in range(size)])  28.7 us
    pallas_call x5, Pallas kernels, call(): pl.pallas_call(kernel, out_shape=outs, in_specs=[pl.BlockSpec(memory_spac...  23 us
    all_to_all x2, starting transfers between devices, exchange(): return lax.all_to_all(v, axes, split_axis=0, concat_axis=0, tiled=True)  14 us
    unnamed x35, local copies, waits for them, and re-layouts  6.56 us
    ppermute x10, waiting for transfers between devices, shift(): return lax.ppermute(v, axis, [(i, (i + by) % size) for i in range(size)])  4.95 us
  transfers between devices with their start and end apart: 12, of which 3 were waited for; matrix products, arithmetic and copies ran while one was open for 2% of the time, Pallas kernels for 13%

profile of v8, /device:TPU:1, one launch (start us, length us, event | category | flops | bytes accessed | tf_op | source)
XLA Modules:
  0.0 141.3 jit_solution(1543651380936048)
XLA Ops:
  0.6 0.8 constant_dynamic-slice_fusion.3
  1.5 28.2 %all_to_all.20 = bf16[8,24,1536]{2,1,0:T(8,128)(2,1)S(1)} all-to-all(bf16[8,24,1536]{2,1,0:T(8,128)(2,1)S(1)} %broadcast_in_dim.6), channel_id=1, replica_groups=mesh['y'=8,'core'=2,'x'=4,'z'=8] {'z'}, dimensions={0} | all-to-all | bytes 1179648 | tf_op jit(solution)/shard_map/all_to_all | solution.py:268
  29.8 3.1 %collective-permute-start.1 = (bf16[96,1536]{1,0:T(8,128)(2,1)S(1)}, bf16[96,1536]{1,0:T(8,128)(2,1)S(1)}, u32[]{:S(2)}, u32[]{:S(2)}) collective-permute-start(bf16[96,1536]{1,0:T(8,128)(2,1)S(1)} %bitcast.40), channel_id=1, source_target_pairs={{0,8},{8,16},{16,24},{24,0},{1,9},{9,17},{17,25},{25,1},{2,10},{10... | collective-permute-start | bytes 884744 | tf_op jit(solution)/shard_map/ppermute | solution.py:264
  32.9 3.4 %collective-permute-start.2 = (bf16[96,1536]{1,0:T(8,128)(2,1)S(1)}, bf16[96,1536]{1,0:T(8,128)(2,1)S(1)}, u32[]{:S(2)}, u32[]{:S(2)}) collective-permute-start(bf16[96,1536]{1,0:T(8,128)(2,1)S(1)} %bitcast.37), channel_id=1, source_target_pairs={{0,24},{8,0},{16,8},{24,16},{1,25},{9,1},{17,9},{25,17},{2,26},{10... | collective-permute-start | bytes 884744 | tf_op jit(solution)/shard_map/ppermute | solution.py:264
  36.3 0.8 pad_maximum_fusion.1
  37.1 10.1 %all-to-all-start = ((bf16[16,8,1536]{2,1,0:T(8,128)(2,1)}), bf16[16,8,1536]{2,1,0:T(8,128)(2,1)S(1)}, u32[]{:S(2)}, u32[]{:S(2)}) async-start(bf16[16,8,1536]{2,1,0:T(8,128)(2,1)} %pad_maximum_fusion.1), calls=%async_computation | async-start | bytes 786432 | tf_op jit(solution)/shard_map/all_to_all | solution.py:268
  47.2 1.9 %collective-permute-start.5 = (bf16[96,1536]{1,0:T(8,128)(2,1)S(1)}, bf16[96,1536]{1,0:T(8,128)(2,1)S(1)}, u32[]{:S(2)}, u32[]{:S(2)}) collective-permute-start(bf16[96,1536]{1,0:T(8,128)(2,1)S(1)} %bitcast.38), channel_id=1, source_target_pairs={{0,8},{8,16},{16,24},{24,0},{1,9},{9,17},{17,25},{25,1},{2,10},{10... | collective-permute-start | bytes 884744 | tf_op jit(solution)/shard_map/ppermute | solution.py:264
  49.2 4.6 %collective-permute-start.6 = (bf16[96,1536]{1,0:T(8,128)(2,1)S(1)}, bf16[96,1536]{1,0:T(8,128)(2,1)S(1)}, u32[]{:S(2)}, u32[]{:S(2)}) collective-permute-start(bf16[96,1536]{1,0:T(8,128)(2,1)S(1)} %bitcast.41), channel_id=1, source_target_pairs={{0,24},{8,0},{16,8},{24,16},{1,25},{9,1},{17,9},{25,17},{2,26},{10... | collective-permute-start | bytes 884744 | tf_op jit(solution)/shard_map/ppermute | solution.py:264
  54.5 0.7 copy-done.9
  55.2 1.9 %collective-permute-start.3 = (bf16[96,1536]{1,0:T(8,128)(2,1)}, bf16[96,1536]{1,0:T(8,128)(2,1)S(1)}, u32[]{:S(2)}, u32[]{:S(2)}) collective-permute-start(bf16[96,1536]{1,0:T(8,128)(2,1)} %get-tuple-element.20.up_low), channel_id=1, source_target_pairs={{0,8},{8,16},{16,24},{24,0},{1,9},{9,17},{17,25},{25,1},{2,10},{10... | collective-permute-start | bytes 884744 | tf_op jit(solution)/shard_map/ppermute | solution.py:264
  57.1 4.6 %collective-permute-start.4 = (bf16[96,1536]{1,0:T(8,128)(2,1)}, bf16[96,1536]{1,0:T(8,128)(2,1)S(1)}, u32[]{:S(2)}, u32[]{:S(2)}) collective-permute-start(bf16[96,1536]{1,0:T(8,128)(2,1)} %get-tuple-element.21.down_high), channel_id=1, source_target_pairs={{0,24},{8,0},{16,8},{24,16},{1,25},{9,1},{17,9},{25,17},{2,26},{10... | collective-permute-start | bytes 884744 | tf_op jit(solution)/shard_map/ppermute | solution.py:264
  64.3 3.1 %collective-permute-start = (bf16[128,1536]{1,0:T(8,128)(2,1)S(1)}, bf16[128,1536]{1,0:T(8,128)(2,1)S(1)}, u32[]{:S(2)}, u32[]{:S(2)}) collective-permute-start(bf16[128,1536]{1,0:T(8,128)(2,1)S(1)} %bitcast.29), channel_id=1, source_target_pairs={{0,32},{32,0},{1,33},{33,1},{2,34},{34,2},{3,35},{35,3},{4,36},{36... | collective-permute-start | bytes 1179656 | tf_op jit(solution)/shard_map/ppermute | solution.py:264
  67.4 0.7 copy-done.6
  68.1 0.7 copy-done.7
  68.8 3.0 %shard_map.86 = (bf16[768,1152]{1,0:T(8,128)(2,1)}, bf16[768,384]{1,0:T(8,128)(2,1)}) custom-call(s32[4]{0:T(128)} %pad_add_fusion.scalars.refs_0_, bf16[96,1536]{1,0:T(8,128)(2,1)} %bitcast.42, bf16[96,1536]{1,0:T(8,128)(2,1)} %bitcast.39, bf16[96,1536]{1,0:T(8,128)(2,1)} %get-tuple-element.20.up_low, bf16[96,1536]{1,0:T(8,128)(2,1)} %copy-done.6, ...), custom_call_target="tpu_custom_call" | custom-call | flops 1000 | bytes 4128784 | tf_op jit(solution)/shard_map/pallas_call | solution.py:237
  72.7 4.9 %shard_map.87 = (bf16[128,1152]{1,0:T(8,128)(2,1)}, f32[6,128,128]{2,1,0:T(8,128)}, bf16[128,384]{1,0:T(8,128)(2,1)}, bf16[768,1152]{1,0:T(8,128)(2,1)}, bf16[38...) custom-call(s32[4]{0:T(128)} %pad_add_fusion.scalars.refs_0_, bf16[128,1536]{1,0:T(8,128)(2,1)} %bitcast.30, ...), custom_call_target="tpu_custom_call" | custom-call | flops 8000000000 | bytes 6491152 | tf_op jit(solution)/shard_map/pallas_call | solution.py:237
  77.6 0.7 copy-done.4
  78.4 4.8 %shard_map.88 = (bf16[128,1152]{1,0:T(8,128)(2,1)}, f32[6,128,128]{2,1,0:T(8,128)}, bf16[128,384]{1,0:T(8,128)(2,1)}, bf16[384,384]{1,0:T(8,128)(2,1)}, bf16[768,384]{1,0:T(8,128)(2,1)}) custom-call(s32[4]{0:T(128)} %pad_add_fusion.scalars.refs_0_, bf16[128,1536]{1,0:T(8,128)(2,1)} %bitcast.31, bf16[128,1536]{1,0:T(8,128)(2,1)} %copy-done.4, ...), custom_call_target="tpu_custom_call" | custom-call | flops 8000000000 | bytes 4328464 | tf_op jit(solution)/shard_map/pallas_call | solution.py:237
  83.2 2.0 %collective-permute-start.8 = (bf16[384,384]{1,0:T(8,128)(2,1)}, bf16[384,384]{1,0:T(8,128)(2,1)S(1)}, u32[]{:S(2)}, u32[]{:S(2)}) collective-permute-start(bf16[384,384]{1,0:T(8,128)(2,1)} %get-tuple-element.34), channel_id=1, source_target_pairs={{0,32},{32,0},{1,33},{33,1},{2,34},{34,2},{3,35},{35,3},{4,36},{36... | collective-permute-start | bytes 884744 | tf_op jit(solution)/shard_map/ppermute | solution.py:264
  85.3 1.7 %collective-permute-done.8 = bf16[384,384]{1,0:T(8,128)(2,1)S(1)} collective-permute-done((bf16[384,384]{1,0:T(8,128)(2,1)}, bf16[384,384]{1,0:T(8,128)(2,1)S(1)}, u32[]{:S(2)}, u32[]{:S(2)}) %collective-permute-start.8) | collective-permute-done | bytes 294944 | tf_op jit(solution)/shard_map/ppermute | solution.py:264
  87.0 0.8 constant_dynamic-update-slice_fusion.refs_12_
  87.8 3.9 %all-to-all-start.2 = ((bf16[32,24,384]{2,1,0:T(8,128)(2,1)}), bf16[32,24,384]{2,1,0:T(8,128)(2,1)S(1)}, u32[]{:S(2)}, u32[]{:S(2)}) async-start(bf16[32,24,384]{2,1,0:T(8,128)(2,1)} %bitcast.34), calls=%async_computation.2 | async-start | bytes 1179648 | tf_op jit(solution)/shard_map/all_to_all | solution.py:268
  91.7 2.0 %collective-permute-start.7 = (bf16[384,384]{1,0:T(8,128)(2,1)S(1)}, bf16[384,384]{1,0:T(8,128)(2,1)S(1)}, u32[]{:S(2)}, u32[]{:S(2)}) collective-permute-start(bf16[384,384]{1,0:T(8,128)(2,1)S(1)} %copy-done.15), channel_id=1, source_target_pairs={{0,32},{32,0},{1,33},{33,1},{2,34},{34,2},{3,35},{35,3},{4,36},{36... | collective-permute-start | bytes 884744 | tf_op jit(solution)/shard_map/ppermute | solution.py:264
  93.7 1.4 %collective-permute-done.7.refs_4_ = bf16[384,384]{1,0:T(8,128)(2,1)S(1)} collective-permute-done((bf16[384,384]{1,0:T(8,128)(2,1)S(1)}, bf16[384,384]{1,0:T(8,128)(2,1)S(1)}, u32[]{:S(2)}, u32[]{:S(2)}) %collective-permute-start.7) | collective-permute-done | bytes 294944 | tf_op jit(solution)/shard_map/ppermute | solution.py:264
  95.9 7.9 %shard_map.89 = (f32[128,1536]{1,0:T(8,128)}, bf16[128,1536]{1,0:T(8,128)(2,1)}) custom-call(s32[4]{0:T(128)} %pad_add_fusion.scalars.refs_0_, bf16[128,1536]{1,0:T(8,128)(2,1)} %bitcast.32, bf16[128,1536]{1,0:T(8,128)(2,1)} %copy-done.4, bf16[384,384]{1,0:T(8,128)(2,1)} %get-tuple-element.24.refs_3_, bf16[384,384]{1,0:T(8,128)(2,1)} %copy-done.5, ...), custom_call_target="tpu_custom_call" | custom-call | flops 1000 | bytes 5898256 | tf_op jit(solution)/shard_map/pallas_call | solution.py:237
  103.7 2.0 %collective-permute-start.9 = (bf16[128,1536]{1,0:T(8,128)(2,1)}, bf16[128,1536]{1,0:T(8,128)(2,1)S(1)}, u32[]{:S(2)}, u32[]{:S(2)}) collective-permute-start(bf16[128,1536]{1,0:T(8,128)(2,1)} %get-tuple-element.36), channel_id=1, source_target_pairs={{0,32},{32,0},{1,33},{33,1},{2,34},{34,2},{3,35},{35,3},{4,36},{36... | collective-permute-start | bytes 1179656 | tf_op jit(solution)/shard_map/ppermute | solution.py:264
  105.8 1.8 %collective-permute-done.9.refs_4_ = bf16[128,1536]{1,0:T(8,128)(2,1)S(1)} collective-permute-done((bf16[128,1536]{1,0:T(8,128)(2,1)}, bf16[128,1536]{1,0:T(8,128)(2,1)S(1)}, u32[]{:S(2)}, u32[]{:S(2)}) %collective-permute-start.9) | collective-permute-done | bytes 393248 | tf_op jit(solution)/shard_map/ppermute | solution.py:264
  107.5 0.8 copy-done.3
  108.3 2.4 %shard_map.90 = bf16[128,1536]{1,0:T(8,128)(2,1)} custom-call(s32[4]{0:T(128)} %pad_add_fusion.scalars.refs_0_, bf16[128,1536]{1,0:T(8,128)(2,1)} %bitcast.33, f32[1,768]{1,0:T(1,128)} %reshape.50.refs_2_.refs_3_, f32[128,1536]{1,0:T(8,128)} %get-tuple-element.35.refs_3_, bf16[128,1536]{1,0:T(8,128)(2,1)} %copy-done.3), custom_call_target="tpu_custom_call" | custom-call | flops 1000 | bytes 1969168 | tf_op jit(solution)/shard_map/pallas_call | solution.py:237
  110.8 1.0 pad_maximum_fusion
  111.9 27.9 %all_to_all.21 = bf16[16,8,2688]{2,1,0:T(8,128)(2,1)S(1)} all-to-all(bf16[16,8,2688]{2,1,0:T(8,128)(2,1)S(1)} %pad_maximum_fusion), channel_id=1, replica_groups=mesh['y'=8,'core'=2,'x'=4,'z'=8] {'y','core'}, dimensions={0} | all-to-all | bytes 1376256 | tf_op jit(solution)/shard_map/all_to_all | solution.py:268
  140.6 0.8 slice_bitcast_fusion
  (51 shorter events, 5.1 us)
Async XLA Ops:
  1.5 34.9 %copy-start.10 = (bf16[1,128,768]{2,1,0:T(8,128)(2,1)S(1)}, bf16[1,128,768]{2,1,0:T(8,128)(2,1)}, u32[]{:S(2)}) copy-start(bf16[1,128,768]{2,1,0:T(8,128)(2,1)} %param.7) | copy-start | bytes 589828
  1.5 34.9 %copy-start.11 = (bf16[1,128,768]{2,1,0:T(8,128)(2,1)S(1)}, bf16[1,128,768]{2,1,0:T(8,128)(2,1)}, u32[]{:S(2)}) copy-start(bf16[1,128,768]{2,1,0:T(8,128)(2,1)} %param.6) | copy-start | bytes 589828
  29.8 25.4 %copy-start.1 = (bf16[4,24,1536]{2,1,0:T(8,128)(2,1)}, bf16[4,24,1536]{2,1,0:T(8,128)(2,1)S(1)}, u32[]{:S(2)}) copy-start(bf16[4,24,1536]{2,1,0:T(8,128)(2,1)S(1)} %get-tuple-element.39) | copy-start | bytes 884740
  29.8 25.4 %copy-start.2 = (bf16[4,24,1536]{2,1,0:T(8,128)(2,1)}, bf16[4,24,1536]{2,1,0:T(8,128)(2,1)S(1)}, u32[]{:S(2)}) copy-start(bf16[4,24,1536]{2,1,0:T(8,128)(2,1)S(1)} %get-tuple-element.40) | copy-start | bytes 884740
  29.8 23.9 %collective-permute-start.1 = (bf16[96,1536]{1,0:T(8,128)(2,1)S(1)}, bf16[96,1536]{1,0:T(8,128)(2,1)S(1)}, u32[]{:S(2)}, u32[]{:S(2)}) collective-permute-start(bf16[96,1536]{1,0:T(8,128)(2,1)S(1)} %bitcast.40), channel_id=1, source_target_pairs={{0,8},{8,16},{16,24},{24,0},{1,9},{9,17},{17,25},{25,1},{2,10},{10... | collective-permute-start | bytes 884744 | tf_op jit(solution)/shard_map/ppermute | solution.py:264
  32.9 20.8 %collective-permute-start.2 = (bf16[96,1536]{1,0:T(8,128)(2,1)S(1)}, bf16[96,1536]{1,0:T(8,128)(2,1)S(1)}, u32[]{:S(2)}, u32[]{:S(2)}) collective-permute-start(bf16[96,1536]{1,0:T(8,128)(2,1)S(1)} %bitcast.37), channel_id=1, source_target_pairs={{0,24},{8,0},{16,8},{24,16},{1,25},{9,1},{17,9},{25,17},{2,26},{10... | collective-permute-start | bytes 884744 | tf_op jit(solution)/shard_map/ppermute | solution.py:264
  37.1 27.1 %all-to-all-start = ((bf16[16,8,1536]{2,1,0:T(8,128)(2,1)}), bf16[16,8,1536]{2,1,0:T(8,128)(2,1)S(1)}, u32[]{:S(2)}, u32[]{:S(2)}) async-start(bf16[16,8,1536]{2,1,0:T(8,128)(2,1)} %pad_maximum_fusion.1), calls=%async_computation | async-start | bytes 786432 | tf_op jit(solution)/shard_map/all_to_all | solution.py:268
  47.2 14.5 %copy-start.16 = (s32[2]{0:T(128)S(1)}, s32[2]{0:T(128)}, u32[]{:S(2)}) copy-start(s32[2]{0:T(128)} %param.11) | copy-start | bytes 28
  47.2 15.8 %copy-start.12 = (f32[768]{0:T(1024)S(1)}, f32[768]{0:T(1024)}, u32[]{:S(2)}) copy-start(f32[768]{0:T(1024)} %param.8) | copy-start | bytes 9220
  47.2 20.2 %collective-permute-start.5 = (bf16[96,1536]{1,0:T(8,128)(2,1)S(1)}, bf16[96,1536]{1,0:T(8,128)(2,1)S(1)}, u32[]{:S(2)}, u32[]{:S(2)}) collective-permute-start(bf16[96,1536]{1,0:T(8,128)(2,1)S(1)} %bitcast.38), channel_id=1, source_target_pairs={{0,8},{8,16},{16,24},{24,0},{1,9},{9,17},{17,25},{25,1},{2,10},{10... | collective-permute-start | bytes 884744 | tf_op jit(solution)/shard_map/ppermute | solution.py:264
  49.2 18.2 %collective-permute-start.6 = (bf16[96,1536]{1,0:T(8,128)(2,1)S(1)}, bf16[96,1536]{1,0:T(8,128)(2,1)S(1)}, u32[]{:S(2)}, u32[]{:S(2)}) collective-permute-start(bf16[96,1536]{1,0:T(8,128)(2,1)S(1)} %bitcast.41), channel_id=1, source_target_pairs={{0,24},{8,0},{16,8},{24,16},{1,25},{9,1},{17,9},{25,17},{2,26},{10... | collective-permute-start | bytes 884744 | tf_op jit(solution)/shard_map/ppermute | solution.py:264
  53.8 0.7 copy-start.8
  54.5 0.7 copy-start.9
  55.2 16.6 %collective-permute-start.3 = (bf16[96,1536]{1,0:T(8,128)(2,1)}, bf16[96,1536]{1,0:T(8,128)(2,1)S(1)}, u32[]{:S(2)}, u32[]{:S(2)}) collective-permute-start(bf16[96,1536]{1,0:T(8,128)(2,1)} %get-tuple-element.20.up_low), channel_id=1, source_target_pairs={{0,8},{8,16},{16,24},{24,0},{1,9},{9,17},{17,25},{25,1},{2,10},{10... | collective-permute-start | bytes 884744 | tf_op jit(solution)/shard_map/ppermute | solution.py:264
  57.1 14.7 %collective-permute-start.4 = (bf16[96,1536]{1,0:T(8,128)(2,1)}, bf16[96,1536]{1,0:T(8,128)(2,1)S(1)}, u32[]{:S(2)}, u32[]{:S(2)}) collective-permute-start(bf16[96,1536]{1,0:T(8,128)(2,1)} %get-tuple-element.21.down_high), channel_id=1, source_target_pairs={{0,24},{8,0},{16,8},{24,16},{1,25},{9,1},{17,9},{25,17},{2,26},{10... | collective-permute-start | bytes 884744 | tf_op jit(solution)/shard_map/ppermute | solution.py:264
  64.3 7.6 %copy-start = (bf16[16,8,1536]{2,1,0:T(8,128)(2,1)}, bf16[16,8,1536]{2,1,0:T(8,128)(2,1)S(1)}, u32[]{:S(2)}) copy-start(bf16[16,8,1536]{2,1,0:T(8,128)(2,1)S(1)} %all-to-all-done) | copy-start | bytes 1179652
  64.3 13.4 %collective-permute-start = (bf16[128,1536]{1,0:T(8,128)(2,1)S(1)}, bf16[128,1536]{1,0:T(8,128)(2,1)S(1)}, u32[]{:S(2)}, u32[]{:S(2)}) collective-permute-start(bf16[128,1536]{1,0:T(8,128)(2,1)S(1)} %bitcast.29), channel_id=1, source_target_pairs={{0,32},{32,0},{1,33},{33,1},{2,34},{34,2},{3,35},{35,3},{4,36},{36... | collective-permute-start | bytes 1179656 | tf_op jit(solution)/shard_map/ppermute | solution.py:264
  67.4 0.7 copy-start.6
  68.1 0.7 copy-start.7
  71.9 0.7 copy-start.13
  71.9 0.8 copy-start.14
  77.6 0.8 copy-start.4
  83.2 8.5 %copy-start.15 = (bf16[384,384]{1,0:T(8,128)(2,1)S(1)}, bf16[384,384]{1,0:T(8,128)(2,1)}, u32[]{:S(2)}) copy-start(bf16[384,384]{1,0:T(8,128)(2,1)} %get-tuple-element.25) | copy-start | bytes 884740
  83.2 3.8 %collective-permute-start.8 = (bf16[384,384]{1,0:T(8,128)(2,1)}, bf16[384,384]{1,0:T(8,128)(2,1)S(1)}, u32[]{:S(2)}, u32[]{:S(2)}) collective-permute-start(bf16[384,384]{1,0:T(8,128)(2,1)} %get-tuple-element.34), channel_id=1, source_target_pairs={{0,32},{32,0},{1,33},{33,1},{2,34},{34,2},{3,35},{35,3},{4,36},{36... | collective-permute-start | bytes 884744 | tf_op jit(solution)/shard_map/ppermute | solution.py:264
  87.8 22.9 %all-to-all-start.2 = ((bf16[32,24,384]{2,1,0:T(8,128)(2,1)}), bf16[32,24,384]{2,1,0:T(8,128)(2,1)S(1)}, u32[]{:S(2)}, u32[]{:S(2)}) async-start(bf16[32,24,384]{2,1,0:T(8,128)(2,1)} %bitcast.34), calls=%async_computation.2 | async-start | bytes 1179648 | tf_op jit(solution)/shard_map/all_to_all | solution.py:268
  91.7 3.5 %collective-permute-start.7 = (bf16[384,384]{1,0:T(8,128)(2,1)S(1)}, bf16[384,384]{1,0:T(8,128)(2,1)S(1)}, u32[]{:S(2)}, u32[]{:S(2)}) collective-permute-start(bf16[384,384]{1,0:T(8,128)(2,1)S(1)} %copy-done.15), channel_id=1, source_target_pairs={{0,32},{32,0},{1,33},{33,1},{2,34},{34,2},{3,35},{35,3},{4,36},{36... | collective-permute-start | bytes 884744 | tf_op jit(solution)/shard_map/ppermute | solution.py:264
  95.1 0.7 copy-start.5
  103.7 3.8 %collective-permute-start.9 = (bf16[128,1536]{1,0:T(8,128)(2,1)}, bf16[128,1536]{1,0:T(8,128)(2,1)S(1)}, u32[]{:S(2)}, u32[]{:S(2)}) collective-permute-start(bf16[128,1536]{1,0:T(8,128)(2,1)} %get-tuple-element.36), channel_id=1, source_target_pairs={{0,32},{32,0},{1,33},{33,1},{2,34},{34,2},{3,35},{35,3},{4,36},{36... | collective-permute-start | bytes 1179656 | tf_op jit(solution)/shard_map/ppermute | solution.py:264
  107.5 0.8 copy-start.3

commit v9 on v7

--- a/solution.py
+++ b/solution.py
@@ -12,7 +12,11 @@
 TM = ("x", "z")
 NEG = -1e30
 VMEM_LIMIT = 56 * 1024 * 1024
-FWD_COST, BWD_COST, END_COST, HALVES_COST = 8_000_000_000, 1000, 1000, 20_000_000_000
+OWN_COST = 8_000_000_000
+NEAR_COST = 8_000_000_000
+STEP_COST = 20_000_000_000
+BWD_COST = 1000
+END_COST = 1000
 
 
 def dot_nn(a, b):
@@ -27,13 +31,20 @@
     return lax.dot_general(a, b, (((0,), (0,)), ((), ())), preferred_element_type=jnp.float32)
 
 
-def low_half(rows):
-    return lax.broadcasted_iota(jnp.int32, (rows, 2 * HD), 1) < HD
+def by_head(pair):
+    low = lax.broadcasted_iota(jnp.int32, pair.shape, 1) < HD
+    zero = jnp.zeros_like(pair)
+    return jnp.concatenate([jnp.where(low, pair, zero), jnp.where(low, zero, pair)])
+
+
+def side_by_side(stacked):
+    half = stacked.shape[0] // 2
+    return jnp.concatenate([stacked[:half], stacked[half:]], axis=1)
 
 
 def same_frame(rows, frames):
-    row_at = lax.broadcasted_iota(jnp.int32, (rows, rows), 0)
-    col_at = lax.broadcasted_iota(jnp.int32, (rows, rows), 1)
+    row_at = lax.broadcasted_iota(jnp.int32, (2 * rows, rows), 0)
+    col_at = lax.broadcasted_iota(jnp.int32, (2 * rows, rows), 1)
     return lax.rem(row_at, frames) == lax.rem(col_at, frames)
 
 
@@ -58,21 +69,17 @@
 
 
 def attend(same, qkv_ref, p_ref, att_ref):
-    rows, mine = att_ref.shape
-    low = low_half(rows)
+    mine = att_ref.shape[1]
     for index, at in enumerate(range(0, mine, 2 * HD)):
         q = qkv_ref[:, at : at + 2 * HD]
         k = qkv_ref[:, mine + at : mine + at + 2 * HD]
         v = qkv_ref[:, 2 * mine + at : 2 * mine + at + 2 * HD]
-        mixed = []
-        for i in range(2):
-            qi = jnp.where(low == (i == 0), q, jnp.zeros_like(q))
-            s = jnp.where(same, dot_nt(qi, k) * HD ** (-0.5), NEG)
-            e = jnp.exp(s - jnp.max(s, axis=-1, keepdims=True))
-            p = e / jnp.sum(e, axis=-1, keepdims=True)
-            p_ref[2 * index + i] = p
-            mixed.append(dot_nn(p.astype(jnp.bfloat16), v))
-        att_ref[:, at : at + 2 * HD] = jnp.where(low, mixed[0], mixed[1]).astype(jnp.bfloat16)
+        s = jnp.where(same, dot_nt(by_head(q), k) * HD ** (-0.5), NEG)
+        e = jnp.exp(s - jnp.max(s, axis=-1, keepdims=True))
+        p = e / jnp.sum(e, axis=-1, keepdims=True)
+        p_ref[index] = p
+        mixed = dot_nn(side_by_side(p.astype(jnp.bfloat16)), by_head(v))
+        att_ref[:, at : at + 2 * HD] = mixed.astype(jnp.bfloat16)
 
 
 def project(rows_ref, gain_ref, w_ref, qkv_ref):
@@ -129,6 +136,7 @@
     gain_ref,
     w_ref,
     own_att_ref,
+    wo_give_ref,
     qkv_ref,
     p_ref,
     att_ref,
@@ -144,7 +152,8 @@
     att = jnp.concatenate([own_att_ref[...], att_ref[...]])
     keep = dot_tn(att, jnp.where(first, low_cols, high_cols))
     gw_ref[pl.ds(pl.multiple_of(core * mid, mid), mid), :] = keep.astype(jnp.bfloat16)
-    give_ref[...] = dot_tn(att, jnp.where(first, high_cols, low_cols)).astype(jnp.bfloat16)
+    give_ref[:mid, :] = dot_tn(att, jnp.where(first, high_cols, low_cols)).astype(jnp.bfloat16)
+    give_ref[mid:, :] = wo_give_ref[...]
 
 
 def bwd_kernel(
@@ -170,43 +179,38 @@
     mine, mid = own_att_ref.shape[1], width // 2
     first = scalars[0] == 0
     att = jnp.concatenate([own_att_ref[...], near_att_ref[...]])
-    kept, got = dot_nn(att, wo_ref[...]), dot_nn(att, got_ref[...])
+    kept, got = dot_nn(att, wo_ref[...]), dot_nn(att, got_ref[mid:, :])
     for at, part in ((0, jnp.where(first, kept, got)), (mid, jnp.where(first, got, kept))):
         sum_ref[:, at : at + mid] = part[:rows]
         other_ref[:, at : at + mid] = part[rows:].astype(jnp.bfloat16)
     gz = masked_grad(frames, scalars, own_ref, near_ref)
     low_cols, high_cols = gz[:, :mid], gz[:, mid:]
     ga_all = dot_nt(jnp.where(first, low_cols, high_cols), wo_ref[...])
-    ga_all += dot_nt(jnp.where(first, high_cols, low_cols), got_ref[...])
+    ga_all += dot_nt(jnp.where(first, high_cols, low_cols), got_ref[mid:, :])
     ga_all = ga_all.astype(jnp.bfloat16)
-    low = low_half(rows)
     sets = ((0, own_qkv_ref, own_p_ref), (rows, near_qkv_ref, near_p_ref))
     for start, qkv_ref, p_ref in sets:
         for index, at in enumerate(range(0, mine, 2 * HD)):
             q = qkv_ref[:, at : at + 2 * HD]
             k = qkv_ref[:, mine + at : mine + at + 2 * HD]
             v = qkv_ref[:, 2 * mine + at : 2 * mine + at + 2 * HD]
-            ga = ga_all[start : start + rows, at : at + 2 * HD]
-            dq, dk, dv = [], [], []
-            for i in range(2):
-                gi = jnp.where(low == (i == 0), ga, jnp.zeros_like(ga))
-                p = p_ref[2 * index + i]
-                gp = dot_nt(gi, v)
-                ds = p * (gp - jnp.sum(p * gp, axis=-1, keepdims=True)) * HD ** (-0.5)
-                ds = ds.astype(jnp.bfloat16)
-                dq.append(dot_nn(ds, k))
-                dk.append(dot_tn(ds, q))
-                dv.append(dot_tn(p.astype(jnp.bfloat16), ga))
+            ga = by_head(ga_all[start : start + rows, at : at + 2 * HD])
+            p = p_ref[index]
+            gp = dot_nt(ga, v)
+            ds = p * (gp - jnp.sum(p * gp, axis=-1, keepdims=True)) * HD ** (-0.5)
+            ds = ds.astype(jnp.bfloat16)
+            dq = dot_nn(side_by_side(ds), by_head(k))
+            dk = dot_tn(ds, by_head(q))
+            dv = dot_tn(p.astype(jnp.bfloat16), ga)
             for j, grad in enumerate((dq, dk, dv)):
-                gqkv_ref[start : start + rows, j * mine + at : j * mine + at + 2 * HD] = jnp.where(
-                    low, grad[0], grad[1]
-                ).astype(jnp.bfloat16)
+                to = j * mine + at
+                gqkv_ref[start : start + rows, to : to + 2 * HD] = grad.astype(jnp.bfloat16)
     gh = dot_nt(gqkv_ref[...], w_ref[...])
     sum_ref[:, width:] = gh[:rows]
     other_ref[:, width:] = gh[rows:].astype(jnp.bfloat16)
 
 
-def end_kernel(frames, scalars, own_ref, gain_ref, sum_ref, got_ref, both_ref):
+def end_kernel(frames, scalars, own_ref, gain_ref, sum_ref, got_ref, term_ref, both_ref):
     rows, width = own_ref.shape[0], own_ref.shape[1] // 2
     valid = valid_rows(rows, frames, scalars[1])
     x = own_ref[:, :width].astype(jnp.float32)
@@ -216,7 +220,14 @@
     inv = inv_rms_of(x)
     inner = jnp.mean(gh * x, axis=-1, keepdims=True)
     gy = own_ref[:, width:].astype(jnp.float32) * valid
-    both_ref[:, width:] = (gy + inv * (gh - x * inv * inv * inner)).astype(jnp.bfloat16)
+    dx = gy + inv * (gh - x * inv * inv * inner)
+    both_ref[:, width : 2 * width] = dx.astype(jnp.bfloat16)
+    term = jnp.sum(term_ref[...].astype(jnp.float32), axis=0)
+    cols = term.shape[1]
+    for i in range(term.shape[0] // frames):
+        part = jnp.tile(term[i * frames : (i + 1) * frames], (rows // frames, 1))
+        to = 2 * width + i * cols
+        both_ref[:, to : to + cols] = part.astype(jnp.bfloat16)
 
 
 def call(kernel, outs, scratch, flops, *operands, behind=()):
@@ -235,25 +246,15 @@
     )(*operands, *behind)
 
 
-def halves(up, down, mid):
-    def kernel(up_ref, down_ref, low_ref, high_ref):
-        low_ref[...] = up_ref[...]
-        high_ref[...] = down_ref[...]
-
-    cols = up.shape[1]
+def step(arrays, *behind):
     return pl.pallas_call(
-        kernel,
-        grid=(1,),
-        out_shape=[jax.ShapeDtypeStruct((mid, cols), up.dtype)] * 2,
-        in_specs=[
-            pl.BlockSpec((mid, cols), lambda i: (0, 0)),
-            pl.BlockSpec((mid, cols), lambda i: (1, 0)),
-        ],
-        out_specs=[pl.BlockSpec((mid, cols), lambda i: (0, 0))] * 2,
-        cost_estimate=pl.CostEstimate(
-            flops=HALVES_COST, bytes_accessed=4 * mid * cols * 2, transcendentals=0
-        ),
-    )(up, down)
+        lambda *refs: None,
+        out_shape=[jax.ShapeDtypeStruct(v.shape, v.dtype) for v in arrays],
+        in_specs=[pl.BlockSpec(memory_space=pl.ANY)] * (len(arrays) + len(behind)),
+        out_specs=[pl.BlockSpec(memory_space=pl.ANY)] * len(arrays),
+        input_output_aliases={i: i for i in range(len(arrays))},
+        cost_estimate=pl.CostEstimate(flops=STEP_COST, bytes_accessed=0, transcendentals=0),
+    )(*arrays, *behind)
 
 
 def shift(v, axis, by):
@@ -280,6 +281,14 @@
     piece, wide = w_qkv.shape
     half, cut = wide // cores, width // cores
 
+    slot_len = frame_dev * tms // SESS
+    start = lax.axis_index(TM) * frame_dev
+    session = start // slot_len
+    left = lengths[session] + session * slot_len - start - y_at * cores * frames
+    scalars = [core_at, left - core_at * frames, left - (1 - core_at) * frames, x_at]
+    scalars = jnp.stack(scalars).astype(jnp.int32)
+    gain = norm_gain.reshape(1, width)
+
     mine = [lax.dynamic_slice(w_qkv, (0, j * width + core_at * cut), (piece, cut)) for j in range(3)]
     mine.append(lax.dynamic_slice(w_out, (0, core_at * cut), (piece, cut)))
     mine = jnp.concatenate(mine, axis=1)
@@ -287,22 +296,14 @@
     block = block.reshape(zs * piece, half + cut)
     up, down = shift(block, "x", 1), shift(block, "x", -1)
     mid = zs * piece // 2
-    far_low, far_high = halves(up, down, mid)
-    far_low, far_high = shift(far_low, "x", 1), shift(far_high, "x", -1)
+    up, down = step((up, down), scalars, gain)
+    far_low, far_high = shift(up[:mid], "x", 1), shift(down[mid:], "x", -1)
 
     both = jnp.concatenate(
         [frames_in.reshape(mics, frames, width), cotangent.reshape(mics, frames, width)], axis=2
     )
     own = exchange(after(both, block), MIC).reshape(rows, 2 * width)
     near = shift(own, "core", 1)
-
-    slot_len = frame_dev * tms // SESS
-    start = lax.axis_index(TM) * frame_dev
-    session = start // slot_len
-    left = lengths[session] + session * slot_len - start - y_at * cores * frames
-    scalars = [core_at, left - core_at * frames, left - (1 - core_at) * frames, x_at]
-    scalars = jnp.stack(scalars).astype(jnp.int32)
-    gain = norm_gain.reshape(1, width)
 
     def shape(dims, dtype):
         return jax.ShapeDtypeStruct(dims, dtype)
@@ -310,52 +311,47 @@
     heads = width // HD // cores
     results = (
         shape((rows, half), bf),
-        shape((heads, rows, rows), f32),
+        shape((heads // 2, 2 * rows, rows), f32),
         shape((rows, cut), bf),
     )
     own_qkv, own_p, own_att, w, wo, wo_give = call(
         lambda *refs: own_kernel(frames, *refs),
         results + (shape((width, half), bf), shape((cut, cut), bf), shape((cut, cut), bf)),
         (pltpu.VMEM((width, cut), bf),),
-        FWD_COST,
+        OWN_COST,
         scalars, own, gain, block, up, down, far_low, far_high,
     )
-    wo_got = shift(wo_give, "core", 1)
     near_qkv, near_p, near_att, give, gw = call(
         lambda *refs: near_kernel(frames, *refs),
-        results + (shape((cut, cut), bf), shape((width, cut), bf)),
+        results + (shape((width, cut), bf), shape((width, cut), bf)),
         (),
-        FWD_COST,
-        scalars, own, near, gain, w, own_att,
+        NEAR_COST,
+        scalars, own, near, gain, w, own_att, wo_give,
     )
 
     got = shift(give, "core", 1)
-    term = lax.dynamic_update_slice(gw, got, ((1 - core_at) * cut, 0))
+    term = lax.dynamic_update_slice(gw, got[:cut], ((1 - core_at) * cut, 0))
 
     sum_part, other_part = call(
         lambda *refs: bwd_kernel(frames, *refs),
         (shape((rows, 2 * width), f32), shape((rows, 2 * width), bf)),
         (pltpu.VMEM((2 * rows, half), bf),),
         BWD_COST,
-        scalars, own, near, wo, wo_got, own_att, near_att, own_qkv, near_qkv, own_p, near_p, w,
+        scalars, own, near, wo, got, own_att, near_att, own_qkv, near_qkv, own_p, near_p, w,
         behind=(term,),
     )
     term = exchange(term.reshape(tms, piece, cut), TM)
-    term = jnp.sum(term.astype(f32), axis=0).astype(bf)
     got_part = shift(other_part, "core", 1)
+    low = piece // frames
     (done,) = call(
         lambda *refs: end_kernel(frames, *refs),
-        (shape((rows, 2 * width), bf),),
+        (shape((rows, 2 * width + low * cut), bf),),
         (),
         END_COST,
-        scalars, own, gain, sum_part, got_part,
-    )
-
-    low = piece // frames
-    term = term.reshape(low, frames, cut).transpose(1, 0, 2).reshape(frames, low * cut)
-    term = jnp.broadcast_to(term[None], (mics, frames, low * cut))
-    sent = jnp.concatenate([done.reshape(mics, frames, 2 * width), term], axis=2)
-    sent = exchange(sent, MIC)
+        scalars, own, gain, sum_part, got_part, term,
+    )
+
+    sent = exchange(done.reshape(mics, frames, 2 * width + low * cut), MIC)
     out = sent[:, :, :width].reshape(1, frame_dev, width)
     dx = sent[:, :, width : 2 * width].reshape(1, frame_dev, width)
     term = jnp.sum(sent[:, :, 2 * width :].astype(f32).reshape(ys, cores, frames, low, cut), axis=0)

time: 140 us -> 141 us (level)
  waiting for transfers between devices: 7.24 us -> 16.1 us
  starting transfers between devices: 41 us -> 34.1 us
  Pallas kernels: 21.6 us -> 17.7 us
  blocking collectives: 56.2 us -> 58.9 us
  local copies, waits for them, and re-layouts: 8.77 us -> 10.2 us
    all_to_all x2, waiting for transfers between devices: 0.1 us -> 9.29 us  [exchange(): return lax.all_to_all(v, axes, split_axis=0, concat_axis=0, tiled=True)]
    ppermute x8 -> x7, starting transfers between devices: 25.6 us -> 20.4 us  [shift(): return lax.ppermute(v, axis, [(i, (i + by) % size) for i in range(size)])]
    all_to_all x2, blocking collectives: 56.2 us -> 58.9 us  [exchange(): return lax.all_to_all(v, axes, split_axis=0, concat_axis=0, tiled=True)]
    pallas_call x4, Pallas kernels: 19.7 us -> 17.7 us  [call(): pl.pallas_call(kernel, out_shape=outs, in_specs=[pl.BlockSpec(memory_spac...]
    slice x0 -> x2, local copies, waits for them, and re-layouts: none -> 1.96 us  [per_device(): far_low, far_high = (shift(up[:mid], 'x', 1), shift(down[mid:], 'x', -1))]
    pallas_call x1, Pallas kernels: 1.89 us -> 0.01 us  [step(): pl.pallas_call(lambda *refs: None, out_shape=[jax.ShapeDtypeStruct(v.shap...]
    all_to_all x2, starting transfers between devices: 15.4 us -> 13.7 us  [exchange(): return lax.all_to_all(v, axes, split_axis=0, concat_axis=0, tiled=True)]
    ppermute x8 -> x7, waiting for transfers between devices: 7.14 us -> 6.85 us  [shift(): return lax.ppermute(v, axis, [(i, (i + by) % size) for i in range(size)])]
  transfers between devices with their start and end apart: 10 -> 9, of which waited for: 5 -> 6; matrix products, arithmetic and copies ran while one was open for 2% -> 3% of each run, Pallas kernels for 12% -> 8%
where the time goes in v9:
time: 141 us; the launch traced here: 140 us
  blocking collectives  58.9 us (42%)
  starting transfers between devices  34.1 us (24%)
  Pallas kernels  17.7 us (13%)
  waiting for transfers between devices  16.1 us (11%)
  local copies, waits for them, and re-layouts  10.2 us (7%)
  between operations  1.55 us (1%)
  other arithmetic  1.5 us (1%)
    all_to_all x2, blocking collectives, exchange(): return lax.all_to_all(v, axes, split_axis=0, concat_axis=0, tiled=True)  58.9 us
    ppermute x7, starting transfers between devices, shift(): return lax.ppermute(v, axis, [(i, (i + by) % size) for i in range(size)])  20.4 us
    pallas_call x4, Pallas kernels, call(): pl.pallas_call(kernel, out_shape=outs, in_specs=[pl.BlockSpec(memory_spac...  17.7 us
    all_to_all x2, starting transfers between devices, exchange(): return lax.all_to_all(v, axes, split_axis=0, concat_axis=0, tiled=True)  13.7 us
    all_to_all x2, waiting for transfers between devices, exchange(): return lax.all_to_all(v, axes, split_axis=0, concat_axis=0, tiled=True)  9.29 us
    ppermute x7, waiting for transfers between devices, shift(): return lax.ppermute(v, axis, [(i, (i + by) % size) for i in range(size)])  6.85 us
    unnamed x29, local copies, waits for them, and re-layouts  4.49 us
  transfers between devices with their start and end apart: 9, of which 6 were waited for; matrix products, arithmetic and copies ran while one was open for 3% of the time, Pallas kernels for 8%

profile of v9, /device:TPU:1, one launch (start us, length us, event | category | flops | bytes accessed | tf_op | source)
XLA Modules:
  0.0 140.1 jit_solution(16388889907183044365)
XLA Ops:
  0.7 0.9 constant_dynamic-slice_fusion.3
  1.6 28.1 %all_to_all.20 = bf16[8,24,1536]{2,1,0:T(8,128)(2,1)S(1)} all-to-all(bf16[8,24,1536]{2,1,0:T(8,128)(2,1)S(1)} %broadcast_in_dim.2), channel_id=1, replica_groups=mesh['y'=8,'core'=2,'x'=4,'z'=8] {'z'}, dimensions={0} | all-to-all | bytes 1179648 | tf_op jit(solution)/shard_map/all_to_all | solution.py:266
  29.7 4.4 %collective-permute-start.2 = (bf16[192,1536]{1,0:T(8,128)(2,1)S(1)}, bf16[192,1536]{1,0:T(8,128)(2,1)S(1)}, u32[]{:S(2)}, u32[]{:S(2)}) collective-permute-start(bf16[192,1536]{1,0:T(8,128)(2,1)S(1)} %bitcast.31), channel_id=1, source_target_pairs={{0,24},{8,0},{16,8},{24,16},{1,25},{9,1},{17,9},{25,17},{2,26},{10... | collective-permute-start | bytes 1769480 | tf_op jit(solution)/shard_map/ppermute | solution.py:262
  34.1 1.9 %collective-permute-start.1 = (bf16[192,1536]{1,0:T(8,128)(2,1)S(1)}, bf16[192,1536]{1,0:T(8,128)(2,1)S(1)}, u32[]{:S(2)}, u32[]{:S(2)}) collective-permute-start(bf16[192,1536]{1,0:T(8,128)(2,1)S(1)} %bitcast.32), channel_id=1, source_target_pairs={{0,8},{8,16},{16,24},{24,0},{1,9},{9,17},{17,25},{25,1},{2,10},{10... | collective-permute-start | bytes 1769480 | tf_op jit(solution)/shard_map/ppermute | solution.py:262
  37.9 0.7 pad_add_fusion.refs_2_.refs_0_
  38.6 0.8 pad_maximum_fusion
  39.4 9.8 %all-to-all-start.1 = ((bf16[16,8,1536]{2,1,0:T(8,128)(2,1)}), bf16[16,8,1536]{2,1,0:T(8,128)(2,1)S(1)}, u32[]{:S(2)}, u32[]{:S(2)}) async-start(bf16[16,8,1536]{2,1,0:T(8,128)(2,1)} %pad_maximum_fusion), calls=%async_computation.1 | async-start | bytes 786432 | tf_op jit(solution)/shard_map/all_to_all | solution.py:266
  49.3 0.7 copy-done.8
  50.0 0.8 copy-done.9
  50.8 1.0 slice.18
  51.8 1.0 slice.19
  52.8 4.9 %collective-permute-start.4 = (bf16[96,1536]{1,0:T(8,128)(2,1)S(1)}, bf16[96,1536]{1,0:T(8,128)(2,1)S(1)}, u32[]{:S(2)}, u32[]{:S(2)}) collective-permute-start(bf16[96,1536]{1,0:T(8,128)(2,1)S(1)} %slice.19), channel_id=1, source_target_pairs={{0,24},{8,0},{16,8},{24,16},{1,25},{9,1},{17,9},{25,17},{2,26},{10... | collective-permute-start | bytes 884744 | tf_op jit(solution)/shard_map/ppermute | solution.py:262
  57.7 1.9 %collective-permute-start.3 = (bf16[96,1536]{1,0:T(8,128)(2,1)S(1)}, bf16[96,1536]{1,0:T(8,128)(2,1)S(1)}, u32[]{:S(2)}, u32[]{:S(2)}) collective-permute-start(bf16[96,1536]{1,0:T(8,128)(2,1)S(1)} %slice.18), channel_id=1, source_target_pairs={{0,8},{8,16},{16,24},{24,0},{1,9},{9,17},{17,25},{25,1},{2,10},{10... | collective-permute-start | bytes 884744 | tf_op jit(solution)/shard_map/ppermute | solution.py:262
  59.6 4.1 %all-to-all-done.1 = bf16[16,8,1536]{2,1,0:T(8,128)(2,1)S(1)} async-done(((bf16[16,8,1536]{2,1,0:T(8,128)(2,1)}), bf16[16,8,1536]{2,1,0:T(8,128)(2,1)S(1)}, u32[]{:S(2)}, u32[]{:S(2)}) %all-to-all-start.1) | async-done | bytes 393248 | tf_op jit(solution)/shard_map/all_to_all | solution.py:266
  63.7 1.9 %collective-permute-start = (bf16[128,1536]{1,0:T(8,128)(2,1)S(1)}, bf16[128,1536]{1,0:T(8,128)(2,1)S(1)}, u32[]{:S(2)}, u32[]{:S(2)}) collective-permute-start(bf16[128,1536]{1,0:T(8,128)(2,1)S(1)} %bitcast.23), channel_id=1, source_target_pairs={{0,32},{32,0},{1,33},{33,1},{2,34},{34,2},{3,35},{35,3},{4,36},{36... | collective-permute-start | bytes 1179656 | tf_op jit(solution)/shard_map/ppermute | solution.py:262
  65.7 3.4 %collective-permute-done.3.refs_6_ = bf16[96,1536]{1,0:T(8,128)(2,1)S(1)} collective-permute-done((bf16[96,1536]{1,0:T(8,128)(2,1)S(1)}, bf16[96,1536]{1,0:T(8,128)(2,1)S(1)}, u32[]{:S(2)}, u32[]{:S(2)}) %collective-permute-start.3) | collective-permute-done | bytes 294944 | tf_op jit(solution)/shard_map/ppermute | solution.py:262
  69.0 0.7 copy-done.12
  69.7 3.9 %shard_map.86 = (bf16[128,1152]{1,0:T(8,128)(2,1)}, f32[3,256,128]{2,1,0:T(8,128)}, bf16[128,384]{1,0:T(8,128)(2,1)}, bf16[768,1152]{1,0:T(8,128)(2,1)}, bf16[38...) custom-call(s32[4]{0:T(128)} %pad_add_fusion.refs_2_.refs_0_, bf16[128,1536]{1,0:T(8,128)(2,1)} %bitcast.24, ...), custom_call_target="tpu_custom_call" | custom-call | flops 8000000000 | bytes 5901328 | tf_op jit(solution)/shard_map/pallas_call | solution.py:235
  73.6 0.7 copy-done.4
  74.4 4.2 %shard_map.87 = (bf16[128,1152]{1,0:T(8,128)(2,1)}, f32[3,256,128]{2,1,0:T(8,128)}, bf16[128,384]{1,0:T(8,128)(2,1)}, bf16[768,384]{1,0:T(8,128)(2,1)}, bf16[768,384]{1,0:T(8,128)(2,1)}) custom-call(s32[4]{0:T(128)} %pad_add_fusion.refs_2_.refs_0_, bf16[128,1536]{1,0:T(8,128)(2,1)} %bitcast.25, bf16[128,1536]{1,0:T(8,128)(2,1)} %copy-done.4, ...), custom_call_target="tpu_custom_call" | custom-call | flops 8000000000 | bytes 4918288 | tf_op jit(solution)/shard_map/pallas_call | solution.py:235
  78.6 3.1 %collective-permute-start.5 = (bf16[768,384]{1,0:T(8,128)(2,1)}, bf16[768,384]{1,0:T(8,128)(2,1)S(1)}, u32[]{:S(2)}, u32[]{:S(2)}) collective-permute-start(bf16[768,384]{1,0:T(8,128)(2,1)} %get-tuple-element.26), channel_id=1, source_target_pairs={{0,32},{32,0},{1,33},{33,1},{2,34},{34,2},{3,35},{35,3},{4,36},{36... | collective-permute-start | bytes 1769480 | tf_op jit(solution)/shard_map/ppermute | solution.py:262
  81.7 1.8 %collective-permute-done.5.refs_4_ = bf16[768,384]{1,0:T(8,128)(2,1)S(1)} collective-permute-done((bf16[768,384]{1,0:T(8,128)(2,1)}, bf16[768,384]{1,0:T(8,128)(2,1)S(1)}, u32[]{:S(2)}, u32[]{:S(2)}) %collective-permute-start.5) | collective-permute-done | bytes 589856 | tf_op jit(solution)/shard_map/ppermute | solution.py:262
  83.5 0.8 slice_dynamic-update-slice_fusion.refs_12_
  84.3 3.9 %all-to-all-start.2 = ((bf16[32,24,384]{2,1,0:T(8,128)(2,1)}), bf16[32,24,384]{2,1,0:T(8,128)(2,1)S(1)}, u32[]{:S(2)}, u32[]{:S(2)}) async-start(bf16[32,24,384]{2,1,0:T(8,128)(2,1)} %bitcast.29), calls=%async_computation.2 | async-start | bytes 1179648 | tf_op jit(solution)/shard_map/all_to_all | solution.py:266
  88.2 6.8 %shard_map.88 = (f32[128,1536]{1,0:T(8,128)}, bf16[128,1536]{1,0:T(8,128)(2,1)}) custom-call(s32[4]{0:T(128)} %pad_add_fusion.refs_2_.refs_0_, bf16[128,1536]{1,0:T(8,128)(2,1)} %bitcast.26, bf16[128,1536]{1,0:T(8,128)(2,1)} %copy-done.4, bf16[384,384]{1,0:T(8,128)(2,1)} %get-tuple-element.22.refs_3_, bf16[768,384]{1,0:T(8,128)(2,1)} %copy-done.2, ...), custom_call_target="tpu_custom_call" | custom-call | flops 1000 | bytes 6193168 | tf_op jit(solution)/shard_map/pallas_call | solution.py:235
  95.0 2.3 %collective-permute-start.6 = (bf16[128,1536]{1,0:T(8,128)(2,1)}, bf16[128,1536]{1,0:T(8,128)(2,1)S(1)}, u32[]{:S(2)}, u32[]{:S(2)}) collective-permute-start(bf16[128,1536]{1,0:T(8,128)(2,1)} %get-tuple-element.34), channel_id=1, source_target_pairs={{0,32},{32,0},{1,33},{33,1},{2,34},{34,2},{3,35},{35,3},{4,36},{36... | collective-permute-start | bytes 1179656 | tf_op jit(solution)/shard_map/ppermute | solution.py:262
  97.3 1.5 %collective-permute-done.6.refs_4_ = bf16[128,1536]{1,0:T(8,128)(2,1)S(1)} collective-permute-done((bf16[128,1536]{1,0:T(8,128)(2,1)}, bf16[128,1536]{1,0:T(8,128)(2,1)S(1)}, u32[]{:S(2)}, u32[]{:S(2)}) %collective-permute-start.6) | collective-permute-done | bytes 393248 | tf_op jit(solution)/shard_map/ppermute | solution.py:262
  98.8 5.2 %all-to-all-done.2.refs_5_ = bf16[32,24,384]{2,1,0:T(8,128)(2,1)S(1)} async-done(((bf16[32,24,384]{2,1,0:T(8,128)(2,1)}), bf16[32,24,384]{2,1,0:T(8,128)(2,1)S(1)}, u32[]{:S(2)}, u32[]{:S(2)}) %all-to-all-start.2) | async-done | bytes 589856 | tf_op jit(solution)/shard_map/all_to_all | solution.py:266
  104.0 0.9 copy-done.1
  104.9 2.8 %shard_map.89 = bf16[128,2688]{1,0:T(8,128)(2,1)} custom-call(s32[4]{0:T(128)} %pad_add_fusion.refs_2_.refs_0_, bf16[128,1536]{1,0:T(8,128)(2,1)} %bitcast.27, f32[1,768]{1,0:T(1,128)} %reshape.47.refs_3_.refs_2_, f32[128,1536]{1,0:T(8,128)} %get-tuple-element.33.refs_3_, bf16[128,1536]{1,0:T(8,128)(2,1)} %copy-done.5, bf16[32,24,384]{2,1,0:T(8,128)(2,1)} %copy-done.1), custom_call_target="tpu_custom_call" | custom-call | flops 1000 | bytes 2853904 | tf_op jit(solution)/shard_map/pallas_call | solution.py:235
  107.7 30.8 %all_to_all.21 = bf16[16,8,2688]{2,1,0:T(8,128)(2,1)S(1)} all-to-all(bf16[16,8,2688]{2,1,0:T(8,128)(2,1)} %bitcast.28), channel_id=1, replica_groups=mesh['y'=8,'core'=2,'x'=4,'z'=8] {'y','core'}, dimensions={0} | all-to-all | bytes 1376256 | tf_op jit(solution)/shard_map/all_to_all | solution.py:266
  139.3 0.8 slice_bitcast_fusion
  (36 shorter events, 2.1 us)
Async XLA Ops:
  0.6 35.4 %copy-start.13 = (s32[2]{0:T(128)S(1)}, s32[2]{0:T(128)}, u32[]{:S(2)}) copy-start(s32[2]{0:T(128)} %param.11) | copy-start | bytes 28
  0.6 36.7 %copy-start.10 = (f32[768]{0:T(1024)S(1)}, f32[768]{0:T(1024)}, u32[]{:S(2)}) copy-start(f32[768]{0:T(1024)} %param.8) | copy-start | bytes 9220
  0.7 37.9 %copy-start.6 = (bf16[1,128,768]{2,1,0:T(8,128)(2,1)S(1)}, bf16[1,128,768]{2,1,0:T(8,128)(2,1)}, u32[]{:S(2)}) copy-start(bf16[1,128,768]{2,1,0:T(8,128)(2,1)} %param.7) | copy-start | bytes 589828
  0.7 37.9 %copy-start.7 = (bf16[1,128,768]{2,1,0:T(8,128)(2,1)S(1)}, bf16[1,128,768]{2,1,0:T(8,128)(2,1)}, u32[]{:S(2)}) copy-start(bf16[1,128,768]{2,1,0:T(8,128)(2,1)} %param.6) | copy-start | bytes 589828
  29.7 21.1 %copy-start.3 = (bf16[8,24,1536]{2,1,0:T(8,128)(2,1)}, bf16[8,24,1536]{2,1,0:T(8,128)(2,1)S(1)}, u32[]{:S(2)}) copy-start(bf16[8,24,1536]{2,1,0:T(8,128)(2,1)S(1)} %all_to_all.20) | copy-start | bytes 1769476
  29.7 19.5 %collective-permute-start.2 = (bf16[192,1536]{1,0:T(8,128)(2,1)S(1)}, bf16[192,1536]{1,0:T(8,128)(2,1)S(1)}, u32[]{:S(2)}, u32[]{:S(2)}) collective-permute-start(bf16[192,1536]{1,0:T(8,128)(2,1)S(1)} %bitcast.31), channel_id=1, source_target_pairs={{0,24},{8,0},{16,8},{24,16},{1,25},{9,1},{17,9},{25,17},{2,26},{10... | collective-permute-start | bytes 1769480 | tf_op jit(solution)/shard_map/ppermute | solution.py:262
  34.1 15.2 %collective-permute-start.1 = (bf16[192,1536]{1,0:T(8,128)(2,1)S(1)}, bf16[192,1536]{1,0:T(8,128)(2,1)S(1)}, u32[]{:S(2)}, u32[]{:S(2)}) collective-permute-start(bf16[192,1536]{1,0:T(8,128)(2,1)S(1)} %bitcast.32), channel_id=1, source_target_pairs={{0,8},{8,16},{16,24},{24,0},{1,9},{9,17},{17,25},{25,1},{2,10},{10... | collective-permute-start | bytes 1769480 | tf_op jit(solution)/shard_map/ppermute | solution.py:262
  39.4 24.4 %all-to-all-start.1 = ((bf16[16,8,1536]{2,1,0:T(8,128)(2,1)}), bf16[16,8,1536]{2,1,0:T(8,128)(2,1)S(1)}, u32[]{:S(2)}, u32[]{:S(2)}) async-start(bf16[16,8,1536]{2,1,0:T(8,128)(2,1)} %pad_maximum_fusion), calls=%async_computation.1 | async-start | bytes 786432 | tf_op jit(solution)/shard_map/all_to_all | solution.py:266
  49.2 0.8 copy-start.8
  50.0 0.8 copy-start.9
  52.8 12.8 %collective-permute-start.4 = (bf16[96,1536]{1,0:T(8,128)(2,1)S(1)}, bf16[96,1536]{1,0:T(8,128)(2,1)S(1)}, u32[]{:S(2)}, u32[]{:S(2)}) collective-permute-start(bf16[96,1536]{1,0:T(8,128)(2,1)S(1)} %slice.19), channel_id=1, source_target_pairs={{0,24},{8,0},{16,8},{24,16},{1,25},{9,1},{17,9},{25,17},{2,26},{10... | collective-permute-start | bytes 884744 | tf_op jit(solution)/shard_map/ppermute | solution.py:262
  57.7 11.3 %collective-permute-start.3 = (bf16[96,1536]{1,0:T(8,128)(2,1)S(1)}, bf16[96,1536]{1,0:T(8,128)(2,1)S(1)}, u32[]{:S(2)}, u32[]{:S(2)}) collective-permute-start(bf16[96,1536]{1,0:T(8,128)(2,1)S(1)} %slice.18), channel_id=1, source_target_pairs={{0,8},{8,16},{16,24},{24,0},{1,9},{9,17},{17,25},{25,1},{2,10},{10... | collective-permute-start | bytes 884744 | tf_op jit(solution)/shard_map/ppermute | solution.py:262
  63.7 5.3 %copy-start = (bf16[16,8,1536]{2,1,0:T(8,128)(2,1)}, bf16[16,8,1536]{2,1,0:T(8,128)(2,1)S(1)}, u32[]{:S(2)}) copy-start(bf16[16,8,1536]{2,1,0:T(8,128)(2,1)S(1)} %all-to-all-done.1) | copy-start | bytes 1179652
  63.7 9.9 %collective-permute-start = (bf16[128,1536]{1,0:T(8,128)(2,1)S(1)}, bf16[128,1536]{1,0:T(8,128)(2,1)S(1)}, u32[]{:S(2)}, u32[]{:S(2)}) collective-permute-start(bf16[128,1536]{1,0:T(8,128)(2,1)S(1)} %bitcast.23), channel_id=1, source_target_pairs={{0,32},{32,0},{1,33},{33,1},{2,34},{34,2},{3,35},{35,3},{4,36},{36... | collective-permute-start | bytes 1179656 | tf_op jit(solution)/shard_map/ppermute | solution.py:262
  65.6 3.4 %copy-start.11 = (bf16[96,1536]{1,0:T(8,128)(2,1)}, bf16[96,1536]{1,0:T(8,128)(2,1)S(1)}, u32[]{:S(2)}) copy-start(bf16[96,1536]{1,0:T(8,128)(2,1)S(1)} %collective-permute-done.4.refs_7_) | copy-start | bytes 884740
  69.0 0.7 copy-start.12
  73.6 0.7 copy-start.4
  78.6 4.9 %collective-permute-start.5 = (bf16[768,384]{1,0:T(8,128)(2,1)}, bf16[768,384]{1,0:T(8,128)(2,1)S(1)}, u32[]{:S(2)}, u32[]{:S(2)}) collective-permute-start(bf16[768,384]{1,0:T(8,128)(2,1)} %get-tuple-element.26), channel_id=1, source_target_pairs={{0,32},{32,0},{1,33},{33,1},{2,34},{34,2},{3,35},{35,3},{4,36},{36... | collective-permute-start | bytes 1769480 | tf_op jit(solution)/shard_map/ppermute | solution.py:262
  83.5 4.7 %copy-start.2 = (bf16[768,384]{1,0:T(8,128)(2,1)}, bf16[768,384]{1,0:T(8,128)(2,1)S(1)}, u32[]{:S(2)}) copy-start(bf16[768,384]{1,0:T(8,128)(2,1)S(1)} %collective-permute-done.5.refs_4_) | copy-start | bytes 1769476
  84.3 19.7 %all-to-all-start.2 = ((bf16[32,24,384]{2,1,0:T(8,128)(2,1)}), bf16[32,24,384]{2,1,0:T(8,128)(2,1)S(1)}, u32[]{:S(2)}, u32[]{:S(2)}) async-start(bf16[32,24,384]{2,1,0:T(8,128)(2,1)} %bitcast.29), calls=%async_computation.2 | async-start | bytes 1179648 | tf_op jit(solution)/shard_map/all_to_all | solution.py:266
  95.0 3.8 %collective-permute-start.6 = (bf16[128,1536]{1,0:T(8,128)(2,1)}, bf16[128,1536]{1,0:T(8,128)(2,1)S(1)}, u32[]{:S(2)}, u32[]{:S(2)}) collective-permute-start(bf16[128,1536]{1,0:T(8,128)(2,1)} %get-tuple-element.34), channel_id=1, source_target_pairs={{0,32},{32,0},{1,33},{33,1},{2,34},{34,2},{3,35},{35,3},{4,36},{36... | collective-permute-start | bytes 1179656 | tf_op jit(solution)/shard_map/ppermute | solution.py:262
  98.8 5.2 %copy-start.5 = (bf16[128,1536]{1,0:T(8,128)(2,1)}, bf16[128,1536]{1,0:T(8,128)(2,1)S(1)}, u32[]{:S(2)}) copy-start(bf16[128,1536]{1,0:T(8,128)(2,1)S(1)} %collective-permute-done.6.refs_4_) | copy-start | bytes 1179652
  104.0 0.9 copy-start.1

commit v10 on v9

--- a/solution.py
+++ b/solution.py
@@ -14,7 +14,6 @@
 VMEM_LIMIT = 56 * 1024 * 1024
 OWN_COST = 8_000_000_000
 NEAR_COST = 8_000_000_000
-STEP_COST = 20_000_000_000
 BWD_COST = 1000
 END_COST = 1000
 
@@ -48,20 +47,24 @@
     return lax.rem(row_at, frames) == lax.rem(col_at, frames)
 
 
-def valid_rows(rows, frames, left):
+def valid_rows(rows, frames, slot_len, lengths, other):
+    start = (lax.axis_index("x") * lax.axis_size("z") + lax.axis_index("z")) * lax.axis_size("y")
+    core = lax.axis_index("core")
+    core = 1 - core if other else core
+    start = ((start + lax.axis_index("y")) * lax.axis_size("core") + core) * frames
+    session = start // slot_len
+    left = lengths[session] + session * slot_len - start
     frame = lax.rem(lax.broadcasted_iota(jnp.int32, (rows, 1), 0), frames)
     return (frame < left).astype(jnp.float32)
 
 
-def masked_grad(frames, scalars, own_ref, near_ref):
+def masked_grad(frames, slot_len, lengths, own_ref, near_ref):
     rows, width = own_ref.shape[0], own_ref.shape[1] // 2
     parts = [
-        (ref[:, width:].astype(jnp.float32) * valid_rows(rows, frames, scalars[1 + i])).astype(
-            jnp.bfloat16
-        )
-        for i, ref in enumerate((own_ref, near_ref))
+        ref[:, width:].astype(jnp.float32) * valid_rows(rows, frames, slot_len, lengths, other)
+        for other, ref in ((False, own_ref), (True, near_ref))
     ]
-    return jnp.concatenate(parts)
+    return jnp.concatenate(parts).astype(jnp.bfloat16)
 
 
 def inv_rms_of(x):
@@ -84,13 +87,14 @@
 
 def project(rows_ref, gain_ref, w_ref, qkv_ref):
     x = rows_ref[:, : w_ref.shape[0]].astype(jnp.float32)
-    normed = (x * inv_rms_of(x) * gain_ref[...]).astype(jnp.bfloat16)
+    normed = (x * inv_rms_of(x) * gain_ref[...].reshape(1, -1)).astype(jnp.bfloat16)
     qkv_ref[...] = dot_nn(normed, w_ref[...]).astype(jnp.bfloat16)
 
 
 def own_kernel(
     frames,
-    scalars,
+    slot_len,
+    lengths,
     own_ref,
     gain_ref,
     block_ref,
@@ -108,7 +112,7 @@
 ):
     rows, mine = att_ref.shape
     width, deep = w_ref.shape[0], block_ref.shape[0]
-    core, x_at = scalars[0], scalars[3]
+    core, x_at = lax.axis_index("core"), lax.axis_index("x")
     far = lax.rem(x_at + 2, XS) * deep
     places = (
         (block_ref, x_at * deep),
@@ -130,7 +134,8 @@
 
 def near_kernel(
     frames,
-    scalars,
+    slot_len,
+    lengths,
     own_ref,
     near_ref,
     gain_ref,
@@ -145,9 +150,9 @@
 ):
     project(near_ref, gain_ref, w_ref, qkv_ref)
     attend(same_frame(att_ref.shape[0], frames), qkv_ref, p_ref, att_ref)
-    core, mid = scalars[0], w_ref.shape[0] // 2
+    core, mid = lax.axis_index("core"), w_ref.shape[0] // 2
     first = core == 0
-    gz = masked_grad(frames, scalars, own_ref, near_ref)
+    gz = masked_grad(frames, slot_len, lengths, own_ref, near_ref)
     low_cols, high_cols = gz[:, :mid], gz[:, mid:]
     att = jnp.concatenate([own_att_ref[...], att_ref[...]])
     keep = dot_tn(att, jnp.where(first, low_cols, high_cols))
@@ -158,7 +163,8 @@
 
 def bwd_kernel(
     frames,
-    scalars,
+    slot_len,
+    lengths,
     own_ref,
     near_ref,
     wo_ref,
@@ -177,13 +183,13 @@
 ):
     rows, width = own_ref.shape[0], own_ref.shape[1] // 2
     mine, mid = own_att_ref.shape[1], width // 2
-    first = scalars[0] == 0
+    first = lax.axis_index("core") == 0
     att = jnp.concatenate([own_att_ref[...], near_att_ref[...]])
     kept, got = dot_nn(att, wo_ref[...]), dot_nn(att, got_ref[mid:, :])
     for at, part in ((0, jnp.where(first, kept, got)), (mid, jnp.where(first, got, kept))):
         sum_ref[:, at : at + mid] = part[:rows]
         other_ref[:, at : at + mid] = part[rows:].astype(jnp.bfloat16)
-    gz = masked_grad(frames, scalars, own_ref, near_ref)
+    gz = masked_grad(frames, slot_len, lengths, own_ref, near_ref)
     low_cols, high_cols = gz[:, :mid], gz[:, mid:]
     ga_all = dot_nt(jnp.where(first, low_cols, high_cols), wo_ref[...])
     ga_all += dot_nt(jnp.where(first, high_cols, low_cols), got_ref[mid:, :])
@@ -210,24 +216,18 @@
     other_ref[:, width:] = gh[rows:].astype(jnp.bfloat16)
 
 
-def end_kernel(frames, scalars, own_ref, gain_ref, sum_ref, got_ref, term_ref, both_ref):
+def end_kernel(frames, slot_len, lengths, own_ref, gain_ref, sum_ref, got_ref, both_ref):
     rows, width = own_ref.shape[0], own_ref.shape[1] // 2
-    valid = valid_rows(rows, frames, scalars[1])
+    valid = valid_rows(rows, frames, slot_len, lengths, False)
     x = own_ref[:, :width].astype(jnp.float32)
     mixed = sum_ref[:, :width] + got_ref[:, :width].astype(jnp.float32)
     both_ref[:, :width] = (valid * (x + mixed)).astype(jnp.bfloat16)
-    gh = (sum_ref[:, width:] + got_ref[:, width:].astype(jnp.float32)) * gain_ref[...]
+    gh = (sum_ref[:, width:] + got_ref[:, width:].astype(jnp.float32)) * gain_ref[...].reshape(1, -1)
     inv = inv_rms_of(x)
     inner = jnp.mean(gh * x, axis=-1, keepdims=True)
     gy = own_ref[:, width:].astype(jnp.float32) * valid
     dx = gy + inv * (gh - x * inv * inv * inner)
-    both_ref[:, width : 2 * width] = dx.astype(jnp.bfloat16)
-    term = jnp.sum(term_ref[...].astype(jnp.float32), axis=0)
-    cols = term.shape[1]
-    for i in range(term.shape[0] // frames):
-        part = jnp.tile(term[i * frames : (i + 1) * frames], (rows // frames, 1))
-        to = 2 * width + i * cols
-        both_ref[:, to : to + cols] = part.astype(jnp.bfloat16)
+    both_ref[:, width:] = dx.astype(jnp.bfloat16)
 
 
 def call(kernel, outs, scratch, flops, *operands, behind=()):
@@ -246,17 +246,6 @@
     )(*operands, *behind)
 
 
-def step(arrays, *behind):
-    return pl.pallas_call(
-        lambda *refs: None,
-        out_shape=[jax.ShapeDtypeStruct(v.shape, v.dtype) for v in arrays],
-        in_specs=[pl.BlockSpec(memory_space=pl.ANY)] * (len(arrays) + len(behind)),
-        out_specs=[pl.BlockSpec(memory_space=pl.ANY)] * len(arrays),
-        input_output_aliases={i: i for i in range(len(arrays))},
-        cost_estimate=pl.CostEstimate(flops=STEP_COST, bytes_accessed=0, transcendentals=0),
-    )(*arrays, *behind)
-
-
 def shift(v, axis, by):
     size = lax.axis_size(axis)
     return lax.ppermute(v, axis, [(i, (i + by) % size) for i in range(size)])
@@ -272,7 +261,7 @@
 
 def per_device(frames_in, cotangent, norm_gain, w_qkv, w_out, lengths):
     bf, f32 = jnp.bfloat16, jnp.float32
-    y_at, core_at, x_at = (lax.axis_index(axis) for axis in ("y", "core", "x"))
+    core_at = lax.axis_index("core")
     ys, cores, zs = (lax.axis_size(axis) for axis in ("y", "core", "z"))
     tms, mics = XS * zs, ys * cores
     frame_dev, width = frames_in.shape[1:]
@@ -280,14 +269,7 @@
     rows = mics * frames
     piece, wide = w_qkv.shape
     half, cut = wide // cores, width // cores
-
-    slot_len = frame_dev * tms // SESS
-    start = lax.axis_index(TM) * frame_dev
-    session = start // slot_len
-    left = lengths[session] + session * slot_len - start - y_at * cores * frames
-    scalars = [core_at, left - core_at * frames, left - (1 - core_at) * frames, x_at]
-    scalars = jnp.stack(scalars).astype(jnp.int32)
-    gain = norm_gain.reshape(1, width)
+    spots = (frames, frame_dev * tms // SESS)
 
     mine = [lax.dynamic_slice(w_qkv, (0, j * width + core_at * cut), (piece, cut)) for j in range(3)]
     mine.append(lax.dynamic_slice(w_out, (0, core_at * cut), (piece, cut)))
@@ -296,7 +278,6 @@
     block = block.reshape(zs * piece, half + cut)
     up, down = shift(block, "x", 1), shift(block, "x", -1)
     mid = zs * piece // 2
-    up, down = step((up, down), scalars, gain)
     far_low, far_high = shift(up[:mid], "x", 1), shift(down[mid:], "x", -1)
 
     both = jnp.concatenate(
@@ -315,43 +296,47 @@
         shape((rows, cut), bf),
     )
     own_qkv, own_p, own_att, w, wo, wo_give = call(
-        lambda *refs: own_kernel(frames, *refs),
+        lambda *refs: own_kernel(*spots, *refs),
         results + (shape((width, half), bf), shape((cut, cut), bf), shape((cut, cut), bf)),
         (pltpu.VMEM((width, cut), bf),),
         OWN_COST,
-        scalars, own, gain, block, up, down, far_low, far_high,
+        lengths, own, norm_gain, block, up, down, far_low, far_high,
     )
     near_qkv, near_p, near_att, give, gw = call(
-        lambda *refs: near_kernel(frames, *refs),
+        lambda *refs: near_kernel(*spots, *refs),
         results + (shape((width, cut), bf), shape((width, cut), bf)),
         (),
         NEAR_COST,
-        scalars, own, near, gain, w, own_att, wo_give,
+        lengths, own, near, norm_gain, w, own_att, wo_give,
     )
 
     got = shift(give, "core", 1)
     term = lax.dynamic_update_slice(gw, got[:cut], ((1 - core_at) * cut, 0))
 
     sum_part, other_part = call(
-        lambda *refs: bwd_kernel(frames, *refs),
+        lambda *refs: bwd_kernel(*spots, *refs),
         (shape((rows, 2 * width), f32), shape((rows, 2 * width), bf)),
         (pltpu.VMEM((2 * rows, half), bf),),
         BWD_COST,
-        scalars, own, near, wo, got, own_att, near_att, own_qkv, near_qkv, own_p, near_p, w,
+        lengths, own, near, wo, got, own_att, near_att, own_qkv, near_qkv, own_p, near_p, w,
         behind=(term,),
     )
     term = exchange(term.reshape(tms, piece, cut), TM)
+    term = jnp.sum(term.astype(f32), axis=0).astype(bf)
     got_part = shift(other_part, "core", 1)
     low = piece // frames
     (done,) = call(
-        lambda *refs: end_kernel(frames, *refs),
-        (shape((rows, 2 * width + low * cut), bf),),
+        lambda *refs: end_kernel(*spots, *refs),
+        (shape((rows, 2 * width), bf),),
         (),
         END_COST,
-        scalars, own, gain, sum_part, got_part, term,
-    )
-
-    sent = exchange(done.reshape(mics, frames, 2 * width + low * cut), MIC)
+        lengths, own, norm_gain, sum_part, got_part,
+    )
+
+    term = term.reshape(low, frames, cut).transpose(1, 0, 2).reshape(frames, low * cut)
+    term = jnp.broadcast_to(term[None], (mics, frames, low * cut))
+    sent = jnp.concatenate([done.reshape(mics, frames, 2 * width), term], axis=2)
+    sent = exchange(sent, MIC)
     out = sent[:, :, :width].reshape(1, frame_dev, width)
     dx = sent[:, :, width : 2 * width].reshape(1, frame_dev, width)
     term = jnp.sum(sent[:, :, 2 * width :].astype(f32).reshape(ys, cores, frames, low, cut), axis=0)

time: 141 us -> 132 us (0.936)
  local copies, waits for them, and re-layouts: 10.2 us -> 4.76 us
  waiting for transfers between devices: 16.1 us -> 12.5 us
    ppermute x7, waiting for transfers between devices: 6.85 us -> 3.37 us  [shift(): return lax.ppermute(v, axis, [(i, (i + by) % size) for i in range(size)])]
    unnamed x29 -> x19, local copies, waits for them, and re-layouts: 4.49 us -> 2.18 us
    slice x2, local copies, waits for them, and re-layouts: 1.96 us -> 0.04 us  [per_device(): far_low, far_high = (shift(up[:mid], 'x', 1), shift(down[mid:], 'x', -1))]
  transfers between devices with their start and end apart: 9 -> 9, of which waited for: 6 -> 4; matrix products, arithmetic and copies ran while one was open for 3% -> 1% of each run, Pallas kernels for 8% -> 10%
where the time goes in v10:
time: 132 us; the launch traced here: 131 us
  blocking collectives  58.9 us (45%)
  starting transfers between devices  34.3 us (26%)
  Pallas kernels  17.4 us (13%)
  waiting for transfers between devices  12.5 us (9%)
  local copies, waits for them, and re-layouts  4.76 us (4%)
  other arithmetic  1.96 us (1%)
    all_to_all x2, blocking collectives, exchange(): return lax.all_to_all(v, axes, split_axis=0, concat_axis=0, tiled=True)  58.9 us
    ppermute x7, starting transfers between devices, shift(): return lax.ppermute(v, axis, [(i, (i + by) % size) for i in range(size)])  20.5 us
    pallas_call x4, Pallas kernels, call(): pl.pallas_call(kernel, out_shape=outs, in_specs=[pl.BlockSpec(memory_spac...  17.4 us
    all_to_all x2, starting transfers between devices, exchange(): return lax.all_to_all(v, axes, split_axis=0, concat_axis=0, tiled=True)  13.8 us
    all_to_all x2, waiting for transfers between devices, exchange(): return lax.all_to_all(v, axes, split_axis=0, concat_axis=0, tiled=True)  9.15 us
    ppermute x7, waiting for transfers between devices, shift(): return lax.ppermute(v, axis, [(i, (i + by) % size) for i in range(size)])  3.37 us
  transfers between devices with their start and end apart: 9, of which 4 were waited for; matrix products, arithmetic and copies ran while one was open for 1% of the time, Pallas kernels for 10%

profile of v10, /device:TPU:1, one launch (start us, length us, event | category | flops | bytes accessed | tf_op | source)
XLA Modules:
  0.0 130.8 jit_solution(17524099355554953521)
XLA Ops:
  0.7 0.8 constant_dynamic-slice_fusion.3
  1.6 28.1 %all_to_all.20 = bf16[8,24,1536]{2,1,0:T(8,128)(2,1)S(1)} all-to-all(bf16[8,24,1536]{2,1,0:T(8,128)(2,1)S(1)} %broadcast_in_dim.6), channel_id=1, replica_groups=mesh['y'=8,'core'=2,'x'=4,'z'=8] {'z'}, dimensions={0} | all-to-all | bytes 1179648 | tf_op jit(solution)/shard_map/all_to_all | solution.py:255
  29.7 4.4 %collective-permute-start.2 = (bf16[192,1536]{1,0:T(8,128)(2,1)S(1)}, bf16[192,1536]{1,0:T(8,128)(2,1)S(1)}, u32[]{:S(2)}, u32[]{:S(2)}) collective-permute-start(bf16[192,1536]{1,0:T(8,128)(2,1)S(1)} %bitcast.31), channel_id=1, source_target_pairs={{0,24},{8,0},{16,8},{24,16},{1,25},{9,1},{17,9},{25,17},{2,26},{10... | collective-permute-start | bytes 1769480 | tf_op jit(solution)/shard_map/ppermute | solution.py:251
  34.1 1.9 %collective-permute-start.1 = (bf16[192,1536]{1,0:T(8,128)(2,1)S(1)}, bf16[192,1536]{1,0:T(8,128)(2,1)S(1)}, u32[]{:S(2)}, u32[]{:S(2)}) collective-permute-start(bf16[192,1536]{1,0:T(8,128)(2,1)S(1)} %bitcast.32), channel_id=1, source_target_pairs={{0,8},{8,16},{16,24},{24,0},{1,9},{9,17},{17,25},{25,1},{2,10},{10... | collective-permute-start | bytes 1769480 | tf_op jit(solution)/shard_map/ppermute | solution.py:251
  36.0 0.8 pad_maximum_fusion.1
  36.8 9.8 %all-to-all-start.1 = ((bf16[16,8,1536]{2,1,0:T(8,128)(2,1)}), bf16[16,8,1536]{2,1,0:T(8,128)(2,1)S(1)}, u32[]{:S(2)}, u32[]{:S(2)}) async-start(bf16[16,8,1536]{2,1,0:T(8,128)(2,1)} %pad_maximum_fusion.1), calls=%async_computation.1 | async-start | bytes 786432 | tf_op jit(solution)/shard_map/all_to_all | solution.py:255
  46.6 4.9 %collective-permute-start.4 = (bf16[96,1536]{1,0:T(8,128)(2,1)S(1)}, bf16[96,1536]{1,0:T(8,128)(2,1)}, u32[]{:S(2)}, u32[]{:S(2)}) collective-permute-start(bf16[96,1536]{1,0:T(8,128)(2,1)S(1)} %slice.25), channel_id=1, source_target_pairs={{0,24},{8,0},{16,8},{24,16},{1,25},{9,1},{17,9},{25,17},{2,26},{10... | collective-permute-start | bytes 884744 | tf_op jit(solution)/shard_map/ppermute | solution.py:251
  51.5 0.0 collective-permute-done.1.refs_4_
  51.6 1.9 %collective-permute-start.3 = (bf16[96,1536]{1,0:T(8,128)(2,1)S(1)}, bf16[96,1536]{1,0:T(8,128)(2,1)}, u32[]{:S(2)}, u32[]{:S(2)}) collective-permute-start(bf16[96,1536]{1,0:T(8,128)(2,1)S(1)} %slice.24), channel_id=1, source_target_pairs={{0,8},{8,16},{16,24},{24,0},{1,9},{9,17},{17,25},{25,1},{2,10},{10... | collective-permute-start | bytes 884744 | tf_op jit(solution)/shard_map/ppermute | solution.py:251
  53.5 7.7 %all-to-all-done.1 = bf16[16,8,1536]{2,1,0:T(8,128)(2,1)S(1)} async-done(((bf16[16,8,1536]{2,1,0:T(8,128)(2,1)}), bf16[16,8,1536]{2,1,0:T(8,128)(2,1)S(1)}, u32[]{:S(2)}, u32[]{:S(2)}) %all-to-all-start.1) | async-done | bytes 393248 | tf_op jit(solution)/shard_map/all_to_all | solution.py:255
  61.1 1.9 %collective-permute-start = (bf16[128,1536]{1,0:T(8,128)(2,1)S(1)}, bf16[128,1536]{1,0:T(8,128)(2,1)S(1)}, u32[]{:S(2)}, u32[]{:S(2)}) collective-permute-start(bf16[128,1536]{1,0:T(8,128)(2,1)S(1)} %bitcast.23), channel_id=1, source_target_pairs={{0,32},{32,0},{1,33},{33,1},{2,34},{34,2},{3,35},{35,3},{4,36},{36... | collective-permute-start | bytes 1179656 | tf_op jit(solution)/shard_map/ppermute | solution.py:251
  63.1 0.0 collective-permute-done.4.refs_7_
  63.1 0.0 collective-permute-done.3.refs_6_
  63.1 4.0 %shard_map.85 = (bf16[128,1152]{1,0:T(8,128)(2,1)}, f32[3,256,128]{2,1,0:T(8,128)}, bf16[128,384]{1,0:T(8,128)(2,1)}, bf16[768,1152]{1,0:T(8,128)(2,1)}, bf16[38...) custom-call(s32[2]{0:T(128)} %refs_0_.7, bf16[128,1536]{1,0:T(8,128)(2,1)} %bitcast.24, f32[768]{0:T(1024)} %refs_2_.3, ...), custom_call_target="tpu_custom_call" | custom-call | flops 8000000000 | bytes 5901320 | tf_op jit(solution)/shard_map/pallas_call | solution.py:235
  67.1 0.0 collective-permute-done.refs_2_
  67.2 0.8 copy-done.3
  67.9 4.2 %shard_map.86 = (bf16[128,1152]{1,0:T(8,128)(2,1)}, f32[3,256,128]{2,1,0:T(8,128)}, bf16[128,384]{1,0:T(8,128)(2,1)}, bf16[768,384]{1,0:T(8,128)(2,1)}, bf16[768,384]{1,0:T(8,128)(2,1)}) custom-call(s32[2]{0:T(128)} %refs_0_.7, bf16[128,1536]{1,0:T(8,128)(2,1)} %bitcast.25, bf16[128,1536]{1,0:T(8,128)(2,1)} %copy-done.3, f32[768]{0:T(1024)} %refs_2_.3, ...), custom_call_target="tpu_custom_call" | custom-call | flops 8000000000 | bytes 4918280 | tf_op jit(solution)/shard_map/pallas_call | solution.py:235
  72.1 3.0 %collective-permute-start.5 = (bf16[768,384]{1,0:T(8,128)(2,1)}, bf16[768,384]{1,0:T(8,128)(2,1)S(1)}, u32[]{:S(2)}, u32[]{:S(2)}) collective-permute-start(bf16[768,384]{1,0:T(8,128)(2,1)} %get-tuple-element.22), channel_id=1, source_target_pairs={{0,32},{32,0},{1,33},{33,1},{2,34},{34,2},{3,35},{35,3},{4,36},{36... | collective-permute-start | bytes 1769480 | tf_op jit(solution)/shard_map/ppermute | solution.py:251
  75.1 1.8 %collective-permute-done.5.refs_4_ = bf16[768,384]{1,0:T(8,128)(2,1)S(1)} collective-permute-done((bf16[768,384]{1,0:T(8,128)(2,1)}, bf16[768,384]{1,0:T(8,128)(2,1)S(1)}, u32[]{:S(2)}, u32[]{:S(2)}) %collective-permute-start.5) | collective-permute-done | bytes 589856 | tf_op jit(solution)/shard_map/ppermute | solution.py:251
  76.9 0.8 slice_dynamic-update-slice_fusion.refs_12_
  77.7 4.0 %all-to-all-start.2 = ((bf16[32,24,384]{2,1,0:T(8,128)(2,1)}), bf16[32,24,384]{2,1,0:T(8,128)(2,1)S(1)}, u32[]{:S(2)}, u32[]{:S(2)}) async-start(bf16[32,24,384]{2,1,0:T(8,128)(2,1)} %bitcast.28), calls=%async_computation.2 | async-start | bytes 1179648 | tf_op jit(solution)/shard_map/all_to_all | solution.py:255
  81.8 6.8 %shard_map.87 = (f32[128,1536]{1,0:T(8,128)}, bf16[128,1536]{1,0:T(8,128)(2,1)}) custom-call(s32[2]{0:T(128)} %refs_0_.7, bf16[128,1536]{1,0:T(8,128)(2,1)} %bitcast.26, bf16[128,1536]{1,0:T(8,128)(2,1)} %copy-done.3, bf16[384,384]{1,0:T(8,128)(2,1)} %get-tuple-element.18.refs_3_, bf16[768,384]{1,0:T(8,128)(2,1)} %copy-done.1, ...), custom_call_target="tpu_custom_call" | custom-call | flops 1000 | bytes 6193160 | tf_op jit(solution)/shard_map/pallas_call | solution.py:235
  88.5 2.5 %collective-permute-start.6 = (bf16[128,1536]{1,0:T(8,128)(2,1)}, bf16[128,1536]{1,0:T(8,128)(2,1)S(1)}, u32[]{:S(2)}, u32[]{:S(2)}) collective-permute-start(bf16[128,1536]{1,0:T(8,128)(2,1)} %get-tuple-element.30), channel_id=1, source_target_pairs={{0,32},{32,0},{1,33},{33,1},{2,34},{34,2},{3,35},{35,3},{4,36},{36... | collective-permute-start | bytes 1179656 | tf_op jit(solution)/shard_map/ppermute | solution.py:251
  91.1 1.5 %collective-permute-done.6.refs_4_ = bf16[128,1536]{1,0:T(8,128)(2,1)S(1)} collective-permute-done((bf16[128,1536]{1,0:T(8,128)(2,1)}, bf16[128,1536]{1,0:T(8,128)(2,1)S(1)}, u32[]{:S(2)}, u32[]{:S(2)}) %collective-permute-start.6) | collective-permute-done | bytes 393248 | tf_op jit(solution)/shard_map/ppermute | solution.py:251
  92.6 0.7 copy-done.4
  93.4 2.4 %shard_map.88 = bf16[128,1536]{1,0:T(8,128)(2,1)} custom-call(s32[2]{0:T(128)} %refs_0_.7, bf16[128,1536]{1,0:T(8,128)(2,1)} %bitcast.27, f32[768]{0:T(1024)} %refs_2_.3, f32[128,1536]{1,0:T(8,128)} %get-tuple-element.29.refs_3_, bf16[128,1536]{1,0:T(8,128)(2,1)} %copy-done.4), custom_call_target="tpu_custom_call" | custom-call | flops 1000 | bytes 1969160 | tf_op jit(solution)/shard_map/pallas_call | solution.py:235
  95.8 1.5 %all-to-all-done.2 = bf16[32,24,384]{2,1,0:T(8,128)(2,1)S(1)} async-done(((bf16[32,24,384]{2,1,0:T(8,128)(2,1)}), bf16[32,24,384]{2,1,0:T(8,128)(2,1)S(1)}, u32[]{:S(2)}, u32[]{:S(2)}) %all-to-all-start.2) | async-done | bytes 589856 | tf_op jit(solution)/shard_map/all_to_all | solution.py:255
  97.3 0.1 reduce_sum.21
  97.4 1.0 pad_maximum_fusion
  98.5 30.8 %all_to_all.21 = bf16[16,8,2688]{2,1,0:T(8,128)(2,1)S(1)} all-to-all(bf16[16,8,2688]{2,1,0:T(8,128)(2,1)S(1)} %pad_maximum_fusion), channel_id=1, replica_groups=mesh['y'=8,'core'=2,'x'=4,'z'=8] {'y','core'}, dimensions={0} | all-to-all | bytes 1376256 | tf_op jit(solution)/shard_map/all_to_all | solution.py:255
  129.4 0.6 copy.10
  130.0 0.8 slice_bitcast_fusion
  (25 shorter events, 0.3 us)
Async XLA Ops:
  0.6 35.4 %copy-start.5 = (bf16[1,128,768]{2,1,0:T(8,128)(2,1)S(1)}, bf16[1,128,768]{2,1,0:T(8,128)(2,1)}, u32[]{:S(2)}) copy-start(bf16[1,128,768]{2,1,0:T(8,128)(2,1)} %param.7) | copy-start | bytes 589828
  0.6 35.4 %copy-start.6 = (bf16[1,128,768]{2,1,0:T(8,128)(2,1)S(1)}, bf16[1,128,768]{2,1,0:T(8,128)(2,1)}, u32[]{:S(2)}) copy-start(bf16[1,128,768]{2,1,0:T(8,128)(2,1)} %param.6) | copy-start | bytes 589828
  29.7 21.9 %copy-start.2 = (bf16[8,24,1536]{2,1,0:T(8,128)(2,1)}, bf16[8,24,1536]{2,1,0:T(8,128)(2,1)S(1)}, u32[]{:S(2)}) copy-start(bf16[8,24,1536]{2,1,0:T(8,128)(2,1)S(1)} %all_to_all.20) | copy-start | bytes 1769476
  29.7 16.9 %collective-permute-start.2 = (bf16[192,1536]{1,0:T(8,128)(2,1)S(1)}, bf16[192,1536]{1,0:T(8,128)(2,1)S(1)}, u32[]{:S(2)}, u32[]{:S(2)}) collective-permute-start(bf16[192,1536]{1,0:T(8,128)(2,1)S(1)} %bitcast.31), channel_id=1, source_target_pairs={{0,24},{8,0},{16,8},{24,16},{1,25},{9,1},{17,9},{25,17},{2,26},{10... | collective-permute-start | bytes 1769480 | tf_op jit(solution)/shard_map/ppermute | solution.py:251
  34.1 17.4 %collective-permute-start.1 = (bf16[192,1536]{1,0:T(8,128)(2,1)S(1)}, bf16[192,1536]{1,0:T(8,128)(2,1)S(1)}, u32[]{:S(2)}, u32[]{:S(2)}) collective-permute-start(bf16[192,1536]{1,0:T(8,128)(2,1)S(1)} %bitcast.32), channel_id=1, source_target_pairs={{0,8},{8,16},{16,24},{24,0},{1,9},{9,17},{17,25},{25,1},{2,10},{10... | collective-permute-start | bytes 1769480 | tf_op jit(solution)/shard_map/ppermute | solution.py:251
  36.8 24.4 %all-to-all-start.1 = ((bf16[16,8,1536]{2,1,0:T(8,128)(2,1)}), bf16[16,8,1536]{2,1,0:T(8,128)(2,1)S(1)}, u32[]{:S(2)}, u32[]{:S(2)}) async-start(bf16[16,8,1536]{2,1,0:T(8,128)(2,1)} %pad_maximum_fusion.1), calls=%async_computation.1 | async-start | bytes 786432 | tf_op jit(solution)/shard_map/all_to_all | solution.py:255
  46.6 16.5 %copy-start.7 = (bf16[192,1536]{1,0:T(8,128)(2,1)}, bf16[192,1536]{1,0:T(8,128)(2,1)S(1)}, u32[]{:S(2)}) copy-start(bf16[192,1536]{1,0:T(8,128)(2,1)S(1)} %collective-permute-done.2.refs_5_) | copy-start | bytes 1769476
  46.6 16.4 %collective-permute-start.4 = (bf16[96,1536]{1,0:T(8,128)(2,1)S(1)}, bf16[96,1536]{1,0:T(8,128)(2,1)}, u32[]{:S(2)}, u32[]{:S(2)}) collective-permute-start(bf16[96,1536]{1,0:T(8,128)(2,1)S(1)} %slice.25), channel_id=1, source_target_pairs={{0,24},{8,0},{16,8},{24,16},{1,25},{9,1},{17,9},{25,17},{2,26},{10... | collective-permute-start | bytes 884744 | tf_op jit(solution)/shard_map/ppermute | solution.py:251
  51.5 11.6 %copy-start.8 = (bf16[192,1536]{1,0:T(8,128)(2,1)}, bf16[192,1536]{1,0:T(8,128)(2,1)S(1)}, u32[]{:S(2)}) copy-start(bf16[192,1536]{1,0:T(8,128)(2,1)S(1)} %collective-permute-done.1.refs_4_) | copy-start | bytes 1769476
  51.6 11.5 %collective-permute-start.3 = (bf16[96,1536]{1,0:T(8,128)(2,1)S(1)}, bf16[96,1536]{1,0:T(8,128)(2,1)}, u32[]{:S(2)}, u32[]{:S(2)}) collective-permute-start(bf16[96,1536]{1,0:T(8,128)(2,1)S(1)} %slice.24), channel_id=1, source_target_pairs={{0,8},{8,16},{16,24},{24,0},{1,9},{9,17},{17,25},{25,1},{2,10},{10... | collective-permute-start | bytes 884744 | tf_op jit(solution)/shard_map/ppermute | solution.py:251
  61.1 2.0 %copy-start = (bf16[16,8,1536]{2,1,0:T(8,128)(2,1)}, bf16[16,8,1536]{2,1,0:T(8,128)(2,1)S(1)}, u32[]{:S(2)}) copy-start(bf16[16,8,1536]{2,1,0:T(8,128)(2,1)S(1)} %all-to-all-done.1) | copy-start | bytes 1179652
  61.1 6.0 %collective-permute-start = (bf16[128,1536]{1,0:T(8,128)(2,1)S(1)}, bf16[128,1536]{1,0:T(8,128)(2,1)S(1)}, u32[]{:S(2)}, u32[]{:S(2)}) collective-permute-start(bf16[128,1536]{1,0:T(8,128)(2,1)S(1)} %bitcast.23), channel_id=1, source_target_pairs={{0,32},{32,0},{1,33},{33,1},{2,34},{34,2},{3,35},{35,3},{4,36},{36... | collective-permute-start | bytes 1179656 | tf_op jit(solution)/shard_map/ppermute | solution.py:251
  67.1 0.8 copy-start.3
  72.1 4.8 %collective-permute-start.5 = (bf16[768,384]{1,0:T(8,128)(2,1)}, bf16[768,384]{1,0:T(8,128)(2,1)S(1)}, u32[]{:S(2)}, u32[]{:S(2)}) collective-permute-start(bf16[768,384]{1,0:T(8,128)(2,1)} %get-tuple-element.22), channel_id=1, source_target_pairs={{0,32},{32,0},{1,33},{33,1},{2,34},{34,2},{3,35},{35,3},{4,36},{36... | collective-permute-start | bytes 1769480 | tf_op jit(solution)/shard_map/ppermute | solution.py:251
  76.9 4.8 %copy-start.1 = (bf16[768,384]{1,0:T(8,128)(2,1)}, bf16[768,384]{1,0:T(8,128)(2,1)S(1)}, u32[]{:S(2)}) copy-start(bf16[768,384]{1,0:T(8,128)(2,1)S(1)} %collective-permute-done.5.refs_4_) | copy-start | bytes 1769476
  77.7 19.6 %all-to-all-start.2 = ((bf16[32,24,384]{2,1,0:T(8,128)(2,1)}), bf16[32,24,384]{2,1,0:T(8,128)(2,1)S(1)}, u32[]{:S(2)}, u32[]{:S(2)}) async-start(bf16[32,24,384]{2,1,0:T(8,128)(2,1)} %bitcast.28), calls=%async_computation.2 | async-start | bytes 1179648 | tf_op jit(solution)/shard_map/all_to_all | solution.py:255
  88.5 4.1 %collective-permute-start.6 = (bf16[128,1536]{1,0:T(8,128)(2,1)}, bf16[128,1536]{1,0:T(8,128)(2,1)S(1)}, u32[]{:S(2)}, u32[]{:S(2)}) collective-permute-start(bf16[128,1536]{1,0:T(8,128)(2,1)} %get-tuple-element.30), channel_id=1, source_target_pairs={{0,32},{32,0},{1,33},{33,1},{2,34},{34,2},{3,35},{35,3},{4,36},{36... | collective-permute-start | bytes 1179656 | tf_op jit(solution)/shard_map/ppermute | solution.py:251
  92.6 0.7 copy-start.4

commit v11 on v10

--- a/solution.py
+++ b/solution.py
@@ -227,7 +227,7 @@
     inner = jnp.mean(gh * x, axis=-1, keepdims=True)
     gy = own_ref[:, width:].astype(jnp.float32) * valid
     dx = gy + inv * (gh - x * inv * inv * inner)
-    both_ref[:, width:] = dx.astype(jnp.bfloat16)
+    both_ref[:, width : 2 * width] = dx.astype(jnp.bfloat16)
 
 
 def call(kernel, outs, scratch, flops, *operands, behind=()):
@@ -327,7 +327,7 @@
     low = piece // frames
     (done,) = call(
         lambda *refs: end_kernel(*spots, *refs),
-        (shape((rows, 2 * width), bf),),
+        (shape((rows, 2 * width + low * cut), bf),),
         (),
         END_COST,
         lengths, own, norm_gain, sum_part, got_part,
@@ -335,8 +335,8 @@
 
     term = term.reshape(low, frames, cut).transpose(1, 0, 2).reshape(frames, low * cut)
     term = jnp.broadcast_to(term[None], (mics, frames, low * cut))
-    sent = jnp.concatenate([done.reshape(mics, frames, 2 * width), term], axis=2)
-    sent = exchange(sent, MIC)
+    sent = done.reshape(mics, frames, 2 * width + low * cut)
+    sent = exchange(lax.dynamic_update_slice(sent, term, (0, 0, 2 * width)), MIC)
     out = sent[:, :, :width].reshape(1, frame_dev, width)
     dx = sent[:, :, width : 2 * width].reshape(1, frame_dev, width)
     term = jnp.sum(sent[:, :, 2 * width :].astype(f32).reshape(ys, cores, frames, low, cut), axis=0)

time: 132 us -> 131 us (level)
  no operation moved by 1% of the time
where the time goes in v11:
time: 131 us
  blocking collectives  59.1 us (45%)
  starting transfers between devices  34.3 us (26%)
  Pallas kernels  17.5 us (13%)
  waiting for transfers between devices  12.4 us (9%)
  local copies, waits for them, and re-layouts  5.53 us (4%)
    all_to_all x2, blocking collectives, exchange(): return lax.all_to_all(v, axes, split_axis=0, concat_axis=0, tiled=True)  59.1 us
    ppermute x7, starting transfers between devices, shift(): return lax.ppermute(v, axis, [(i, (i + by) % size) for i in range(size)])  20.5 us
    pallas_call x4, Pallas kernels, call(): pl.pallas_call(kernel, out_shape=outs, in_specs=[pl.BlockSpec(memory_spac...  17.5 us
    all_to_all x2, starting transfers between devices, exchange(): return lax.all_to_all(v, axes, split_axis=0, concat_axis=0, tiled=True)  13.8 us
    all_to_all x2, waiting for transfers between devices, exchange(): return lax.all_to_all(v, axes, split_axis=0, concat_axis=0, tiled=True)  9.04 us
    ppermute x7, waiting for transfers between devices, shift(): return lax.ppermute(v, axis, [(i, (i + by) % size) for i in range(size)])  3.37 us
  transfers between devices with their start and end apart: 9, of which 4 were waited for; matrix products, arithmetic and copies ran while one was open for 1% of the time, Pallas kernels for 10%

profile of v11, /device:TPU:1, one launch (start us, length us, event | category | flops | bytes accessed | tf_op | source)
XLA Modules:
  0.0 130.7 jit_solution(3710960382521639891)
XLA Ops:
  0.7 0.8 constant_dynamic-slice_fusion.3
  1.6 28.1 %all_to_all.20 = bf16[8,24,1536]{2,1,0:T(8,128)(2,1)S(1)} all-to-all(bf16[8,24,1536]{2,1,0:T(8,128)(2,1)S(1)} %broadcast_in_dim.6), channel_id=1, replica_groups=mesh['y'=8,'core'=2,'x'=4,'z'=8] {'z'}, dimensions={0} | all-to-all | bytes 1179648 | tf_op jit(solution)/shard_map/all_to_all | solution.py:255
  29.7 4.4 %collective-permute-start.2 = (bf16[192,1536]{1,0:T(8,128)(2,1)S(1)}, bf16[192,1536]{1,0:T(8,128)(2,1)S(1)}, u32[]{:S(2)}, u32[]{:S(2)}) collective-permute-start(bf16[192,1536]{1,0:T(8,128)(2,1)S(1)} %bitcast.31), channel_id=1, source_target_pairs={{0,24},{8,0},{16,8},{24,16},{1,25},{9,1},{17,9},{25,17},{2,26},{10... | collective-permute-start | bytes 1769480 | tf_op jit(solution)/shard_map/ppermute | solution.py:251
  34.1 1.9 %collective-permute-start.1 = (bf16[192,1536]{1,0:T(8,128)(2,1)S(1)}, bf16[192,1536]{1,0:T(8,128)(2,1)S(1)}, u32[]{:S(2)}, u32[]{:S(2)}) collective-permute-start(bf16[192,1536]{1,0:T(8,128)(2,1)S(1)} %bitcast.32), channel_id=1, source_target_pairs={{0,8},{8,16},{16,24},{24,0},{1,9},{9,17},{17,25},{25,1},{2,10},{10... | collective-permute-start | bytes 1769480 | tf_op jit(solution)/shard_map/ppermute | solution.py:251
  36.0 0.8 pad_maximum_fusion
  36.8 9.8 %all-to-all-start.1 = ((bf16[16,8,1536]{2,1,0:T(8,128)(2,1)}), bf16[16,8,1536]{2,1,0:T(8,128)(2,1)S(1)}, u32[]{:S(2)}, u32[]{:S(2)}) async-start(bf16[16,8,1536]{2,1,0:T(8,128)(2,1)} %pad_maximum_fusion), calls=%async_computation.1 | async-start | bytes 786432 | tf_op jit(solution)/shard_map/all_to_all | solution.py:255
  46.6 0.0 collective-permute-done.2.refs_5_
  46.6 4.9 %collective-permute-start.4 = (bf16[96,1536]{1,0:T(8,128)(2,1)S(1)}, bf16[96,1536]{1,0:T(8,128)(2,1)}, u32[]{:S(2)}, u32[]{:S(2)}) collective-permute-start(bf16[96,1536]{1,0:T(8,128)(2,1)S(1)} %slice.25), channel_id=1, source_target_pairs={{0,24},{8,0},{16,8},{24,16},{1,25},{9,1},{17,9},{25,17},{2,26},{10... | collective-permute-start | bytes 884744 | tf_op jit(solution)/shard_map/ppermute | solution.py:251
  51.5 0.0 collective-permute-done.1.refs_4_
  51.5 1.9 %collective-permute-start.3 = (bf16[96,1536]{1,0:T(8,128)(2,1)S(1)}, bf16[96,1536]{1,0:T(8,128)(2,1)}, u32[]{:S(2)}, u32[]{:S(2)}) collective-permute-start(bf16[96,1536]{1,0:T(8,128)(2,1)S(1)} %slice.24), channel_id=1, source_target_pairs={{0,8},{8,16},{16,24},{24,0},{1,9},{9,17},{17,25},{25,1},{2,10},{10... | collective-permute-start | bytes 884744 | tf_op jit(solution)/shard_map/ppermute | solution.py:251
  53.5 7.7 %all-to-all-done.1 = bf16[16,8,1536]{2,1,0:T(8,128)(2,1)S(1)} async-done(((bf16[16,8,1536]{2,1,0:T(8,128)(2,1)}), bf16[16,8,1536]{2,1,0:T(8,128)(2,1)S(1)}, u32[]{:S(2)}, u32[]{:S(2)}) %all-to-all-start.1) | async-done | bytes 393248 | tf_op jit(solution)/shard_map/all_to_all | solution.py:255
  61.1 1.9 %collective-permute-start = (bf16[128,1536]{1,0:T(8,128)(2,1)S(1)}, bf16[128,1536]{1,0:T(8,128)(2,1)S(1)}, u32[]{:S(2)}, u32[]{:S(2)}) collective-permute-start(bf16[128,1536]{1,0:T(8,128)(2,1)S(1)} %bitcast.23), channel_id=1, source_target_pairs={{0,32},{32,0},{1,33},{33,1},{2,34},{34,2},{3,35},{35,3},{4,36},{36... | collective-permute-start | bytes 1179656 | tf_op jit(solution)/shard_map/ppermute | solution.py:251
  63.1 0.0 collective-permute-done.4.refs_7_
  63.1 0.0 collective-permute-done.3.refs_6_
  63.1 4.0 %shard_map.85 = (bf16[128,1152]{1,0:T(8,128)(2,1)}, f32[3,256,128]{2,1,0:T(8,128)}, bf16[128,384]{1,0:T(8,128)(2,1)}, bf16[768,1152]{1,0:T(8,128)(2,1)}, bf16[38...) custom-call(s32[2]{0:T(128)} %refs_0_.7, bf16[128,1536]{1,0:T(8,128)(2,1)} %bitcast.24, f32[768]{0:T(1024)} %refs_2_.3, ...), custom_call_target="tpu_custom_call" | custom-call | flops 8000000000 | bytes 5901320 | tf_op jit(solution)/shard_map/pallas_call | solution.py:235
  67.2 0.8 copy-done.3
  67.9 4.2 %shard_map.86 = (bf16[128,1152]{1,0:T(8,128)(2,1)}, f32[3,256,128]{2,1,0:T(8,128)}, bf16[128,384]{1,0:T(8,128)(2,1)}, bf16[768,384]{1,0:T(8,128)(2,1)}, bf16[768,384]{1,0:T(8,128)(2,1)}) custom-call(s32[2]{0:T(128)} %refs_0_.7, bf16[128,1536]{1,0:T(8,128)(2,1)} %bitcast.25, bf16[128,1536]{1,0:T(8,128)(2,1)} %copy-done.3, f32[768]{0:T(1024)} %refs_2_.3, ...), custom_call_target="tpu_custom_call" | custom-call | flops 8000000000 | bytes 4918280 | tf_op jit(solution)/shard_map/pallas_call | solution.py:235
  72.1 3.0 %collective-permute-start.5 = (bf16[768,384]{1,0:T(8,128)(2,1)}, bf16[768,384]{1,0:T(8,128)(2,1)S(1)}, u32[]{:S(2)}, u32[]{:S(2)}) collective-permute-start(bf16[768,384]{1,0:T(8,128)(2,1)} %get-tuple-element.22), channel_id=1, source_target_pairs={{0,32},{32,0},{1,33},{33,1},{2,34},{34,2},{3,35},{35,3},{4,36},{36... | collective-permute-start | bytes 1769480 | tf_op jit(solution)/shard_map/ppermute | solution.py:251
  75.1 1.8 %collective-permute-done.5.refs_4_ = bf16[768,384]{1,0:T(8,128)(2,1)S(1)} collective-permute-done((bf16[768,384]{1,0:T(8,128)(2,1)}, bf16[768,384]{1,0:T(8,128)(2,1)S(1)}, u32[]{:S(2)}, u32[]{:S(2)}) %collective-permute-start.5) | collective-permute-done | bytes 589856 | tf_op jit(solution)/shard_map/ppermute | solution.py:251
  76.9 0.8 slice_dynamic-update-slice_fusion.refs_12_
  77.7 4.0 %all-to-all-start.2 = ((bf16[32,24,384]{2,1,0:T(8,128)(2,1)}), bf16[32,24,384]{2,1,0:T(8,128)(2,1)S(1)}, u32[]{:S(2)}, u32[]{:S(2)}) async-start(bf16[32,24,384]{2,1,0:T(8,128)(2,1)} %bitcast.29), calls=%async_computation.2 | async-start | bytes 1179648 | tf_op jit(solution)/shard_map/all_to_all | solution.py:255
  81.8 6.8 %shard_map.87 = (f32[128,1536]{1,0:T(8,128)}, bf16[128,1536]{1,0:T(8,128)(2,1)}) custom-call(s32[2]{0:T(128)} %refs_0_.7, bf16[128,1536]{1,0:T(8,128)(2,1)} %bitcast.26, bf16[128,1536]{1,0:T(8,128)(2,1)} %copy-done.3, bf16[384,384]{1,0:T(8,128)(2,1)} %get-tuple-element.18.refs_3_, bf16[768,384]{1,0:T(8,128)(2,1)} %copy-done.1, ...), custom_call_target="tpu_custom_call" | custom-call | flops 1000 | bytes 6193160 | tf_op jit(solution)/shard_map/pallas_call | solution.py:235
  88.6 2.5 %collective-permute-start.6 = (bf16[128,1536]{1,0:T(8,128)(2,1)}, bf16[128,1536]{1,0:T(8,128)(2,1)S(1)}, u32[]{:S(2)}, u32[]{:S(2)}) collective-permute-start(bf16[128,1536]{1,0:T(8,128)(2,1)} %get-tuple-element.30), channel_id=1, source_target_pairs={{0,32},{32,0},{1,33},{33,1},{2,34},{34,2},{3,35},{35,3},{4,36},{36... | collective-permute-start | bytes 1179656 | tf_op jit(solution)/shard_map/ppermute | solution.py:251
  91.1 1.5 %collective-permute-done.6.refs_4_ = bf16[128,1536]{1,0:T(8,128)(2,1)S(1)} collective-permute-done((bf16[128,1536]{1,0:T(8,128)(2,1)}, bf16[128,1536]{1,0:T(8,128)(2,1)S(1)}, u32[]{:S(2)}, u32[]{:S(2)}) %collective-permute-start.6) | collective-permute-done | bytes 393248 | tf_op jit(solution)/shard_map/ppermute | solution.py:251
  92.7 0.8 copy-done.4
  93.4 2.5 %shard_map.88 = bf16[128,2688]{1,0:T(8,128)(2,1)} custom-call(s32[2]{0:T(128)} %refs_0_.7, bf16[128,1536]{1,0:T(8,128)(2,1)} %bitcast.27, f32[768]{0:T(1024)} %refs_2_.3, f32[128,1536]{1,0:T(8,128)} %get-tuple-element.29.refs_3_, bf16[128,1536]{1,0:T(8,128)(2,1)} %copy-done.4), custom_call_target="tpu_custom_call" | custom-call | flops 1000 | bytes 2264072 | tf_op jit(solution)/shard_map/pallas_call | solution.py:235
  95.9 1.4 %all-to-all-done.2 = bf16[32,24,384]{2,1,0:T(8,128)(2,1)S(1)} async-done(((bf16[32,24,384]{2,1,0:T(8,128)(2,1)}), bf16[32,24,384]{2,1,0:T(8,128)(2,1)S(1)}, u32[]{:S(2)}, u32[]{:S(2)}) %all-to-all-start.2) | async-done | bytes 589856 | tf_op jit(solution)/shard_map/all_to_all | solution.py:255
  97.3 0.1 reduce_sum.21
  97.4 0.8 broadcast_dynamic-update-slice_fusion
  98.2 31.0 %all_to_all.21 = bf16[16,8,2688]{2,1,0:T(8,128)(2,1)S(1)} all-to-all(bf16[16,8,2688]{2,1,0:T(8,128)(2,1)} %broadcast_dynamic-update-slice_fusion), channel_id=1, replica_groups=mesh['y'=8,'core'=2,'x'=4,'z'=8] {'y','core'}, dimensions={0} | all-to-all | bytes 1376256 | tf_op jit(solution)/shard_map/all_to_all | solution.py:255
  129.3 0.6 copy.10
  129.9 0.8 slice_bitcast_fusion
  (24 shorter events, 0.2 us)
Async XLA Ops:
  0.6 35.4 %copy-start.5 = (bf16[1,128,768]{2,1,0:T(8,128)(2,1)S(1)}, bf16[1,128,768]{2,1,0:T(8,128)(2,1)}, u32[]{:S(2)}) copy-start(bf16[1,128,768]{2,1,0:T(8,128)(2,1)} %param.7) | copy-start | bytes 589828
  0.6 35.4 %copy-start.6 = (bf16[1,128,768]{2,1,0:T(8,128)(2,1)S(1)}, bf16[1,128,768]{2,1,0:T(8,128)(2,1)}, u32[]{:S(2)}) copy-start(bf16[1,128,768]{2,1,0:T(8,128)(2,1)} %param.6) | copy-start | bytes 589828
  29.7 33.4 %copy-start.2 = (bf16[8,24,1536]{2,1,0:T(8,128)(2,1)}, bf16[8,24,1536]{2,1,0:T(8,128)(2,1)S(1)}, u32[]{:S(2)}) copy-start(bf16[8,24,1536]{2,1,0:T(8,128)(2,1)S(1)} %all_to_all.20) | copy-start | bytes 1769476
  29.7 16.9 %collective-permute-start.2 = (bf16[192,1536]{1,0:T(8,128)(2,1)S(1)}, bf16[192,1536]{1,0:T(8,128)(2,1)S(1)}, u32[]{:S(2)}, u32[]{:S(2)}) collective-permute-start(bf16[192,1536]{1,0:T(8,128)(2,1)S(1)} %bitcast.31), channel_id=1, source_target_pairs={{0,24},{8,0},{16,8},{24,16},{1,25},{9,1},{17,9},{25,17},{2,26},{10... | collective-permute-start | bytes 1769480 | tf_op jit(solution)/shard_map/ppermute | solution.py:251
  34.1 17.4 %collective-permute-start.1 = (bf16[192,1536]{1,0:T(8,128)(2,1)S(1)}, bf16[192,1536]{1,0:T(8,128)(2,1)S(1)}, u32[]{:S(2)}, u32[]{:S(2)}) collective-permute-start(bf16[192,1536]{1,0:T(8,128)(2,1)S(1)} %bitcast.32), channel_id=1, source_target_pairs={{0,8},{8,16},{16,24},{24,0},{1,9},{9,17},{17,25},{25,1},{2,10},{10... | collective-permute-start | bytes 1769480 | tf_op jit(solution)/shard_map/ppermute | solution.py:251
  36.8 24.4 %all-to-all-start.1 = ((bf16[16,8,1536]{2,1,0:T(8,128)(2,1)}), bf16[16,8,1536]{2,1,0:T(8,128)(2,1)S(1)}, u32[]{:S(2)}, u32[]{:S(2)}) async-start(bf16[16,8,1536]{2,1,0:T(8,128)(2,1)} %pad_maximum_fusion), calls=%async_computation.1 | async-start | bytes 786432 | tf_op jit(solution)/shard_map/all_to_all | solution.py:255
  46.6 16.5 %copy-start.7 = (bf16[192,1536]{1,0:T(8,128)(2,1)}, bf16[192,1536]{1,0:T(8,128)(2,1)S(1)}, u32[]{:S(2)}) copy-start(bf16[192,1536]{1,0:T(8,128)(2,1)S(1)} %collective-permute-done.2.refs_5_) | copy-start | bytes 1769476
  46.6 16.4 %collective-permute-start.4 = (bf16[96,1536]{1,0:T(8,128)(2,1)S(1)}, bf16[96,1536]{1,0:T(8,128)(2,1)}, u32[]{:S(2)}, u32[]{:S(2)}) collective-permute-start(bf16[96,1536]{1,0:T(8,128)(2,1)S(1)} %slice.25), channel_id=1, source_target_pairs={{0,24},{8,0},{16,8},{24,16},{1,25},{9,1},{17,9},{25,17},{2,26},{10... | collective-permute-start | bytes 884744 | tf_op jit(solution)/shard_map/ppermute | solution.py:251
  51.5 11.6 %copy-start.8 = (bf16[192,1536]{1,0:T(8,128)(2,1)}, bf16[192,1536]{1,0:T(8,128)(2,1)S(1)}, u32[]{:S(2)}) copy-start(bf16[192,1536]{1,0:T(8,128)(2,1)S(1)} %collective-permute-done.1.refs_4_) | copy-start | bytes 1769476
  51.5 11.5 %collective-permute-start.3 = (bf16[96,1536]{1,0:T(8,128)(2,1)S(1)}, bf16[96,1536]{1,0:T(8,128)(2,1)}, u32[]{:S(2)}, u32[]{:S(2)}) collective-permute-start(bf16[96,1536]{1,0:T(8,128)(2,1)S(1)} %slice.24), channel_id=1, source_target_pairs={{0,8},{8,16},{16,24},{24,0},{1,9},{9,17},{17,25},{25,1},{2,10},{10... | collective-permute-start | bytes 884744 | tf_op jit(solution)/shard_map/ppermute | solution.py:251
  61.1 2.0 %copy-start = (bf16[16,8,1536]{2,1,0:T(8,128)(2,1)}, bf16[16,8,1536]{2,1,0:T(8,128)(2,1)S(1)}, u32[]{:S(2)}) copy-start(bf16[16,8,1536]{2,1,0:T(8,128)(2,1)S(1)} %all-to-all-done.1) | copy-start | bytes 1179652
  61.1 6.0 %collective-permute-start = (bf16[128,1536]{1,0:T(8,128)(2,1)S(1)}, bf16[128,1536]{1,0:T(8,128)(2,1)S(1)}, u32[]{:S(2)}, u32[]{:S(2)}) collective-permute-start(bf16[128,1536]{1,0:T(8,128)(2,1)S(1)} %bitcast.23), channel_id=1, source_target_pairs={{0,32},{32,0},{1,33},{33,1},{2,34},{34,2},{3,35},{35,3},{4,36},{36... | collective-permute-start | bytes 1179656 | tf_op jit(solution)/shard_map/ppermute | solution.py:251
  67.2 0.8 copy-start.3
  72.1 4.8 %collective-permute-start.5 = (bf16[768,384]{1,0:T(8,128)(2,1)}, bf16[768,384]{1,0:T(8,128)(2,1)S(1)}, u32[]{:S(2)}, u32[]{:S(2)}) collective-permute-start(bf16[768,384]{1,0:T(8,128)(2,1)} %get-tuple-element.22), channel_id=1, source_target_pairs={{0,32},{32,0},{1,33},{33,1},{2,34},{34,2},{3,35},{35,3},{4,36},{36... | collective-permute-start | bytes 1769480 | tf_op jit(solution)/shard_map/ppermute | solution.py:251
  76.9 4.8 %copy-start.1 = (bf16[768,384]{1,0:T(8,128)(2,1)}, bf16[768,384]{1,0:T(8,128)(2,1)S(1)}, u32[]{:S(2)}) copy-start(bf16[768,384]{1,0:T(8,128)(2,1)S(1)} %collective-permute-done.5.refs_4_) | copy-start | bytes 1769476
  77.7 19.6 %all-to-all-start.2 = ((bf16[32,24,384]{2,1,0:T(8,128)(2,1)}), bf16[32,24,384]{2,1,0:T(8,128)(2,1)S(1)}, u32[]{:S(2)}, u32[]{:S(2)}) async-start(bf16[32,24,384]{2,1,0:T(8,128)(2,1)} %bitcast.29), calls=%async_computation.2 | async-start | bytes 1179648 | tf_op jit(solution)/shard_map/all_to_all | solution.py:255
  88.6 4.1 %collective-permute-start.6 = (bf16[128,1536]{1,0:T(8,128)(2,1)}, bf16[128,1536]{1,0:T(8,128)(2,1)S(1)}, u32[]{:S(2)}, u32[]{:S(2)}) collective-permute-start(bf16[128,1536]{1,0:T(8,128)(2,1)} %get-tuple-element.30), channel_id=1, source_target_pairs={{0,32},{32,0},{1,33},{33,1},{2,34},{34,2},{3,35},{35,3},{4,36},{36... | collective-permute-start | bytes 1179656 | tf_op jit(solution)/shard_map/ppermute | solution.py:251
  92.7 0.8 copy-start.4

commit v12 on v11

--- a/solution.py
+++ b/solution.py
@@ -85,10 +85,9 @@
         att_ref[:, at : at + 2 * HD] = mixed.astype(jnp.bfloat16)
 
 
-def project(rows_ref, gain_ref, w_ref, qkv_ref):
-    x = rows_ref[:, : w_ref.shape[0]].astype(jnp.float32)
-    normed = (x * inv_rms_of(x) * gain_ref[...].reshape(1, -1)).astype(jnp.bfloat16)
-    qkv_ref[...] = dot_nn(normed, w_ref[...]).astype(jnp.bfloat16)
+def normalised(rows_ref, gain_ref):
+    x = rows_ref[:, : rows_ref.shape[1] // 2].astype(jnp.float32)
+    return (x * inv_rms_of(x) * gain_ref[...].reshape(1, -1)).astype(jnp.bfloat16)
 
 
 def own_kernel(
@@ -109,6 +108,7 @@
     wo_ref,
     give_ref,
     all_ref,
+    sems,
 ):
     rows, mine = att_ref.shape
     width, deep = w_ref.shape[0], block_ref.shape[0]
@@ -121,14 +121,24 @@
         (far_low_ref, far),
         (far_high_ref, far + deep // 2),
     )
-    for ref, at in places:
+    copies = []
+    for i, (ref, at) in enumerate(places):
         here = pl.ds(pl.multiple_of(at, deep // 2), ref.shape[0])
-        w_ref[here, :] = ref[:, : 3 * mine]
-        all_ref[here, :] = ref[:, 3 * mine :]
+        for j, (cols, to) in enumerate(
+            ((pl.ds(0, 3 * mine), w_ref), (pl.ds(3 * mine, mine), all_ref))
+        ):
+            copies.append(
+                pltpu.make_async_copy(ref.at[:, cols], to.at[here, :], sems.at[2 * i + j])
+            )
+    for copy in copies:
+        copy.start()
     mid = width // 2
+    normed = normalised(own_ref, gain_ref)
+    for copy in copies:
+        copy.wait()
     wo_ref[...] = all_ref[pl.ds(pl.multiple_of(core * mid, mid), mid), :]
     give_ref[...] = all_ref[pl.ds(pl.multiple_of((1 - core) * mid, mid), mid), :]
-    project(own_ref, gain_ref, w_ref, qkv_ref)
+    qkv_ref[...] = dot_nn(normed, w_ref[...]).astype(jnp.bfloat16)
     attend(same_frame(rows, frames), qkv_ref, p_ref, att_ref)
 
 
@@ -139,16 +149,22 @@
     own_ref,
     near_ref,
     gain_ref,
-    w_ref,
     own_att_ref,
     wo_give_ref,
+    w_ref,
     qkv_ref,
     p_ref,
     att_ref,
     give_ref,
     gw_ref,
+    held_ref,
+    sem,
 ):
-    project(near_ref, gain_ref, w_ref, qkv_ref)
+    copy = pltpu.make_async_copy(w_ref, held_ref, sem)
+    copy.start()
+    normed = normalised(near_ref, gain_ref)
+    copy.wait()
+    qkv_ref[...] = dot_nn(normed, held_ref[...]).astype(jnp.bfloat16)
     attend(same_frame(att_ref.shape[0], frames), qkv_ref, p_ref, att_ref)
     core, mid = lax.axis_index("core"), w_ref.shape[0] // 2
     first = core == 0
@@ -298,16 +314,16 @@
     own_qkv, own_p, own_att, w, wo, wo_give = call(
         lambda *refs: own_kernel(*spots, *refs),
         results + (shape((width, half), bf), shape((cut, cut), bf), shape((cut, cut), bf)),
-        (pltpu.VMEM((width, cut), bf),),
+        (pltpu.VMEM((width, cut), bf), pltpu.SemaphoreType.DMA((10,))),
         OWN_COST,
-        lengths, own, norm_gain, block, up, down, far_low, far_high,
+        lengths, own, norm_gain, behind=(block, up, down, far_low, far_high),
     )
     near_qkv, near_p, near_att, give, gw = call(
         lambda *refs: near_kernel(*spots, *refs),
         results + (shape((width, cut), bf), shape((width, cut), bf)),
-        (),
+        (pltpu.VMEM((width, half), bf), pltpu.SemaphoreType.DMA),
         NEAR_COST,
-        lengths, own, near, norm_gain, w, own_att, wo_give,
+        lengths, own, near, norm_gain, own_att, wo_give, behind=(w,),
     )
 
     got = shift(give, "core", 1)

time: 131 us -> 133 us (1.015)
  Pallas kernels: 17.5 us -> 18.9 us
    pallas_call x4, Pallas kernels: 17.5 us -> 18.9 us  [call(): pl.pallas_call(kernel, out_shape=outs, in_specs=[pl.BlockSpec(memory_spac...]
where the time goes in v12:
time: 133 us; the launch traced here: 132 us
  blocking collectives  59.1 us (44%)
  starting transfers between devices  34.4 us (26%)
  Pallas kernels  18.9 us (14%)
  waiting for transfers between devices  12.4 us (9%)
  local copies, waits for them, and re-layouts  5.53 us (4%)
    all_to_all x2, blocking collectives, exchange(): return lax.all_to_all(v, axes, split_axis=0, concat_axis=0, tiled=True)  59.1 us
    ppermute x7, starting transfers between devices, shift(): return lax.ppermute(v, axis, [(i, (i + by) % size) for i in range(size)])  20.5 us
    pallas_call x4, Pallas kernels, call(): pl.pallas_call(kernel, out_shape=outs, in_specs=[pl.BlockSpec(memory_spac...  18.9 us
    all_to_all x2, starting transfers between devices, exchange(): return lax.all_to_all(v, axes, split_axis=0, concat_axis=0, tiled=True)  13.8 us
    all_to_all x2, waiting for transfers between devices, exchange(): return lax.all_to_all(v, axes, split_axis=0, concat_axis=0, tiled=True)  9.04 us
    ppermute x7, waiting for transfers between devices, shift(): return lax.ppermute(v, axis, [(i, (i + by) % size) for i in range(size)])  3.37 us
  transfers between devices with their start and end apart: 9, of which 4 were waited for; matrix products, arithmetic and copies ran while one was open for 1% of the time, Pallas kernels for 10%

profile of v12, /device:TPU:1, one launch (start us, length us, event | category | flops | bytes accessed | tf_op | source)
XLA Modules:
  0.0 132.1 jit_solution(5612531841598144068)
XLA Ops:
  0.7 0.8 constant_dynamic-slice_fusion.3
  1.6 28.1 %all_to_all.20 = bf16[8,24,1536]{2,1,0:T(8,128)(2,1)S(1)} all-to-all(bf16[8,24,1536]{2,1,0:T(8,128)(2,1)S(1)} %broadcast_in_dim.6), channel_id=1, replica_groups=mesh['y'=8,'core'=2,'x'=4,'z'=8] {'z'}, dimensions={0} | all-to-all | bytes 1179648 | tf_op jit(solution)/shard_map/all_to_all | solution.py:271
  29.7 4.4 %collective-permute-start.2 = (bf16[192,1536]{1,0:T(8,128)(2,1)S(1)}, bf16[192,1536]{1,0:T(8,128)(2,1)S(1)}, u32[]{:S(2)}, u32[]{:S(2)}) collective-permute-start(bf16[192,1536]{1,0:T(8,128)(2,1)S(1)} %bitcast.31), channel_id=1, source_target_pairs={{0,24},{8,0},{16,8},{24,16},{1,25},{9,1},{17,9},{25,17},{2,26},{10... | collective-permute-start | bytes 1769480 | tf_op jit(solution)/shard_map/ppermute | solution.py:267
  34.1 1.9 %collective-permute-start.1 = (bf16[192,1536]{1,0:T(8,128)(2,1)S(1)}, bf16[192,1536]{1,0:T(8,128)(2,1)S(1)}, u32[]{:S(2)}, u32[]{:S(2)}) collective-permute-start(bf16[192,1536]{1,0:T(8,128)(2,1)S(1)} %bitcast.32), channel_id=1, source_target_pairs={{0,8},{8,16},{16,24},{24,0},{1,9},{9,17},{17,25},{25,1},{2,10},{10... | collective-permute-start | bytes 1769480 | tf_op jit(solution)/shard_map/ppermute | solution.py:267
  36.0 0.8 pad_maximum_fusion
  36.8 9.8 %all-to-all-start.1 = ((bf16[16,8,1536]{2,1,0:T(8,128)(2,1)}), bf16[16,8,1536]{2,1,0:T(8,128)(2,1)S(1)}, u32[]{:S(2)}, u32[]{:S(2)}) async-start(bf16[16,8,1536]{2,1,0:T(8,128)(2,1)} %pad_maximum_fusion), calls=%async_computation.1 | async-start | bytes 786432 | tf_op jit(solution)/shard_map/all_to_all | solution.py:271
  46.6 0.0 collective-permute-done.2.refs_5_
  46.6 4.9 %collective-permute-start.4 = (bf16[96,1536]{1,0:T(8,128)(2,1)S(1)}, bf16[96,1536]{1,0:T(8,128)(2,1)}, u32[]{:S(2)}, u32[]{:S(2)}) collective-permute-start(bf16[96,1536]{1,0:T(8,128)(2,1)S(1)} %slice.25), channel_id=1, source_target_pairs={{0,24},{8,0},{16,8},{24,16},{1,25},{9,1},{17,9},{25,17},{2,26},{10... | collective-permute-start | bytes 884744 | tf_op jit(solution)/shard_map/ppermute | solution.py:267
  51.5 0.0 collective-permute-done.1.refs_4_
  51.5 1.9 %collective-permute-start.3 = (bf16[96,1536]{1,0:T(8,128)(2,1)S(1)}, bf16[96,1536]{1,0:T(8,128)(2,1)}, u32[]{:S(2)}, u32[]{:S(2)}) collective-permute-start(bf16[96,1536]{1,0:T(8,128)(2,1)S(1)} %slice.24), channel_id=1, source_target_pairs={{0,8},{8,16},{16,24},{24,0},{1,9},{9,17},{17,25},{25,1},{2,10},{10... | collective-permute-start | bytes 884744 | tf_op jit(solution)/shard_map/ppermute | solution.py:267
  53.5 7.7 %all-to-all-done.1 = bf16[16,8,1536]{2,1,0:T(8,128)(2,1)S(1)} async-done(((bf16[16,8,1536]{2,1,0:T(8,128)(2,1)}), bf16[16,8,1536]{2,1,0:T(8,128)(2,1)S(1)}, u32[]{:S(2)}, u32[]{:S(2)}) %all-to-all-start.1) | async-done | bytes 393248 | tf_op jit(solution)/shard_map/all_to_all | solution.py:271
  61.1 1.9 %collective-permute-start = (bf16[128,1536]{1,0:T(8,128)(2,1)S(1)}, bf16[128,1536]{1,0:T(8,128)(2,1)S(1)}, u32[]{:S(2)}, u32[]{:S(2)}) collective-permute-start(bf16[128,1536]{1,0:T(8,128)(2,1)S(1)} %bitcast.23), channel_id=1, source_target_pairs={{0,32},{32,0},{1,33},{33,1},{2,34},{34,2},{3,35},{35,3},{4,36},{36... | collective-permute-start | bytes 1179656 | tf_op jit(solution)/shard_map/ppermute | solution.py:267
  63.1 0.0 collective-permute-done.4.refs_7_
  63.1 0.0 collective-permute-done.3.refs_6_
  63.1 4.5 %shard_map.85 = (bf16[128,1152]{1,0:T(8,128)(2,1)}, f32[3,256,128]{2,1,0:T(8,128)}, bf16[128,384]{1,0:T(8,128)(2,1)}, bf16[768,1152]{1,0:T(8,128)(2,1)}, bf16[38...) custom-call(s32[2]{0:T(128)} %refs_0_.7, bf16[128,1536]{1,0:T(8,128)(2,1)} %bitcast.24, f32[768]{0:T(1024)} %refs_2_.3, ...), custom_call_target="tpu_custom_call" | custom-call | flops 8000000000 | bytes 3542024 | tf_op jit(solution)/shard_map/pallas_call | solution.py:251
  67.7 0.8 copy-done.3
  68.4 5.1 %shard_map.86 = (bf16[128,1152]{1,0:T(8,128)(2,1)}, f32[3,256,128]{2,1,0:T(8,128)}, bf16[128,384]{1,0:T(8,128)(2,1)}, bf16[768,384]{1,0:T(8,128)(2,1)}, bf16[768,384]{1,0:T(8,128)(2,1)}) custom-call(s32[2]{0:T(128)} %refs_0_.7, bf16[128,1536]{1,0:T(8,128)(2,1)} %bitcast.25, bf16[128,1536]{1,0:T(8,128)(2,1)} %copy-done.3, f32[768]{0:T(1024)} %refs_2_.3, ...), custom_call_target="tpu_custom_call" | custom-call | flops 8000000000 | bytes 3148808 | tf_op jit(solution)/shard_map/pallas_call | solution.py:251
  73.5 3.0 %collective-permute-start.5 = (bf16[768,384]{1,0:T(8,128)(2,1)}, bf16[768,384]{1,0:T(8,128)(2,1)S(1)}, u32[]{:S(2)}, u32[]{:S(2)}) collective-permute-start(bf16[768,384]{1,0:T(8,128)(2,1)} %get-tuple-element.22), channel_id=1, source_target_pairs={{0,32},{32,0},{1,33},{33,1},{2,34},{34,2},{3,35},{35,3},{4,36},{36... | collective-permute-start | bytes 1769480 | tf_op jit(solution)/shard_map/ppermute | solution.py:267
  76.5 1.8 %collective-permute-done.5.refs_4_ = bf16[768,384]{1,0:T(8,128)(2,1)S(1)} collective-permute-done((bf16[768,384]{1,0:T(8,128)(2,1)}, bf16[768,384]{1,0:T(8,128)(2,1)S(1)}, u32[]{:S(2)}, u32[]{:S(2)}) %collective-permute-start.5) | collective-permute-done | bytes 589856 | tf_op jit(solution)/shard_map/ppermute | solution.py:267
  78.3 0.8 slice_dynamic-update-slice_fusion.refs_12_
  79.1 4.0 %all-to-all-start.2 = ((bf16[32,24,384]{2,1,0:T(8,128)(2,1)}), bf16[32,24,384]{2,1,0:T(8,128)(2,1)S(1)}, u32[]{:S(2)}, u32[]{:S(2)}) async-start(bf16[32,24,384]{2,1,0:T(8,128)(2,1)} %bitcast.29), calls=%async_computation.2 | async-start | bytes 1179648 | tf_op jit(solution)/shard_map/all_to_all | solution.py:271
  83.2 6.8 %shard_map.87 = (f32[128,1536]{1,0:T(8,128)}, bf16[128,1536]{1,0:T(8,128)(2,1)}) custom-call(s32[2]{0:T(128)} %refs_0_.7, bf16[128,1536]{1,0:T(8,128)(2,1)} %bitcast.26, bf16[128,1536]{1,0:T(8,128)(2,1)} %copy-done.3, bf16[384,384]{1,0:T(8,128)(2,1)} %get-tuple-element.18.refs_3_, bf16[768,384]{1,0:T(8,128)(2,1)} %copy-done.1, ...), custom_call_target="tpu_custom_call" | custom-call | flops 1000 | bytes 6193160 | tf_op jit(solution)/shard_map/pallas_call | solution.py:251
  90.0 2.5 %collective-permute-start.6 = (bf16[128,1536]{1,0:T(8,128)(2,1)}, bf16[128,1536]{1,0:T(8,128)(2,1)S(1)}, u32[]{:S(2)}, u32[]{:S(2)}) collective-permute-start(bf16[128,1536]{1,0:T(8,128)(2,1)} %get-tuple-element.30), channel_id=1, source_target_pairs={{0,32},{32,0},{1,33},{33,1},{2,34},{34,2},{3,35},{35,3},{4,36},{36... | collective-permute-start | bytes 1179656 | tf_op jit(solution)/shard_map/ppermute | solution.py:267
  92.5 1.5 %collective-permute-done.6.refs_4_ = bf16[128,1536]{1,0:T(8,128)(2,1)S(1)} collective-permute-done((bf16[128,1536]{1,0:T(8,128)(2,1)}, bf16[128,1536]{1,0:T(8,128)(2,1)S(1)}, u32[]{:S(2)}, u32[]{:S(2)}) %collective-permute-start.6) | collective-permute-done | bytes 393248 | tf_op jit(solution)/shard_map/ppermute | solution.py:267
  94.1 0.8 copy-done.4
  94.8 2.5 %shard_map.88 = bf16[128,2688]{1,0:T(8,128)(2,1)} custom-call(s32[2]{0:T(128)} %refs_0_.7, bf16[128,1536]{1,0:T(8,128)(2,1)} %bitcast.27, f32[768]{0:T(1024)} %refs_2_.3, f32[128,1536]{1,0:T(8,128)} %get-tuple-element.29.refs_3_, bf16[128,1536]{1,0:T(8,128)(2,1)} %copy-done.4), custom_call_target="tpu_custom_call" | custom-call | flops 1000 | bytes 2264072 | tf_op jit(solution)/shard_map/pallas_call | solution.py:251
  97.4 1.4 %all-to-all-done.2 = bf16[32,24,384]{2,1,0:T(8,128)(2,1)S(1)} async-done(((bf16[32,24,384]{2,1,0:T(8,128)(2,1)}), bf16[32,24,384]{2,1,0:T(8,128)(2,1)S(1)}, u32[]{:S(2)}, u32[]{:S(2)}) %all-to-all-start.2) | async-done | bytes 589856 | tf_op jit(solution)/shard_map/all_to_all | solution.py:271
  98.7 0.1 reduce_sum.21
  98.8 0.8 broadcast_dynamic-update-slice_fusion
  99.6 31.0 %all_to_all.21 = bf16[16,8,2688]{2,1,0:T(8,128)(2,1)S(1)} all-to-all(bf16[16,8,2688]{2,1,0:T(8,128)(2,1)} %broadcast_dynamic-update-slice_fusion), channel_id=1, replica_groups=mesh['y'=8,'core'=2,'x'=4,'z'=8] {'y','core'}, dimensions={0} | all-to-all | bytes 1376256 | tf_op jit(solution)/shard_map/all_to_all | solution.py:271
  130.7 0.6 copy.10
  131.3 0.8 slice_bitcast_fusion
  (24 shorter events, 0.2 us)
Async XLA Ops:
  0.6 35.4 %copy-start.5 = (bf16[1,128,768]{2,1,0:T(8,128)(2,1)S(1)}, bf16[1,128,768]{2,1,0:T(8,128)(2,1)}, u32[]{:S(2)}) copy-start(bf16[1,128,768]{2,1,0:T(8,128)(2,1)} %param.7) | copy-start | bytes 589828
  0.6 35.4 %copy-start.6 = (bf16[1,128,768]{2,1,0:T(8,128)(2,1)S(1)}, bf16[1,128,768]{2,1,0:T(8,128)(2,1)}, u32[]{:S(2)}) copy-start(bf16[1,128,768]{2,1,0:T(8,128)(2,1)} %param.6) | copy-start | bytes 589828
  29.7 33.4 %copy-start.2 = (bf16[8,24,1536]{2,1,0:T(8,128)(2,1)}, bf16[8,24,1536]{2,1,0:T(8,128)(2,1)S(1)}, u32[]{:S(2)}) copy-start(bf16[8,24,1536]{2,1,0:T(8,128)(2,1)S(1)} %all_to_all.20) | copy-start | bytes 1769476
  29.7 16.9 %collective-permute-start.2 = (bf16[192,1536]{1,0:T(8,128)(2,1)S(1)}, bf16[192,1536]{1,0:T(8,128)(2,1)S(1)}, u32[]{:S(2)}, u32[]{:S(2)}) collective-permute-start(bf16[192,1536]{1,0:T(8,128)(2,1)S(1)} %bitcast.31), channel_id=1, source_target_pairs={{0,24},{8,0},{16,8},{24,16},{1,25},{9,1},{17,9},{25,17},{2,26},{10... | collective-permute-start | bytes 1769480 | tf_op jit(solution)/shard_map/ppermute | solution.py:267
  34.1 17.4 %collective-permute-start.1 = (bf16[192,1536]{1,0:T(8,128)(2,1)S(1)}, bf16[192,1536]{1,0:T(8,128)(2,1)S(1)}, u32[]{:S(2)}, u32[]{:S(2)}) collective-permute-start(bf16[192,1536]{1,0:T(8,128)(2,1)S(1)} %bitcast.32), channel_id=1, source_target_pairs={{0,8},{8,16},{16,24},{24,0},{1,9},{9,17},{17,25},{25,1},{2,10},{10... | collective-permute-start | bytes 1769480 | tf_op jit(solution)/shard_map/ppermute | solution.py:267
  36.8 24.4 %all-to-all-start.1 = ((bf16[16,8,1536]{2,1,0:T(8,128)(2,1)}), bf16[16,8,1536]{2,1,0:T(8,128)(2,1)S(1)}, u32[]{:S(2)}, u32[]{:S(2)}) async-start(bf16[16,8,1536]{2,1,0:T(8,128)(2,1)} %pad_maximum_fusion), calls=%async_computation.1 | async-start | bytes 786432 | tf_op jit(solution)/shard_map/all_to_all | solution.py:271
  46.6 16.5 %copy-start.7 = (bf16[192,1536]{1,0:T(8,128)(2,1)}, bf16[192,1536]{1,0:T(8,128)(2,1)S(1)}, u32[]{:S(2)}) copy-start(bf16[192,1536]{1,0:T(8,128)(2,1)S(1)} %collective-permute-done.2.refs_5_) | copy-start | bytes 1769476
  46.6 16.4 %collective-permute-start.4 = (bf16[96,1536]{1,0:T(8,128)(2,1)S(1)}, bf16[96,1536]{1,0:T(8,128)(2,1)}, u32[]{:S(2)}, u32[]{:S(2)}) collective-permute-start(bf16[96,1536]{1,0:T(8,128)(2,1)S(1)} %slice.25), channel_id=1, source_target_pairs={{0,24},{8,0},{16,8},{24,16},{1,25},{9,1},{17,9},{25,17},{2,26},{10... | collective-permute-start | bytes 884744 | tf_op jit(solution)/shard_map/ppermute | solution.py:267
  51.5 11.6 %copy-start.8 = (bf16[192,1536]{1,0:T(8,128)(2,1)}, bf16[192,1536]{1,0:T(8,128)(2,1)S(1)}, u32[]{:S(2)}) copy-start(bf16[192,1536]{1,0:T(8,128)(2,1)S(1)} %collective-permute-done.1.refs_4_) | copy-start | bytes 1769476
  51.5 11.5 %collective-permute-start.3 = (bf16[96,1536]{1,0:T(8,128)(2,1)S(1)}, bf16[96,1536]{1,0:T(8,128)(2,1)}, u32[]{:S(2)}, u32[]{:S(2)}) collective-permute-start(bf16[96,1536]{1,0:T(8,128)(2,1)S(1)} %slice.24), channel_id=1, source_target_pairs={{0,8},{8,16},{16,24},{24,0},{1,9},{9,17},{17,25},{25,1},{2,10},{10... | collective-permute-start | bytes 884744 | tf_op jit(solution)/shard_map/ppermute | solution.py:267
  61.1 2.0 %copy-start = (bf16[16,8,1536]{2,1,0:T(8,128)(2,1)}, bf16[16,8,1536]{2,1,0:T(8,128)(2,1)S(1)}, u32[]{:S(2)}) copy-start(bf16[16,8,1536]{2,1,0:T(8,128)(2,1)S(1)} %all-to-all-done.1) | copy-start | bytes 1179652
  61.1 6.5 %collective-permute-start = (bf16[128,1536]{1,0:T(8,128)(2,1)S(1)}, bf16[128,1536]{1,0:T(8,128)(2,1)S(1)}, u32[]{:S(2)}, u32[]{:S(2)}) collective-permute-start(bf16[128,1536]{1,0:T(8,128)(2,1)S(1)} %bitcast.23), channel_id=1, source_target_pairs={{0,32},{32,0},{1,33},{33,1},{2,34},{34,2},{3,35},{35,3},{4,36},{36... | collective-permute-start | bytes 1179656 | tf_op jit(solution)/shard_map/ppermute | solution.py:267
  67.7 0.8 copy-start.3
  73.5 4.8 %collective-permute-start.5 = (bf16[768,384]{1,0:T(8,128)(2,1)}, bf16[768,384]{1,0:T(8,128)(2,1)S(1)}, u32[]{:S(2)}, u32[]{:S(2)}) collective-permute-start(bf16[768,384]{1,0:T(8,128)(2,1)} %get-tuple-element.22), channel_id=1, source_target_pairs={{0,32},{32,0},{1,33},{33,1},{2,34},{34,2},{3,35},{35,3},{4,36},{36... | collective-permute-start | bytes 1769480 | tf_op jit(solution)/shard_map/ppermute | solution.py:267
  78.3 4.8 %copy-start.1 = (bf16[768,384]{1,0:T(8,128)(2,1)}, bf16[768,384]{1,0:T(8,128)(2,1)S(1)}, u32[]{:S(2)}) copy-start(bf16[768,384]{1,0:T(8,128)(2,1)S(1)} %collective-permute-done.5.refs_4_) | copy-start | bytes 1769476
  79.1 19.6 %all-to-all-start.2 = ((bf16[32,24,384]{2,1,0:T(8,128)(2,1)}), bf16[32,24,384]{2,1,0:T(8,128)(2,1)S(1)}, u32[]{:S(2)}, u32[]{:S(2)}) async-start(bf16[32,24,384]{2,1,0:T(8,128)(2,1)} %bitcast.29), calls=%async_computation.2 | async-start | bytes 1179648 | tf_op jit(solution)/shard_map/all_to_all | solution.py:271
  90.0 4.1 %collective-permute-start.6 = (bf16[128,1536]{1,0:T(8,128)(2,1)}, bf16[128,1536]{1,0:T(8,128)(2,1)S(1)}, u32[]{:S(2)}, u32[]{:S(2)}) collective-permute-start(bf16[128,1536]{1,0:T(8,128)(2,1)} %get-tuple-element.30), channel_id=1, source_target_pairs={{0,32},{32,0},{1,33},{33,1},{2,34},{34,2},{3,35},{35,3},{4,36},{36... | collective-permute-start | bytes 1179656 | tf_op jit(solution)/shard_map/ppermute | solution.py:267
  94.1 0.8 copy-start.4

commit v13 on v11

--- a/solution.py
+++ b/solution.py
@@ -141,7 +141,6 @@
     gain_ref,
     w_ref,
     own_att_ref,
-    wo_give_ref,
     qkv_ref,
     p_ref,
     att_ref,
@@ -157,8 +156,7 @@
     att = jnp.concatenate([own_att_ref[...], att_ref[...]])
     keep = dot_tn(att, jnp.where(first, low_cols, high_cols))
     gw_ref[pl.ds(pl.multiple_of(core * mid, mid), mid), :] = keep.astype(jnp.bfloat16)
-    give_ref[:mid, :] = dot_tn(att, jnp.where(first, high_cols, low_cols)).astype(jnp.bfloat16)
-    give_ref[mid:, :] = wo_give_ref[...]
+    give_ref[...] = dot_tn(att, jnp.where(first, high_cols, low_cols)).astype(jnp.bfloat16)
 
 
 def bwd_kernel(
@@ -185,14 +183,14 @@
     mine, mid = own_att_ref.shape[1], width // 2
     first = lax.axis_index("core") == 0
     att = jnp.concatenate([own_att_ref[...], near_att_ref[...]])
-    kept, got = dot_nn(att, wo_ref[...]), dot_nn(att, got_ref[mid:, :])
+    kept, got = dot_nn(att, wo_ref[...]), dot_nn(att, got_ref[...])
     for at, part in ((0, jnp.where(first, kept, got)), (mid, jnp.where(first, got, kept))):
         sum_ref[:, at : at + mid] = part[:rows]
         other_ref[:, at : at + mid] = part[rows:].astype(jnp.bfloat16)
     gz = masked_grad(frames, slot_len, lengths, own_ref, near_ref)
     low_cols, high_cols = gz[:, :mid], gz[:, mid:]
     ga_all = dot_nt(jnp.where(first, low_cols, high_cols), wo_ref[...])
-    ga_all += dot_nt(jnp.where(first, high_cols, low_cols), got_ref[mid:, :])
+    ga_all += dot_nt(jnp.where(first, high_cols, low_cols), got_ref[...])
     ga_all = ga_all.astype(jnp.bfloat16)
     sets = ((0, own_qkv_ref, own_p_ref), (rows, near_qkv_ref, near_p_ref))
     for start, qkv_ref, p_ref in sets:
@@ -304,21 +302,22 @@
     )
     near_qkv, near_p, near_att, give, gw = call(
         lambda *refs: near_kernel(*spots, *refs),
-        results + (shape((width, cut), bf), shape((width, cut), bf)),
+        results + (shape((cut, cut), bf), shape((width, cut), bf)),
         (),
         NEAR_COST,
-        lengths, own, near, norm_gain, w, own_att, wo_give,
+        lengths, own, near, norm_gain, w, own_att,
     )
 
     got = shift(give, "core", 1)
-    term = lax.dynamic_update_slice(gw, got[:cut], ((1 - core_at) * cut, 0))
+    wo_got = shift(wo_give, "core", 1)
+    term = lax.dynamic_update_slice(gw, got, ((1 - core_at) * cut, 0))
 
     sum_part, other_part = call(
         lambda *refs: bwd_kernel(*spots, *refs),
         (shape((rows, 2 * width), f32), shape((rows, 2 * width), bf)),
         (pltpu.VMEM((2 * rows, half), bf),),
         BWD_COST,
-        lengths, own, near, wo, got, own_att, near_att, own_qkv, near_qkv, own_p, near_p, w,
+        lengths, own, near, wo, wo_got, own_att, near_att, own_qkv, near_qkv, own_p, near_p, w,
         behind=(term,),
     )
     term = exchange(term.reshape(tms, piece, cut), TM)

time: 131 us -> 131 us (level)
  blocking collectives: 59.1 us -> 55.7 us
  starting transfers between devices: 34.3 us -> 36.7 us
    all_to_all x2, blocking collectives: 59.1 us -> 55.7 us  [exchange(): return lax.all_to_all(v, axes, split_axis=0, concat_axis=0, tiled=True)]
    ppermute x7 -> x8, starting transfers between devices: 20.5 us -> 22.3 us  [shift(): return lax.ppermute(v, axis, [(i, (i + by) % size) for i in range(size)])]
    all_to_all x2, waiting for transfers between devices: 9.04 us -> 7.67 us  [exchange(): return lax.all_to_all(v, axes, split_axis=0, concat_axis=0, tiled=True)]
    unnamed x19 -> x23, local copies, waits for them, and re-layouts: 2.19 us -> 3.55 us
    ppermute x7 -> x8, waiting for transfers between devices: 3.37 us -> 4.14 us  [shift(): return lax.ppermute(v, axis, [(i, (i + by) % size) for i in range(size)])]
  transfers between devices with their start and end apart: 9 -> 10, of which waited for: 4 -> 4; matrix products, arithmetic and copies ran while one was open for 1% -> 1% of each run, Pallas kernels for 10% -> 10%
where the time goes in v13:
time: 131 us; the launch traced here: 130 us
  blocking collectives  55.7 us (43%)
  starting transfers between devices  36.7 us (28%)
  Pallas kernels  17.2 us (13%)
  waiting for transfers between devices  11.8 us (9%)
  local copies, waits for them, and re-layouts  6.82 us (5%)
    all_to_all x2, blocking collectives, exchange(): return lax.all_to_all(v, axes, split_axis=0, concat_axis=0, tiled=True)  55.7 us
    ppermute x8, starting transfers between devices, shift(): return lax.ppermute(v, axis, [(i, (i + by) % size) for i in range(size)])  22.3 us
    pallas_call x4, Pallas kernels, call(): pl.pallas_call(kernel, out_shape=outs, in_specs=[pl.BlockSpec(memory_spac...  17.2 us
    all_to_all x2, starting transfers between devices, exchange(): return lax.all_to_all(v, axes, split_axis=0, concat_axis=0, tiled=True)  14.4 us
    all_to_all x2, waiting for transfers between devices, exchange(): return lax.all_to_all(v, axes, split_axis=0, concat_axis=0, tiled=True)  7.67 us
    ppermute x8, waiting for transfers between devices, shift(): return lax.ppermute(v, axis, [(i, (i + by) % size) for i in range(size)])  4.14 us
    unnamed x23, local copies, waits for them, and re-layouts  3.55 us
  transfers between devices with their start and end apart: 10, of which 4 were waited for; matrix products, arithmetic and copies ran while one was open for 1% of the time, Pallas kernels for 10%

profile of v13, /device:TPU:1, one launch (start us, length us, event | category | flops | bytes accessed | tf_op | source)
XLA Modules:
  0.0 130.1 jit_solution(10482411053586661904)
XLA Ops:
  0.7 0.8 constant_dynamic-slice_fusion.3
  1.6 28.1 %all_to_all.20 = bf16[8,24,1536]{2,1,0:T(8,128)(2,1)S(1)} all-to-all(bf16[8,24,1536]{2,1,0:T(8,128)(2,1)S(1)} %broadcast_in_dim.6), channel_id=1, replica_groups=mesh['y'=8,'core'=2,'x'=4,'z'=8] {'z'}, dimensions={0} | all-to-all | bytes 1179648 | tf_op jit(solution)/shard_map/all_to_all | solution.py:253
  29.7 4.4 %collective-permute-start.2 = (bf16[192,1536]{1,0:T(8,128)(2,1)S(1)}, bf16[192,1536]{1,0:T(8,128)(2,1)S(1)}, u32[]{:S(2)}, u32[]{:S(2)}) collective-permute-start(bf16[192,1536]{1,0:T(8,128)(2,1)S(1)} %bitcast.31), channel_id=1, source_target_pairs={{0,24},{8,0},{16,8},{24,16},{1,25},{9,1},{17,9},{25,17},{2,26},{10... | collective-permute-start | bytes 1769480 | tf_op jit(solution)/shard_map/ppermute | solution.py:249
  34.1 1.9 %collective-permute-start.1 = (bf16[192,1536]{1,0:T(8,128)(2,1)S(1)}, bf16[192,1536]{1,0:T(8,128)(2,1)S(1)}, u32[]{:S(2)}, u32[]{:S(2)}) collective-permute-start(bf16[192,1536]{1,0:T(8,128)(2,1)S(1)} %bitcast.32), channel_id=1, source_target_pairs={{0,8},{8,16},{16,24},{24,0},{1,9},{9,17},{17,25},{25,1},{2,10},{10... | collective-permute-start | bytes 1769480 | tf_op jit(solution)/shard_map/ppermute | solution.py:249
  36.0 0.8 pad_maximum_fusion
  36.8 9.8 %all-to-all-start.1 = ((bf16[16,8,1536]{2,1,0:T(8,128)(2,1)}), bf16[16,8,1536]{2,1,0:T(8,128)(2,1)S(1)}, u32[]{:S(2)}, u32[]{:S(2)}) async-start(bf16[16,8,1536]{2,1,0:T(8,128)(2,1)} %pad_maximum_fusion), calls=%async_computation.1 | async-start | bytes 786432 | tf_op jit(solution)/shard_map/all_to_all | solution.py:253
  46.6 0.0 collective-permute-done.2.refs_5_
  46.6 4.9 %collective-permute-start.4 = (bf16[96,1536]{1,0:T(8,128)(2,1)S(1)}, bf16[96,1536]{1,0:T(8,128)(2,1)S(1)}, u32[]{:S(2)}, u32[]{:S(2)}) collective-permute-start(bf16[96,1536]{1,0:T(8,128)(2,1)S(1)} %slice.21), channel_id=1, source_target_pairs={{0,24},{8,0},{16,8},{24,16},{1,25},{9,1},{17,9},{25,17},{2,26},{10... | collective-permute-start | bytes 884744 | tf_op jit(solution)/shard_map/ppermute | solution.py:249
  51.5 1.9 %collective-permute-start.3 = (bf16[96,1536]{1,0:T(8,128)(2,1)S(1)}, bf16[96,1536]{1,0:T(8,128)(2,1)}, u32[]{:S(2)}, u32[]{:S(2)}) collective-permute-start(bf16[96,1536]{1,0:T(8,128)(2,1)S(1)} %slice.20), channel_id=1, source_target_pairs={{0,8},{8,16},{16,24},{24,0},{1,9},{9,17},{17,25},{25,1},{2,10},{10... | collective-permute-start | bytes 884744 | tf_op jit(solution)/shard_map/ppermute | solution.py:249
  53.5 7.7 %all-to-all-done.1 = bf16[16,8,1536]{2,1,0:T(8,128)(2,1)S(1)} async-done(((bf16[16,8,1536]{2,1,0:T(8,128)(2,1)}), bf16[16,8,1536]{2,1,0:T(8,128)(2,1)S(1)}, u32[]{:S(2)}, u32[]{:S(2)}) %all-to-all-start.1) | async-done | bytes 393248 | tf_op jit(solution)/shard_map/all_to_all | solution.py:253
  61.1 1.9 %collective-permute-start = (bf16[128,1536]{1,0:T(8,128)(2,1)S(1)}, bf16[128,1536]{1,0:T(8,128)(2,1)S(1)}, u32[]{:S(2)}, u32[]{:S(2)}) collective-permute-start(bf16[128,1536]{1,0:T(8,128)(2,1)S(1)} %bitcast.23), channel_id=1, source_target_pairs={{0,32},{32,0},{1,33},{33,1},{2,34},{34,2},{3,35},{35,3},{4,36},{36... | collective-permute-start | bytes 1179656 | tf_op jit(solution)/shard_map/ppermute | solution.py:249
  63.1 0.7 copy-done.10
  63.8 4.0 %shard_map.85 = (bf16[128,1152]{1,0:T(8,128)(2,1)}, f32[3,256,128]{2,1,0:T(8,128)}, bf16[128,384]{1,0:T(8,128)(2,1)}, bf16[768,1152]{1,0:T(8,128)(2,1)}, bf16[38...) custom-call(s32[2]{0:T(128)} %refs_0_.7, bf16[128,1536]{1,0:T(8,128)(2,1)} %bitcast.24, f32[768]{0:T(1024)} %refs_2_.3, ...), custom_call_target="tpu_custom_call" | custom-call | flops 8000000000 | bytes 5901320 | tf_op jit(solution)/shard_map/pallas_call | solution.py:233
  67.8 0.7 copy-done.3
  68.6 4.0 %shard_map.86 = (bf16[128,1152]{1,0:T(8,128)(2,1)}, f32[3,256,128]{2,1,0:T(8,128)}, bf16[128,384]{1,0:T(8,128)(2,1)}, bf16[384,384]{1,0:T(8,128)(2,1)}, bf16[768,384]{1,0:T(8,128)(2,1)}) custom-call(s32[2]{0:T(128)} %refs_0_.7, bf16[128,1536]{1,0:T(8,128)(2,1)} %bitcast.25, bf16[128,1536]{1,0:T(8,128)(2,1)} %copy-done.3, f32[768]{0:T(1024)} %refs_2_.3, ...), custom_call_target="tpu_custom_call" | custom-call | flops 8000000000 | bytes 4328456 | tf_op jit(solution)/shard_map/pallas_call | solution.py:233
  72.6 2.5 %collective-permute-start.6 = (bf16[384,384]{1,0:T(8,128)(2,1)}, bf16[384,384]{1,0:T(8,128)(2,1)S(1)}, u32[]{:S(2)}, u32[]{:S(2)}) collective-permute-start(bf16[384,384]{1,0:T(8,128)(2,1)} %get-tuple-element.28), channel_id=1, source_target_pairs={{0,32},{32,0},{1,33},{33,1},{2,34},{34,2},{3,35},{35,3},{4,36},{36... | collective-permute-start | bytes 884744 | tf_op jit(solution)/shard_map/ppermute | solution.py:249
  75.1 1.4 %collective-permute-done.6 = bf16[384,384]{1,0:T(8,128)(2,1)S(1)} collective-permute-done((bf16[384,384]{1,0:T(8,128)(2,1)}, bf16[384,384]{1,0:T(8,128)(2,1)S(1)}, u32[]{:S(2)}, u32[]{:S(2)}) %collective-permute-start.6) | collective-permute-done | bytes 294944 | tf_op jit(solution)/shard_map/ppermute | solution.py:249
  76.5 0.8 constant_dynamic-update-slice_fusion.refs_12_
  77.3 4.6 %all-to-all-start.2 = ((bf16[32,24,384]{2,1,0:T(8,128)(2,1)}), bf16[32,24,384]{2,1,0:T(8,128)(2,1)S(1)}, u32[]{:S(2)}, u32[]{:S(2)}) async-start(bf16[32,24,384]{2,1,0:T(8,128)(2,1)} %bitcast.29), calls=%async_computation.2 | async-start | bytes 1179648 | tf_op jit(solution)/shard_map/all_to_all | solution.py:253
  81.9 2.5 %collective-permute-start.5 = (bf16[384,384]{1,0:T(8,128)(2,1)S(1)}, bf16[384,384]{1,0:T(8,128)(2,1)S(1)}, u32[]{:S(2)}, u32[]{:S(2)}) collective-permute-start(bf16[384,384]{1,0:T(8,128)(2,1)S(1)} %copy-done.9), channel_id=1, source_target_pairs={{0,32},{32,0},{1,33},{33,1},{2,34},{34,2},{3,35},{35,3},{4,36},{36... | collective-permute-start | bytes 884744 | tf_op jit(solution)/shard_map/ppermute | solution.py:249
  84.5 1.2 collective-permute-done.5.refs_4_
  85.6 0.7 copy-done.4
  86.4 6.6 %shard_map.87 = (f32[128,1536]{1,0:T(8,128)}, bf16[128,1536]{1,0:T(8,128)(2,1)}) custom-call(s32[2]{0:T(128)} %refs_0_.7, bf16[128,1536]{1,0:T(8,128)(2,1)} %bitcast.26, bf16[128,1536]{1,0:T(8,128)(2,1)} %copy-done.3, bf16[384,384]{1,0:T(8,128)(2,1)} %get-tuple-element.18.refs_3_, bf16[384,384]{1,0:T(8,128)(2,1)} %copy-done.4, ...), custom_call_target="tpu_custom_call" | custom-call | flops 1000 | bytes 5898248 | tf_op jit(solution)/shard_map/pallas_call | solution.py:233
  93.0 2.3 %collective-permute-start.7 = (bf16[128,1536]{1,0:T(8,128)(2,1)}, bf16[128,1536]{1,0:T(8,128)(2,1)S(1)}, u32[]{:S(2)}, u32[]{:S(2)}) collective-permute-start(bf16[128,1536]{1,0:T(8,128)(2,1)} %get-tuple-element.30), channel_id=1, source_target_pairs={{0,32},{32,0},{1,33},{33,1},{2,34},{34,2},{3,35},{35,3},{4,36},{36... | collective-permute-start | bytes 1179656 | tf_op jit(solution)/shard_map/ppermute | solution.py:249
  95.3 1.5 %collective-permute-done.7.refs_4_ = bf16[128,1536]{1,0:T(8,128)(2,1)S(1)} collective-permute-done((bf16[128,1536]{1,0:T(8,128)(2,1)}, bf16[128,1536]{1,0:T(8,128)(2,1)S(1)}, u32[]{:S(2)}, u32[]{:S(2)}) %collective-permute-start.7) | collective-permute-done | bytes 393248 | tf_op jit(solution)/shard_map/ppermute | solution.py:249
  96.8 0.8 copy-done.2
  97.6 2.5 %shard_map.88 = bf16[128,2688]{1,0:T(8,128)(2,1)} custom-call(s32[2]{0:T(128)} %refs_0_.7, bf16[128,1536]{1,0:T(8,128)(2,1)} %bitcast.27, f32[768]{0:T(1024)} %refs_2_.3, f32[128,1536]{1,0:T(8,128)} %get-tuple-element.29.refs_3_, bf16[128,1536]{1,0:T(8,128)(2,1)} %copy-done.2), custom_call_target="tpu_custom_call" | custom-call | flops 1000 | bytes 2264072 | tf_op jit(solution)/shard_map/pallas_call | solution.py:233
  100.1 0.1 reduce_sum.21
  100.2 0.7 broadcast_dynamic-update-slice_fusion
  101.0 27.6 %all_to_all.21 = bf16[16,8,2688]{2,1,0:T(8,128)(2,1)S(1)} all-to-all(bf16[16,8,2688]{2,1,0:T(8,128)(2,1)} %broadcast_dynamic-update-slice_fusion), channel_id=1, replica_groups=mesh['y'=8,'core'=2,'x'=4,'z'=8] {'y','core'}, dimensions={0} | all-to-all | bytes 1376256 | tf_op jit(solution)/shard_map/all_to_all | solution.py:253
  128.7 0.6 copy.10
  129.3 0.8 slice_bitcast_fusion
  (30 shorter events, 0.2 us)
Async XLA Ops:
  0.6 35.4 %copy-start.5 = (bf16[1,128,768]{2,1,0:T(8,128)(2,1)S(1)}, bf16[1,128,768]{2,1,0:T(8,128)(2,1)}, u32[]{:S(2)}) copy-start(bf16[1,128,768]{2,1,0:T(8,128)(2,1)} %param.7) | copy-start | bytes 589828
  0.6 35.4 %copy-start.6 = (bf16[1,128,768]{2,1,0:T(8,128)(2,1)S(1)}, bf16[1,128,768]{2,1,0:T(8,128)(2,1)}, u32[]{:S(2)}) copy-start(bf16[1,128,768]{2,1,0:T(8,128)(2,1)} %param.6) | copy-start | bytes 589828
  29.7 33.4 %copy-start.1 = (bf16[8,24,1536]{2,1,0:T(8,128)(2,1)}, bf16[8,24,1536]{2,1,0:T(8,128)(2,1)S(1)}, u32[]{:S(2)}) copy-start(bf16[8,24,1536]{2,1,0:T(8,128)(2,1)S(1)} %all_to_all.20) | copy-start | bytes 1769476
  29.7 16.9 %collective-permute-start.2 = (bf16[192,1536]{1,0:T(8,128)(2,1)S(1)}, bf16[192,1536]{1,0:T(8,128)(2,1)S(1)}, u32[]{:S(2)}, u32[]{:S(2)}) collective-permute-start(bf16[192,1536]{1,0:T(8,128)(2,1)S(1)} %bitcast.31), channel_id=1, source_target_pairs={{0,24},{8,0},{16,8},{24,16},{1,25},{9,1},{17,9},{25,17},{2,26},{10... | collective-permute-start | bytes 1769480 | tf_op jit(solution)/shard_map/ppermute | solution.py:249
  34.1 17.4 %collective-permute-start.1 = (bf16[192,1536]{1,0:T(8,128)(2,1)S(1)}, bf16[192,1536]{1,0:T(8,128)(2,1)S(1)}, u32[]{:S(2)}, u32[]{:S(2)}) collective-permute-start(bf16[192,1536]{1,0:T(8,128)(2,1)S(1)} %bitcast.32), channel_id=1, source_target_pairs={{0,8},{8,16},{16,24},{24,0},{1,9},{9,17},{17,25},{25,1},{2,10},{10... | collective-permute-start | bytes 1769480 | tf_op jit(solution)/shard_map/ppermute | solution.py:249
  36.8 24.4 %all-to-all-start.1 = ((bf16[16,8,1536]{2,1,0:T(8,128)(2,1)}), bf16[16,8,1536]{2,1,0:T(8,128)(2,1)S(1)}, u32[]{:S(2)}, u32[]{:S(2)}) async-start(bf16[16,8,1536]{2,1,0:T(8,128)(2,1)} %pad_maximum_fusion), calls=%async_computation.1 | async-start | bytes 786432 | tf_op jit(solution)/shard_map/all_to_all | solution.py:253
  46.6 16.5 %copy-start.7 = (bf16[192,1536]{1,0:T(8,128)(2,1)}, bf16[192,1536]{1,0:T(8,128)(2,1)S(1)}, u32[]{:S(2)}) copy-start(bf16[192,1536]{1,0:T(8,128)(2,1)S(1)} %collective-permute-done.2.refs_5_) | copy-start | bytes 1769476
  46.6 16.4 %collective-permute-start.4 = (bf16[96,1536]{1,0:T(8,128)(2,1)S(1)}, bf16[96,1536]{1,0:T(8,128)(2,1)S(1)}, u32[]{:S(2)}, u32[]{:S(2)}) collective-permute-start(bf16[96,1536]{1,0:T(8,128)(2,1)S(1)} %slice.21), channel_id=1, source_target_pairs={{0,24},{8,0},{16,8},{24,16},{1,25},{9,1},{17,9},{25,17},{2,26},{10... | collective-permute-start | bytes 884744 | tf_op jit(solution)/shard_map/ppermute | solution.py:249
  51.5 11.6 %copy-start.8 = (bf16[192,1536]{1,0:T(8,128)(2,1)}, bf16[192,1536]{1,0:T(8,128)(2,1)S(1)}, u32[]{:S(2)}) copy-start(bf16[192,1536]{1,0:T(8,128)(2,1)S(1)} %collective-permute-done.1.refs_4_) | copy-start | bytes 1769476
  51.5 11.5 %collective-permute-start.3 = (bf16[96,1536]{1,0:T(8,128)(2,1)S(1)}, bf16[96,1536]{1,0:T(8,128)(2,1)}, u32[]{:S(2)}, u32[]{:S(2)}) collective-permute-start(bf16[96,1536]{1,0:T(8,128)(2,1)S(1)} %slice.20), channel_id=1, source_target_pairs={{0,8},{8,16},{16,24},{24,0},{1,9},{9,17},{17,25},{25,1},{2,10},{10... | collective-permute-start | bytes 884744 | tf_op jit(solution)/shard_map/ppermute | solution.py:249
  61.1 2.0 %copy-start = (bf16[16,8,1536]{2,1,0:T(8,128)(2,1)}, bf16[16,8,1536]{2,1,0:T(8,128)(2,1)S(1)}, u32[]{:S(2)}) copy-start(bf16[16,8,1536]{2,1,0:T(8,128)(2,1)S(1)} %all-to-all-done.1) | copy-start | bytes 1179652
  61.1 6.7 %collective-permute-start = (bf16[128,1536]{1,0:T(8,128)(2,1)S(1)}, bf16[128,1536]{1,0:T(8,128)(2,1)S(1)}, u32[]{:S(2)}, u32[]{:S(2)}) collective-permute-start(bf16[128,1536]{1,0:T(8,128)(2,1)S(1)} %bitcast.23), channel_id=1, source_target_pairs={{0,32},{32,0},{1,33},{33,1},{2,34},{34,2},{3,35},{35,3},{4,36},{36... | collective-permute-start | bytes 1179656 | tf_op jit(solution)/shard_map/ppermute | solution.py:249
  63.1 0.7 copy-start.10
  67.8 0.8 copy-start.3
  72.6 9.3 %copy-start.9 = (bf16[384,384]{1,0:T(8,128)(2,1)S(1)}, bf16[384,384]{1,0:T(8,128)(2,1)}, u32[]{:S(2)}) copy-start(bf16[384,384]{1,0:T(8,128)(2,1)} %get-tuple-element.19) | copy-start | bytes 884740
  72.6 3.9 %collective-permute-start.6 = (bf16[384,384]{1,0:T(8,128)(2,1)}, bf16[384,384]{1,0:T(8,128)(2,1)S(1)}, u32[]{:S(2)}, u32[]{:S(2)}) collective-permute-start(bf16[384,384]{1,0:T(8,128)(2,1)} %get-tuple-element.28), channel_id=1, source_target_pairs={{0,32},{32,0},{1,33},{33,1},{2,34},{34,2},{3,35},{35,3},{4,36},{36... | collective-permute-start | bytes 884744 | tf_op jit(solution)/shard_map/ppermute | solution.py:249
  77.3 22.8 %all-to-all-start.2 = ((bf16[32,24,384]{2,1,0:T(8,128)(2,1)}), bf16[32,24,384]{2,1,0:T(8,128)(2,1)S(1)}, u32[]{:S(2)}, u32[]{:S(2)}) async-start(bf16[32,24,384]{2,1,0:T(8,128)(2,1)} %bitcast.29), calls=%async_computation.2 | async-start | bytes 1179648 | tf_op jit(solution)/shard_map/all_to_all | solution.py:253
  81.9 3.7 %collective-permute-start.5 = (bf16[384,384]{1,0:T(8,128)(2,1)S(1)}, bf16[384,384]{1,0:T(8,128)(2,1)S(1)}, u32[]{:S(2)}, u32[]{:S(2)}) collective-permute-start(bf16[384,384]{1,0:T(8,128)(2,1)S(1)} %copy-done.9), channel_id=1, source_target_pairs={{0,32},{32,0},{1,33},{33,1},{2,34},{34,2},{3,35},{35,3},{4,36},{36... | collective-permute-start | bytes 884744 | tf_op jit(solution)/shard_map/ppermute | solution.py:249
  85.6 0.7 copy-start.4
  93.0 3.8 %collective-permute-start.7 = (bf16[128,1536]{1,0:T(8,128)(2,1)}, bf16[128,1536]{1,0:T(8,128)(2,1)S(1)}, u32[]{:S(2)}, u32[]{:S(2)}) collective-permute-start(bf16[128,1536]{1,0:T(8,128)(2,1)} %get-tuple-element.30), channel_id=1, source_target_pairs={{0,32},{32,0},{1,33},{33,1},{2,34},{34,2},{3,35},{35,3},{4,36},{36... | collective-permute-start | bytes 1179656 | tf_op jit(solution)/shard_map/ppermute | solution.py:249
  96.8 0.8 copy-start.2

commit v14 on v13

--- a/solution.py
+++ b/solution.py
@@ -14,7 +14,7 @@
 VMEM_LIMIT = 56 * 1024 * 1024
 OWN_COST = 8_000_000_000
 NEAR_COST = 8_000_000_000
-BWD_COST = 1000
+BWD_COST = 8_000_000_000
 END_COST = 1000
 
 

time: 131 us -> 132 us (level)
  blocking collectives: 55.7 us -> 58.8 us
  waiting for transfers between devices: 11.8 us -> 9.64 us
    all_to_all x2, blocking collectives: 55.7 us -> 58.8 us  [exchange(): return lax.all_to_all(v, axes, split_axis=0, concat_axis=0, tiled=True)]
    ppermute x8, waiting for transfers between devices: 4.14 us -> 1.56 us  [shift(): return lax.ppermute(v, axis, [(i, (i + by) % size) for i in range(size)])]
  transfers between devices with their start and end apart: 10 -> 10, of which waited for: 4 -> 3; matrix products, arithmetic and copies ran while one was open for 1% -> 1% of each run, Pallas kernels for 10% -> 10%
where the time goes in v14:
time: 132 us; the launch traced here: 131 us
  blocking collectives  58.8 us (45%)
  starting transfers between devices  36.4 us (28%)
  Pallas kernels  17.3 us (13%)
  waiting for transfers between devices  9.64 us (7%)
  local copies, waits for them, and re-layouts  6.82 us (5%)
    all_to_all x2, blocking collectives, exchange(): return lax.all_to_all(v, axes, split_axis=0, concat_axis=0, tiled=True)  58.8 us
    ppermute x8, starting transfers between devices, shift(): return lax.ppermute(v, axis, [(i, (i + by) % size) for i in range(size)])  21.9 us
    pallas_call x4, Pallas kernels, call(): pl.pallas_call(kernel, out_shape=outs, in_specs=[pl.BlockSpec(memory_spac...  17.3 us
    all_to_all x2, starting transfers between devices, exchange(): return lax.all_to_all(v, axes, split_axis=0, concat_axis=0, tiled=True)  14.4 us
    all_to_all x2, waiting for transfers between devices, exchange(): return lax.all_to_all(v, axes, split_axis=0, concat_axis=0, tiled=True)  8.08 us
    unnamed x23, local copies, waits for them, and re-layouts  3.54 us
  transfers between devices with their start and end apart: 10, of which 3 were waited for; matrix products, arithmetic and copies ran while one was open for 1% of the time, Pallas kernels for 10%

profile of v14, /device:TPU:1, one launch (start us, length us, event | category | flops | bytes accessed | tf_op | source)
XLA Modules:
  0.0 130.7 jit_solution(1445446342952249400)
XLA Ops:
  0.7 0.8 constant_dynamic-slice_fusion.3
  1.6 28.1 %all_to_all.20 = bf16[8,24,1536]{2,1,0:T(8,128)(2,1)S(1)} all-to-all(bf16[8,24,1536]{2,1,0:T(8,128)(2,1)S(1)} %broadcast_in_dim.6), channel_id=1, replica_groups=mesh['y'=8,'core'=2,'x'=4,'z'=8] {'z'}, dimensions={0} | all-to-all | bytes 1179648 | tf_op jit(solution)/shard_map/all_to_all | solution.py:253
  29.7 4.4 %collective-permute-start.2 = (bf16[192,1536]{1,0:T(8,128)(2,1)S(1)}, bf16[192,1536]{1,0:T(8,128)(2,1)S(1)}, u32[]{:S(2)}, u32[]{:S(2)}) collective-permute-start(bf16[192,1536]{1,0:T(8,128)(2,1)S(1)} %bitcast.30), channel_id=1, source_target_pairs={{0,24},{8,0},{16,8},{24,16},{1,25},{9,1},{17,9},{25,17},{2,26},{10... | collective-permute-start | bytes 1769480 | tf_op jit(solution)/shard_map/ppermute | solution.py:249
  34.1 1.9 %collective-permute-start.1 = (bf16[192,1536]{1,0:T(8,128)(2,1)S(1)}, bf16[192,1536]{1,0:T(8,128)(2,1)S(1)}, u32[]{:S(2)}, u32[]{:S(2)}) collective-permute-start(bf16[192,1536]{1,0:T(8,128)(2,1)S(1)} %bitcast.31), channel_id=1, source_target_pairs={{0,8},{8,16},{16,24},{24,0},{1,9},{9,17},{17,25},{25,1},{2,10},{10... | collective-permute-start | bytes 1769480 | tf_op jit(solution)/shard_map/ppermute | solution.py:249
  36.0 0.8 pad_maximum_fusion
  36.8 9.8 %all-to-all-start.1 = ((bf16[16,8,1536]{2,1,0:T(8,128)(2,1)}), bf16[16,8,1536]{2,1,0:T(8,128)(2,1)S(1)}, u32[]{:S(2)}, u32[]{:S(2)}) async-start(bf16[16,8,1536]{2,1,0:T(8,128)(2,1)} %pad_maximum_fusion), calls=%async_computation.1 | async-start | bytes 786432 | tf_op jit(solution)/shard_map/all_to_all | solution.py:253
  46.6 0.0 collective-permute-done.2.refs_5_
  46.6 4.9 %collective-permute-start.4 = (bf16[96,1536]{1,0:T(8,128)(2,1)S(1)}, bf16[96,1536]{1,0:T(8,128)(2,1)S(1)}, u32[]{:S(2)}, u32[]{:S(2)}) collective-permute-start(bf16[96,1536]{1,0:T(8,128)(2,1)S(1)} %slice.21), channel_id=1, source_target_pairs={{0,24},{8,0},{16,8},{24,16},{1,25},{9,1},{17,9},{25,17},{2,26},{10... | collective-permute-start | bytes 884744 | tf_op jit(solution)/shard_map/ppermute | solution.py:249
  51.5 1.9 %collective-permute-start.3 = (bf16[96,1536]{1,0:T(8,128)(2,1)S(1)}, bf16[96,1536]{1,0:T(8,128)(2,1)}, u32[]{:S(2)}, u32[]{:S(2)}) collective-permute-start(bf16[96,1536]{1,0:T(8,128)(2,1)S(1)} %slice.20), channel_id=1, source_target_pairs={{0,8},{8,16},{16,24},{24,0},{1,9},{9,17},{17,25},{25,1},{2,10},{10... | collective-permute-start | bytes 884744 | tf_op jit(solution)/shard_map/ppermute | solution.py:249
  53.5 7.7 %all-to-all-done.1 = bf16[16,8,1536]{2,1,0:T(8,128)(2,1)S(1)} async-done(((bf16[16,8,1536]{2,1,0:T(8,128)(2,1)}), bf16[16,8,1536]{2,1,0:T(8,128)(2,1)S(1)}, u32[]{:S(2)}, u32[]{:S(2)}) %all-to-all-start.1) | async-done | bytes 393248 | tf_op jit(solution)/shard_map/all_to_all | solution.py:253
  61.1 1.9 %collective-permute-start = (bf16[128,1536]{1,0:T(8,128)(2,1)S(1)}, bf16[128,1536]{1,0:T(8,128)(2,1)S(1)}, u32[]{:S(2)}, u32[]{:S(2)}) collective-permute-start(bf16[128,1536]{1,0:T(8,128)(2,1)S(1)} %bitcast.24), channel_id=1, source_target_pairs={{0,32},{32,0},{1,33},{33,1},{2,34},{34,2},{3,35},{35,3},{4,36},{36... | collective-permute-start | bytes 1179656 | tf_op jit(solution)/shard_map/ppermute | solution.py:249
  63.1 0.0 collective-permute-done.3.refs_6_
  63.1 0.7 copy-done.10
  63.8 4.0 %shard_map.85 = (bf16[128,1152]{1,0:T(8,128)(2,1)}, f32[3,256,128]{2,1,0:T(8,128)}, bf16[128,384]{1,0:T(8,128)(2,1)}, bf16[768,1152]{1,0:T(8,128)(2,1)}, bf16[38...) custom-call(s32[2]{0:T(128)} %refs_0_.7, bf16[128,1536]{1,0:T(8,128)(2,1)} %bitcast.25, f32[768]{0:T(1024)} %refs_2_.3, ...), custom_call_target="tpu_custom_call" | custom-call | flops 8000000000 | bytes 5901320 | tf_op jit(solution)/shard_map/pallas_call | solution.py:233
  67.8 0.7 copy-done.7
  68.6 4.0 %shard_map.86 = (bf16[128,1152]{1,0:T(8,128)(2,1)}, f32[3,256,128]{2,1,0:T(8,128)}, bf16[128,384]{1,0:T(8,128)(2,1)}, bf16[384,384]{1,0:T(8,128)(2,1)}, bf16[768,384]{1,0:T(8,128)(2,1)}) custom-call(s32[2]{0:T(128)} %refs_0_.7, bf16[128,1536]{1,0:T(8,128)(2,1)} %bitcast.26, bf16[128,1536]{1,0:T(8,128)(2,1)} %copy-done.7, f32[768]{0:T(1024)} %refs_2_.3, ...), custom_call_target="tpu_custom_call" | custom-call | flops 8000000000 | bytes 4328456 | tf_op jit(solution)/shard_map/pallas_call | solution.py:233
  72.6 2.4 %collective-permute-start.6 = (bf16[384,384]{1,0:T(8,128)(2,1)}, bf16[384,384]{1,0:T(8,128)(2,1)S(1)}, u32[]{:S(2)}, u32[]{:S(2)}) collective-permute-start(bf16[384,384]{1,0:T(8,128)(2,1)} %get-tuple-element.28), channel_id=1, source_target_pairs={{0,32},{32,0},{1,33},{33,1},{2,34},{34,2},{3,35},{35,3},{4,36},{36... | collective-permute-start | bytes 884744 | tf_op jit(solution)/shard_map/ppermute | solution.py:249
  75.0 1.9 %collective-permute-start.5 = (bf16[384,384]{1,0:T(8,128)(2,1)S(1)}, bf16[384,384]{1,0:T(8,128)(2,1)S(1)}, u32[]{:S(2)}, u32[]{:S(2)}) collective-permute-start(bf16[384,384]{1,0:T(8,128)(2,1)S(1)} %copy-done.8), channel_id=1, source_target_pairs={{0,32},{32,0},{1,33},{33,1},{2,34},{34,2},{3,35},{35,3},{4,36},{36... | collective-permute-start | bytes 884744 | tf_op jit(solution)/shard_map/ppermute | solution.py:249
  77.0 0.8 constant_dynamic-update-slice_fusion.refs_12_
  77.8 4.6 %all-to-all-start.2 = ((bf16[32,24,384]{2,1,0:T(8,128)(2,1)}), bf16[32,24,384]{2,1,0:T(8,128)(2,1)S(1)}, u32[]{:S(2)}, u32[]{:S(2)}) async-start(bf16[32,24,384]{2,1,0:T(8,128)(2,1)} %bitcast.33), calls=%async_computation.2 | async-start | bytes 1179648 | tf_op jit(solution)/shard_map/all_to_all | solution.py:253
  82.4 0.7 copy-done.9
  83.1 6.6 %shard_map.87 = (f32[128,1536]{1,0:T(8,128)}, bf16[128,1536]{1,0:T(8,128)(2,1)}) custom-call(s32[2]{0:T(128)} %refs_0_.7, bf16[128,1536]{1,0:T(8,128)(2,1)} %bitcast.27, bf16[128,1536]{1,0:T(8,128)(2,1)} %copy-done.7, bf16[384,384]{1,0:T(8,128)(2,1)} %get-tuple-element.18.refs_3_, bf16[384,384]{1,0:T(8,128)(2,1)} %copy-done.9, ...), custom_call_target="tpu_custom_call" | custom-call | flops 8000000000 | bytes 5898248 | tf_op jit(solution)/shard_map/pallas_call | solution.py:233
  89.8 2.6 %collective-permute-start.7 = (bf16[128,1536]{1,0:T(8,128)(2,1)}, bf16[128,1536]{1,0:T(8,128)(2,1)S(1)}, u32[]{:S(2)}, u32[]{:S(2)}) collective-permute-start(bf16[128,1536]{1,0:T(8,128)(2,1)} %get-tuple-element.30), channel_id=1, source_target_pairs={{0,32},{32,0},{1,33},{33,1},{2,34},{34,2},{3,35},{35,3},{4,36},{36... | collective-permute-start | bytes 1179656 | tf_op jit(solution)/shard_map/ppermute | solution.py:249
  92.4 1.5 %collective-permute-done.7.refs_4_ = bf16[128,1536]{1,0:T(8,128)(2,1)S(1)} collective-permute-done((bf16[128,1536]{1,0:T(8,128)(2,1)}, bf16[128,1536]{1,0:T(8,128)(2,1)S(1)}, u32[]{:S(2)}, u32[]{:S(2)}) %collective-permute-start.7) | collective-permute-done | bytes 393248 | tf_op jit(solution)/shard_map/ppermute | solution.py:249
  93.9 0.8 copy-done.2
  94.7 2.5 %shard_map.88 = bf16[128,2688]{1,0:T(8,128)(2,1)} custom-call(s32[2]{0:T(128)} %refs_0_.7, bf16[128,1536]{1,0:T(8,128)(2,1)} %bitcast.28, f32[768]{0:T(1024)} %refs_2_.3, f32[128,1536]{1,0:T(8,128)} %get-tuple-element.29.refs_3_, bf16[128,1536]{1,0:T(8,128)(2,1)} %copy-done.2), custom_call_target="tpu_custom_call" | custom-call | flops 1000 | bytes 2264072 | tf_op jit(solution)/shard_map/pallas_call | solution.py:233
  97.2 0.4 all-to-all-done.2
  97.7 0.1 reduce_sum.21
  97.7 0.7 broadcast_dynamic-update-slice_fusion
  98.5 30.7 %all_to_all.21 = bf16[16,8,2688]{2,1,0:T(8,128)(2,1)S(1)} all-to-all(bf16[16,8,2688]{2,1,0:T(8,128)(2,1)} %broadcast_dynamic-update-slice_fusion), channel_id=1, replica_groups=mesh['y'=8,'core'=2,'x'=4,'z'=8] {'y','core'}, dimensions={0} | all-to-all | bytes 1376256 | tf_op jit(solution)/shard_map/all_to_all | solution.py:253
  129.3 0.6 copy.10
  130.0 0.8 slice_bitcast_fusion
  (30 shorter events, 0.2 us)
Async XLA Ops:
  0.6 35.4 %copy-start.3 = (bf16[1,128,768]{2,1,0:T(8,128)(2,1)S(1)}, bf16[1,128,768]{2,1,0:T(8,128)(2,1)}, u32[]{:S(2)}) copy-start(bf16[1,128,768]{2,1,0:T(8,128)(2,1)} %param.7) | copy-start | bytes 589828
  0.6 35.4 %copy-start.4 = (bf16[1,128,768]{2,1,0:T(8,128)(2,1)S(1)}, bf16[1,128,768]{2,1,0:T(8,128)(2,1)}, u32[]{:S(2)}) copy-start(bf16[1,128,768]{2,1,0:T(8,128)(2,1)} %param.6) | copy-start | bytes 589828
  29.7 33.4 %copy-start.1 = (bf16[8,24,1536]{2,1,0:T(8,128)(2,1)}, bf16[8,24,1536]{2,1,0:T(8,128)(2,1)S(1)}, u32[]{:S(2)}) copy-start(bf16[8,24,1536]{2,1,0:T(8,128)(2,1)S(1)} %all_to_all.20) | copy-start | bytes 1769476
  29.7 16.9 %collective-permute-start.2 = (bf16[192,1536]{1,0:T(8,128)(2,1)S(1)}, bf16[192,1536]{1,0:T(8,128)(2,1)S(1)}, u32[]{:S(2)}, u32[]{:S(2)}) collective-permute-start(bf16[192,1536]{1,0:T(8,128)(2,1)S(1)} %bitcast.30), channel_id=1, source_target_pairs={{0,24},{8,0},{16,8},{24,16},{1,25},{9,1},{17,9},{25,17},{2,26},{10... | collective-permute-start | bytes 1769480 | tf_op jit(solution)/shard_map/ppermute | solution.py:249
  34.1 17.4 %collective-permute-start.1 = (bf16[192,1536]{1,0:T(8,128)(2,1)S(1)}, bf16[192,1536]{1,0:T(8,128)(2,1)S(1)}, u32[]{:S(2)}, u32[]{:S(2)}) collective-permute-start(bf16[192,1536]{1,0:T(8,128)(2,1)S(1)} %bitcast.31), channel_id=1, source_target_pairs={{0,8},{8,16},{16,24},{24,0},{1,9},{9,17},{17,25},{25,1},{2,10},{10... | collective-permute-start | bytes 1769480 | tf_op jit(solution)/shard_map/ppermute | solution.py:249
  36.8 24.4 %all-to-all-start.1 = ((bf16[16,8,1536]{2,1,0:T(8,128)(2,1)}), bf16[16,8,1536]{2,1,0:T(8,128)(2,1)S(1)}, u32[]{:S(2)}, u32[]{:S(2)}) async-start(bf16[16,8,1536]{2,1,0:T(8,128)(2,1)} %pad_maximum_fusion), calls=%async_computation.1 | async-start | bytes 786432 | tf_op jit(solution)/shard_map/all_to_all | solution.py:253
  46.6 16.5 %copy-start.5 = (bf16[192,1536]{1,0:T(8,128)(2,1)}, bf16[192,1536]{1,0:T(8,128)(2,1)S(1)}, u32[]{:S(2)}) copy-start(bf16[192,1536]{1,0:T(8,128)(2,1)S(1)} %collective-permute-done.2.refs_5_) | copy-start | bytes 1769476
  46.6 16.4 %collective-permute-start.4 = (bf16[96,1536]{1,0:T(8,128)(2,1)S(1)}, bf16[96,1536]{1,0:T(8,128)(2,1)S(1)}, u32[]{:S(2)}, u32[]{:S(2)}) collective-permute-start(bf16[96,1536]{1,0:T(8,128)(2,1)S(1)} %slice.21), channel_id=1, source_target_pairs={{0,24},{8,0},{16,8},{24,16},{1,25},{9,1},{17,9},{25,17},{2,26},{10... | collective-permute-start | bytes 884744 | tf_op jit(solution)/shard_map/ppermute | solution.py:249
  51.5 11.6 %copy-start.6 = (bf16[192,1536]{1,0:T(8,128)(2,1)}, bf16[192,1536]{1,0:T(8,128)(2,1)S(1)}, u32[]{:S(2)}) copy-start(bf16[192,1536]{1,0:T(8,128)(2,1)S(1)} %collective-permute-done.1.refs_4_) | copy-start | bytes 1769476
  51.5 11.5 %collective-permute-start.3 = (bf16[96,1536]{1,0:T(8,128)(2,1)S(1)}, bf16[96,1536]{1,0:T(8,128)(2,1)}, u32[]{:S(2)}, u32[]{:S(2)}) collective-permute-start(bf16[96,1536]{1,0:T(8,128)(2,1)S(1)} %slice.20), channel_id=1, source_target_pairs={{0,8},{8,16},{16,24},{24,0},{1,9},{9,17},{17,25},{25,1},{2,10},{10... | collective-permute-start | bytes 884744 | tf_op jit(solution)/shard_map/ppermute | solution.py:249
  61.1 2.0 %copy-start = (bf16[16,8,1536]{2,1,0:T(8,128)(2,1)}, bf16[16,8,1536]{2,1,0:T(8,128)(2,1)S(1)}, u32[]{:S(2)}) copy-start(bf16[16,8,1536]{2,1,0:T(8,128)(2,1)S(1)} %all-to-all-done.1) | copy-start | bytes 1179652
  61.1 6.7 %collective-permute-start = (bf16[128,1536]{1,0:T(8,128)(2,1)S(1)}, bf16[128,1536]{1,0:T(8,128)(2,1)S(1)}, u32[]{:S(2)}, u32[]{:S(2)}) collective-permute-start(bf16[128,1536]{1,0:T(8,128)(2,1)S(1)} %bitcast.24), channel_id=1, source_target_pairs={{0,32},{32,0},{1,33},{33,1},{2,34},{34,2},{3,35},{35,3},{4,36},{36... | collective-permute-start | bytes 1179656 | tf_op jit(solution)/shard_map/ppermute | solution.py:249
  63.1 0.7 copy-start.10
  67.8 0.8 copy-start.7
  68.6 6.4 %copy-start.8 = (bf16[384,384]{1,0:T(8,128)(2,1)S(1)}, bf16[384,384]{1,0:T(8,128)(2,1)}, u32[]{:S(2)}) copy-start(bf16[384,384]{1,0:T(8,128)(2,1)} %get-tuple-element.19) | copy-start | bytes 884740
  72.6 4.3 %collective-permute-start.6 = (bf16[384,384]{1,0:T(8,128)(2,1)}, bf16[384,384]{1,0:T(8,128)(2,1)S(1)}, u32[]{:S(2)}, u32[]{:S(2)}) collective-permute-start(bf16[384,384]{1,0:T(8,128)(2,1)} %get-tuple-element.28), channel_id=1, source_target_pairs={{0,32},{32,0},{1,33},{33,1},{2,34},{34,2},{3,35},{35,3},{4,36},{36... | collective-permute-start | bytes 884744 | tf_op jit(solution)/shard_map/ppermute | solution.py:249
  75.0 7.3 %collective-permute-start.5 = (bf16[384,384]{1,0:T(8,128)(2,1)S(1)}, bf16[384,384]{1,0:T(8,128)(2,1)S(1)}, u32[]{:S(2)}, u32[]{:S(2)}) collective-permute-start(bf16[384,384]{1,0:T(8,128)(2,1)S(1)} %copy-done.8), channel_id=1, source_target_pairs={{0,32},{32,0},{1,33},{33,1},{2,34},{34,2},{3,35},{35,3},{4,36},{36... | collective-permute-start | bytes 884744 | tf_op jit(solution)/shard_map/ppermute | solution.py:249
  77.8 19.9 %all-to-all-start.2 = ((bf16[32,24,384]{2,1,0:T(8,128)(2,1)}), bf16[32,24,384]{2,1,0:T(8,128)(2,1)S(1)}, u32[]{:S(2)}, u32[]{:S(2)}) async-start(bf16[32,24,384]{2,1,0:T(8,128)(2,1)} %bitcast.33), calls=%async_computation.2 | async-start | bytes 1179648 | tf_op jit(solution)/shard_map/all_to_all | solution.py:253
  82.4 0.7 copy-start.9
  89.8 4.2 %collective-permute-start.7 = (bf16[128,1536]{1,0:T(8,128)(2,1)}, bf16[128,1536]{1,0:T(8,128)(2,1)S(1)}, u32[]{:S(2)}, u32[]{:S(2)}) collective-permute-start(bf16[128,1536]{1,0:T(8,128)(2,1)} %get-tuple-element.30), channel_id=1, source_target_pairs={{0,32},{32,0},{1,33},{33,1},{2,34},{34,2},{3,35},{35,3},{4,36},{36... | collective-permute-start | bytes 1179656 | tf_op jit(solution)/shard_map/ppermute | solution.py:249
  93.9 0.8 copy-start.2

commit v15 on v13

--- a/solution.py
+++ b/solution.py
@@ -80,8 +80,9 @@
         s = jnp.where(same, dot_nt(by_head(q), k) * HD ** (-0.5), NEG)
         e = jnp.exp(s - jnp.max(s, axis=-1, keepdims=True))
         p = e / jnp.sum(e, axis=-1, keepdims=True)
-        p_ref[index] = p
-        mixed = dot_nn(side_by_side(p.astype(jnp.bfloat16)), by_head(v))
+        p_low = p.astype(jnp.bfloat16)
+        p_ref[index] = p_low
+        mixed = dot_nn(side_by_side(p_low), by_head(v))
         att_ref[:, at : at + 2 * HD] = mixed.astype(jnp.bfloat16)
 
 
@@ -199,13 +200,14 @@
             k = qkv_ref[:, mine + at : mine + at + 2 * HD]
             v = qkv_ref[:, 2 * mine + at : 2 * mine + at + 2 * HD]
             ga = by_head(ga_all[start : start + rows, at : at + 2 * HD])
-            p = p_ref[index]
+            p_low = p_ref[index]
+            p = p_low.astype(jnp.float32)
             gp = dot_nt(ga, v)
             ds = p * (gp - jnp.sum(p * gp, axis=-1, keepdims=True)) * HD ** (-0.5)
             ds = ds.astype(jnp.bfloat16)
             dq = dot_nn(side_by_side(ds), by_head(k))
             dk = dot_tn(ds, by_head(q))
-            dv = dot_tn(p.astype(jnp.bfloat16), ga)
+            dv = dot_tn(p_low, ga)
             for j, grad in enumerate((dq, dk, dv)):
                 to = j * mine + at
                 gqkv_ref[start : start + rows, to : to + 2 * HD] = grad.astype(jnp.bfloat16)
@@ -290,7 +292,7 @@
     heads = width // HD // cores
     results = (
         shape((rows, half), bf),
-        shape((heads // 2, 2 * rows, rows), f32),
+        shape((heads // 2, 2 * rows, rows), bf),
         shape((rows, cut), bf),
     )
     own_qkv, own_p, own_att, w, wo, wo_give = call(

time: 131 us -> 130 us (level)
  no operation moved by 1% of the time
where the time goes in v15:
time: 130 us; the launch traced here: 129 us
  blocking collectives  55.6 us (43%)
  starting transfers between devices  35.9 us (28%)
  Pallas kernels  17.1 us (13%)
  waiting for transfers between devices  12.1 us (9%)
  local copies, waits for them, and re-layouts  6.81 us (5%)
    all_to_all x2, blocking collectives, exchange(): return lax.all_to_all(v, axes, split_axis=0, concat_axis=0, tiled=True)  55.6 us
    ppermute x8, starting transfers between devices, shift(): return lax.ppermute(v, axis, [(i, (i + by) % size) for i in range(size)])  21.9 us
    pallas_call x4, Pallas kernels, call(): pl.pallas_call(kernel, out_shape=outs, in_specs=[pl.BlockSpec(memory_spac...  17.1 us
    all_to_all x2, starting transfers between devices, exchange(): return lax.all_to_all(v, axes, split_axis=0, concat_axis=0, tiled=True)  14 us
    all_to_all x2, waiting for transfers between devices, exchange(): return lax.all_to_all(v, axes, split_axis=0, concat_axis=0, tiled=True)  7.95 us
    ppermute x8, waiting for transfers between devices, shift(): return lax.ppermute(v, axis, [(i, (i + by) % size) for i in range(size)])  4.2 us
    unnamed x23, local copies, waits for them, and re-layouts  3.54 us
  transfers between devices with their start and end apart: 10, of which 4 were waited for; matrix products, arithmetic and copies ran while one was open for 1% of the time, Pallas kernels for 10%

profile of v15, /device:TPU:1, one launch (start us, length us, event | category | flops | bytes accessed | tf_op | source)
XLA Modules:
  0.0 129.3 jit_solution(1142072980599102664)
XLA Ops:
  0.7 0.8 constant_dynamic-slice_fusion.3
  1.6 28.1 %all_to_all.20 = bf16[8,24,1536]{2,1,0:T(8,128)(2,1)S(1)} all-to-all(bf16[8,24,1536]{2,1,0:T(8,128)(2,1)S(1)} %broadcast_in_dim.6), channel_id=1, replica_groups=mesh['y'=8,'core'=2,'x'=4,'z'=8] {'z'}, dimensions={0} | all-to-all | bytes 1179648 | tf_op jit(solution)/shard_map/all_to_all | solution.py:255
  29.7 3.1 %collective-permute-start.1 = (bf16[192,1536]{1,0:T(8,128)(2,1)S(1)}, bf16[192,1536]{1,0:T(8,128)(2,1)S(1)}, u32[]{:S(2)}, u32[]{:S(2)}) collective-permute-start(bf16[192,1536]{1,0:T(8,128)(2,1)S(1)} %bitcast.31), channel_id=1, source_target_pairs={{0,8},{8,16},{16,24},{24,0},{1,9},{9,17},{17,25},{25,1},{2,10},{10... | collective-permute-start | bytes 1769480 | tf_op jit(solution)/shard_map/ppermute | solution.py:251
  32.8 3.4 %collective-permute-start.2 = (bf16[192,1536]{1,0:T(8,128)(2,1)S(1)}, bf16[192,1536]{1,0:T(8,128)(2,1)S(1)}, u32[]{:S(2)}, u32[]{:S(2)}) collective-permute-start(bf16[192,1536]{1,0:T(8,128)(2,1)S(1)} %bitcast.32), channel_id=1, source_target_pairs={{0,24},{8,0},{16,8},{24,16},{1,25},{9,1},{17,9},{25,17},{2,26},{10... | collective-permute-start | bytes 1769480 | tf_op jit(solution)/shard_map/ppermute | solution.py:251
  36.2 0.8 pad_maximum_fusion
  37.0 10.1 %all-to-all-start.1 = ((bf16[16,8,1536]{2,1,0:T(8,128)(2,1)}), bf16[16,8,1536]{2,1,0:T(8,128)(2,1)S(1)}, u32[]{:S(2)}, u32[]{:S(2)}) async-start(bf16[16,8,1536]{2,1,0:T(8,128)(2,1)} %pad_maximum_fusion), calls=%async_computation.1 | async-start | bytes 786432 | tf_op jit(solution)/shard_map/all_to_all | solution.py:255
  47.1 0.0 collective-permute-done.1.refs_4_
  47.1 1.9 %collective-permute-start.3 = (bf16[96,1536]{1,0:T(8,128)(2,1)S(1)}, bf16[96,1536]{1,0:T(8,128)(2,1)S(1)}, u32[]{:S(2)}, u32[]{:S(2)}) collective-permute-start(bf16[96,1536]{1,0:T(8,128)(2,1)S(1)} %slice.20), channel_id=1, source_target_pairs={{0,8},{8,16},{16,24},{24,0},{1,9},{9,17},{17,25},{25,1},{2,10},{10... | collective-permute-start | bytes 884744 | tf_op jit(solution)/shard_map/ppermute | solution.py:251
  49.1 4.6 %collective-permute-start.4 = (bf16[96,1536]{1,0:T(8,128)(2,1)S(1)}, bf16[96,1536]{1,0:T(8,128)(2,1)}, u32[]{:S(2)}, u32[]{:S(2)}) collective-permute-start(bf16[96,1536]{1,0:T(8,128)(2,1)S(1)} %slice.21), channel_id=1, source_target_pairs={{0,24},{8,0},{16,8},{24,16},{1,25},{9,1},{17,9},{25,17},{2,26},{10... | collective-permute-start | bytes 884744 | tf_op jit(solution)/shard_map/ppermute | solution.py:251
  53.7 7.9 %all-to-all-done.1 = bf16[16,8,1536]{2,1,0:T(8,128)(2,1)S(1)} async-done(((bf16[16,8,1536]{2,1,0:T(8,128)(2,1)}), bf16[16,8,1536]{2,1,0:T(8,128)(2,1)S(1)}, u32[]{:S(2)}, u32[]{:S(2)}) %all-to-all-start.1) | async-done | bytes 393248 | tf_op jit(solution)/shard_map/all_to_all | solution.py:255
  61.6 1.9 %collective-permute-start = (bf16[128,1536]{1,0:T(8,128)(2,1)S(1)}, bf16[128,1536]{1,0:T(8,128)(2,1)S(1)}, u32[]{:S(2)}, u32[]{:S(2)}) collective-permute-start(bf16[128,1536]{1,0:T(8,128)(2,1)S(1)} %bitcast.23), channel_id=1, source_target_pairs={{0,32},{32,0},{1,33},{33,1},{2,34},{34,2},{3,35},{35,3},{4,36},{36... | collective-permute-start | bytes 1179656 | tf_op jit(solution)/shard_map/ppermute | solution.py:251
  63.6 0.7 copy-done.10
  64.3 4.0 %shard_map.85 = (bf16[128,1152]{1,0:T(8,128)(2,1)}, bf16[3,256,128]{2,1,0:T(8,128)(2,1)}, bf16[128,384]{1,0:T(8,128)(2,1)}, bf16[768,1152]{1,0:T(8,128)(2,1)}, b...) custom-call(s32[2]{0:T(128)} %refs_0_.7, bf16[128,1536]{1,0:T(8,128)(2,1)} %bitcast.24, f32[768]{0:T(1024)} %refs_2_.3, ...), custom_call_target="tpu_custom_call" | custom-call | flops 8000000000 | bytes 5704712 | tf_op jit(solution)/shard_map/pallas_call | solution.py:235
  68.3 0.7 copy-done.2
  69.0 4.0 %shard_map.86 = (bf16[128,1152]{1,0:T(8,128)(2,1)}, bf16[3,256,128]{2,1,0:T(8,128)(2,1)}, bf16[128,384]{1,0:T(8,128)(2,1)}, bf16[384,384]{1,0:T(8,128)(2,1)}, bf16[768,384]{1,0:T(8,128)(2,1)}) custom-call(s32[2]{0:T(128)} %refs_0_.7, bf16[128,1536]{1,0:T(8,128)(2,1)} %bitcast.25, bf16[128,1536]{1,0:T(8,128)(2,1)} %copy-done.2, f32[768]{0:T(1024)} %refs_2_.3, ...), custom_call_target="tpu_custom_call" | custom-call | flops 8000000000 | bytes 4131848 | tf_op jit(solution)/shard_map/pallas_call | solution.py:235
  73.0 2.5 %collective-permute-start.6 = (bf16[384,384]{1,0:T(8,128)(2,1)}, bf16[384,384]{1,0:T(8,128)(2,1)S(1)}, u32[]{:S(2)}, u32[]{:S(2)}) collective-permute-start(bf16[384,384]{1,0:T(8,128)(2,1)} %get-tuple-element.28), channel_id=1, source_target_pairs={{0,32},{32,0},{1,33},{33,1},{2,34},{34,2},{3,35},{35,3},{4,36},{36... | collective-permute-start | bytes 884744 | tf_op jit(solution)/shard_map/ppermute | solution.py:251
  75.5 1.4 %collective-permute-done.6 = bf16[384,384]{1,0:T(8,128)(2,1)S(1)} collective-permute-done((bf16[384,384]{1,0:T(8,128)(2,1)}, bf16[384,384]{1,0:T(8,128)(2,1)S(1)}, u32[]{:S(2)}, u32[]{:S(2)}) %collective-permute-start.6) | collective-permute-done | bytes 294944 | tf_op jit(solution)/shard_map/ppermute | solution.py:251
  76.9 0.8 constant_dynamic-update-slice_fusion.refs_12_
  77.7 3.9 %all-to-all-start.2 = ((bf16[32,24,384]{2,1,0:T(8,128)(2,1)}), bf16[32,24,384]{2,1,0:T(8,128)(2,1)S(1)}, u32[]{:S(2)}, u32[]{:S(2)}) async-start(bf16[32,24,384]{2,1,0:T(8,128)(2,1)} %bitcast.29), calls=%async_computation.2 | async-start | bytes 1179648 | tf_op jit(solution)/shard_map/all_to_all | solution.py:255
  81.6 2.3 %collective-permute-start.5 = (bf16[384,384]{1,0:T(8,128)(2,1)S(1)}, bf16[384,384]{1,0:T(8,128)(2,1)S(1)}, u32[]{:S(2)}, u32[]{:S(2)}) collective-permute-start(bf16[384,384]{1,0:T(8,128)(2,1)S(1)} %copy-done.9), channel_id=1, source_target_pairs={{0,32},{32,0},{1,33},{33,1},{2,34},{34,2},{3,35},{35,3},{4,36},{36... | collective-permute-start | bytes 884744 | tf_op jit(solution)/shard_map/ppermute | solution.py:251
  83.9 1.2 collective-permute-done.5.refs_4_
  85.1 0.7 copy-done.4
  85.8 6.5 %shard_map.87 = (f32[128,1536]{1,0:T(8,128)}, bf16[128,1536]{1,0:T(8,128)(2,1)}) custom-call(s32[2]{0:T(128)} %refs_0_.7, bf16[128,1536]{1,0:T(8,128)(2,1)} %bitcast.26, bf16[128,1536]{1,0:T(8,128)(2,1)} %copy-done.2, bf16[384,384]{1,0:T(8,128)(2,1)} %get-tuple-element.18.refs_3_, bf16[384,384]{1,0:T(8,128)(2,1)} %copy-done.4, ...), custom_call_target="tpu_custom_call" | custom-call | flops 1000 | bytes 5505032 | tf_op jit(solution)/shard_map/pallas_call | solution.py:235
  92.4 2.2 %collective-permute-start.7 = (bf16[128,1536]{1,0:T(8,128)(2,1)}, bf16[128,1536]{1,0:T(8,128)(2,1)S(1)}, u32[]{:S(2)}, u32[]{:S(2)}) collective-permute-start(bf16[128,1536]{1,0:T(8,128)(2,1)} %get-tuple-element.30), channel_id=1, source_target_pairs={{0,32},{32,0},{1,33},{33,1},{2,34},{34,2},{3,35},{35,3},{4,36},{36... | collective-permute-start | bytes 1179656 | tf_op jit(solution)/shard_map/ppermute | solution.py:251
  94.6 1.6 %collective-permute-done.7.refs_4_ = bf16[128,1536]{1,0:T(8,128)(2,1)S(1)} collective-permute-done((bf16[128,1536]{1,0:T(8,128)(2,1)}, bf16[128,1536]{1,0:T(8,128)(2,1)S(1)}, u32[]{:S(2)}, u32[]{:S(2)}) %collective-permute-start.7) | collective-permute-done | bytes 393248 | tf_op jit(solution)/shard_map/ppermute | solution.py:251
  96.2 0.8 copy-done.3
  96.9 2.5 %shard_map.88 = bf16[128,2688]{1,0:T(8,128)(2,1)} custom-call(s32[2]{0:T(128)} %refs_0_.7, bf16[128,1536]{1,0:T(8,128)(2,1)} %bitcast.27, f32[768]{0:T(1024)} %refs_2_.3, f32[128,1536]{1,0:T(8,128)} %get-tuple-element.29.refs_3_, bf16[128,1536]{1,0:T(8,128)(2,1)} %copy-done.3), custom_call_target="tpu_custom_call" | custom-call | flops 1000 | bytes 2264072 | tf_op jit(solution)/shard_map/pallas_call | solution.py:235
  99.5 0.1 reduce_sum.21
  99.6 0.7 broadcast_dynamic-update-slice_fusion
  100.3 27.5 %all_to_all.21 = bf16[16,8,2688]{2,1,0:T(8,128)(2,1)S(1)} all-to-all(bf16[16,8,2688]{2,1,0:T(8,128)(2,1)} %broadcast_dynamic-update-slice_fusion), channel_id=1, replica_groups=mesh['y'=8,'core'=2,'x'=4,'z'=8] {'y','core'}, dimensions={0} | all-to-all | bytes 1376256 | tf_op jit(solution)/shard_map/all_to_all | solution.py:255
  127.9 0.6 copy.10
  128.5 0.8 slice_bitcast_fusion
  (30 shorter events, 0.2 us)
Async XLA Ops:
  0.6 35.5 %copy-start.6 = (bf16[1,128,768]{2,1,0:T(8,128)(2,1)S(1)}, bf16[1,128,768]{2,1,0:T(8,128)(2,1)}, u32[]{:S(2)}) copy-start(bf16[1,128,768]{2,1,0:T(8,128)(2,1)} %param.6) | copy-start | bytes 589828
  0.6 35.5 %copy-start.5 = (bf16[1,128,768]{2,1,0:T(8,128)(2,1)S(1)}, bf16[1,128,768]{2,1,0:T(8,128)(2,1)}, u32[]{:S(2)}) copy-start(bf16[1,128,768]{2,1,0:T(8,128)(2,1)} %param.7) | copy-start | bytes 589828
  29.7 33.9 %copy-start.1 = (bf16[8,24,1536]{2,1,0:T(8,128)(2,1)}, bf16[8,24,1536]{2,1,0:T(8,128)(2,1)S(1)}, u32[]{:S(2)}) copy-start(bf16[8,24,1536]{2,1,0:T(8,128)(2,1)S(1)} %all_to_all.20) | copy-start | bytes 1769476
  29.7 17.4 %collective-permute-start.1 = (bf16[192,1536]{1,0:T(8,128)(2,1)S(1)}, bf16[192,1536]{1,0:T(8,128)(2,1)S(1)}, u32[]{:S(2)}, u32[]{:S(2)}) collective-permute-start(bf16[192,1536]{1,0:T(8,128)(2,1)S(1)} %bitcast.31), channel_id=1, source_target_pairs={{0,8},{8,16},{16,24},{24,0},{1,9},{9,17},{17,25},{25,1},{2,10},{10... | collective-permute-start | bytes 1769480 | tf_op jit(solution)/shard_map/ppermute | solution.py:251
  32.8 16.2 %collective-permute-start.2 = (bf16[192,1536]{1,0:T(8,128)(2,1)S(1)}, bf16[192,1536]{1,0:T(8,128)(2,1)S(1)}, u32[]{:S(2)}, u32[]{:S(2)}) collective-permute-start(bf16[192,1536]{1,0:T(8,128)(2,1)S(1)} %bitcast.32), channel_id=1, source_target_pairs={{0,24},{8,0},{16,8},{24,16},{1,25},{9,1},{17,9},{25,17},{2,26},{10... | collective-permute-start | bytes 1769480 | tf_op jit(solution)/shard_map/ppermute | solution.py:251
  37.0 24.6 %all-to-all-start.1 = ((bf16[16,8,1536]{2,1,0:T(8,128)(2,1)}), bf16[16,8,1536]{2,1,0:T(8,128)(2,1)S(1)}, u32[]{:S(2)}, u32[]{:S(2)}) async-start(bf16[16,8,1536]{2,1,0:T(8,128)(2,1)} %pad_maximum_fusion), calls=%async_computation.1 | async-start | bytes 786432 | tf_op jit(solution)/shard_map/all_to_all | solution.py:255
  47.1 16.5 %copy-start.7 = (bf16[192,1536]{1,0:T(8,128)(2,1)}, bf16[192,1536]{1,0:T(8,128)(2,1)S(1)}, u32[]{:S(2)}) copy-start(bf16[192,1536]{1,0:T(8,128)(2,1)S(1)} %collective-permute-done.1.refs_4_) | copy-start | bytes 1769476
  47.1 16.4 %collective-permute-start.3 = (bf16[96,1536]{1,0:T(8,128)(2,1)S(1)}, bf16[96,1536]{1,0:T(8,128)(2,1)S(1)}, u32[]{:S(2)}, u32[]{:S(2)}) collective-permute-start(bf16[96,1536]{1,0:T(8,128)(2,1)S(1)} %slice.20), channel_id=1, source_target_pairs={{0,8},{8,16},{16,24},{24,0},{1,9},{9,17},{17,25},{25,1},{2,10},{10... | collective-permute-start | bytes 884744 | tf_op jit(solution)/shard_map/ppermute | solution.py:251
  49.0 14.5 %copy-start.8 = (bf16[192,1536]{1,0:T(8,128)(2,1)}, bf16[192,1536]{1,0:T(8,128)(2,1)S(1)}, u32[]{:S(2)}) copy-start(bf16[192,1536]{1,0:T(8,128)(2,1)S(1)} %collective-permute-done.2.refs_5_) | copy-start | bytes 1769476
  49.1 14.5 %collective-permute-start.4 = (bf16[96,1536]{1,0:T(8,128)(2,1)S(1)}, bf16[96,1536]{1,0:T(8,128)(2,1)}, u32[]{:S(2)}, u32[]{:S(2)}) collective-permute-start(bf16[96,1536]{1,0:T(8,128)(2,1)S(1)} %slice.21), channel_id=1, source_target_pairs={{0,24},{8,0},{16,8},{24,16},{1,25},{9,1},{17,9},{25,17},{2,26},{10... | collective-permute-start | bytes 884744 | tf_op jit(solution)/shard_map/ppermute | solution.py:251
  61.6 2.0 %copy-start = (bf16[16,8,1536]{2,1,0:T(8,128)(2,1)}, bf16[16,8,1536]{2,1,0:T(8,128)(2,1)S(1)}, u32[]{:S(2)}) copy-start(bf16[16,8,1536]{2,1,0:T(8,128)(2,1)S(1)} %all-to-all-done.1) | copy-start | bytes 1179652
  61.6 6.6 %collective-permute-start = (bf16[128,1536]{1,0:T(8,128)(2,1)S(1)}, bf16[128,1536]{1,0:T(8,128)(2,1)S(1)}, u32[]{:S(2)}, u32[]{:S(2)}) collective-permute-start(bf16[128,1536]{1,0:T(8,128)(2,1)S(1)} %bitcast.23), channel_id=1, source_target_pairs={{0,32},{32,0},{1,33},{33,1},{2,34},{34,2},{3,35},{35,3},{4,36},{36... | collective-permute-start | bytes 1179656 | tf_op jit(solution)/shard_map/ppermute | solution.py:251
  63.5 0.7 copy-start.10
  68.2 0.8 copy-start.2
  73.0 8.6 %copy-start.9 = (bf16[384,384]{1,0:T(8,128)(2,1)S(1)}, bf16[384,384]{1,0:T(8,128)(2,1)}, u32[]{:S(2)}) copy-start(bf16[384,384]{1,0:T(8,128)(2,1)} %get-tuple-element.19) | copy-start | bytes 884740
  73.0 3.9 %collective-permute-start.6 = (bf16[384,384]{1,0:T(8,128)(2,1)}, bf16[384,384]{1,0:T(8,128)(2,1)S(1)}, u32[]{:S(2)}, u32[]{:S(2)}) collective-permute-start(bf16[384,384]{1,0:T(8,128)(2,1)} %get-tuple-element.28), channel_id=1, source_target_pairs={{0,32},{32,0},{1,33},{33,1},{2,34},{34,2},{3,35},{35,3},{4,36},{36... | collective-permute-start | bytes 884744 | tf_op jit(solution)/shard_map/ppermute | solution.py:251
  77.7 21.8 %all-to-all-start.2 = ((bf16[32,24,384]{2,1,0:T(8,128)(2,1)}), bf16[32,24,384]{2,1,0:T(8,128)(2,1)S(1)}, u32[]{:S(2)}, u32[]{:S(2)}) async-start(bf16[32,24,384]{2,1,0:T(8,128)(2,1)} %bitcast.29), calls=%async_computation.2 | async-start | bytes 1179648 | tf_op jit(solution)/shard_map/all_to_all | solution.py:255
  81.6 3.5 %collective-permute-start.5 = (bf16[384,384]{1,0:T(8,128)(2,1)S(1)}, bf16[384,384]{1,0:T(8,128)(2,1)S(1)}, u32[]{:S(2)}, u32[]{:S(2)}) collective-permute-start(bf16[384,384]{1,0:T(8,128)(2,1)S(1)} %copy-done.9), channel_id=1, source_target_pairs={{0,32},{32,0},{1,33},{33,1},{2,34},{34,2},{3,35},{35,3},{4,36},{36... | collective-permute-start | bytes 884744 | tf_op jit(solution)/shard_map/ppermute | solution.py:251
  85.1 0.7 copy-start.4
  92.4 3.8 %collective-permute-start.7 = (bf16[128,1536]{1,0:T(8,128)(2,1)}, bf16[128,1536]{1,0:T(8,128)(2,1)S(1)}, u32[]{:S(2)}, u32[]{:S(2)}) collective-permute-start(bf16[128,1536]{1,0:T(8,128)(2,1)} %get-tuple-element.30), channel_id=1, source_target_pairs={{0,32},{32,0},{1,33},{33,1},{2,34},{34,2},{3,35},{35,3},{4,36},{36... | collective-permute-start | bytes 1179656 | tf_op jit(solution)/shard_map/ppermute | solution.py:251
  96.2 0.8 copy-start.3
